TPU v7x, 32 devices: a whole 2x2x4 slice. The times are simulated.
32 devices in a mesh: img: 8 (over y, x, core), slab: 4 (over z).
Axes of the slice: x: 2, y: 2, z: 4, core: 2. Of those that a mesh axis runs over, the one named last changes fastest.
Arguments:
- images: bfloat16 [512, 32768], P('img'), may hold values from -6 to 6
- references: bfloat16 [2, 128, 32768], P(None, 'slab'), may hold values from -6 to 6
- orientations: int32 [512, 2, 64], P('img'), may hold values from 0 to 127
- ctf_table: float32 [512, 64], P('img'), may hold values from -1 to 1
- inv_noise: float32 [512], P('img'), may hold values from 0.002 to 0.02
- class_weight: float32 [2], replicated, may hold values from 0.2 to 5
Outputs:
- updated_volume: float32 [2, 128, 32768], P(None, 'slab', 'img')
All inputs are finite; a program needn't handle non-finite values.
Results may differ from a plain program's by a relative error of at most 0.0065.
Values sent between devices are 32-bit elements; how exact they have to be, the bound alone decides.
No kernel may reach another device: no remote copies, remote signals or barrier semaphores. Data moves between devices by JAX's collectives and lax.ppermute only.
A program may use at most 192 MiB of HBM per device.

v0:
```python
import jax
import jax.numpy as jnp
from jax import lax
from jax.sharding import PartitionSpec as P

BOX = 128
SHELLS = 64


def shell_index():
    position = jnp.arange(BOX * BOX, dtype=jnp.int32)
    column = position % BOX - BOX // 2
    row_place = position // BOX - BOX // 2
    radius_sq = column * column + row_place * row_place
    levels = jnp.arange(1, SHELLS, dtype=jnp.int32)
    inside = (2 * levels[None, :] * levels[None, :] <= radius_sq[:, None]).astype(jnp.int32)
    return jnp.sum(inside, axis=1)


def contract_first(left, right):
    return lax.dot_general(
        left, right, (((0,), (0,)), ((), ())), preferred_element_type=jnp.float32
    )


def contract_last(left, right):
    return lax.dot_general(
        left, right, (((1,), (1,)), ((), ())), preferred_element_type=jnp.float32
    )


def shards(images, references, orientations, ctf_table, inv_noise, class_weight):
    batch = images.shape[0]
    classes, local_planes, width = references.shape
    pixels = width // 2
    levels = jnp.arange(SHELLS, dtype=jnp.int32)
    selector = (shell_index()[None, :] == levels[:, None]).astype(jnp.float32)
    ctf_pixel = jnp.dot(
        ctf_table, selector, precision=lax.Precision.HIGHEST, preferred_element_type=jnp.float32
    )
    weighted = (images.astype(jnp.float32) * jnp.repeat(ctf_pixel, 2, axis=1)).astype(jnp.bfloat16)
    ctf_square = (ctf_pixel * ctf_pixel).astype(jnp.bfloat16)
    planes = references.reshape(classes * local_planes, width)
    spread = references.astype(jnp.float32).reshape(classes * local_planes, pixels, 2)
    power = jnp.sum(spread * spread, axis=2).astype(jnp.bfloat16)
    intersection = contract_last(weighted, planes)
    energy = contract_last(ctf_square, power)
    local_table = (2.0 * intersection - energy).reshape(batch, classes, local_planes)
    offset = lax.axis_index("slab") * local_planes
    relative = orientations - offset
    inside = (relative >= 0) & (relative < local_planes)
    prior = jnp.log(class_weight)[None, :, None]
    table = lax.all_gather(local_table, "slab", axis=2, tiled=True)
    picked = jnp.take_along_axis(table, orientations, axis=2)
    scores = prior + inv_noise[:, None, None] * picked
    peak = jnp.max(scores, axis=(1, 2), keepdims=True)
    expo = jnp.exp(scores - peak)
    resp = expo / jnp.sum(expo, axis=(1, 2), keepdims=True)
    local_resp = jnp.where(inside, resp, 0.0)
    plane_ids = jnp.arange(local_planes, dtype=jnp.int32)
    hits = (relative[:, :, :, None] == plane_ids[None, None, None, :]).astype(jnp.float32)
    per_plane = jnp.einsum("bkl,bklp->bkp", local_resp, hits).astype(jnp.bfloat16)
    flat_plane = per_plane.reshape(batch, classes * local_planes)
    share = width // lax.axis_size("img")
    shell_squares = (ctf_table * ctf_table).astype(jnp.bfloat16)
    local_shells = contract_first(shell_squares, flat_plane)
    numerator = lax.psum_scatter(
        contract_first(weighted, flat_plane), "img", scatter_dimension=0, tiled=True
    )
    shell_sums = lax.psum(local_shells, "img")
    first_pixel = lax.axis_index("img") * (share // 2)
    pixel_select = lax.dynamic_slice_in_dim(selector, first_pixel, share // 2, 1)
    pixel_weights = lax.dot_general(
        pixel_select,
        shell_sums,
        (((0,), (0,)), ((), ())),
        precision=lax.Precision.HIGHEST,
        preferred_element_type=jnp.float32,
    )
    weight_sum = jnp.repeat(pixel_weights, 2, axis=0)
    updated = numerator / (weight_sum + 1.0)
    return jnp.transpose(updated).reshape(classes, local_planes, share)


def solution(mesh):
    return jax.shard_map(
        shards,
        mesh=mesh,
        in_specs=(
            P("img", None),
            P(None, "slab", None),
            P("img", None, None),
            P("img", None),
            P("img"),
            P(),
        ),
        out_specs=P(None, "slab", "img"),
        check_vma=False,
    )
```

profile of v0, /device:TPU:0, one launch (start us, length us, event | category | flops | bytes accessed | tf_op | source)
XLA Modules:
  0.0 394.7 jit_solution(5890838617544843644)
XLA Ops:
  6.6 6.0 %convert_multiply_fusion = f32[2,32,32768]{2,1,0:T(8,128)} fusion(bf16[2,32,32768]{2,1,0:T(8,128)(2,1)} %param.7), kind=kLoop, calls=%fused_computation.3 | loop fusion | flops 4194304 | bytes 12582912 | tf_op jit(solution)/shard_map/mul | solution.py:45
  12.5 37.3 %copy.38 = f32[2,32,32768]{1,0,2:T(2,128)} copy(f32[2,32,32768]{2,1,0:T(8,128)} %convert_multiply_fusion) | data formatting | bytes 16777216 | tf_op jit(solution)/shard_map/mul | solution.py:45
  49.9 37.1 %mul.80 = f32[64,16384,2]{0,2,1:T(2,128)} reshape(f32[2,32,32768]{1,0,2:T(2,128)} %copy.38) | data formatting | bytes 16777216 | tf_op jit(solution)/shard_map/mul | solution.py:45
  87.0 0.6 convert_reduce_fusion
  87.6 3.9 convolution_bitcast_fusion
  91.5 6.9 %copy.37 = f32[64,16384]{0,1:T(8,128)} copy(f32[64,16384]{1,0:T(8,128)} %convolution_bitcast_fusion) | data formatting | bytes 8388608 | tf_op jit(solution)/shard_map/dot_general | solution.py:38
  98.4 73.1 %reduce_sum.28 = bf16[64,16384]{0,1:T(8,128)(2,1)} reduce(f32[64,16384,2]{0,2,1:T(2,128)} %mul.80, f32[]{:T(128)} %constant.69.clone.1), dimensions={2}, to_apply=%region_1.2 | reduce | flops 1048576 | bytes 10485764 | tf_op jit(solution)/shard_map/reduce_sum | solution.py:45
  171.6 4.3 %fusion = f32[64,64]{1,0:T(8,128)S(1)} fusion(bf16[64,16384]{0,1:T(8,128)(2,1)} %reduce_sum.28, f32[64,16384]{1,0:T(8,128)} %convolution_bitcast_fusion), kind=kOutput, calls=%fused_computation.4 | convolution fusion | flops 136314880 | bytes 6307840 | tf_op jit(solution)/shard_map/dot_general | solution.py:27
  175.9 8.5 %copy.36 = bf16[64,32768]{0,1:T(8,128)(2,1)} copy(bf16[64,32768]{1,0:T(8,128)(2,1)} %param.6) | data formatting | bytes 8388608 | tf_op args[0]
  184.4 9.6 %broadcast_in_dim.11 = f32[64,16384,2]{0,2,1:T(2,128)} broadcast(f32[64,16384]{0,1:T(8,128)} %copy.37), dimensions={0,1} | broadcast | bytes 12582912 | tf_op jit(solution)/shard_map/broadcast_in_dim | solution.py:41
  194.3 10.8 %fusion.3 = f32[64,64]{1,0:T(8,128)S(1)} fusion(f32[64,64]{1,0:T(8,128)S(1)} %fusion, bf16[64,32768]{1,0:T(8,128)(2,1)S(1)} %bitcast.31, f32[64,32768]{0,1:T(8,128)} %bitcast.29, bf16[64,32768]{0,1:T(8,128)(2,1)} %copy.36), kind=kOutput, calls=%fused_computation.13 | convolution fusion | flops 274735104 | bytes 16809984 | tf_op jit(solution)/shard_map/dot_general | solution.py:27
  205.3 15.0 %all_gather.3 = f32[64,2,128]{0,1,2:T(2,128)S(1)} all-gather(f32[64,2,32]{0,1,2:T(2,128)S(1)} %copy.40), channel_id=1, replica_groups=mesh['img'=8,'slab'=4] {'slab'}, dimensions={2}, use_global_device_ids=true | all-gather | bytes 81920 | tf_op jit(solution)/shard_map/all_gather | solution.py:53
  220.5 74.6 %gather_fusion = f32[8192]{0:T(1024)S(1)} fusion(f32[64,2,128]{0,1,2:T(2,128)S(1)} %all_gather.3, s32[8192]{0:T(1024)S(1)} %reshape.74), kind=kCustom, calls=%fused_computation | custom fusion | bytes 163840 | tf_op jit(solution)/shard_map/jit(take_along_axis)/gather | solution.py:54
  295.3 0.9 fusion.24
  296.3 1.0 fusion.20
  297.5 0.7 fusion.2
  298.2 14.4 %fusion.23 = f32[32768,64]{0,1:T(8,128)} fusion(bf16[64,64]{0,1:T(8,128)(2,1)S(1)} %bitcast.33, f32[64,32768]{0,1:T(8,128)} %bitcast.30, bf16[64,32768]{0,1:T(8,128)(2,1)} %copy.36), kind=kOutput, calls=%fused_computation.46 | convolution fusion | flops 274726912 | bytes 20979712 | tf_op jit(solution)/shard_map/dot_general | solution.py:21
  312.8 22.4 %psum.7 = f32[64,64]{1,0:T(8,128)S(1)} all-reduce(f32[64,64]{1,0:T(8,128)S(1)} %fusion.21), channel_id=1, replica_groups=mesh['img'=8,'slab'=4] {'img'}, use_global_device_ids=true, to_apply=%region_5.6 | all-reduce | flops 4096 | bytes 32768 | tf_op jit(solution)/shard_map/psum | solution.py:70
  335.2 0.5 iota_compare_fusion
  335.7 0.4 convolution_add_fusion
  336.5 0.8 broadcast_in_dim.15
  337.2 0.6 copy.42
  337.8 47.6 %reduce-scatter.2.cloned.1.call-done = f32[4096,64]{0,1:T(8,128)} async-done(((f32[32768,64]{0,1:T(8,128)}), f32[4096,64]{0,1:T(8,128)}) %reduce-scatter.2.cloned.1.call-update) | async-done | bytes 1048592 | tf_op jit(solution)/shard_map/reduce_scatter | solution.py:67
  385.5 2.3 div.23
  (24 shorter events, 1.6 us)
Async XLA Ops:
  6.5 379.0 %reduce-scatter.2.cloned.1.call-start = ((), (), s32[]{:S(2)}) async-start(), calls=%async_computation.1 | async-start | bytes 9437184 | tf_op jit(solution)/shard_map/reduce_scatter | solution.py:67
  49.9 37.7 %copy-start.2 = (f32[64,64]{1,0:T(8,128)S(1)}, f32[64,64]{1,0:T(8,128)}, u32[]{:S(2)}) copy-start(f32[64,64]{1,0:T(8,128)} %param.9) | copy-start | bytes 49156
  184.4 9.9 %copy-start = (bf16[2,32,32768]{2,1,0:T(8,128)(2,1)S(1)}, bf16[2,32,32768]{2,1,0:T(8,128)(2,1)}, u32[]{:S(2)}) copy-start(bf16[2,32,32768]{2,1,0:T(8,128)(2,1)} %param.7) | copy-start | bytes 12582916
  194.3 26.0 %copy-start.1 = (s32[64,2,64]{2,1,0:T(2,128)S(1)}, s32[64,2,64]{2,1,0:T(2,128)}, u32[]{:S(2)}) copy-start(s32[64,2,64]{2,1,0:T(2,128)} %param.8) | copy-start | bytes 98308
  220.5 74.8 %copy-start.4 = (f32[2]{0:T(128)S(1)}, f32[2]{0:T(128)}, u32[]{:S(2)}) copy-start(f32[2]{0:T(128)} %param.11) | copy-start | bytes 28
  220.5 74.8 %copy-start.3 = (f32[64]{0:T(128)S(1)}, f32[64]{0:T(128)}, u32[]{:S(2)}) copy-start(f32[64]{0:T(128)} %param.10) | copy-start | bytes 772
Sparse Core Ops, SparseCore 0:
  312.7 72.6 reduce-scatter.1
where the time goes:
time: 397 us; the launch traced here: 395 us
  local copies, waits for them, and re-layouts  177 us (45%)
  other arithmetic  84.8 us (21%)
  waiting for transfers between devices  47.7 us (12%)
  blocking collectives  37.4 us (9%)
  matrix products  34.7 us (9%)
  between operations  13.5 us (3%)
    gather x3, local copies, waits for them, and re-layouts, shards(): picked = jnp.take_along_axis(table, orientations, axis=2)  74.8 us
    mul x2, local copies, waits for them, and re-layouts, shards(): power = jnp.sum(spread * spread, axis=2).astype(jnp.bfloat16)  74.5 us
    reduce_sum x1, other arithmetic, shards(): power = jnp.sum(spread * spread, axis=2).astype(jnp.bfloat16)  73.1 us
    reduce_scatter x1, waiting for transfers between devices, shards(): lax.psum_scatter(contract_first(weighted, flat_plane), 'img', scatter_dim...  47.6 us
    psum x1, blocking collectives, shards(): shell_sums = lax.psum(local_shells, 'img')  22.4 us
    dot_general x2, matrix products, contract_last(): lax.dot_general(left, right, (((1,), (1,)), ((), ())), preferred_element_...  15.2 us
    all_gather x1, blocking collectives, shards(): table = lax.all_gather(local_table, 'slab', axis=2, tiled=True)  15 us
    dot_general x2, matrix products, contract_first(): lax.dot_general(left, right, (((0,), (0,)), ((), ())), preferred_element_...  14.6 us
  transfers between devices with their start and end apart: 1, of which 1 were waited for; matrix products, arithmetic and copies ran while one was open for 1% of the time, Pallas kernels for 0%

commit v1 on v0

v1 whole, which is shorter than its diff:
```python
import functools
import math

import jax
import jax.numpy as jnp
import numpy as np
from jax import lax
from jax.experimental import pallas as pl
from jax.experimental.pallas import tpu as pltpu
from jax.sharding import PartitionSpec as P

F32 = jnp.float32
BF16 = jnp.bfloat16
LANES = 128
VMEM_LIMIT = 48 * 1024 * 1024


def entry_shells(width, shells):
    pixels = width // 2
    box = math.isqrt(pixels)
    place = np.arange(pixels)
    column = place % box - box // 2
    row = place // box - box // 2
    radius = column * column + row * row
    levels = np.arange(1, shells)
    shell = np.sum(2 * levels[None, :] ** 2 <= radius[:, None], axis=1)
    return np.repeat(shell, 2).astype(np.int32)[None, :]


def params(**more):
    return pltpu.CompilerParams(vmem_limit_bytes=VMEM_LIMIT, **more)


def lanes_wide(table):
    rows, shells = table.shape
    if shells == LANES:
        return table
    return jnp.concatenate([table, jnp.zeros((rows, LANES - shells), table.dtype)], axis=1)


def spread(table, index):
    return jnp.take_along_axis(table, jnp.broadcast_to(index, table.shape), axis=1)


def contract_last(left, right):
    return lax.dot_general(left, right, (((1,), (1,)), ((), ())), preferred_element_type=F32)


def estep_kernel(
    chips, me_ref, index_ref, image_ref, plane_ref, ctf_ref, noise_ref, prior_ref,
    give_ref, keep_ref, score_ref, table, weighted, squared, energy_of, total,
):
    step = pl.program_id(0)

    @pl.when(step == 0)
    def _():
        table[...] = lanes_wide(ctf_ref[...])
        total[...] = jnp.zeros_like(total)

    held = table[...]
    for start in range(0, image_ref.shape[1], LANES):
        cut = slice(start, start + LANES)
        ctf = spread(held, index_ref[:, cut])
        weighted[:, cut] = (image_ref[:, cut].astype(F32) * ctf).astype(BF16)
        squared[:, cut] = (ctf * ctf).astype(BF16)
        plane = plane_ref[:, cut].astype(F32)
        energy_of[:, cut] = (plane * plane).astype(BF16)
    fit = contract_last(weighted[...], plane_ref[...])
    energy = contract_last(squared[...], energy_of[...])
    total[...] += 2.0 * fit - energy

    @pl.when(step < chips)
    def _():
        give_ref[0] = weighted[...].astype(F32)

    @pl.when(step >= chips)
    def _():
        keep_ref[0] = weighted[...]

    @pl.when(step == pl.num_programs(0) - 1)
    def _():
        rows = total.shape[0]
        noise = jnp.broadcast_to(noise_ref[...], (rows, rows))
        diagonal = lax.broadcasted_iota(jnp.int32, (rows, rows), 0) == lax.broadcasted_iota(
            jnp.int32, (rows, rows), 1
        )
        column = jnp.sum(jnp.where(diagonal, noise, 0.0), axis=1, keepdims=True)
        classes = prior_ref.shape[0]
        lane = lax.broadcasted_iota(jnp.int32, total.shape, 1)
        each = total.shape[1] // classes
        weight = jnp.full(total.shape, prior_ref[0], F32)
        for one in range(1, classes):
            weight = jnp.where(lane >= one * each, prior_ref[one], weight)
        score_ref[...] = jnp.log(weight) + column * total[...]


def estep(me, index, images, planes, ctf_table, inv_noise, class_weight, share):
    rows, width = images.shape
    parts = width // share
    chips = parts // 2
    count = planes.shape[0]
    shells = ctf_table.shape[1]

    def block(step, me_ref):
        mine = me_ref[0]
        chip = (mine // 2) ^ (step % chips)
        core = jnp.where(step < chips, 1 - mine % 2, mine % 2)
        return 0, chip * 2 + core

    def whole(step, me_ref):
        return 0, 0

    grid_spec = pltpu.PrefetchScalarGridSpec(
        num_scalar_prefetch=1,
        grid=(parts,),
        in_specs=[
            pl.BlockSpec((1, share), block),
            pl.BlockSpec((rows, share), block),
            pl.BlockSpec((count, share), block),
            pl.BlockSpec((rows, shells), whole),
            pl.BlockSpec((1, rows), whole),
            pl.BlockSpec(memory_space=pltpu.SMEM),
        ],
        out_specs=[
            pl.BlockSpec((1, rows, share), lambda s, m: (jnp.minimum(s, chips - 1), 0, 0)),
            pl.BlockSpec((1, rows, share), lambda s, m: (jnp.maximum(s - chips, 0), 0, 0)),
            pl.BlockSpec((rows, count), whole),
        ],
        scratch_shapes=[
            pltpu.VMEM((rows, LANES), F32),
            pltpu.VMEM((rows, share), BF16),
            pltpu.VMEM((rows, share), BF16),
            pltpu.VMEM((count, share), BF16),
            pltpu.VMEM((rows, count), F32),
        ],
    )
    return pl.pallas_call(
        functools.partial(estep_kernel, chips),
        grid_spec=grid_spec,
        out_shape=[
            jax.ShapeDtypeStruct((chips, rows, share), F32),
            jax.ShapeDtypeStruct((chips, rows, share), BF16),
            jax.ShapeDtypeStruct((rows, count), F32),
        ],
        compiler_params=params(),
        name="estep",
    )(me, index, images, planes, ctf_table, inv_noise.reshape(1, rows), class_weight)


def count_kernel(slabs, slab_ref, list_ref, out_ref):
    rows, listed = list_ref.shape
    classes = out_ref.shape[0]
    each = listed // classes
    width = out_ref.shape[2]
    local = width // slabs
    lane = lax.broadcasted_iota(jnp.int32, (rows, width), 1)
    home = lax.rem(slab_ref[0] - lane // local + slabs, slabs)
    plane = home * local + lax.rem(lane, local)
    for one in range(classes):
        sums = jnp.zeros((rows, width), F32)
        for entry in range(each):
            place = one * each + entry
            sums += jnp.where(list_ref[:, place : place + 1] == plane, 1.0, 0.0)
        out_ref[one] = sums


def count_planes(slab, orientations, width, slabs):
    rows, classes, each = orientations.shape
    return pl.pallas_call(
        functools.partial(count_kernel, slabs),
        in_specs=[
            pl.BlockSpec(memory_space=pltpu.SMEM),
            pl.BlockSpec(memory_space=pltpu.VMEM),
        ],
        out_specs=pl.BlockSpec(memory_space=pltpu.VMEM),
        out_shape=jax.ShapeDtypeStruct((classes, rows, width), F32),
        compiler_params=params(),
        cost_estimate=pl.CostEstimate(flops=10**7, bytes_accessed=10**6, transcendentals=0),
        name="count",
    )(slab, orientations.reshape(rows, classes * each))


def weigh_kernel(*refs):
    count_ref, out_ref = refs[0], refs[-1]
    scores = [ref[...] for ref in refs[1:-1]]
    classes = count_ref.shape[0]
    local = scores[0].shape[1] // classes
    fits, counts = [], []
    for one in range(classes):
        cut = slice(one * local, (one + 1) * local)
        counts.append(count_ref[one])
        fit = jnp.concatenate([score[:, cut] for score in scores], axis=1)
        fits.append(jnp.where(counts[-1] > 0.0, fit, -jnp.inf))
    peak = functools.reduce(jnp.maximum, [jnp.max(fit, axis=1, keepdims=True) for fit in fits])
    raw = [count * jnp.exp(fit - peak) for count, fit in zip(counts, fits)]
    total = functools.reduce(jnp.add, [jnp.sum(part, axis=1, keepdims=True) for part in raw])
    own = jnp.concatenate([part[:, :local] for part in raw], axis=1) / total
    out_ref[...] = own.T


def weigh(counts, scores):
    rows, planes = scores[0].shape
    return pl.pallas_call(
        weigh_kernel,
        out_shape=jax.ShapeDtypeStruct((planes, rows), F32),
        compiler_params=params(),
        name="weigh",
    )(counts, *scores)


def sums_kernel(items, cells, own_w_ref, sib_w_ref, own_ctf_ref, sib_ctf_ref, keep_ref, got_ref, out_ref, *shell_ref):
    weights = jnp.concatenate([own_w_ref[...], sib_w_ref[...]], axis=1).astype(BF16)
    rows = keep_ref.shape[1]
    images = jnp.concatenate([keep_ref[0], got_ref[0].astype(BF16)], axis=0)
    out_ref[0] = jnp.dot(weights, images, preferred_element_type=F32)
    if shell_ref:

        @pl.when(pl.program_id(1) == 0)
        def _():
            ctf = jnp.concatenate([own_ctf_ref[...], sib_ctf_ref[...]], axis=0)
            square = lanes_wide((ctf * ctf).astype(BF16))
            shell_ref[0][0] = jnp.dot(weights, square, preferred_element_type=F32)


def partial_sums(bits, half, own_w, sib_w, own_ctf, sib_ctf, keep, got, tile):
    first, step, number = bits
    chips, rows, share = keep.shape
    planes = own_w.shape[0]
    cells = share // (2 * tile)

    def source(item, cell):
        return first + step * item, 0, 2 * cell + half

    def whole(item, cell):
        return 0, 0

    small = [pl.BlockSpec(array.shape, whole) for array in (own_w, sib_w, own_ctf, sib_ctf)]
    out_specs = [pl.BlockSpec((1, planes, tile), lambda item, cell: (item, 0, cell))]
    out_shape = [jax.ShapeDtypeStruct((number, planes, cells * tile), F32)]
    if half == 0:
        out_specs.append(pl.BlockSpec((1, planes, LANES), lambda item, cell: (item, 0, 0)))
        out_shape.append(jax.ShapeDtypeStruct((number, planes, LANES), F32))
    return pl.pallas_call(
        functools.partial(sums_kernel, number, cells),
        grid=(number, cells),
        in_specs=small
        + [pl.BlockSpec((1, rows, tile), source), pl.BlockSpec((1, rows, tile), source)],
        out_specs=out_specs,
        out_shape=out_shape,
        compiler_params=params(),
        name="sums",
    )(own_w, sib_w, own_ctf, sib_ctf, keep, got)


def finish_kernel(number, index_ref, *refs):
    out_ref = refs[-1]
    shells = functools.reduce(jnp.add, [ref[0] for ref in refs[:number]])
    left = functools.reduce(jnp.add, [ref[0] for ref in refs[number : 2 * number]])
    right = functools.reduce(jnp.add, [ref[0] for ref in refs[2 * number : 3 * number]])
    tile = left.shape[1]
    for side, block in ((0, left), (1, right)):
        for start in range(0, tile, LANES):
            cut = slice(side * tile + start, side * tile + start + LANES)
            weight = spread(shells, index_ref[:, cut])
            out_ref[:, cut] = block[:, start : start + LANES] / (weight + 1.0)


def finish(index, me, shells, left, right, share, tile):
    planes = left[0].shape[1]
    number = len(left)
    cells = share // (2 * tile)
    side = pl.BlockSpec((1, planes, tile), lambda cell, m: (0, 0, cell))
    grid_spec = pltpu.PrefetchScalarGridSpec(
        num_scalar_prefetch=1,
        grid=(cells,),
        in_specs=[pl.BlockSpec((1, 2 * tile), lambda cell, m: (0, m[0] * cells + cell))]
        + [pl.BlockSpec((1, planes, LANES), lambda cell, m: (0, 0, 0))] * number
        + [side] * (2 * number),
        out_specs=pl.BlockSpec((planes, 2 * tile), lambda cell, m: (0, cell)),
    )

    def body(me_ref, *refs):
        finish_kernel(number, *refs)

    return pl.pallas_call(
        body,
        grid_spec=grid_spec,
        out_shape=jax.ShapeDtypeStruct((planes, share), F32),
        compiler_params=params(),
        name="finish",
    )(me, index, *shells, *left, *right)


def swap(array, bit, size):
    return lax.ppermute(array, "img", [(one, one ^ bit) for one in range(size)])


def shards(images, references, orientations, ctf_table, inv_noise, class_weight):
    rows, width = images.shape
    classes, local_planes, _ = references.shape
    size = lax.axis_size("img")
    slabs = lax.axis_size("slab")
    chips = size // 2
    share = width // size
    tile = share // 4
    me = lax.axis_index("img").astype(jnp.int32).reshape(1)
    slab = lax.axis_index("slab").astype(jnp.int32).reshape(1)
    index = jnp.asarray(entry_shells(width, ctf_table.shape[1]))
    planes = references.reshape(classes * local_planes, width)

    give, keep, score = estep(me, index, images, planes, ctf_table, inv_noise, class_weight, share)
    sib_ctf = swap(ctf_table, 1, size)
    scores = [score] + [
        lax.ppermute(score, "slab", [(one, (one + hop) % slabs) for one in range(slabs)])
        for hop in range(1, slabs)
    ]
    got = swap(give, 1, size)
    counts = count_planes(slab, orientations, slabs * local_planes, slabs)
    own_w = weigh(counts, scores)
    sib_w = swap(own_w, 1, size)

    sums = functools.partial(
        partial_sums,
        own_w=own_w, sib_w=sib_w, own_ctf=ctf_table, sib_ctf=sib_ctf, keep=keep, got=got, tile=tile,
    )
    top = chips // 2
    send_left, send_shells = sums((1, 2, top), 0)
    left_in = swap(send_left, 2, size)
    (send_right,) = sums((top, 1, top), 1)
    right_in = swap(send_right, 2 * top, size)
    shells_in = swap(send_shells, 2, size)
    keep_left, keep_shells = sums((0, 2, top), 0)
    (keep_right,) = sums((0, 1, top), 1)

    lefts, rights, shells = [keep_left, left_in], [keep_right, right_in], [keep_shells, shells_in]
    bit = 2
    while bit < chips:
        number = rights[-1].shape[0] // 2
        left_out = sum(part[1::2] for part in lefts)
        shells_out = sum(part[1::2] for part in shells)
        right_out = sum(part[number:] for part in rights)
        if number > 1:
            lefts = [part[0::2] for part in lefts]
            shells = [part[0::2] for part in shells]
            rights = [part[:number] for part in rights]
        lefts.append(swap(left_out, 2 * bit, size))
        rights.append(swap(right_out, chips // bit, size))
        shells.append(swap(shells_out, 2 * bit, size))
        bit *= 2
    out = finish(index, me, shells, lefts, rights, share, tile)
    return out.reshape(classes, local_planes, share)


def solution(mesh):
    return jax.shard_map(
        shards,
        mesh=mesh,
        in_specs=(
            P("img", None),
            P(None, "slab", None),
            P("img", None, None),
            P("img", None),
            P("img"),
            P(),
        ),
        out_specs=P(None, "slab", "img"),
        check_vma=False,
    )
```

time: 397 us -> 77.5 us (0.20)
  local copies, waits for them, and re-layouts: 177 us -> 2.33 us
  other arithmetic: 84.8 us -> 0.12 us
  blocking collectives: 37.4 us -> 0 us
  matrix products: 34.7 us -> 0 us
  Pallas kernels: 0 us -> 26.7 us
  waiting for transfers between devices: 47.7 us -> 34.3 us
  between operations: 13.5 us -> 0.1 us
  starting transfers between devices: 0.01 us -> 13.4 us
    gather x3 -> x0, local copies, waits for them, and re-layouts: 74.8 us -> none  [shards(): picked = jnp.take_along_axis(table, orientations, axis=2)]
    reduce_sum x3 -> x0, other arithmetic: 74.7 us -> none  [the longest x1 73.1 us: shards(): power = jnp.sum(spread * spread, axis=2).astype(jnp.bfloat16)]
    mul x2 -> x0, local copies, waits for them, and re-layouts: 74.5 us -> none  [shards(): power = jnp.sum(spread * spread, axis=2).astype(jnp.bfloat16)]
    reduce_scatter x1 -> x0, waiting for transfers between devices: 47.6 us -> none  [shards(): lax.psum_scatter(contract_first(weighted, flat_plane), 'img', scatter_dim...]
    dot_general x7 -> x0, matrix products: 34.7 us -> none  [the longest x2 15.2 us: contract_last(): lax.dot_general(left, right, (((1,), (1,)), ((), ())), preferred_element_...]
    ppermute x0 -> x12, waiting for transfers between devices: none -> 34.3 us  [the longest x9 31.1 us: swap(): return lax.ppermute(array, 'img', [(one, one ^ bit) for one in range(size)])]
    pallas_call x0 -> x8, Pallas kernels: none -> 26.7 us  [the longest x1 11.9 us: estep(): pl.pallas_call(functools.partial(estep_kernel, chips), grid_spec=grid_spe...]
    psum x1 -> x0, blocking collectives: 22.4 us -> none  [shards(): shell_sums = lax.psum(local_shells, 'img')]
  transfers between devices with their start and end apart: 1 -> 12, of which waited for: 1 -> 7; matrix products, arithmetic and copies ran while one was open for 1% -> 0% of each run, Pallas kernels for 0% -> 14%
where the time goes in v1:
time: 77.5 us; the launch traced here: 77 us
  waiting for transfers between devices  34.3 us (44%)
  Pallas kernels  26.7 us (34%)
  starting transfers between devices  13.4 us (17%)
  local copies, waits for them, and re-layouts  2.33 us (3%)
    ppermute x9, waiting for transfers between devices, swap(): return lax.ppermute(array, 'img', [(one, one ^ bit) for one in range(size)])  31.1 us
    pallas_call x1, Pallas kernels, estep(): pl.pallas_call(functools.partial(estep_kernel, chips), grid_spec=grid_spe...  11.9 us
    pallas_call x4, Pallas kernels, partial_sums(): pl.pallas_call(functools.partial(sums_kernel, number, cells), grid=(numbe...  11.6 us
    ppermute x9, starting transfers between devices, swap(): return lax.ppermute(array, 'img', [(one, one ^ bit) for one in range(size)])  7.8 us
    ppermute x3, starting transfers between devices, shards(): lax.ppermute(score, 'slab', [(one, (one + hop) % slabs) for one in range(...  5.6 us
    ppermute x3, waiting for transfers between devices, shards(): lax.ppermute(score, 'slab', [(one, (one + hop) % slabs) for one in range(...  3.23 us
    unnamed x10, local copies, waits for them, and re-layouts  2.22 us
    pallas_call x1, Pallas kernels, finish(): pl.pallas_call(body, grid_spec=grid_spec, out_shape=jax.ShapeDtypeStruct(...  1.61 us
  transfers between devices with their start and end apart: 12, of which 7 were waited for; matrix products, arithmetic and copies ran while one was open for 0% of the time, Pallas kernels for 14%

profile of v1, /device:TPU:0, one launch (start us, length us, event | category | flops | bytes accessed | tf_op | source)
XLA Modules:
  0.0 77.0 jit_solution(8048781469382020166)
XLA Ops:
  0.0 0.9 %copy-done = s32[1,32768]{1,0:T(1,128)S(1)} copy-done((s32[1,32768]{1,0:T(1,128)S(1)}, s32[1,32768]{1,0:T(1,128)}, u32[]{:S(2)}) %copy-start) | copy-done | bytes 131096
  0.9 0.7 copy-done.2
  1.6 0.7 copy-done.3
  2.2 11.9 %estep.1 = (f32[4,64,4096]{2,1,0:T(8,128)}, bf16[4,64,4096]{2,1,0:T(8,128)(2,1)S(1)}, f32[64,64]{1,0:T(8,128)S(1)}) custom-call(s32[1]{0:T(128)} %bitcast.me_ref, s32[1,32768]{1,0:T(1,128)S(1)} %copy-done, bf16[64,32768]{1,0:T(8,128)(2,1)} %image_ref.1, bf16[64,32768]{1,0:T(8,128)(2,1)} %bitcast.6, f32[64,64]{1,0:T(8,128)} %own_ctf_ref.7, ...), custom_call_target="tpu_custom_call" | custom-call | tf_op jit(solution)/shard_map/estep/pallas_call | solution.py:137
  14.6 4.6 %collective-permute-start.2 = (f32[64,64]{1,0:T(8,128)S(1)}, f32[64,64]{1,0:T(8,128)S(1)}, u32[]{:S(2)}, u32[]{:S(2)}) collective-permute-start(f32[64,64]{1,0:T(8,128)S(1)} %get-tuple-element.12.refs_1_), channel_id=1, source_target_pairs={{0,3},{1,0},{2,1},{3,2},{4,7},{5,4},{6,5},{7,6},{8,11},{9,8},{10,9... | collective-permute-start | bytes 49160 | tf_op jit(solution)/shard_map/ppermute | solution.py:314
  19.2 1.0 %collective-permute-start = (f32[64,64]{1,0:T(8,128)S(1)}, f32[64,64]{1,0:T(8,128)S(1)}, u32[]{:S(2)}, u32[]{:S(2)}) collective-permute-start(f32[64,64]{1,0:T(8,128)S(1)} %get-tuple-element.12.refs_1_), channel_id=1, source_target_pairs={{0,1},{1,2},{2,3},{3,0},{4,5},{5,6},{6,7},{7,4},{8,9},{9,10},{10,1... | collective-permute-start | bytes 49160 | tf_op jit(solution)/shard_map/ppermute | solution.py:314
  20.3 1.3 %count.1.refs_0_ = f32[2,64,128]{2,1,0:T(8,128)S(1)} custom-call(s32[1]{0:T(128)} %bitcast.1.slab_ref, s32[64,128]{1,0:T(8,128)S(1)} %reshape.20.list_ref), custom_call_target="tpu_custom_call" | custom-call | flops 10000000 | bytes 1000000 | tf_op jit(solution)/shard_map/count/pallas_call | solution.py:169
  21.6 2.7 %collective-permute-done.1.refs_3_ = f32[64,64]{1,0:T(8,128)S(1)} collective-permute-done((f32[64,64]{1,0:T(8,128)S(1)}, f32[64,64]{1,0:T(8,128)S(1)}, u32[]{:S(2)}, u32[]{:S(2)}) %collective-permute-start.1) | collective-permute-done | bytes 16416 | tf_op jit(solution)/shard_map/ppermute | solution.py:314
  24.3 0.6 collective-permute-done.refs_2_
  25.3 1.2 %collective-permute-done.3.sib_w_ref = f32[64,64]{1,0:T(8,128)S(1)} collective-permute-done((f32[64,64]{1,0:T(8,128)S(1)}, f32[64,64]{1,0:T(8,128)S(1)}, u32[]{:S(2)}, u32[]{:S(2)}) %collective-permute-start.3) | collective-permute-done | bytes 16416 | tf_op jit(solution)/shard_map/ppermute | solution.py:295
  26.5 2.8 %sums.7 = f32[2,64,2048]{2,1,0:T(8,128)S(1)} custom-call(f32[64,64]{1,0:T(8,128)S(1)} %weigh.1.own_w_ref, f32[64,64]{1,0:T(8,128)S(1)} %collective-permute-done.3.sib_w_ref, f32[64,64]{1,0:T(8,128)} %own_ctf_ref.7, f32[64,64]{1,0:T(8,128)S(1)} %collective-permute-done.4.sib_ctf_ref, bf16[4,64,4096]{2,1,0:T(8,128)(2,1)S(1)} %get-tuple-element.13.keep_ref, ...), custom_call_target="tpu_custom_call" | custom-call | tf_op jit(solution)/shard_map/sums/pallas_call | solution.py:243
  29.2 1.6 %collective-permute-start.10 = (f32[2,64,2048]{2,1,0:T(8,128)S(1)}, f32[2,64,2048]{2,1,0:T(8,128)S(1)}, u32[]{:S(2)}, u32[]{:S(2)}) collective-permute-start(f32[2,64,2048]{2,1,0:T(8,128)S(1)} %sums.7), channel_id=1, source_target_pairs={{0,16},{4,20},{8,24},{12,28},{16,0},{20,4},{24,8},{28,12},{1,17},{... | collective-permute-start | bytes 3145736 | tf_op jit(solution)/shard_map/ppermute | solution.py:295
  30.8 3.0 %sums.5 = (f32[2,64,2048]{2,1,0:T(8,128)S(1)}, f32[2,64,128]{2,1,0:T(8,128)S(1)}) custom-call(f32[64,64]{1,0:T(8,128)S(1)} %weigh.1.own_w_ref, f32[64,64]{1,0:T(8,128)S(1)} %collective-permute-done.3.sib_w_ref, f32[64,64]{1,0:T(8,128)} %own_ctf_ref.7, f32[64,64]{1,0:T(8,128)S(1)} %collective-permute-done.4.sib_ctf_ref, ...), custom_call_target="tpu_custom_call" | custom-call | tf_op jit(solution)/shard_map/sums/pallas_call | solution.py:243
  33.8 1.6 %collective-permute-start.8 = (f32[2,64,2048]{2,1,0:T(8,128)S(1)}, f32[2,64,2048]{2,1,0:T(8,128)S(1)}, u32[]{:S(2)}, u32[]{:S(2)}) collective-permute-start(f32[2,64,2048]{2,1,0:T(8,128)S(1)} %get-tuple-element.18), channel_id=1, source_target_pairs={{0,8},{4,12},{8,0},{12,4},{16,24},{20,28},{24,16},{28,20},{1,9},{5... | collective-permute-start | bytes 3145736 | tf_op jit(solution)/shard_map/ppermute | solution.py:295
  35.4 2.8 %sums.6.refs_7_ = f32[2,64,2048]{2,1,0:T(8,128)S(1)} custom-call(f32[64,64]{1,0:T(8,128)S(1)} %weigh.1.own_w_ref, f32[64,64]{1,0:T(8,128)S(1)} %collective-permute-done.3.sib_w_ref, f32[64,64]{1,0:T(8,128)} %own_ctf_ref.7, f32[64,64]{1,0:T(8,128)S(1)} %collective-permute-done.4.sib_ctf_ref, bf16[4,64,4096]{2,1,0:T(8,128)(2,1)S(1)} %get-tuple-element.13.keep_ref, ...), custom_call_target="tpu_custom_call" | custom-call | tf_op jit(solution)/shard_map/sums/pallas_call | solution.py:243
  38.2 3.0 %sums.4 = (f32[2,64,2048]{2,1,0:T(8,128)S(1)}, f32[2,64,128]{2,1,0:T(8,128)S(1)}) custom-call(f32[64,64]{1,0:T(8,128)S(1)} %weigh.1.own_w_ref, f32[64,64]{1,0:T(8,128)S(1)} %collective-permute-done.3.sib_w_ref, f32[64,64]{1,0:T(8,128)} %own_ctf_ref.7, f32[64,64]{1,0:T(8,128)S(1)} %collective-permute-done.4.sib_ctf_ref, ...), custom_call_target="tpu_custom_call" | custom-call | tf_op jit(solution)/shard_map/sums/pallas_call | solution.py:243
  41.2 13.3 %collective-permute-done.10.refs_8_ = f32[2,64,2048]{2,1,0:T(8,128)S(1)} collective-permute-done((f32[2,64,2048]{2,1,0:T(8,128)S(1)}, f32[2,64,2048]{2,1,0:T(8,128)S(1)}, u32[]{:S(2)}, u32[]{:S(2)}) %collective-permute-start.10) | collective-permute-done | bytes 1048608 | tf_op jit(solution)/shard_map/ppermute | solution.py:295
  54.6 1.6 %collective-permute-start.11 = (f32[1,64,2048]{2,1,0:T(8,128)S(1)}, f32[1,64,2048]{2,1,0:T(8,128)S(1)}, u32[]{:S(2)}, u32[]{:S(2)}) collective-permute-start(f32[1,64,2048]{2,1,0:T(8,128)S(1)} %slice_add_fusion), channel_id=1, source_target_pairs={{0,8},{4,12},{8,0},{12,4},{16,24},{20,28},{24,16},{28,20},{1,9},{5... | collective-permute-start | bytes 1572872 | tf_op jit(solution)/shard_map/ppermute | solution.py:295
  56.2 3.8 %collective-permute-done.8.refs_5_ = f32[2,64,2048]{2,1,0:T(8,128)S(1)} collective-permute-done((f32[2,64,2048]{2,1,0:T(8,128)S(1)}, f32[2,64,2048]{2,1,0:T(8,128)S(1)}, u32[]{:S(2)}, u32[]{:S(2)}) %collective-permute-start.8) | collective-permute-done | bytes 1048608 | tf_op jit(solution)/shard_map/ppermute | solution.py:295
  60.0 0.6 collective-permute-start.9
  60.6 1.5 %collective-permute-start.6 = (f32[2,64,128]{2,1,0:T(8,128)S(1)}, f32[2,64,128]{2,1,0:T(8,128)S(1)}, u32[]{:S(2)}, u32[]{:S(2)}) collective-permute-start(f32[2,64,128]{2,1,0:T(8,128)S(1)} %get-tuple-element.16), channel_id=1, source_target_pairs={{0,8},{4,12},{8,0},{12,4},{16,24},{20,28},{24,16},{28,20},{1,9},{5... | collective-permute-start | bytes 196616 | tf_op jit(solution)/shard_map/ppermute | solution.py:295
  62.1 9.4 %collective-permute-done.6.refs_2_ = f32[2,64,128]{2,1,0:T(8,128)S(1)} collective-permute-done((f32[2,64,128]{2,1,0:T(8,128)S(1)}, f32[2,64,128]{2,1,0:T(8,128)S(1)}, u32[]{:S(2)}, u32[]{:S(2)}) %collective-permute-start.6) | collective-permute-done | bytes 65568 | tf_op jit(solution)/shard_map/ppermute | solution.py:295
  72.0 3.4 %collective-permute-done.7.refs_3_ = f32[1,64,128]{2,1,0:T(8,128)S(1)} collective-permute-done((f32[1,64,128]{2,1,0:T(8,128)S(1)}, f32[1,64,128]{2,1,0:T(8,128)S(1)}, u32[]{:S(2)}, u32[]{:S(2)}) %collective-permute-start.7) | collective-permute-done | bytes 32800 | tf_op jit(solution)/shard_map/ppermute | solution.py:295
  75.4 1.6 %finish.1 = f32[64,4096]{1,0:T(8,128)} custom-call(s32[1]{0:T(128)} %bitcast.me_ref, s32[1,32768]{1,0:T(1,128)S(1)} %copy-done.1, f32[2,64,128]{2,1,0:T(8,128)S(1)} %get-tuple-element.15.refs_1_, f32[2,64,128]{2,1,0:T(8,128)S(1)} %collective-permute-done.6.refs_2_, f32[1,64,128]{2,1,0:T(8,128)S(1)} %collective-permute-done.7.refs_3_, ...), custom_call_target="tpu_custom_call" | custom-call | tf_op jit(solution)/shard_map/finish/pallas_call | solution.py:285
  (22 shorter events, 1.6 us)
Async XLA Ops:
  0.0 0.9 %copy-start = (s32[1,32768]{1,0:T(1,128)S(1)}, s32[1,32768]{1,0:T(1,128)}, u32[]{:S(2)}) copy-start(s32[1,32768]{1,0:T(1,128)} %constant.11.clone.index_ref.refs_0_) | copy-start | bytes 393220
  0.9 0.7 copy-start.2
  1.6 0.7 copy-start.3
  2.2 18.0 %copy-start.4 = (s32[64,2,64]{2,1,0:T(2,128)S(1)}, s32[64,2,64]{2,1,0:T(2,128)}, u32[]{:S(2)}) copy-start(s32[64,2,64]{2,1,0:T(2,128)} %param.9) | copy-start | bytes 98308
  14.1 12.4 %collective-permute-start.5 = (f32[4,64,4096]{2,1,0:T(8,128)}, f32[4,64,4096]{2,1,0:T(8,128)}, u32[]{:S(2)}, u32[]{:S(2)}) collective-permute-start(f32[4,64,4096]{2,1,0:T(8,128)} %get-tuple-element.14), channel_id=1, source_target_pairs={{0,4},{4,0},{8,12},{12,8},{16,20},{20,16},{24,28},{28,24},{1,5},{5... | collective-permute-start | bytes 12582920 | tf_op jit(solution)/shard_map/ppermute | solution.py:295
  14.6 7.1 %collective-permute-start.2 = (f32[64,64]{1,0:T(8,128)S(1)}, f32[64,64]{1,0:T(8,128)S(1)}, u32[]{:S(2)}, u32[]{:S(2)}) collective-permute-start(f32[64,64]{1,0:T(8,128)S(1)} %get-tuple-element.12.refs_1_), channel_id=1, source_target_pairs={{0,3},{1,0},{2,1},{3,2},{4,7},{5,4},{6,5},{7,6},{8,11},{9,8},{10,9... | collective-permute-start | bytes 49160 | tf_op jit(solution)/shard_map/ppermute | solution.py:314
  19.1 5.2 %collective-permute-start.1 = (f32[64,64]{1,0:T(8,128)S(1)}, f32[64,64]{1,0:T(8,128)S(1)}, u32[]{:S(2)}, u32[]{:S(2)}) collective-permute-start(f32[64,64]{1,0:T(8,128)S(1)} %get-tuple-element.12.refs_1_), channel_id=1, source_target_pairs={{0,2},{1,3},{2,0},{3,1},{4,6},{5,7},{6,4},{7,5},{8,10},{9,11},{10,... | collective-permute-start | bytes 49160 | tf_op jit(solution)/shard_map/ppermute | solution.py:314
  19.2 5.7 %collective-permute-start = (f32[64,64]{1,0:T(8,128)S(1)}, f32[64,64]{1,0:T(8,128)S(1)}, u32[]{:S(2)}, u32[]{:S(2)}) collective-permute-start(f32[64,64]{1,0:T(8,128)S(1)} %get-tuple-element.12.refs_1_), channel_id=1, source_target_pairs={{0,1},{1,2},{2,3},{3,0},{4,5},{5,6},{6,7},{7,4},{8,9},{9,10},{10,1... | collective-permute-start | bytes 49160 | tf_op jit(solution)/shard_map/ppermute | solution.py:314
  20.2 5.1 %collective-permute-start.4 = (f32[64,64]{1,0:T(8,128)}, f32[64,64]{1,0:T(8,128)S(1)}, u32[]{:S(2)}, u32[]{:S(2)}) collective-permute-start(f32[64,64]{1,0:T(8,128)} %own_ctf_ref.7), channel_id=1, source_target_pairs={{0,4},{4,0},{8,12},{12,8},{16,20},{20,16},{24,28},{28,24},{1,5},{5... | collective-permute-start | bytes 49160 | tf_op jit(solution)/shard_map/ppermute | solution.py:295
  25.2 1.2 %collective-permute-start.3 = (f32[64,64]{1,0:T(8,128)S(1)}, f32[64,64]{1,0:T(8,128)S(1)}, u32[]{:S(2)}, u32[]{:S(2)}) collective-permute-start(f32[64,64]{1,0:T(8,128)S(1)} %weigh.1.own_w_ref), channel_id=1, source_target_pairs={{0,4},{4,0},{8,12},{12,8},{16,20},{20,16},{24,28},{28,24},{1,5},{5... | collective-permute-start | bytes 49160 | tf_op jit(solution)/shard_map/ppermute | solution.py:295
  29.2 25.3 %collective-permute-start.10 = (f32[2,64,2048]{2,1,0:T(8,128)S(1)}, f32[2,64,2048]{2,1,0:T(8,128)S(1)}, u32[]{:S(2)}, u32[]{:S(2)}) collective-permute-start(f32[2,64,2048]{2,1,0:T(8,128)S(1)} %sums.7), channel_id=1, source_target_pairs={{0,16},{4,20},{8,24},{12,28},{16,0},{20,4},{24,8},{28,12},{1,17},{... | collective-permute-start | bytes 3145736 | tf_op jit(solution)/shard_map/ppermute | solution.py:295
  33.8 26.1 %collective-permute-start.8 = (f32[2,64,2048]{2,1,0:T(8,128)S(1)}, f32[2,64,2048]{2,1,0:T(8,128)S(1)}, u32[]{:S(2)}, u32[]{:S(2)}) collective-permute-start(f32[2,64,2048]{2,1,0:T(8,128)S(1)} %get-tuple-element.18), channel_id=1, source_target_pairs={{0,8},{4,12},{8,0},{12,4},{16,24},{20,28},{24,16},{28,20},{1,9},{5... | collective-permute-start | bytes 3145736 | tf_op jit(solution)/shard_map/ppermute | solution.py:295
  38.2 37.2 %copy-start.1 = (s32[1,32768]{1,0:T(1,128)S(1)}, s32[1,32768]{1,0:T(1,128)}, u32[]{:S(2)}) copy-start(s32[1,32768]{1,0:T(1,128)} %constant.11.clone.index_ref.refs_0_) | copy-start | bytes 393220
  54.6 20.8 %collective-permute-start.11 = (f32[1,64,2048]{2,1,0:T(8,128)S(1)}, f32[1,64,2048]{2,1,0:T(8,128)S(1)}, u32[]{:S(2)}, u32[]{:S(2)}) collective-permute-start(f32[1,64,2048]{2,1,0:T(8,128)S(1)} %slice_add_fusion), channel_id=1, source_target_pairs={{0,8},{4,12},{8,0},{12,4},{16,24},{20,28},{24,16},{28,20},{1,9},{5... | collective-permute-start | bytes 1572872 | tf_op jit(solution)/shard_map/ppermute | solution.py:295
  60.0 15.4 %collective-permute-start.9 = (f32[1,64,2048]{2,1,0:T(8,128)S(1)}, f32[1,64,2048]{2,1,0:T(8,128)S(1)}, u32[]{:S(2)}, u32[]{:S(2)}) collective-permute-start(f32[1,64,2048]{2,1,0:T(8,128)S(1)} %slice_add_fusion.1), channel_id=1, source_target_pairs={{0,16},{4,20},{8,24},{12,28},{16,0},{20,4},{24,8},{28,12},{1,17},{... | collective-permute-start | bytes 1572872 | tf_op jit(solution)/shard_map/ppermute | solution.py:295
  60.6 10.9 %collective-permute-start.6 = (f32[2,64,128]{2,1,0:T(8,128)S(1)}, f32[2,64,128]{2,1,0:T(8,128)S(1)}, u32[]{:S(2)}, u32[]{:S(2)}) collective-permute-start(f32[2,64,128]{2,1,0:T(8,128)S(1)} %get-tuple-element.16), channel_id=1, source_target_pairs={{0,8},{4,12},{8,0},{12,4},{16,24},{20,28},{24,16},{28,20},{1,9},{5... | collective-permute-start | bytes 196616 | tf_op jit(solution)/shard_map/ppermute | solution.py:295
  71.5 3.9 %collective-permute-start.7 = (f32[1,64,128]{2,1,0:T(8,128)S(1)}, f32[1,64,128]{2,1,0:T(8,128)S(1)}, u32[]{:S(2)}, u32[]{:S(2)}) collective-permute-start(f32[1,64,128]{2,1,0:T(8,128)S(1)} %slice_add_fusion.2), channel_id=1, source_target_pairs={{0,16},{4,20},{8,24},{12,28},{16,0},{20,4},{24,8},{28,12},{1,17},{... | collective-permute-start | bytes 98312 | tf_op jit(solution)/shard_map/ppermute | solution.py:295

commit v2 on v1

v2 whole, which is shorter than its diff:
```python
import functools
import math

import jax
import jax.numpy as jnp
import numpy as np
from jax import lax
from jax.experimental import pallas as pl
from jax.experimental.pallas import tpu as pltpu
from jax.sharding import PartitionSpec as P

F32 = jnp.float32
BF16 = jnp.bfloat16
LANES = 128
VMEM_LIMIT = 60 * 1024 * 1024


def entry_shells(width, shells):
    pixels = width // 2
    box = math.isqrt(pixels)
    place = np.arange(pixels)
    column = place % box - box // 2
    row = place // box - box // 2
    radius = column * column + row * row
    levels = np.arange(1, shells)
    shell = np.sum(2 * levels[None, :] ** 2 <= radius[:, None], axis=1)
    return np.repeat(shell, 2).astype(np.int32)[None, :]


def params(**more):
    return pltpu.CompilerParams(vmem_limit_bytes=VMEM_LIMIT, **more)


def lanes_wide(table):
    rows, shells = table.shape
    if shells == LANES:
        return table
    return jnp.concatenate([table, jnp.zeros((rows, LANES - shells), table.dtype)], axis=1)


def spread(table, index):
    return jnp.take_along_axis(table, jnp.broadcast_to(index, table.shape), axis=1)


def contract_last(left, right):
    return lax.dot_general(left, right, (((1,), (1,)), ((), ())), preferred_element_type=F32)


def estep_kernel(
    blocks, me_ref, index_hbm, image_hbm, plane_hbm, ctf_hbm, give_hbm, keep_hbm, score_ref,
    index, image, plane, ctf_held, weighted, give, squared, energy_of, small_sem, in_sem, out_sem,
):
    rows, width = image.shape
    chips, _, share = give.shape
    box = math.isqrt(width // 2)
    line = 2 * box
    deep = box // (2 * blocks)
    span = deep * line

    small = [
        pltpu.make_async_copy(index_hbm, index, small_sem.at[0]),
        pltpu.make_async_copy(ctf_hbm, ctf_held, small_sem.at[1]),
    ]
    incoming = []
    for block in range(blocks):
        copies = []
        for side, start in enumerate((block * span, width - (block + 1) * span)):
            cut = pl.ds(start, span)
            copies += [
                pltpu.make_async_copy(
                    image_hbm.at[:, cut], image.at[:, cut], in_sem.at[block, side, 0]
                ),
                pltpu.make_async_copy(
                    plane_hbm.at[:, cut], plane.at[:, cut], in_sem.at[block, side, 1]
                ),
            ]
        incoming.append(copies)
    for copy in small + [copy for copies in incoming for copy in copies]:
        copy.start()
    for copy in small:
        copy.wait()
    table = lanes_wide(ctf_held[...])

    def weigh_image(cut, ctf):
        weighted[:, cut] = (image[:, cut].astype(F32) * ctf).astype(BF16)

    def square(cut):
        part = plane[:, cut].astype(F32)
        return part * part

    def expand(row, slot, place):
        mirror = box - row if 0 < row < box // 2 else None
        for start in range(0, line, LANES):
            cut = slice(row * line + start, row * line + start + LANES)
            ctf = spread(table, index[:, cut])
            weigh_image(cut, ctf)
            power = square(cut)
            if mirror is not None:
                other = slice(mirror * line + start, mirror * line + start + LANES)
                weigh_image(other, ctf)
                power += square(other)
            held = slice(place + start, place + start + LANES)
            squared[slot, :, held] = (ctf * ctf).astype(BF16)
            energy_of[slot, :, held] = power.astype(BF16)

    def fit(start, stop):
        return contract_last(weighted[:, start:stop], plane[:, start:stop])

    def energy(slot, size):
        return contract_last(squared[slot, :, :size], energy_of[slot, :, :size])

    def block_table(block):
        low, high = fit(block * span, (block + 1) * span), width - block * span
        stop = high + line if block else high
        low += fit(high - span + line, stop)
        return 2.0 * low - energy(block % 2, span)

    chip, core = me_ref[0] // 2, lax.rem(me_ref[0], 2)
    outgoing = []

    def hand_over(done):
        for pair in range(chips):
            first, last = 2 * pair * share // line, -(-2 * (pair + 1) * share // line)
            if pair in handed or not all(row in done for row in range(first, last)):
                continue
            handed.add(pair)
            place = pair ^ chip
            given = pl.ds(pl.multiple_of((2 * pair + 1 - core) * share, share), share)
            kept = pl.ds(pl.multiple_of((2 * pair + core) * share, share), share)
            give[place] = weighted[:, given].astype(F32)
            outgoing.extend([
                pltpu.make_async_copy(give.at[place], give_hbm.at[place], out_sem.at[pair, 0]),
                pltpu.make_async_copy(weighted.at[:, kept], keep_hbm.at[place], out_sem.at[pair, 1]),
            ])
            outgoing[-2].start()
            outgoing[-1].start()

    handed, done = set(), set()
    total = jnp.zeros(score_ref.shape, F32)
    for block in range(blocks):
        for copy in incoming[block]:
            copy.wait()
        for row in range(block * deep, (block + 1) * deep):
            expand(row, block % 2, (row - block * deep) * line)
            done |= {row, box - row}
        if block == blocks - 1:
            expand(box // 2, 2, 0)
            done.add(box // 2)
        if block:
            total += block_table(block - 1)
        hand_over(done)
    total += block_table(blocks - 1)
    middle = width // 2
    total += 2.0 * fit(middle, middle + line) - energy(2, line)
    score_ref[...] = total
    for copy in outgoing:
        copy.wait()


def estep(me, index, images, planes, ctf_table, share):
    rows, width = images.shape
    chips = width // share // 2
    count = planes.shape[0]
    blocks = 4
    span = width // (2 * blocks)
    held = pl.BlockSpec(memory_space=pl.ANY)
    return pl.pallas_call(
        functools.partial(estep_kernel, blocks),
        in_specs=[pl.BlockSpec(memory_space=pltpu.SMEM)] + [held] * 4,
        out_specs=[held, held, pl.BlockSpec(memory_space=pltpu.VMEM)],
        out_shape=[
            jax.ShapeDtypeStruct((chips, rows, share), F32),
            jax.ShapeDtypeStruct((chips, rows, share), BF16),
            jax.ShapeDtypeStruct((rows, count), F32),
        ],
        scratch_shapes=[
            pltpu.VMEM(index.shape, jnp.int32),
            pltpu.VMEM((rows, width), BF16),
            pltpu.VMEM((count, width), BF16),
            pltpu.VMEM(ctf_table.shape, F32),
            pltpu.VMEM((rows, width), BF16),
            pltpu.VMEM((chips, rows, share), F32),
            pltpu.VMEM((3, rows, span), BF16),
            pltpu.VMEM((3, count, span), BF16),
            pltpu.SemaphoreType.DMA((2,)),
            pltpu.SemaphoreType.DMA((blocks, 2, 2)),
            pltpu.SemaphoreType.DMA((chips, 2)),
        ],
        compiler_params=params(),
        name="estep",
    )(me, index, images, planes, ctf_table)


def count_kernel(slabs, slab_ref, prior_ref, noise_ref, list_ref, base_ref, scale_ref):
    rows, listed = list_ref.shape
    classes, _, width = base_ref.shape
    each = listed // classes
    local = width // slabs
    lane = lax.broadcasted_iota(jnp.int32, (rows, width), 1)
    home = lax.rem(slab_ref[0] - lane // local + slabs, slabs)
    plane = home * local + lax.rem(lane, local)
    for one in range(classes):
        sums = jnp.zeros((rows, width), F32)
        for entry in range(each):
            place = one * each + entry
            sums += jnp.where(list_ref[:, place : place + 1] == plane, 1.0, 0.0)
        base_ref[one] = jnp.where(sums > 0.0, jnp.log(sums) + jnp.log(prior_ref[:, one : one + 1]), -jnp.inf)
    noise = jnp.broadcast_to(noise_ref[...], (rows, rows))
    diagonal = lax.broadcasted_iota(jnp.int32, (rows, rows), 0) == lax.broadcasted_iota(
        jnp.int32, (rows, rows), 1
    )
    column = jnp.sum(jnp.where(diagonal, noise, 0.0), axis=1, keepdims=True)
    scale_ref[...] = jnp.broadcast_to(column, (rows, width))


def count_planes(slab, class_weight, inv_noise, orientations, width, slabs):
    rows, classes, each = orientations.shape
    vmem = pl.BlockSpec(memory_space=pltpu.VMEM)
    return pl.pallas_call(
        functools.partial(count_kernel, slabs),
        in_specs=[pl.BlockSpec(memory_space=pltpu.SMEM), vmem, vmem, vmem],
        out_specs=[vmem, vmem],
        out_shape=[
            jax.ShapeDtypeStruct((classes, rows, width), F32),
            jax.ShapeDtypeStruct((rows, width), F32),
        ],
        compiler_params=params(),
        cost_estimate=pl.CostEstimate(flops=10**7, bytes_accessed=10**6, transcendentals=0),
        name="count",
    )(
        slab,
        class_weight.reshape(1, classes),
        inv_noise.reshape(1, rows),
        orientations.reshape(rows, classes * each),
    )


def weigh_kernel(base_ref, scale_ref, *refs):
    out_ref = refs[-1]
    tables = [ref[...] for ref in refs[:-1]]
    classes = base_ref.shape[0]
    local = tables[0].shape[1] // classes
    scores = []
    for one in range(classes):
        cut = slice(one * local, (one + 1) * local)
        fit = jnp.concatenate([table[:, cut] for table in tables], axis=1)
        scores.append(base_ref[one] + scale_ref[...] * fit)
    peak = functools.reduce(jnp.maximum, [jnp.max(score, axis=1, keepdims=True) for score in scores])
    raw = [jnp.exp(score - peak) for score in scores]
    total = functools.reduce(jnp.add, [jnp.sum(part, axis=1, keepdims=True) for part in raw])
    own = jnp.concatenate([part[:, :local] for part in raw], axis=1) / total
    out_ref[...] = own.T


def weigh(base, scale, tables):
    rows, planes = tables[0].shape
    return pl.pallas_call(
        weigh_kernel,
        out_shape=jax.ShapeDtypeStruct((planes, rows), F32),
        compiler_params=params(),
        name="weigh",
    )(base, scale, *tables)


def sums_kernel(items, with_shells, own_w_ref, sib_w_ref, own_ctf_ref, sib_ctf_ref, keep_hbm, got_hbm, *refs):
    outs = refs[: len(items)]
    shell_ref = refs[len(items)] if with_shells else None
    keep, got, sums, in_sem, out_sem = refs[-5:]
    tile = keep_hbm.shape[2] // 4
    number, _, wide = keep.shape
    cells = wide // tile
    places = [(out, slot, k, side) for out, (side, ks) in enumerate(items) for slot, k in enumerate(ks)]
    incoming, outgoing = [], []
    for place, (out, slot, k, side) in enumerate(places):
        copies = []
        for cell in range(cells):
            source = slice((2 * cell + side) * tile, (2 * cell + side + 1) * tile)
            target = slice(cell * tile, (cell + 1) * tile)
            copies += [
                pltpu.make_async_copy(
                    keep_hbm.at[k, :, source], keep.at[place, :, target], in_sem.at[place, cell, 0]
                ),
                pltpu.make_async_copy(
                    got_hbm.at[k, :, source], got.at[place, :, target], in_sem.at[place, cell, 1]
                ),
            ]
        incoming.append(copies)
        outgoing.append(pltpu.make_async_copy(sums.at[place], outs[out].at[slot], out_sem.at[place]))
    for copy in [copy for copies in incoming for copy in copies]:
        copy.start()
    weights = jnp.concatenate([own_w_ref[...], sib_w_ref[...]], axis=1).astype(BF16)
    if with_shells:
        ctf = jnp.concatenate([own_ctf_ref[...], sib_ctf_ref[...]], axis=0)
        square = lanes_wide((ctf * ctf).astype(BF16))
        shell_ref[...] = jnp.dot(weights, square, preferred_element_type=F32)
    for place in range(number):
        for copy in incoming[place]:
            copy.wait()
        images = jnp.concatenate([keep[place], got[place].astype(BF16)], axis=0)
        sums[place] = jnp.dot(weights, images, preferred_element_type=F32)
        outgoing[place].start()
    for copy in outgoing:
        copy.wait()


def partial_sums(items, with_shells, own_w, sib_w, own_ctf, sib_ctf, keep, got):
    chips, rows, share = keep.shape
    planes = own_w.shape[0]
    wide = share // 2
    number = sum(len(ks) for _, ks in items)
    held = pl.BlockSpec(memory_space=pl.ANY)
    vmem = pl.BlockSpec(memory_space=pltpu.VMEM)
    out_specs = [held] * len(items)
    out_shape = [jax.ShapeDtypeStruct((len(ks), planes, wide), F32) for _, ks in items]
    if with_shells:
        out_specs.append(vmem)
        out_shape.append(jax.ShapeDtypeStruct((planes, LANES), F32))
    return pl.pallas_call(
        functools.partial(sums_kernel, items, with_shells),
        in_specs=[vmem] * 4 + [held] * 2,
        out_specs=out_specs,
        out_shape=out_shape,
        scratch_shapes=[
            pltpu.VMEM((number, rows, wide), BF16),
            pltpu.VMEM((number, rows, wide), F32),
            pltpu.VMEM((number, planes, wide), F32),
            pltpu.SemaphoreType.DMA((number, 2, 2)),
            pltpu.SemaphoreType.DMA((number,)),
        ],
        compiler_params=params(),
        cost_estimate=pl.CostEstimate(
            flops=4 * planes * rows * wide * number,
            bytes_accessed=10 * planes * wide * number,
            transcendentals=0,
        ),
        name="sums",
    )(own_w, sib_w, own_ctf, sib_ctf, keep, got)


def finish_kernel(number, me_ref, index_ref, shell_ref, *refs):
    out_ref = refs[-1]
    left = functools.reduce(jnp.add, [ref[0] for ref in refs[:number]])
    right = functools.reduce(jnp.add, [ref[0] for ref in refs[number : 2 * number]])
    shells = shell_ref[...]
    tile = left.shape[1]
    for side, block in ((0, left), (1, right)):
        for start in range(0, tile, LANES):
            cut = slice(side * tile + start, side * tile + start + LANES)
            weight = spread(shells, index_ref[:, cut])
            out_ref[:, cut] = block[:, start : start + LANES] / (weight + 1.0)


def finish(me, index, shells, left, right, share):
    planes = left[0].shape[1]
    tile = share // 4
    number = len(left)
    cells = share // (2 * tile)
    side = pl.BlockSpec((1, planes, tile), lambda cell, m: (0, 0, cell))
    grid_spec = pltpu.PrefetchScalarGridSpec(
        num_scalar_prefetch=1,
        grid=(cells,),
        in_specs=[
            pl.BlockSpec((1, 2 * tile), lambda cell, m: (0, m[0] * cells + cell)),
            pl.BlockSpec((planes, LANES), lambda cell, m: (0, 0)),
        ]
        + [side] * (2 * number),
        out_specs=pl.BlockSpec((planes, 2 * tile), lambda cell, m: (0, cell)),
    )
    return pl.pallas_call(
        functools.partial(finish_kernel, number),
        grid_spec=grid_spec,
        out_shape=jax.ShapeDtypeStruct((planes, share), F32),
        compiler_params=params(),
        name="finish",
    )(me, index, shells, *left, *right)


def swap(array, bit, size):
    return lax.ppermute(array, "img", [(one, one ^ bit) for one in range(size)])


def shards(images, references, orientations, ctf_table, inv_noise, class_weight):
    rows, width = images.shape
    classes, local_planes, _ = references.shape
    size = lax.axis_size("img")
    slabs = lax.axis_size("slab")
    chips = size // 2
    share = width // size
    me = lax.axis_index("img").astype(jnp.int32).reshape(1)
    slab = lax.axis_index("slab").astype(jnp.int32).reshape(1)
    index = entry_shells(width, ctf_table.shape[1])
    top_index = jnp.asarray(index[:, : width // 2 + 2 * math.isqrt(width // 2)])
    index = jnp.asarray(index)
    planes = references.reshape(classes * local_planes, width)

    give, keep, table = estep(me, top_index, images, planes, ctf_table, share)
    sib_ctf = swap(ctf_table, 1, size)
    tables = [table] + [
        lax.ppermute(table, "slab", [(one, (one + hop) % slabs) for one in range(slabs)])
        for hop in range(1, slabs)
    ]
    got = swap(give, 1, size)
    base, scale = count_planes(
        slab, class_weight, inv_noise, orientations, slabs * local_planes, slabs
    )
    own_w = weigh(base, scale, tables)
    sib_w = swap(own_w, 1, size)

    sums = functools.partial(
        partial_sums,
        own_w=own_w, sib_w=sib_w, own_ctf=ctf_table, sib_ctf=sib_ctf, keep=keep, got=got,
    )
    top = chips // 2
    send_left, send_right = sums(
        ((0, tuple(range(1, chips, 2))), (1, tuple(range(top, chips)))), False
    )
    left_in = swap(send_left, 2, size)
    right_in = swap(send_right, 2 * top, size)
    keep_left, keep_right, shells = sums(
        ((0, tuple(range(0, chips, 2))), (1, tuple(range(top)))), True
    )
    lefts, rights = [keep_left, left_in], [keep_right, right_in]
    bit = 2
    while bit < chips:
        number = rights[-1].shape[0] // 2
        left_out = sum(part[1::2] for part in lefts)
        right_out = sum(part[number:] for part in rights)
        if number > 1:
            lefts = [part[0::2] for part in lefts]
            rights = [part[:number] for part in rights]
        lefts.append(swap(left_out, 2 * bit, size))
        rights.append(swap(right_out, chips // bit, size))
        bit *= 2
    bit = 2
    while bit < size:
        shells = shells + swap(shells, bit, size)
        bit *= 2
    out = finish(me, index, shells, lefts, rights, share)
    return out.reshape(classes, local_planes, share)


def solution(mesh):
    return jax.shard_map(
        shards,
        mesh=mesh,
        in_specs=(
            P("img", None),
            P(None, "slab", None),
            P("img", None, None),
            P("img", None),
            P("img"),
            P(),
        ),
        out_specs=P(None, "slab", "img"),
        check_vma=False,
    )
```

time: 77.5 us -> 83.1 us (1.072)
  other arithmetic: 0.12 us -> 4.29 us
  waiting for transfers between devices: 34.3 us -> 35.8 us
  Pallas kernels: 26.7 us -> 25.4 us
  local copies, waits for them, and re-layouts: 2.33 us -> 3.53 us
    pallas_call x6 -> x4, Pallas kernels: 25 us -> 20.7 us  [the longest x1 9.43 us: estep(): pl.pallas_call(functools.partial(estep_kernel, blocks), in_specs=[pl.Bloc...]
    ppermute x9, waiting for transfers between devices: 31.1 us -> 34.4 us  [swap(): return lax.ppermute(array, 'img', [(one, one ^ bit) for one in range(size)])]
    ppermute x3, waiting for transfers between devices: 3.23 us -> 1.36 us  [shards(): lax.ppermute(table, 'slab', [(one, (one + hop) % slabs) for one in range(...]
    pallas_call x1, Pallas kernels: 0.36 us -> 1.87 us  [weigh(): pl.pallas_call(weigh_kernel, out_shape=jax.ShapeDtypeStruct((planes, rows...]
    pallas_call x1, Pallas kernels: 1.35 us -> 2.81 us  [count_planes(): pl.pallas_call(functools.partial(count_kernel, slabs), in_specs=[pl.Block...]
    add x1, other arithmetic: 0.06 us -> 1.45 us  [shards(): right_out = sum((part[number:] for part in rights))]
    add x1, other arithmetic: 0.06 us -> 1.45 us  [shards(): left_out = sum((part[1::2] for part in lefts))]
    add x1 -> x2, other arithmetic: 0.01 us -> 1.38 us  [shards(): shells = shells + swap(shells, bit, size)]
  transfers between devices with their start and end apart: 12 -> 12, of which waited for: 7 -> 6; matrix products, arithmetic and copies ran while one was open for 0% -> 6% of each run, Pallas kernels for 14% -> 11%
where the time goes in v2:
time: 83.1 us; the launch traced here: 82.6 us
  waiting for transfers between devices  35.8 us (43%)
  Pallas kernels  25.4 us (31%)
  starting transfers between devices  13.5 us (16%)
  other arithmetic  4.29 us (5%)
  local copies, waits for them, and re-layouts  3.53 us (4%)
    ppermute x9, waiting for transfers between devices, swap(): return lax.ppermute(array, 'img', [(one, one ^ bit) for one in range(size)])  34.4 us
    pallas_call x1, Pallas kernels, estep(): pl.pallas_call(functools.partial(estep_kernel, blocks), in_specs=[pl.Bloc...  9.43 us
    pallas_call x2, Pallas kernels, partial_sums(): pl.pallas_call(functools.partial(sums_kernel, items, with_shells), in_spe...  8.37 us
    ppermute x9, starting transfers between devices, swap(): return lax.ppermute(array, 'img', [(one, one ^ bit) for one in range(size)])  7.75 us
    ppermute x3, starting transfers between devices, shards(): lax.ppermute(table, 'slab', [(one, (one + hop) % slabs) for one in range(...  5.72 us
    pallas_call x1, Pallas kernels, finish(): pl.pallas_call(functools.partial(finish_kernel, number), grid_spec=grid_s...  2.91 us
    pallas_call x1, Pallas kernels, count_planes(): pl.pallas_call(functools.partial(count_kernel, slabs), in_specs=[pl.Block...  2.81 us
    unnamed x22, local copies, waits for them, and re-layouts  2.81 us
  transfers between devices with their start and end apart: 12, of which 6 were waited for; matrix products, arithmetic and copies ran while one was open for 6% of the time, Pallas kernels for 11%

profile of v2, /device:TPU:0, one launch (start us, length us, event | category | flops | bytes accessed | tf_op | source)
XLA Modules:
  0.0 82.6 jit_solution(620376922125613683)
XLA Ops:
  0.0 9.4 %estep.1 = (f32[4,64,4096]{2,1,0:T(8,128)}, bf16[4,64,4096]{2,1,0:T(8,128)(2,1)}, f32[64,64]{1,0:T(8,128)}) custom-call(s32[1]{0:T(128)} %bitcast.me_ref, s32[1,16640]{1,0:T(1,128)} %constant.13.clone.index_hbm, bf16[64,32768]{1,0:T(8,128)(2,1)} %image_hbm.1, bf16[64,32768]{1,0:T(8,128)(2,1)} %bitcast.6, f32[64,64]{1,0:T(8,128)} %own_ctf_ref.3), custom_call_target="tpu_custom_call" | custom-call | tf_op jit(solution)/shard_map/estep/pallas_call | solution.py:167
  9.9 4.7 %collective-permute-start.2 = (f32[64,64]{1,0:T(8,128)}, f32[64,64]{1,0:T(8,128)S(1)}, u32[]{:S(2)}, u32[]{:S(2)}) collective-permute-start(f32[64,64]{1,0:T(8,128)} %get-tuple-element.17.refs_0_), channel_id=1, source_target_pairs={{0,3},{1,0},{2,1},{3,2},{4,7},{5,4},{6,5},{7,6},{8,11},{9,8},{10,9... | collective-permute-start | bytes 49160 | tf_op jit(solution)/shard_map/ppermute | solution.py:399
  14.6 1.0 %collective-permute-start = (f32[64,64]{1,0:T(8,128)}, f32[64,64]{1,0:T(8,128)S(1)}, u32[]{:S(2)}, u32[]{:S(2)}) collective-permute-start(f32[64,64]{1,0:T(8,128)} %get-tuple-element.17.refs_0_), channel_id=1, source_target_pairs={{0,1},{1,2},{2,3},{3,0},{4,5},{5,6},{6,7},{7,4},{8,9},{9,10},{10,1... | collective-permute-start | bytes 49160 | tf_op jit(solution)/shard_map/ppermute | solution.py:399
  15.6 0.7 reshape.25.list_ref
  16.4 2.8 %count.1 = (f32[2,64,128]{2,1,0:T(8,128)}, f32[64,128]{1,0:T(8,128)}) custom-call(s32[1]{0:T(128)} %bitcast.1.slab_ref, f32[1,2]{1,0:T(1,128)} %bitcast.7, f32[1,64]{1,0:T(1,128)} %bitcast.8, s32[64,128]{1,0:T(8,128)} %reshape.25.list_ref), custom_call_target="tpu_custom_call" | custom-call | flops 10000000 | bytes 1000000 | tf_op jit(solution)/shard_map/count/pallas_call | solution.py:219
  19.2 0.8 collective-permute-done.1.refs_2_
  21.2 1.9 %weigh.1.own_w_ref = f32[64,64]{1,0:T(8,128)} custom-call(f32[2,64,128]{2,1,0:T(8,128)} %get-tuple-element.15.base_ref, f32[64,128]{1,0:T(8,128)} %get-tuple-element.16.scale_ref, f32[64,64]{1,0:T(8,128)} %get-tuple-element.17.refs_0_, f32[64,64]{1,0:T(8,128)} %copy-done.10, f32[64,64]{1,0:T(8,128)} %copy-done.9, f32[64,64]{1,0:T(8,128)} %copy-done.8), custom_call_target="tpu_custom_call" | custom-call | tf_op jit(solution)/shard_map/weigh/pallas_call | solution.py:257
  23.0 1.4 %collective-permute-done.3.sib_w_ref = f32[64,64]{1,0:T(8,128)S(1)} collective-permute-done((f32[64,64]{1,0:T(8,128)}, f32[64,64]{1,0:T(8,128)S(1)}, u32[]{:S(2)}, u32[]{:S(2)}) %collective-permute-start.3) | collective-permute-done | bytes 16416 | tf_op jit(solution)/shard_map/ppermute | solution.py:379
  25.1 3.9 %sums.3 = (f32[2,64,2048]{2,1,0:T(8,128)}, f32[2,64,2048]{2,1,0:T(8,128)}) custom-call(f32[64,64]{1,0:T(8,128)} %weigh.1.own_w_ref, f32[64,64]{1,0:T(8,128)} %copy-done.6, f32[64,64]{1,0:T(8,128)} %own_ctf_ref.3, f32[64,64]{1,0:T(8,128)} %copy-done.5, bf16[4,64,4096]{2,1,0:T(8,128)(2,1)} %get-tuple-element.18.keep_hbm, ...), custom_call_target="tpu_custom_call" | custom-call | flops 134217728 | bytes 5242880 | tf_op jit(solution)/shard_map/sums/pallas_call | solution.py:318
  28.9 1.7 %collective-permute-start.8 = (f32[2,64,2048]{2,1,0:T(8,128)}, f32[2,64,2048]{2,1,0:T(8,128)S(1)}, u32[]{:S(2)}, u32[]{:S(2)}) collective-permute-start(f32[2,64,2048]{2,1,0:T(8,128)} %get-tuple-element.22), channel_id=1, source_target_pairs={{0,8},{4,12},{8,0},{12,4},{16,24},{20,28},{24,16},{28,20},{1,9},{5... | collective-permute-start | bytes 3145736 | tf_op jit(solution)/shard_map/ppermute | solution.py:379
  30.6 1.4 %collective-permute-start.10 = (f32[2,64,2048]{2,1,0:T(8,128)}, f32[2,64,2048]{2,1,0:T(8,128)S(1)}, u32[]{:S(2)}, u32[]{:S(2)}) collective-permute-start(f32[2,64,2048]{2,1,0:T(8,128)} %get-tuple-element.24), channel_id=1, source_target_pairs={{0,16},{4,20},{8,24},{12,28},{16,0},{20,4},{24,8},{28,12},{1,17},{... | collective-permute-start | bytes 3145736 | tf_op jit(solution)/shard_map/ppermute | solution.py:379
  32.0 4.5 %sums.2 = (f32[2,64,2048]{2,1,0:T(8,128)}, f32[2,64,2048]{2,1,0:T(8,128)}, f32[64,128]{1,0:T(8,128)}) custom-call(f32[64,64]{1,0:T(8,128)} %weigh.1.own_w_ref, f32[64,64]{1,0:T(8,128)} %copy-done.6, f32[64,64]{1,0:T(8,128)} %own_ctf_ref.3, f32[64,64]{1,0:T(8,128)} %copy-done.5, bf16[4,64,4096]{2,1,0:T(8,128)(2,1)} %get-tuple-element.18.keep_hbm, ...), custom_call_target="tpu_custom_call" | custom-call | flops 134217728 | bytes 5242880 | tf_op jit(solution)/shard_map/sums/pallas_call | solution.py:318
  36.5 17.9 %collective-permute-done.8.refs_1_ = f32[2,64,2048]{2,1,0:T(8,128)S(1)} collective-permute-done((f32[2,64,2048]{2,1,0:T(8,128)}, f32[2,64,2048]{2,1,0:T(8,128)S(1)}, u32[]{:S(2)}, u32[]{:S(2)}) %collective-permute-start.8) | collective-permute-done | bytes 1048608 | tf_op jit(solution)/shard_map/ppermute | solution.py:379
  54.4 1.5 %slice_add_fusion.1 = f32[1,64,2048]{2,1,0:T(8,128)S(1)} fusion(f32[2,64,2048]{2,1,0:T(8,128)S(1)} %collective-permute-done.8.refs_1_, f32[2,64,2048]{2,1,0:T(8,128)} %get-tuple-element.21.refs_0_), kind=kLoop, calls=%fused_computation.1 | loop fusion | flops 131072 | bytes 1572864 | tf_op jit(solution)/shard_map/add | solution.py:426
  55.9 1.7 %collective-permute-start.9 = (f32[1,64,2048]{2,1,0:T(8,128)S(1)}, f32[1,64,2048]{2,1,0:T(8,128)S(1)}, u32[]{:S(2)}, u32[]{:S(2)}) collective-permute-start(f32[1,64,2048]{2,1,0:T(8,128)S(1)} %slice_add_fusion.1), channel_id=1, source_target_pairs={{0,16},{4,20},{8,24},{12,28},{16,0},{20,4},{24,8},{28,12},{1,17},{... | collective-permute-start | bytes 1572872 | tf_op jit(solution)/shard_map/ppermute | solution.py:379
  57.6 1.5 %slice_add_fusion = f32[1,64,2048]{2,1,0:T(8,128)S(1)} fusion(f32[2,64,2048]{2,1,0:T(8,128)S(1)} %collective-permute-done.10.refs_4_, f32[2,64,2048]{2,1,0:T(8,128)} %get-tuple-element.23.refs_3_), kind=kLoop, calls=%fused_computation | loop fusion | flops 131072 | bytes 1572864 | tf_op jit(solution)/shard_map/add | solution.py:427
  59.1 1.4 %collective-permute-start.11 = (f32[1,64,2048]{2,1,0:T(8,128)S(1)}, f32[1,64,2048]{2,1,0:T(8,128)S(1)}, u32[]{:S(2)}, u32[]{:S(2)}) collective-permute-start(f32[1,64,2048]{2,1,0:T(8,128)S(1)} %slice_add_fusion), channel_id=1, source_target_pairs={{0,8},{4,12},{8,0},{12,4},{16,24},{20,28},{24,16},{28,20},{1,9},{5... | collective-permute-start | bytes 1572872 | tf_op jit(solution)/shard_map/ppermute | solution.py:379
  60.5 0.7 collective-permute-start.6
  61.2 11.6 %collective-permute-done.6 = f32[64,128]{1,0:T(8,128)S(1)} collective-permute-done((f32[64,128]{1,0:T(8,128)}, f32[64,128]{1,0:T(8,128)S(1)}, u32[]{:S(2)}, u32[]{:S(2)}) %collective-permute-start.6) | collective-permute-done | bytes 32800 | tf_op jit(solution)/shard_map/ppermute | solution.py:379
  72.7 0.8 add.12
  73.9 3.6 %collective-permute-done.7 = f32[64,128]{1,0:T(8,128)S(1)} collective-permute-done((f32[64,128]{1,0:T(8,128)S(1)}, f32[64,128]{1,0:T(8,128)S(1)}, u32[]{:S(2)}, u32[]{:S(2)}) %collective-permute-start.7) | collective-permute-done | bytes 32800 | tf_op jit(solution)/shard_map/ppermute | solution.py:379
  78.1 0.8 copy-done.2
  78.8 0.8 copy-done.3
  79.6 2.9 %finish.1 = f32[64,4096]{1,0:T(8,128)} custom-call(s32[1]{0:T(128)} %bitcast.me_ref, s32[1,32768]{1,0:T(1,128)} %constant.14.clone.index_ref, f32[64,128]{1,0:T(8,128)} %add.13.shell_ref, f32[2,64,2048]{2,1,0:T(8,128)} %get-tuple-element.21.refs_0_, f32[2,64,2048]{2,1,0:T(8,128)} %copy-done, f32[1,64,2048]{2,1,0:T(8,128)} %copy-done.2, ...), custom_call_target="tpu_custom_call" | custom-call | tf_op jit(solution)/shard_map/finish/pallas_call | solution.py:369
  (33 shorter events, 3.3 us)
Async XLA Ops:
  0.0 15.6 %copy-start.4 = (f32[64,64]{1,0:T(8,128)S(1)}, f32[64,64]{1,0:T(8,128)}, u32[]{:S(2)}) copy-start(f32[64,64]{1,0:T(8,128)} %own_ctf_ref.3) | copy-start | bytes 49156
  0.0 15.6 %copy-start.7 = (s32[64,2,64]{2,1,0:T(2,128)S(1)}, s32[64,2,64]{2,1,0:T(2,128)}, u32[]{:S(2)}) copy-start(s32[64,2,64]{2,1,0:T(2,128)} %param.10) | copy-start | bytes 98308
  9.4 15.0 %collective-permute-start.5 = (f32[4,64,4096]{2,1,0:T(8,128)}, f32[4,64,4096]{2,1,0:T(8,128)}, u32[]{:S(2)}, u32[]{:S(2)}) collective-permute-start(f32[4,64,4096]{2,1,0:T(8,128)} %get-tuple-element.19), channel_id=1, source_target_pairs={{0,4},{4,0},{8,12},{12,8},{16,20},{20,16},{24,28},{28,24},{1,5},{5... | collective-permute-start | bytes 12582920 | tf_op jit(solution)/shard_map/ppermute | solution.py:379
  9.9 9.3 %collective-permute-start.2 = (f32[64,64]{1,0:T(8,128)}, f32[64,64]{1,0:T(8,128)S(1)}, u32[]{:S(2)}, u32[]{:S(2)}) collective-permute-start(f32[64,64]{1,0:T(8,128)} %get-tuple-element.17.refs_0_), channel_id=1, source_target_pairs={{0,3},{1,0},{2,1},{3,2},{4,7},{5,4},{6,5},{7,6},{8,11},{9,8},{10,9... | collective-permute-start | bytes 49160 | tf_op jit(solution)/shard_map/ppermute | solution.py:399
  14.6 5.4 %collective-permute-start.1 = (f32[64,64]{1,0:T(8,128)}, f32[64,64]{1,0:T(8,128)S(1)}, u32[]{:S(2)}, u32[]{:S(2)}) collective-permute-start(f32[64,64]{1,0:T(8,128)} %get-tuple-element.17.refs_0_), channel_id=1, source_target_pairs={{0,2},{1,3},{2,0},{3,1},{4,6},{5,7},{6,4},{7,5},{8,10},{9,11},{10,... | collective-permute-start | bytes 49160 | tf_op jit(solution)/shard_map/ppermute | solution.py:399
  14.6 5.9 %collective-permute-start = (f32[64,64]{1,0:T(8,128)}, f32[64,64]{1,0:T(8,128)S(1)}, u32[]{:S(2)}, u32[]{:S(2)}) collective-permute-start(f32[64,64]{1,0:T(8,128)} %get-tuple-element.17.refs_0_), channel_id=1, source_target_pairs={{0,1},{1,2},{2,3},{3,0},{4,5},{5,6},{6,7},{7,4},{8,9},{9,10},{10,1... | collective-permute-start | bytes 49160 | tf_op jit(solution)/shard_map/ppermute | solution.py:399
  15.6 7.4 %collective-permute-start.4 = (f32[64,64]{1,0:T(8,128)S(1)}, f32[64,64]{1,0:T(8,128)S(1)}, u32[]{:S(2)}, u32[]{:S(2)}) collective-permute-start(f32[64,64]{1,0:T(8,128)S(1)} %copy-done.4), channel_id=1, source_target_pairs={{0,4},{4,0},{8,12},{12,8},{16,20},{20,16},{24,28},{28,24},{1,5},{5... | collective-permute-start | bytes 49160 | tf_op jit(solution)/shard_map/ppermute | solution.py:379
  19.2 1.4 %copy-start.8 = (f32[64,64]{1,0:T(8,128)}, f32[64,64]{1,0:T(8,128)S(1)}, u32[]{:S(2)}) copy-start(f32[64,64]{1,0:T(8,128)S(1)} %collective-permute-done.2.refs_3_) | copy-start | bytes 49156
  20.0 0.6 copy-start.9
  20.5 0.6 copy-start.10
  23.0 1.4 %collective-permute-start.3 = (f32[64,64]{1,0:T(8,128)}, f32[64,64]{1,0:T(8,128)S(1)}, u32[]{:S(2)}, u32[]{:S(2)}) collective-permute-start(f32[64,64]{1,0:T(8,128)} %weigh.1.own_w_ref), channel_id=1, source_target_pairs={{0,4},{4,0},{8,12},{12,8},{16,20},{20,16},{24,28},{28,24},{1,5},{5... | collective-permute-start | bytes 49160 | tf_op jit(solution)/shard_map/ppermute | solution.py:379
  23.0 1.4 %copy-start.5 = (f32[64,64]{1,0:T(8,128)}, f32[64,64]{1,0:T(8,128)S(1)}, u32[]{:S(2)}) copy-start(f32[64,64]{1,0:T(8,128)S(1)} %collective-permute-done.4.sib_ctf_ref) | copy-start | bytes 49156
  24.4 0.6 copy-start.6
  28.9 25.5 %collective-permute-start.8 = (f32[2,64,2048]{2,1,0:T(8,128)}, f32[2,64,2048]{2,1,0:T(8,128)S(1)}, u32[]{:S(2)}, u32[]{:S(2)}) collective-permute-start(f32[2,64,2048]{2,1,0:T(8,128)} %get-tuple-element.22), channel_id=1, source_target_pairs={{0,8},{4,12},{8,0},{12,4},{16,24},{20,28},{24,16},{28,20},{1,9},{5... | collective-permute-start | bytes 3145736 | tf_op jit(solution)/shard_map/ppermute | solution.py:379
  30.6 27.0 %collective-permute-start.10 = (f32[2,64,2048]{2,1,0:T(8,128)}, f32[2,64,2048]{2,1,0:T(8,128)S(1)}, u32[]{:S(2)}, u32[]{:S(2)}) collective-permute-start(f32[2,64,2048]{2,1,0:T(8,128)} %get-tuple-element.24), channel_id=1, source_target_pairs={{0,16},{4,20},{8,24},{12,28},{16,0},{20,4},{24,8},{28,12},{1,17},{... | collective-permute-start | bytes 3145736 | tf_op jit(solution)/shard_map/ppermute | solution.py:379
  54.4 23.6 %copy-start = (f32[2,64,2048]{2,1,0:T(8,128)}, f32[2,64,2048]{2,1,0:T(8,128)S(1)}, u32[]{:S(2)}) copy-start(f32[2,64,2048]{2,1,0:T(8,128)S(1)} %collective-permute-done.8.refs_1_) | copy-start | bytes 3145732
  55.9 22.1 %collective-permute-start.9 = (f32[1,64,2048]{2,1,0:T(8,128)S(1)}, f32[1,64,2048]{2,1,0:T(8,128)S(1)}, u32[]{:S(2)}, u32[]{:S(2)}) collective-permute-start(f32[1,64,2048]{2,1,0:T(8,128)S(1)} %slice_add_fusion.1), channel_id=1, source_target_pairs={{0,16},{4,20},{8,24},{12,28},{16,0},{20,4},{24,8},{28,12},{1,17},{... | collective-permute-start | bytes 1572872 | tf_op jit(solution)/shard_map/ppermute | solution.py:379
  57.6 20.4 %copy-start.1 = (f32[2,64,2048]{2,1,0:T(8,128)}, f32[2,64,2048]{2,1,0:T(8,128)S(1)}, u32[]{:S(2)}) copy-start(f32[2,64,2048]{2,1,0:T(8,128)S(1)} %collective-permute-done.10.refs_4_) | copy-start | bytes 3145732
  59.1 19.0 %collective-permute-start.11 = (f32[1,64,2048]{2,1,0:T(8,128)S(1)}, f32[1,64,2048]{2,1,0:T(8,128)S(1)}, u32[]{:S(2)}, u32[]{:S(2)}) collective-permute-start(f32[1,64,2048]{2,1,0:T(8,128)S(1)} %slice_add_fusion), channel_id=1, source_target_pairs={{0,8},{4,12},{8,0},{12,4},{16,24},{20,28},{24,16},{28,20},{1,9},{5... | collective-permute-start | bytes 1572872 | tf_op jit(solution)/shard_map/ppermute | solution.py:379
  60.5 12.2 %collective-permute-start.6 = (f32[64,128]{1,0:T(8,128)}, f32[64,128]{1,0:T(8,128)S(1)}, u32[]{:S(2)}, u32[]{:S(2)}) collective-permute-start(f32[64,128]{1,0:T(8,128)} %get-tuple-element.20), channel_id=1, source_target_pairs={{0,8},{4,12},{8,0},{12,4},{16,24},{20,28},{24,16},{28,20},{1,9},{5... | collective-permute-start | bytes 98312 | tf_op jit(solution)/shard_map/ppermute | solution.py:379
  73.5 3.9 %collective-permute-start.7 = (f32[64,128]{1,0:T(8,128)S(1)}, f32[64,128]{1,0:T(8,128)S(1)}, u32[]{:S(2)}, u32[]{:S(2)}) collective-permute-start(f32[64,128]{1,0:T(8,128)S(1)} %add.12), channel_id=1, source_target_pairs={{0,16},{4,20},{8,24},{12,28},{16,0},{20,4},{24,8},{28,12},{1,17},{... | collective-permute-start | bytes 98312 | tf_op jit(solution)/shard_map/ppermute | solution.py:379
  78.0 0.8 copy-start.2
  78.8 0.8 copy-start.3

commit v3 on v2

--- a/solution.py
+++ b/solution.py
@@ -12,7 +12,7 @@
 F32 = jnp.float32
 BF16 = jnp.bfloat16
 LANES = 128
-VMEM_LIMIT = 60 * 1024 * 1024
+MIB = 1024 * 1024
 
 
 def entry_shells(width, shells):
@@ -27,8 +27,8 @@
     return np.repeat(shell, 2).astype(np.int32)[None, :]
 
 
-def params(**more):
-    return pltpu.CompilerParams(vmem_limit_bytes=VMEM_LIMIT, **more)
+def params(mib):
+    return pltpu.CompilerParams(vmem_limit_bytes=mib * MIB)
 
 
 def lanes_wide(table):
@@ -164,9 +164,10 @@
     blocks = 4
     span = width // (2 * blocks)
     held = pl.BlockSpec(memory_space=pl.ANY)
+    far = pl.BlockSpec(memory_space=pltpu.HBM)
     return pl.pallas_call(
         functools.partial(estep_kernel, blocks),
-        in_specs=[pl.BlockSpec(memory_space=pltpu.SMEM)] + [held] * 4,
+        in_specs=[pl.BlockSpec(memory_space=pltpu.SMEM)] + [far] * 4,
         out_specs=[held, held, pl.BlockSpec(memory_space=pltpu.VMEM)],
         out_shape=[
             jax.ShapeDtypeStruct((chips, rows, share), F32),
@@ -186,9 +187,9 @@
             pltpu.SemaphoreType.DMA((blocks, 2, 2)),
             pltpu.SemaphoreType.DMA((chips, 2)),
         ],
-        compiler_params=params(),
+        compiler_params=params(28),
         name="estep",
-    )(me, index, images, planes, ctf_table)
+    )(me, *[pltpu.with_memory_space_constraint(part, pltpu.HBM) for part in (index, images, planes, ctf_table)])
 
 
 def count_kernel(slabs, slab_ref, prior_ref, noise_ref, list_ref, base_ref, scale_ref):
@@ -224,7 +225,7 @@
             jax.ShapeDtypeStruct((classes, rows, width), F32),
             jax.ShapeDtypeStruct((rows, width), F32),
         ],
-        compiler_params=params(),
+        compiler_params=params(4),
         cost_estimate=pl.CostEstimate(flops=10**7, bytes_accessed=10**6, transcendentals=0),
         name="count",
     )(
@@ -257,19 +258,18 @@
     return pl.pallas_call(
         weigh_kernel,
         out_shape=jax.ShapeDtypeStruct((planes, rows), F32),
-        compiler_params=params(),
+        compiler_params=params(4),
         name="weigh",
     )(base, scale, *tables)
 
 
-def sums_kernel(items, with_shells, own_w_ref, sib_w_ref, own_ctf_ref, sib_ctf_ref, keep_hbm, got_hbm, *refs):
+def sums_kernel(items, own_w_ref, sib_w_ref, own_ctf_ref, sib_ctf_ref, keep_hbm, got_hbm, *refs):
     outs = refs[: len(items)]
-    shell_ref = refs[len(items)] if with_shells else None
     keep, got, sums, in_sem, out_sem = refs[-5:]
     tile = keep_hbm.shape[2] // 4
     number, _, wide = keep.shape
     cells = wide // tile
-    places = [(out, slot, k, side) for out, (side, ks) in enumerate(items) for slot, k in enumerate(ks)]
+    places = [(out, slot, k, out) for out, ks in enumerate(items) for slot, k in enumerate(ks)]
     incoming, outgoing = [], []
     for place, (out, slot, k, side) in enumerate(places):
         copies = []
@@ -285,49 +285,48 @@
                 ),
             ]
         incoming.append(copies)
-        outgoing.append(pltpu.make_async_copy(sums.at[place], outs[out].at[slot], out_sem.at[place]))
+        filled = sums.at[place] if side == 0 else sums.at[place, :, :wide]
+        outgoing.append(pltpu.make_async_copy(filled, outs[out].at[slot], out_sem.at[place]))
     for copy in [copy for copies in incoming for copy in copies]:
         copy.start()
     weights = jnp.concatenate([own_w_ref[...], sib_w_ref[...]], axis=1).astype(BF16)
-    if with_shells:
-        ctf = jnp.concatenate([own_ctf_ref[...], sib_ctf_ref[...]], axis=0)
-        square = lanes_wide((ctf * ctf).astype(BF16))
-        shell_ref[...] = jnp.dot(weights, square, preferred_element_type=F32)
-    for place in range(number):
+    ctf = jnp.concatenate([own_ctf_ref[...], sib_ctf_ref[...]], axis=0)
+    shells = jnp.dot(weights, lanes_wide((ctf * ctf).astype(BF16)), preferred_element_type=F32)
+    for place, (_, _, _, side) in enumerate(places):
         for copy in incoming[place]:
             copy.wait()
         images = jnp.concatenate([keep[place], got[place].astype(BF16)], axis=0)
-        sums[place] = jnp.dot(weights, images, preferred_element_type=F32)
+        sums[place, :, :wide] = jnp.dot(weights, images, preferred_element_type=F32)
+        if side == 0:
+            sums[place, :, wide:] = shells
         outgoing[place].start()
     for copy in outgoing:
         copy.wait()
 
 
-def partial_sums(items, with_shells, own_w, sib_w, own_ctf, sib_ctf, keep, got):
+def partial_sums(items, own_w, sib_w, own_ctf, sib_ctf, keep, got):
     chips, rows, share = keep.shape
     planes = own_w.shape[0]
     wide = share // 2
-    number = sum(len(ks) for _, ks in items)
+    number = sum(len(ks) for ks in items)
     held = pl.BlockSpec(memory_space=pl.ANY)
     vmem = pl.BlockSpec(memory_space=pltpu.VMEM)
-    out_specs = [held] * len(items)
-    out_shape = [jax.ShapeDtypeStruct((len(ks), planes, wide), F32) for _, ks in items]
-    if with_shells:
-        out_specs.append(vmem)
-        out_shape.append(jax.ShapeDtypeStruct((planes, LANES), F32))
     return pl.pallas_call(
-        functools.partial(sums_kernel, items, with_shells),
+        functools.partial(sums_kernel, items),
         in_specs=[vmem] * 4 + [held] * 2,
-        out_specs=out_specs,
-        out_shape=out_shape,
+        out_specs=[held] * 2,
+        out_shape=[
+            jax.ShapeDtypeStruct((len(ks), planes, wide + extra), F32)
+            for ks, extra in zip(items, (LANES, 0))
+        ],
         scratch_shapes=[
             pltpu.VMEM((number, rows, wide), BF16),
             pltpu.VMEM((number, rows, wide), F32),
-            pltpu.VMEM((number, planes, wide), F32),
+            pltpu.VMEM((number, planes, wide + LANES), F32),
             pltpu.SemaphoreType.DMA((number, 2, 2)),
             pltpu.SemaphoreType.DMA((number,)),
         ],
-        compiler_params=params(),
+        compiler_params=params(12),
         cost_estimate=pl.CostEstimate(
             flops=4 * planes * rows * wide * number,
             bytes_accessed=10 * planes * wide * number,
@@ -337,11 +336,11 @@
     )(own_w, sib_w, own_ctf, sib_ctf, keep, got)
 
 
-def finish_kernel(number, me_ref, index_ref, shell_ref, *refs):
+def finish_kernel(numbers, me_ref, index_ref, *refs):
     out_ref = refs[-1]
-    left = functools.reduce(jnp.add, [ref[0] for ref in refs[:number]])
-    right = functools.reduce(jnp.add, [ref[0] for ref in refs[number : 2 * number]])
-    shells = shell_ref[...]
+    left = functools.reduce(jnp.add, [ref[0] for ref in refs[: numbers[0]]])
+    shells = functools.reduce(jnp.add, [ref[0] for ref in refs[numbers[0] : 2 * numbers[0]]])
+    right = functools.reduce(jnp.add, [ref[0] for ref in refs[2 * numbers[0] : -1]])
     tile = left.shape[1]
     for side, block in ((0, left), (1, right)):
         for start in range(0, tile, LANES):
@@ -350,29 +349,33 @@
             out_ref[:, cut] = block[:, start : start + LANES] / (weight + 1.0)
 
 
-def finish(me, index, shells, left, right, share):
-    planes = left[0].shape[1]
+def finish(me, index, left, right, share):
+    planes = left[0][0].shape[1]
     tile = share // 4
-    number = len(left)
     cells = share // (2 * tile)
-    side = pl.BlockSpec((1, planes, tile), lambda cell, m: (0, 0, cell))
+
+    def side(place):
+        return pl.BlockSpec((1, planes, tile), lambda cell, m: (place, 0, cell))
+
+    def tail(place):
+        return pl.BlockSpec((1, planes, LANES), lambda cell, m: (place, 0, share // 2 // LANES))
+
     grid_spec = pltpu.PrefetchScalarGridSpec(
         num_scalar_prefetch=1,
         grid=(cells,),
-        in_specs=[
-            pl.BlockSpec((1, 2 * tile), lambda cell, m: (0, m[0] * cells + cell)),
-            pl.BlockSpec((planes, LANES), lambda cell, m: (0, 0)),
-        ]
-        + [side] * (2 * number),
+        in_specs=[pl.BlockSpec((1, 2 * tile), lambda cell, m: (0, m[0] * cells + cell))]
+        + [side(place) for _, place in left]
+        + [tail(place) for _, place in left]
+        + [side(place) for _, place in right],
         out_specs=pl.BlockSpec((planes, 2 * tile), lambda cell, m: (0, cell)),
     )
     return pl.pallas_call(
-        functools.partial(finish_kernel, number),
+        functools.partial(finish_kernel, (len(left), len(right))),
         grid_spec=grid_spec,
         out_shape=jax.ShapeDtypeStruct((planes, share), F32),
-        compiler_params=params(),
+        compiler_params=params(12),
         name="finish",
-    )(me, index, shells, *left, *right)
+    )(me, index, *[part for part, _ in left + left + right])
 
 
 def swap(array, bit, size):
@@ -410,32 +413,39 @@
         partial_sums,
         own_w=own_w, sib_w=sib_w, own_ctf=ctf_table, sib_ctf=sib_ctf, keep=keep, got=got,
     )
-    top = chips // 2
-    send_left, send_right = sums(
-        ((0, tuple(range(1, chips, 2))), (1, tuple(range(top, chips)))), False
-    )
-    left_in = swap(send_left, 2, size)
-    right_in = swap(send_right, 2 * top, size)
-    keep_left, keep_right, shells = sums(
-        ((0, tuple(range(0, chips, 2))), (1, tuple(range(top)))), True
-    )
-    lefts, rights = [keep_left, left_in], [keep_right, right_in]
-    bit = 2
-    while bit < chips:
-        number = rights[-1].shape[0] // 2
-        left_out = sum(part[1::2] for part in lefts)
-        right_out = sum(part[number:] for part in rights)
-        if number > 1:
-            lefts = [part[0::2] for part in lefts]
-            rights = [part[:number] for part in rights]
-        lefts.append(swap(left_out, 2 * bit, size))
-        rights.append(swap(right_out, chips // bit, size))
-        bit *= 2
-    bit = 2
-    while bit < size:
-        shells = shells + swap(shells, bit, size)
-        bit *= 2
-    out = finish(me, index, shells, lefts, rights, share)
+    low = [1 << place for place in range(chips.bit_length() - 1)]
+    orders = (low, low[::-1])
+    first = [[k for k in range(chips) if k & order[0]] for order in orders]
+    onward = [[k for k in ks if k & order[1]] for ks, order in zip(first, orders)]
+    direct = [[k for k in ks if not k & order[1]] for ks, order in zip(first, orders)]
+    stay = [[k for k in range(chips) if not k & order[0]] for order in orders]
+    parts = [{k: [] for k in ks} for ks in stay]
+
+    def deliver(side, ks, array, bit):
+        arrived = swap(array, 2 * bit, size)
+        for place, k in enumerate(ks):
+            parts[side][k ^ bit].append((arrived, place))
+
+    def compute(groups):
+        return sums(tuple(tuple(ks) for ks in groups))
+
+    sent = compute(onward)
+    for side in (0, 1):
+        deliver(side, onward[side], sent[side], orders[side][0])
+    sent = compute(direct)
+    for side in (0, 1):
+        deliver(side, direct[side], sent[side], orders[side][0])
+    kept = compute(stay)
+    for side in (0, 1):
+        for place, k in enumerate(stay[side]):
+            parts[side][k].append((kept[side], place))
+    for turn in range(1, len(low)):
+        for side in (0, 1):
+            bit = orders[side][turn]
+            ks = [k for k in parts[side] if k & bit]
+            sent = jnp.stack([sum(part[place] for part, place in parts[side].pop(k)) for k in ks])
+            deliver(side, ks, sent, bit)
+    out = finish(me, index, parts[0][0], parts[1][0], share)
     return out.reshape(classes, local_planes, share)
 
 

time: 83.1 us -> 62 us (0.75)
  Pallas kernels: 25.4 us -> 17.9 us
  waiting for transfers between devices: 35.8 us -> 29.1 us
  other arithmetic: 4.29 us -> 0.11 us
  local copies, waits for them, and re-layouts: 3.53 us -> 0.12 us
  starting transfers between devices: 13.5 us -> 14.5 us
    ppermute x9, waiting for transfers between devices: 34.4 us -> 28 us  [swap(): return lax.ppermute(array, 'img', [(one, one ^ bit) for one in range(size)])]
    add x4 -> x2, other arithmetic: 4.29 us -> 0.11 us  [shards(): sum((part[place] for part, place in parts[side].pop(k)))]
    pallas_call x3 -> x4, Pallas kernels: 11.3 us -> 7.55 us  [the longest x3 5.79 us: partial_sums(): pl.pallas_call(functools.partial(sums_kernel, items), in_specs=[vmem] * 4...]
    unnamed x22 -> x10, local copies, waits for them, and re-layouts: 2.81 us -> 0.02 us
    pallas_call x1, Pallas kernels: 1.87 us -> 0.36 us  [weigh(): pl.pallas_call(weigh_kernel, out_shape=jax.ShapeDtypeStruct((planes, rows...]
    pallas_call x1, Pallas kernels: 2.81 us -> 1.38 us  [count_planes(): pl.pallas_call(functools.partial(count_kernel, slabs), in_specs=[pl.Block...]
    ppermute x3, starting transfers between devices: 5.72 us -> 6.61 us  [shards(): lax.ppermute(table, 'slab', [(one, (one + hop) % slabs) for one in range(...]
    pallas_call x1, Pallas kernels: 9.43 us -> 8.56 us  [estep(): pl.pallas_call(functools.partial(estep_kernel, blocks), in_specs=[pl.Bloc...]
  transfers between devices with their start and end apart: 12 -> 12, of which waited for: 6 -> 6; matrix products, arithmetic and copies ran while one was open for 6% -> 0% of each run, Pallas kernels for 11% -> 9%
where the time goes in v3:
time: 62 us; the launch traced here: 61.8 us
  waiting for transfers between devices  29.1 us (47%)
  Pallas kernels  17.9 us (29%)
  starting transfers between devices  14.5 us (23%)
    ppermute x9, waiting for transfers between devices, swap(): return lax.ppermute(array, 'img', [(one, one ^ bit) for one in range(size)])  28 us
    pallas_call x1, Pallas kernels, estep(): pl.pallas_call(functools.partial(estep_kernel, blocks), in_specs=[pl.Bloc...  8.56 us
    ppermute x9, starting transfers between devices, swap(): return lax.ppermute(array, 'img', [(one, one ^ bit) for one in range(size)])  7.9 us
    ppermute x3, starting transfers between devices, shards(): lax.ppermute(table, 'slab', [(one, (one + hop) % slabs) for one in range(...  6.61 us
    pallas_call x3, Pallas kernels, partial_sums(): pl.pallas_call(functools.partial(sums_kernel, items), in_specs=[vmem] * 4...  5.79 us
    pallas_call x1, Pallas kernels, finish(): pl.pallas_call(functools.partial(finish_kernel, (len(left), len(right))),...  1.77 us
    pallas_call x1, Pallas kernels, count_planes(): pl.pallas_call(functools.partial(count_kernel, slabs), in_specs=[pl.Block...  1.38 us
  transfers between devices with their start and end apart: 12, of which 6 were waited for; matrix products, arithmetic and copies ran while one was open for 0% of the time, Pallas kernels for 9%

profile of v3, /device:TPU:0, one launch (start us, length us, event | category | flops | bytes accessed | tf_op | source)
XLA Modules:
  0.0 61.8 jit_solution(17799769773798167748)
XLA Ops:
  0.0 8.6 %estep.1 = (f32[4,64,4096]{2,1,0:T(8,128)}, bf16[4,64,4096]{2,1,0:T(8,128)(2,1)S(1)}, f32[64,64]{1,0:T(8,128)S(1)}) custom-call(s32[1]{0:T(128)} %bitcast.me_ref, s32[1,16640]{1,0:T(1,128)} %constant.13.clone.index_hbm, bf16[64,32768]{1,0:T(8,128)(2,1)} %image_hbm.1, bf16[64,32768]{1,0:T(8,128)(2,1)} %bitcast.8, f32[64,64]{1,0:T(8,128)} %own_ctf_ref.5), custom_call_target="tpu_custom_call" | custom-call | tf_op jit(solution)/shard_map/estep/pallas_call | solution.py:168
  8.6 0.5 collective-permute-start.5
  9.1 2.7 %collective-permute-start = (f32[64,64]{1,0:T(8,128)S(1)}, f32[64,64]{1,0:T(8,128)S(1)}, u32[]{:S(2)}, u32[]{:S(2)}) collective-permute-start(f32[64,64]{1,0:T(8,128)S(1)} %get-tuple-element.18.refs_0_), channel_id=1, source_target_pairs={{0,1},{1,2},{2,3},{3,0},{4,5},{5,6},{6,7},{7,4},{8,9},{9,10},{10,1... | collective-permute-start | bytes 49160 | tf_op jit(solution)/shard_map/ppermute | solution.py:402
  11.8 2.6 %collective-permute-start.1 = (f32[64,64]{1,0:T(8,128)S(1)}, f32[64,64]{1,0:T(8,128)S(1)}, u32[]{:S(2)}, u32[]{:S(2)}) collective-permute-start(f32[64,64]{1,0:T(8,128)S(1)} %get-tuple-element.18.refs_0_), channel_id=1, source_target_pairs={{0,2},{1,3},{2,0},{3,1},{4,6},{5,7},{6,4},{7,5},{8,10},{9,11},{10,... | collective-permute-start | bytes 49160 | tf_op jit(solution)/shard_map/ppermute | solution.py:402
  14.3 1.3 %collective-permute-start.2 = (f32[64,64]{1,0:T(8,128)S(1)}, f32[64,64]{1,0:T(8,128)S(1)}, u32[]{:S(2)}, u32[]{:S(2)}) collective-permute-start(f32[64,64]{1,0:T(8,128)S(1)} %get-tuple-element.18.refs_0_), channel_id=1, source_target_pairs={{0,3},{1,0},{2,1},{3,2},{4,7},{5,4},{6,5},{7,6},{8,11},{9,8},{10,9... | collective-permute-start | bytes 49160 | tf_op jit(solution)/shard_map/ppermute | solution.py:402
  15.7 0.1 reshape.25.list_ref
  15.8 1.4 %count.1 = (f32[2,64,128]{2,1,0:T(8,128)S(1)}, f32[64,128]{1,0:T(8,128)S(1)}) custom-call(s32[1]{0:T(128)} %bitcast.1.slab_ref, f32[1,2]{1,0:T(1,128)S(1)} %bitcast.6, f32[1,64]{1,0:T(1,128)S(1)} %bitcast.7, s32[64,128]{1,0:T(8,128)S(1)} %reshape.25.list_ref), custom_call_target="tpu_custom_call" | custom-call | flops 10000000 | bytes 1000000 | tf_op jit(solution)/shard_map/count/pallas_call | solution.py:220
  17.2 1.0 %collective-permute-done.2.refs_3_ = f32[64,64]{1,0:T(8,128)S(1)} collective-permute-done((f32[64,64]{1,0:T(8,128)S(1)}, f32[64,64]{1,0:T(8,128)S(1)}, u32[]{:S(2)}, u32[]{:S(2)}) %collective-permute-start.2) | collective-permute-done | bytes 16416 | tf_op jit(solution)/shard_map/ppermute | solution.py:402
  18.3 0.4 weigh.1.own_w_ref
  18.7 1.2 %collective-permute-done.3.sib_w_ref = f32[64,64]{1,0:T(8,128)S(1)} collective-permute-done((f32[64,64]{1,0:T(8,128)S(1)}, f32[64,64]{1,0:T(8,128)S(1)}, u32[]{:S(2)}, u32[]{:S(2)}) %collective-permute-start.3) | collective-permute-done | bytes 16416 | tf_op jit(solution)/shard_map/ppermute | solution.py:382
  19.9 1.7 %sums.5 = (f32[1,64,2176]{2,1,0:T(8,128)S(1)}, f32[1,64,2048]{2,1,0:T(8,128)S(1)}) custom-call(f32[64,64]{1,0:T(8,128)S(1)} %weigh.1.own_w_ref, f32[64,64]{1,0:T(8,128)S(1)} %collective-permute-done.3.sib_w_ref, f32[64,64]{1,0:T(8,128)S(1)} %copy-done, f32[64,64]{1,0:T(8,128)S(1)} %collective-permute-done.4.sib_ctf_ref, ...), custom_call_target="tpu_custom_call" | custom-call | flops 67108864 | bytes 2621440 | tf_op jit(solution)/shard_map/sums/pallas_call | solution.py:314
  21.6 1.5 %collective-permute-start.7 = (f32[1,64,2176]{2,1,0:T(8,128)S(1)}, f32[1,64,2176]{2,1,0:T(8,128)S(1)}, u32[]{:S(2)}, u32[]{:S(2)}) collective-permute-start(f32[1,64,2176]{2,1,0:T(8,128)S(1)} %get-tuple-element.23), channel_id=1, source_target_pairs={{0,8},{4,12},{8,0},{12,4},{16,24},{20,28},{24,16},{28,20},{1,9},{5... | collective-permute-start | bytes 1671176 | tf_op jit(solution)/shard_map/ppermute | solution.py:382
  23.1 1.6 %collective-permute-start.10 = (f32[1,64,2048]{2,1,0:T(8,128)S(1)}, f32[1,64,2048]{2,1,0:T(8,128)S(1)}, u32[]{:S(2)}, u32[]{:S(2)}) collective-permute-start(f32[1,64,2048]{2,1,0:T(8,128)S(1)} %get-tuple-element.26), channel_id=1, source_target_pairs={{0,16},{4,20},{8,24},{12,28},{16,0},{20,4},{24,8},{28,12},{1,17},{... | collective-permute-start | bytes 1572872 | tf_op jit(solution)/shard_map/ppermute | solution.py:382
  24.7 1.7 %sums.3 = (f32[1,64,2176]{2,1,0:T(8,128)S(1)}, f32[1,64,2048]{2,1,0:T(8,128)S(1)}) custom-call(f32[64,64]{1,0:T(8,128)S(1)} %weigh.1.own_w_ref, f32[64,64]{1,0:T(8,128)S(1)} %collective-permute-done.3.sib_w_ref, f32[64,64]{1,0:T(8,128)S(1)} %copy-done, f32[64,64]{1,0:T(8,128)S(1)} %collective-permute-done.4.sib_ctf_ref, ...), custom_call_target="tpu_custom_call" | custom-call | flops 67108864 | bytes 2621440 | tf_op jit(solution)/shard_map/sums/pallas_call | solution.py:314
  26.4 0.6 collective-permute-start.6
  27.0 0.5 collective-permute-start.9
  27.5 2.4 %sums.4 = (f32[2,64,2176]{2,1,0:T(8,128)S(1)}, f32[2,64,2048]{2,1,0:T(8,128)S(1)}) custom-call(f32[64,64]{1,0:T(8,128)S(1)} %weigh.1.own_w_ref, f32[64,64]{1,0:T(8,128)S(1)} %collective-permute-done.3.sib_w_ref, f32[64,64]{1,0:T(8,128)S(1)} %copy-done, f32[64,64]{1,0:T(8,128)S(1)} %collective-permute-done.4.sib_ctf_ref, ...), custom_call_target="tpu_custom_call" | custom-call | flops 134217728 | bytes 5242880 | tf_op jit(solution)/shard_map/sums/pallas_call | solution.py:314
  29.9 7.3 %collective-permute-done.7 = f32[1,64,2176]{2,1,0:T(8,128)S(1)} collective-permute-done((f32[1,64,2176]{2,1,0:T(8,128)S(1)}, f32[1,64,2176]{2,1,0:T(8,128)S(1)}, u32[]{:S(2)}, u32[]{:S(2)}) %collective-permute-start.7) | collective-permute-done | bytes 557088 | tf_op jit(solution)/shard_map/ppermute | solution.py:382
  37.2 1.6 %collective-permute-start.8 = (f32[1,64,2176]{2,1,0:T(8,128)S(1)}, f32[1,64,2176]{2,1,0:T(8,128)S(1)}, u32[]{:S(2)}, u32[]{:S(2)}) collective-permute-start(f32[1,64,2176]{2,1,0:T(8,128)S(1)} %slice_add_fusion), channel_id=1, source_target_pairs={{0,16},{4,20},{8,24},{12,28},{16,0},{20,4},{24,8},{28,12},{1,17},{... | collective-permute-start | bytes 1671176 | tf_op jit(solution)/shard_map/ppermute | solution.py:382
  38.8 1.6 %collective-permute-start.11 = (f32[1,64,2048]{2,1,0:T(8,128)S(1)}, f32[1,64,2048]{2,1,0:T(8,128)S(1)}, u32[]{:S(2)}, u32[]{:S(2)}) collective-permute-start(f32[1,64,2048]{2,1,0:T(8,128)S(1)} %slice_add_fusion.1), channel_id=1, source_target_pairs={{0,8},{4,12},{8,0},{12,4},{16,24},{20,28},{24,16},{28,20},{1,9},{5... | collective-permute-start | bytes 1572872 | tf_op jit(solution)/shard_map/ppermute | solution.py:382
  40.4 8.8 %collective-permute-done.9.refs_6_ = f32[1,64,2048]{2,1,0:T(8,128)S(1)} collective-permute-done((f32[1,64,2048]{2,1,0:T(8,128)S(1)}, f32[1,64,2048]{2,1,0:T(8,128)S(1)}, u32[]{:S(2)}, u32[]{:S(2)}) %collective-permute-start.9) | collective-permute-done | bytes 524320 | tf_op jit(solution)/shard_map/ppermute | solution.py:382
  49.2 10.3 %collective-permute-done.11.refs_8_ = f32[1,64,2048]{2,1,0:T(8,128)S(1)} collective-permute-done((f32[1,64,2048]{2,1,0:T(8,128)S(1)}, f32[1,64,2048]{2,1,0:T(8,128)S(1)}, u32[]{:S(2)}, u32[]{:S(2)}) %collective-permute-start.11) | collective-permute-done | bytes 524320 | tf_op jit(solution)/shard_map/ppermute | solution.py:382
  59.5 0.5 collective-permute-done.8.refs_2_.refs_5_
  60.0 1.8 %finish.1 = f32[64,4096]{1,0:T(8,128)} custom-call(s32[1]{0:T(128)} %bitcast.me_ref, s32[1,32768]{1,0:T(1,128)S(1)} %copy-done.1, f32[1,64,2176]{2,1,0:T(8,128)S(1)} %collective-permute-done.6.refs_0_.refs_3_, f32[2,64,2176]{2,1,0:T(8,128)S(1)} %get-tuple-element.22.refs_1_.refs_4_, f32[1,64,2176]{2,1,0:T(8,128)S(1)} %collective-permute-done.8.refs_2_.refs_5_, ...), custom_call_target="tpu_custom_call" | custom-call | tf_op jit(solution)/shard_map/finish/pallas_call | solution.py:372
  (20 shorter events, 0.2 us)
Async XLA Ops:
  0.0 15.7 %copy-start = (f32[64,64]{1,0:T(8,128)S(1)}, f32[64,64]{1,0:T(8,128)}, u32[]{:S(2)}) copy-start(f32[64,64]{1,0:T(8,128)} %own_ctf_ref.5) | copy-start | bytes 49156
  0.0 15.7 %copy-start.4 = (s32[64,2,64]{2,1,0:T(2,128)S(1)}, s32[64,2,64]{2,1,0:T(2,128)}, u32[]{:S(2)}) copy-start(s32[64,2,64]{2,1,0:T(2,128)} %param.10) | copy-start | bytes 98308
  0.0 15.8 %copy-start.2 = (f32[2]{0:T(128)S(1)}, f32[2]{0:T(128)}, u32[]{:S(2)}) copy-start(f32[2]{0:T(128)} %param.13) | copy-start | bytes 28
  0.0 15.8 %copy-start.3 = (f32[64]{0:T(128)S(1)}, f32[64]{0:T(128)}, u32[]{:S(2)}) copy-start(f32[64]{0:T(128)} %param.12) | copy-start | bytes 772
  8.6 11.3 %collective-permute-start.5 = (f32[4,64,4096]{2,1,0:T(8,128)}, f32[4,64,4096]{2,1,0:T(8,128)}, u32[]{:S(2)}, u32[]{:S(2)}) collective-permute-start(f32[4,64,4096]{2,1,0:T(8,128)} %get-tuple-element.20), channel_id=1, source_target_pairs={{0,4},{4,0},{8,12},{12,8},{16,20},{20,16},{24,28},{28,24},{1,5},{5... | collective-permute-start | bytes 12582920 | tf_op jit(solution)/shard_map/ppermute | solution.py:382
  9.1 8.1 %collective-permute-start = (f32[64,64]{1,0:T(8,128)S(1)}, f32[64,64]{1,0:T(8,128)S(1)}, u32[]{:S(2)}, u32[]{:S(2)}) collective-permute-start(f32[64,64]{1,0:T(8,128)S(1)} %get-tuple-element.18.refs_0_), channel_id=1, source_target_pairs={{0,1},{1,2},{2,3},{3,0},{4,5},{5,6},{6,7},{7,4},{8,9},{9,10},{10,1... | collective-permute-start | bytes 49160 | tf_op jit(solution)/shard_map/ppermute | solution.py:402
  11.8 5.5 %collective-permute-start.1 = (f32[64,64]{1,0:T(8,128)S(1)}, f32[64,64]{1,0:T(8,128)S(1)}, u32[]{:S(2)}, u32[]{:S(2)}) collective-permute-start(f32[64,64]{1,0:T(8,128)S(1)} %get-tuple-element.18.refs_0_), channel_id=1, source_target_pairs={{0,2},{1,3},{2,0},{3,1},{4,6},{5,7},{6,4},{7,5},{8,10},{9,11},{10,... | collective-permute-start | bytes 49160 | tf_op jit(solution)/shard_map/ppermute | solution.py:402
  14.3 3.9 %collective-permute-start.2 = (f32[64,64]{1,0:T(8,128)S(1)}, f32[64,64]{1,0:T(8,128)S(1)}, u32[]{:S(2)}, u32[]{:S(2)}) collective-permute-start(f32[64,64]{1,0:T(8,128)S(1)} %get-tuple-element.18.refs_0_), channel_id=1, source_target_pairs={{0,3},{1,0},{2,1},{3,2},{4,7},{5,4},{6,5},{7,6},{8,11},{9,8},{10,9... | collective-permute-start | bytes 49160 | tf_op jit(solution)/shard_map/ppermute | solution.py:402
  15.7 3.0 %collective-permute-start.4 = (f32[64,64]{1,0:T(8,128)S(1)}, f32[64,64]{1,0:T(8,128)S(1)}, u32[]{:S(2)}, u32[]{:S(2)}) collective-permute-start(f32[64,64]{1,0:T(8,128)S(1)} %copy-done), channel_id=1, source_target_pairs={{0,4},{4,0},{8,12},{12,8},{16,20},{20,16},{24,28},{28,24},{1,5},{5... | collective-permute-start | bytes 49160 | tf_op jit(solution)/shard_map/ppermute | solution.py:382
  18.6 1.2 %collective-permute-start.3 = (f32[64,64]{1,0:T(8,128)S(1)}, f32[64,64]{1,0:T(8,128)S(1)}, u32[]{:S(2)}, u32[]{:S(2)}) collective-permute-start(f32[64,64]{1,0:T(8,128)S(1)} %weigh.1.own_w_ref), channel_id=1, source_target_pairs={{0,4},{4,0},{8,12},{12,8},{16,20},{20,16},{24,28},{28,24},{1,5},{5... | collective-permute-start | bytes 49160 | tf_op jit(solution)/shard_map/ppermute | solution.py:382
  21.6 15.5 %collective-permute-start.7 = (f32[1,64,2176]{2,1,0:T(8,128)S(1)}, f32[1,64,2176]{2,1,0:T(8,128)S(1)}, u32[]{:S(2)}, u32[]{:S(2)}) collective-permute-start(f32[1,64,2176]{2,1,0:T(8,128)S(1)} %get-tuple-element.23), channel_id=1, source_target_pairs={{0,8},{4,12},{8,0},{12,4},{16,24},{20,28},{24,16},{28,20},{1,9},{5... | collective-permute-start | bytes 1671176 | tf_op jit(solution)/shard_map/ppermute | solution.py:382
  23.1 15.6 %collective-permute-start.10 = (f32[1,64,2048]{2,1,0:T(8,128)S(1)}, f32[1,64,2048]{2,1,0:T(8,128)S(1)}, u32[]{:S(2)}, u32[]{:S(2)}) collective-permute-start(f32[1,64,2048]{2,1,0:T(8,128)S(1)} %get-tuple-element.26), channel_id=1, source_target_pairs={{0,16},{4,20},{8,24},{12,28},{16,0},{20,4},{24,8},{28,12},{1,17},{... | collective-permute-start | bytes 1572872 | tf_op jit(solution)/shard_map/ppermute | solution.py:382
  26.4 22.8 %collective-permute-start.6 = (f32[1,64,2176]{2,1,0:T(8,128)S(1)}, f32[1,64,2176]{2,1,0:T(8,128)S(1)}, u32[]{:S(2)}, u32[]{:S(2)}) collective-permute-start(f32[1,64,2176]{2,1,0:T(8,128)S(1)} %get-tuple-element.21), channel_id=1, source_target_pairs={{0,8},{4,12},{8,0},{12,4},{16,24},{20,28},{24,16},{28,20},{1,9},{5... | collective-permute-start | bytes 1671176 | tf_op jit(solution)/shard_map/ppermute | solution.py:382
  27.0 33.0 %copy-start.1 = (s32[1,32768]{1,0:T(1,128)S(1)}, s32[1,32768]{1,0:T(1,128)}, u32[]{:S(2)}) copy-start(s32[1,32768]{1,0:T(1,128)} %constant.14.clone.index_ref) | copy-start | bytes 393220
  27.0 22.2 %collective-permute-start.9 = (f32[1,64,2048]{2,1,0:T(8,128)S(1)}, f32[1,64,2048]{2,1,0:T(8,128)S(1)}, u32[]{:S(2)}, u32[]{:S(2)}) collective-permute-start(f32[1,64,2048]{2,1,0:T(8,128)S(1)} %get-tuple-element.24), channel_id=1, source_target_pairs={{0,16},{4,20},{8,24},{12,28},{16,0},{20,4},{24,8},{28,12},{1,17},{... | collective-permute-start | bytes 1572872 | tf_op jit(solution)/shard_map/ppermute | solution.py:382
  37.2 22.8 %collective-permute-start.8 = (f32[1,64,2176]{2,1,0:T(8,128)S(1)}, f32[1,64,2176]{2,1,0:T(8,128)S(1)}, u32[]{:S(2)}, u32[]{:S(2)}) collective-permute-start(f32[1,64,2176]{2,1,0:T(8,128)S(1)} %slice_add_fusion), channel_id=1, source_target_pairs={{0,16},{4,20},{8,24},{12,28},{16,0},{20,4},{24,8},{28,12},{1,17},{... | collective-permute-start | bytes 1671176 | tf_op jit(solution)/shard_map/ppermute | solution.py:382
  38.8 20.7 %collective-permute-start.11 = (f32[1,64,2048]{2,1,0:T(8,128)S(1)}, f32[1,64,2048]{2,1,0:T(8,128)S(1)}, u32[]{:S(2)}, u32[]{:S(2)}) collective-permute-start(f32[1,64,2048]{2,1,0:T(8,128)S(1)} %slice_add_fusion.1), channel_id=1, source_target_pairs={{0,8},{4,12},{8,0},{12,4},{16,24},{20,28},{24,16},{28,20},{1,9},{5... | collective-permute-start | bytes 1572872 | tf_op jit(solution)/shard_map/ppermute | solution.py:382

commit v4 on v3

--- a/solution.py
+++ b/solution.py
@@ -47,8 +47,8 @@
 
 
 def estep_kernel(
-    blocks, me_ref, index_hbm, image_hbm, plane_hbm, ctf_hbm, give_hbm, keep_hbm, score_ref,
-    index, image, plane, ctf_held, weighted, give, squared, energy_of, small_sem, in_sem, out_sem,
+    blocks, me_ref, index_hbm, image_hbm, plane_hbm, ctf_hbm, give, weighted, score_ref,
+    index, image, plane, ctf_held, squared, energy_of, small_sem, in_sem,
 ):
     rows, width = image.shape
     chips, _, share = give.shape
@@ -116,7 +116,6 @@
         return 2.0 * low - energy(block % 2, span)
 
     chip, core = me_ref[0] // 2, lax.rem(me_ref[0], 2)
-    outgoing = []
 
     def hand_over(done):
         for pair in range(chips):
@@ -124,16 +123,8 @@
             if pair in handed or not all(row in done for row in range(first, last)):
                 continue
             handed.add(pair)
-            place = pair ^ chip
             given = pl.ds(pl.multiple_of((2 * pair + 1 - core) * share, share), share)
-            kept = pl.ds(pl.multiple_of((2 * pair + core) * share, share), share)
-            give[place] = weighted[:, given].astype(F32)
-            outgoing.extend([
-                pltpu.make_async_copy(give.at[place], give_hbm.at[place], out_sem.at[pair, 0]),
-                pltpu.make_async_copy(weighted.at[:, kept], keep_hbm.at[place], out_sem.at[pair, 1]),
-            ])
-            outgoing[-2].start()
-            outgoing[-1].start()
+            give[pair ^ chip] = weighted[:, given].astype(F32)
 
     handed, done = set(), set()
     total = jnp.zeros(score_ref.shape, F32)
@@ -153,8 +144,6 @@
     middle = width // 2
     total += 2.0 * fit(middle, middle + line) - energy(2, line)
     score_ref[...] = total
-    for copy in outgoing:
-        copy.wait()
 
 
 def estep(me, index, images, planes, ctf_table, share):
@@ -163,15 +152,16 @@
     count = planes.shape[0]
     blocks = 4
     span = width // (2 * blocks)
-    held = pl.BlockSpec(memory_space=pl.ANY)
+    vmem = pl.BlockSpec(memory_space=pltpu.VMEM)
     far = pl.BlockSpec(memory_space=pltpu.HBM)
+    operands = (index, images, planes, ctf_table)
     return pl.pallas_call(
         functools.partial(estep_kernel, blocks),
         in_specs=[pl.BlockSpec(memory_space=pltpu.SMEM)] + [far] * 4,
-        out_specs=[held, held, pl.BlockSpec(memory_space=pltpu.VMEM)],
+        out_specs=[vmem] * 3,
         out_shape=[
             jax.ShapeDtypeStruct((chips, rows, share), F32),
-            jax.ShapeDtypeStruct((chips, rows, share), BF16),
+            jax.ShapeDtypeStruct((rows, width), BF16),
             jax.ShapeDtypeStruct((rows, count), F32),
         ],
         scratch_shapes=[
@@ -179,17 +169,14 @@
             pltpu.VMEM((rows, width), BF16),
             pltpu.VMEM((count, width), BF16),
             pltpu.VMEM(ctf_table.shape, F32),
-            pltpu.VMEM((rows, width), BF16),
-            pltpu.VMEM((chips, rows, share), F32),
             pltpu.VMEM((3, rows, span), BF16),
             pltpu.VMEM((3, count, span), BF16),
             pltpu.SemaphoreType.DMA((2,)),
             pltpu.SemaphoreType.DMA((blocks, 2, 2)),
-            pltpu.SemaphoreType.DMA((chips, 2)),
         ],
         compiler_params=params(28),
         name="estep",
-    )(me, *[pltpu.with_memory_space_constraint(part, pltpu.HBM) for part in (index, images, planes, ctf_table)])
+    )(me, *[pltpu.with_memory_space_constraint(operand, pltpu.HBM) for operand in operands])
 
 
 def count_kernel(slabs, slab_ref, prior_ref, noise_ref, list_ref, base_ref, scale_ref):
@@ -198,7 +185,7 @@
     each = listed // classes
     local = width // slabs
     lane = lax.broadcasted_iota(jnp.int32, (rows, width), 1)
-    home = lax.rem(slab_ref[0] - lane // local + slabs, slabs)
+    home = slab_ref[0] ^ (lane // local)
     plane = home * local + lax.rem(lane, local)
     for one in range(classes):
         sums = jnp.zeros((rows, width), F32)
@@ -238,14 +225,17 @@
 
 def weigh_kernel(base_ref, scale_ref, *refs):
     out_ref = refs[-1]
-    tables = [ref[...] for ref in refs[:-1]]
     classes = base_ref.shape[0]
-    local = tables[0].shape[1] // classes
+    planes = out_ref.shape[0]
+    local = planes // classes
     scores = []
     for one in range(classes):
-        cut = slice(one * local, (one + 1) * local)
-        fit = jnp.concatenate([table[:, cut] for table in tables], axis=1)
-        scores.append(base_ref[one] + scale_ref[...] * fit)
+        parts = [
+            ref[:, start + one * local : start + (one + 1) * local]
+            for ref in refs[:-1]
+            for start in range(0, ref.shape[1], planes)
+        ]
+        scores.append(base_ref[one] + scale_ref[...] * jnp.concatenate(parts, axis=1))
     peak = functools.reduce(jnp.maximum, [jnp.max(score, axis=1, keepdims=True) for score in scores])
     raw = [jnp.exp(score - peak) for score in scores]
     total = functools.reduce(jnp.add, [jnp.sum(part, axis=1, keepdims=True) for part in raw])
@@ -253,129 +243,118 @@
     out_ref[...] = own.T
 
 
-def weigh(base, scale, tables):
-    rows, planes = tables[0].shape
+def weigh(base, scale, tables, planes):
     return pl.pallas_call(
         weigh_kernel,
-        out_shape=jax.ShapeDtypeStruct((planes, rows), F32),
+        out_shape=jax.ShapeDtypeStruct((planes, base.shape[1]), F32),
         compiler_params=params(4),
         name="weigh",
     )(base, scale, *tables)
 
 
-def sums_kernel(items, own_w_ref, sib_w_ref, own_ctf_ref, sib_ctf_ref, keep_hbm, got_hbm, *refs):
-    outs = refs[: len(items)]
-    keep, got, sums, in_sem, out_sem = refs[-5:]
-    tile = keep_hbm.shape[2] // 4
-    number, _, wide = keep.shape
-    cells = wide // tile
-    places = [(out, slot, k, out) for out, ks in enumerate(items) for slot, k in enumerate(ks)]
-    incoming, outgoing = [], []
-    for place, (out, slot, k, side) in enumerate(places):
-        copies = []
-        for cell in range(cells):
-            source = slice((2 * cell + side) * tile, (2 * cell + side + 1) * tile)
-            target = slice(cell * tile, (cell + 1) * tile)
-            copies += [
-                pltpu.make_async_copy(
-                    keep_hbm.at[k, :, source], keep.at[place, :, target], in_sem.at[place, cell, 0]
-                ),
-                pltpu.make_async_copy(
-                    got_hbm.at[k, :, source], got.at[place, :, target], in_sem.at[place, cell, 1]
-                ),
-            ]
-        incoming.append(copies)
-        filled = sums.at[place] if side == 0 else sums.at[place, :, :wide]
-        outgoing.append(pltpu.make_async_copy(filled, outs[out].at[slot], out_sem.at[place]))
-    for copy in [copy for copies in incoming for copy in copies]:
-        copy.start()
+def sums_kernel(items, me_ref, own_w_ref, sib_w_ref, own_ctf_ref, sib_ctf_ref, weighted_ref, got_ref, *outs):
+    share = got_ref.shape[2]
+    tile = share // 4
+    wide = share // 2
+    chip, core = me_ref[0] // 2, lax.rem(me_ref[0], 2)
     weights = jnp.concatenate([own_w_ref[...], sib_w_ref[...]], axis=1).astype(BF16)
     ctf = jnp.concatenate([own_ctf_ref[...], sib_ctf_ref[...]], axis=0)
     shells = jnp.dot(weights, lanes_wide((ctf * ctf).astype(BF16)), preferred_element_type=F32)
-    for place, (_, _, _, side) in enumerate(places):
-        for copy in incoming[place]:
-            copy.wait()
-        images = jnp.concatenate([keep[place], got[place].astype(BF16)], axis=0)
-        sums[place, :, :wide] = jnp.dot(weights, images, preferred_element_type=F32)
-        if side == 0:
-            sums[place, :, wide:] = shells
-        outgoing[place].start()
-    for copy in outgoing:
-        copy.wait()
-
-
-def partial_sums(items, own_w, sib_w, own_ctf, sib_ctf, keep, got):
-    chips, rows, share = keep.shape
+    for side, ks in enumerate(items):
+        for slot, k in enumerate(ks):
+            start = pl.multiple_of(((k ^ chip) * 2 + core) * share, share)
+            for cell in range(wide // tile):
+                place = (2 * cell + side) * tile
+                images = jnp.concatenate(
+                    [
+                        weighted_ref[:, pl.ds(pl.multiple_of(start + place, tile), tile)],
+                        got_ref[k, :, place : place + tile].astype(BF16),
+                    ],
+                    axis=0,
+                )
+                outs[side][slot, :, cell * tile : (cell + 1) * tile] = jnp.dot(
+                    weights, images, preferred_element_type=F32
+                )
+            if side == 0:
+                outs[side][slot, :, wide:] = shells
+
+
+def partial_sums(items, me, own_w, sib_w, own_ctf, sib_ctf, weighted, got):
+    chips, rows, share = got.shape
     planes = own_w.shape[0]
     wide = share // 2
     number = sum(len(ks) for ks in items)
-    held = pl.BlockSpec(memory_space=pl.ANY)
     vmem = pl.BlockSpec(memory_space=pltpu.VMEM)
     return pl.pallas_call(
         functools.partial(sums_kernel, items),
-        in_specs=[vmem] * 4 + [held] * 2,
-        out_specs=[held] * 2,
+        in_specs=[pl.BlockSpec(memory_space=pltpu.SMEM)] + [vmem] * 6,
+        out_specs=[vmem] * 2,
         out_shape=[
             jax.ShapeDtypeStruct((len(ks), planes, wide + extra), F32)
             for ks, extra in zip(items, (LANES, 0))
         ],
-        scratch_shapes=[
-            pltpu.VMEM((number, rows, wide), BF16),
-            pltpu.VMEM((number, rows, wide), F32),
-            pltpu.VMEM((number, planes, wide + LANES), F32),
-            pltpu.SemaphoreType.DMA((number, 2, 2)),
-            pltpu.SemaphoreType.DMA((number,)),
-        ],
-        compiler_params=params(12),
+        compiler_params=params(16),
         cost_estimate=pl.CostEstimate(
             flops=4 * planes * rows * wide * number,
             bytes_accessed=10 * planes * wide * number,
             transcendentals=0,
         ),
         name="sums",
-    )(own_w, sib_w, own_ctf, sib_ctf, keep, got)
-
-
-def finish_kernel(numbers, me_ref, index_ref, *refs):
-    out_ref = refs[-1]
-    left = functools.reduce(jnp.add, [ref[0] for ref in refs[: numbers[0]]])
-    shells = functools.reduce(jnp.add, [ref[0] for ref in refs[numbers[0] : 2 * numbers[0]]])
-    right = functools.reduce(jnp.add, [ref[0] for ref in refs[2 * numbers[0] : -1]])
-    tile = left.shape[1]
-    for side, block in ((0, left), (1, right)):
-        for start in range(0, tile, LANES):
-            cut = slice(side * tile + start, side * tile + start + LANES)
-            weight = spread(shells, index_ref[:, cut])
-            out_ref[:, cut] = block[:, start : start + LANES] / (weight + 1.0)
+    )(me, own_w, sib_w, own_ctf, sib_ctf, weighted, got)
+
+
+def finish_kernel(numbers, me_ref, index_hbm, *refs):
+    total = sum(numbers)
+    parts, (out_hbm, index, out, in_sem, out_sem) = refs[:total], refs[total:]
+    planes, share = out.shape
+    tile = share // 4
+    wide = share // 2
+    mine = pl.ds(pl.multiple_of(me_ref[0] * share, share), share)
+    fetch = pltpu.make_async_copy(index_hbm.at[:, mine], index, in_sem)
+    fetch.start()
+    left, right = parts[: numbers[0]], parts[numbers[0] :]
+    shells = functools.reduce(jnp.add, [ref[0, :, wide:] for ref in left])
+    fetch.wait()
+    stores = []
+    for cell in range(2):
+        for side, refs in ((0, left), (1, right)):
+            for start in range(0, tile, LANES):
+                place = (2 * cell + side) * tile + start
+                cut = slice(cell * tile + start, cell * tile + start + LANES)
+                block = functools.reduce(jnp.add, [ref[0, :, cut] for ref in refs])
+                weight = spread(shells, index[:, place : place + LANES])
+                out[:, place : place + LANES] = block / (weight + 1.0)
+        cut = slice(cell * wide, (cell + 1) * wide)
+        stores.append(pltpu.make_async_copy(out.at[:, cut], out_hbm.at[:, cut], out_sem.at[cell]))
+        stores[-1].start()
+    for store in stores:
+        store.wait()
 
 
 def finish(me, index, left, right, share):
     planes = left[0][0].shape[1]
-    tile = share // 4
-    cells = share // (2 * tile)
-
-    def side(place):
-        return pl.BlockSpec((1, planes, tile), lambda cell, m: (place, 0, cell))
-
-    def tail(place):
-        return pl.BlockSpec((1, planes, LANES), lambda cell, m: (place, 0, share // 2 // LANES))
-
-    grid_spec = pltpu.PrefetchScalarGridSpec(
-        num_scalar_prefetch=1,
-        grid=(cells,),
-        in_specs=[pl.BlockSpec((1, 2 * tile), lambda cell, m: (0, m[0] * cells + cell))]
-        + [side(place) for _, place in left]
-        + [tail(place) for _, place in left]
-        + [side(place) for _, place in right],
-        out_specs=pl.BlockSpec((planes, 2 * tile), lambda cell, m: (0, cell)),
-    )
+    numbers = len(left), len(right)
+    held = pl.BlockSpec(memory_space=pl.ANY)
+
+    def first(part, place):
+        return pl.BlockSpec((1,) + part.shape[1:], lambda step: (place, 0, 0))
+
     return pl.pallas_call(
-        functools.partial(finish_kernel, (len(left), len(right))),
-        grid_spec=grid_spec,
+        functools.partial(finish_kernel, numbers),
+        grid=(1,),
+        in_specs=[pl.BlockSpec(memory_space=pltpu.SMEM), held]
+        + [first(part, place) if part.shape[0] > 1 else pl.BlockSpec(memory_space=pltpu.VMEM) for part, place in left + right],
+        out_specs=held,
         out_shape=jax.ShapeDtypeStruct((planes, share), F32),
+        scratch_shapes=[
+            pltpu.VMEM((1, share), jnp.int32),
+            pltpu.VMEM((planes, share), F32),
+            pltpu.SemaphoreType.DMA(()),
+            pltpu.SemaphoreType.DMA((2,)),
+        ],
         compiler_params=params(12),
         name="finish",
-    )(me, index, *[part for part, _ in left + left + right])
+    )(me, index, *[part for part, _ in left + right])
 
 
 def swap(array, bit, size):
@@ -396,22 +375,25 @@
     index = jnp.asarray(index)
     planes = references.reshape(classes * local_planes, width)
 
-    give, keep, table = estep(me, top_index, images, planes, ctf_table, share)
+    give, weighted, table = estep(me, top_index, images, planes, ctf_table, share)
     sib_ctf = swap(ctf_table, 1, size)
-    tables = [table] + [
-        lax.ppermute(table, "slab", [(one, (one + hop) % slabs) for one in range(slabs)])
-        for hop in range(1, slabs)
-    ]
+    tables, bit = [table], 1
+    while bit < slabs:
+        held = tables[0] if len(tables) == 1 else jnp.concatenate(tables, axis=1)
+        tables = [
+            held, lax.ppermute(held, "slab", [(one, one ^ bit) for one in range(slabs)])
+        ]
+        bit *= 2
     got = swap(give, 1, size)
     base, scale = count_planes(
         slab, class_weight, inv_noise, orientations, slabs * local_planes, slabs
     )
-    own_w = weigh(base, scale, tables)
+    own_w = weigh(base, scale, tables, classes * local_planes)
     sib_w = swap(own_w, 1, size)
 
     sums = functools.partial(
         partial_sums,
-        own_w=own_w, sib_w=sib_w, own_ctf=ctf_table, sib_ctf=sib_ctf, keep=keep, got=got,
+        me=me, own_w=own_w, sib_w=sib_w, own_ctf=ctf_table, sib_ctf=sib_ctf, weighted=weighted, got=got,
     )
     low = [1 << place for place in range(chips.bit_length() - 1)]
     orders = (low, low[::-1])

time: 62 us -> 68 us (1.097)
  local copies, waits for them, and re-layouts: 0.12 us -> 4.31 us
  Pallas kernels: 17.9 us -> 20.1 us
  starting transfers between devices: 14.5 us -> 13.6 us
    unnamed x10 -> x14, local copies, waits for them, and re-layouts: 0.02 us -> 4.2 us
    pallas_call x5, Pallas kernels: 7.91 us -> 9.41 us  [the longest x3 7.8 us: partial_sums(): pl.pallas_call(functools.partial(sums_kernel, items), in_specs=[pl.BlockS...]
    ppermute x3 -> x2, waiting for transfers between devices: 1.05 us -> 2.53 us  [shards(): lax.ppermute(held, 'slab', [(one, one ^ bit) for one in range(slabs)])]
    ppermute x9, waiting for transfers between devices: 28 us -> 26.9 us  [swap(): return lax.ppermute(array, 'img', [(one, one ^ bit) for one in range(size)])]
    ppermute x3 -> x2, starting transfers between devices: 6.61 us -> 5.49 us  [shards(): lax.ppermute(held, 'slab', [(one, one ^ bit) for one in range(slabs)])]
    pallas_call x1, Pallas kernels: 8.56 us -> 9.35 us  [estep(): pl.pallas_call(functools.partial(estep_kernel, blocks), in_specs=[pl.Bloc...]
  transfers between devices with their start and end apart: 12 -> 11, of which waited for: 6 -> 7; matrix products, arithmetic and copies ran while one was open for 0% -> 0% of each run, Pallas kernels for 9% -> 10%
where the time goes in v4:
time: 68 us; the launch traced here: 67.8 us
  waiting for transfers between devices  29.4 us (43%)
  Pallas kernels  20.1 us (30%)
  starting transfers between devices  13.6 us (20%)
  local copies, waits for them, and re-layouts  4.31 us (6%)
    ppermute x9, waiting for transfers between devices, swap(): return lax.ppermute(array, 'img', [(one, one ^ bit) for one in range(size)])  26.9 us
    pallas_call x1, Pallas kernels, estep(): pl.pallas_call(functools.partial(estep_kernel, blocks), in_specs=[pl.Bloc...  9.35 us
    ppermute x9, starting transfers between devices, swap(): return lax.ppermute(array, 'img', [(one, one ^ bit) for one in range(size)])  8.11 us
    pallas_call x3, Pallas kernels, partial_sums(): pl.pallas_call(functools.partial(sums_kernel, items), in_specs=[pl.BlockS...  7.8 us
    ppermute x2, starting transfers between devices, shards(): lax.ppermute(held, 'slab', [(one, one ^ bit) for one in range(slabs)])  5.49 us
    unnamed x14, local copies, waits for them, and re-layouts  4.2 us
    ppermute x2, waiting for transfers between devices, shards(): lax.ppermute(held, 'slab', [(one, one ^ bit) for one in range(slabs)])  2.53 us
    pallas_call x1, Pallas kernels, count_planes(): pl.pallas_call(functools.partial(count_kernel, slabs), in_specs=[pl.Block...  1.38 us
  transfers between devices with their start and end apart: 11, of which 7 were waited for; matrix products, arithmetic and copies ran while one was open for 0% of the time, Pallas kernels for 10%

profile of v4, /device:TPU:0, one launch (start us, length us, event | category | flops | bytes accessed | tf_op | source)
XLA Modules:
  0.0 67.8 jit_solution(6064083728188852171)
XLA Ops:
  0.0 9.4 %estep.1 = (f32[4,64,4096]{2,1,0:T(8,128)}, bf16[64,32768]{1,0:T(8,128)(2,1)S(1)}, f32[64,64]{1,0:T(8,128)S(1)}) custom-call(s32[1]{0:T(128)} %bitcast.me_ref, s32[1,16640]{1,0:T(1,128)} %constant.13.clone.index_hbm, bf16[64,32768]{1,0:T(8,128)(2,1)} %image_hbm.1, bf16[64,32768]{1,0:T(8,128)(2,1)} %bitcast.8, f32[64,64]{1,0:T(8,128)} %own_ctf_ref.5), custom_call_target="tpu_custom_call" | custom-call | tf_op jit(solution)/shard_map/estep/pallas_call | solution.py:158
  9.4 2.0 %copy-done = bf16[64,32768]{1,0:T(8,128)(2,1)} copy-done((bf16[64,32768]{1,0:T(8,128)(2,1)}, bf16[64,32768]{1,0:T(8,128)(2,1)S(1)}, u32[]{:S(2)}) %copy-start) | copy-done | bytes 4194328
  11.4 0.5 collective-permute-start.4
  11.8 2.6 %collective-permute-start = (f32[64,64]{1,0:T(8,128)S(1)}, f32[64,64]{1,0:T(8,128)S(1)}, u32[]{:S(2)}, u32[]{:S(2)}) collective-permute-start(f32[64,64]{1,0:T(8,128)S(1)} %get-tuple-element.18), channel_id=1, source_target_pairs={{0,1},{1,0},{2,3},{3,2},{4,5},{5,4},{6,7},{7,6},{8,9},{9,8},{10,11... | collective-permute-start | bytes 49160 | tf_op jit(solution)/shard_map/ppermute | solution.py:384
  14.4 2.1 %collective-permute-done = f32[64,64]{1,0:T(8,128)S(1)} collective-permute-done((f32[64,64]{1,0:T(8,128)S(1)}, f32[64,64]{1,0:T(8,128)S(1)}, u32[]{:S(2)}, u32[]{:S(2)}) %collective-permute-start) | collective-permute-done | bytes 16416 | tf_op jit(solution)/shard_map/ppermute | solution.py:384
  16.6 2.9 %collective-permute-start.1 = (f32[64,128]{1,0:T(8,128)S(1)}, f32[64,128]{1,0:T(8,128)S(1)}, u32[]{:S(2)}, u32[]{:S(2)}) collective-permute-start(f32[64,128]{1,0:T(8,128)S(1)} %pad_maximum_fusion.refs_0_), channel_id=1, source_target_pairs={{0,2},{1,3},{2,0},{3,1},{4,6},{5,7},{6,4},{7,5},{8,10},{9,11},{10,... | collective-permute-start | bytes 98312 | tf_op jit(solution)/shard_map/ppermute | solution.py:384
  19.6 1.4 %count.1 = (f32[2,64,128]{2,1,0:T(8,128)S(1)}, f32[64,128]{1,0:T(8,128)S(1)}) custom-call(s32[1]{0:T(128)} %bitcast.1.slab_ref, f32[1,2]{1,0:T(1,128)S(1)} %bitcast.6, f32[1,64]{1,0:T(1,128)S(1)} %bitcast.7, s32[64,128]{1,0:T(8,128)S(1)} %reshape.25.list_ref), custom_call_target="tpu_custom_call" | custom-call | flops 10000000 | bytes 1000000 | tf_op jit(solution)/shard_map/count/pallas_call | solution.py:207
  21.0 0.5 collective-permute-done.1.refs_1_
  21.4 0.3 weigh.1.own_w_ref
  21.9 1.2 %collective-permute-done.2.sib_w_ref = f32[64,64]{1,0:T(8,128)S(1)} collective-permute-done((f32[64,64]{1,0:T(8,128)S(1)}, f32[64,64]{1,0:T(8,128)S(1)}, u32[]{:S(2)}, u32[]{:S(2)}) %collective-permute-start.2) | collective-permute-done | bytes 16416 | tf_op jit(solution)/shard_map/ppermute | solution.py:361
  23.0 2.2 %copy-done.1 = bf16[64,32768]{1,0:T(8,128)(2,1)S(1)} copy-done((bf16[64,32768]{1,0:T(8,128)(2,1)S(1)}, bf16[64,32768]{1,0:T(8,128)(2,1)}, u32[]{:S(2)}) %copy-start.1) | copy-done | bytes 4194328
  25.2 2.6 %sums.5 = (f32[1,64,2176]{2,1,0:T(8,128)S(1)}, f32[1,64,2048]{2,1,0:T(8,128)S(1)}) custom-call(s32[1]{0:T(128)} %bitcast.me_ref, f32[64,64]{1,0:T(8,128)S(1)} %weigh.1.own_w_ref, f32[64,64]{1,0:T(8,128)S(1)} %collective-permute-done.2.sib_w_ref, f32[64,64]{1,0:T(8,128)S(1)} %copy-done.2, f32[64,64]{1,0:T(8,128)S(1)} %collective-permute-done.3.sib_ctf_ref, ...), custom_call_target="tpu_custom_call" | custom-call | flops 67108864 | bytes 2621440 | tf_op jit(solution)/shard_map/sums/pallas_call | solution.py:288
  27.8 1.8 %collective-permute-start.6 = (f32[1,64,2176]{2,1,0:T(8,128)S(1)}, f32[1,64,2176]{2,1,0:T(8,128)S(1)}, u32[]{:S(2)}, u32[]{:S(2)}) collective-permute-start(f32[1,64,2176]{2,1,0:T(8,128)S(1)} %get-tuple-element.23), channel_id=1, source_target_pairs={{0,8},{4,12},{8,0},{12,4},{16,24},{20,28},{24,16},{28,20},{1,9},{5... | collective-permute-start | bytes 1671176 | tf_op jit(solution)/shard_map/ppermute | solution.py:361
  29.6 1.5 %collective-permute-start.9 = (f32[1,64,2048]{2,1,0:T(8,128)S(1)}, f32[1,64,2048]{2,1,0:T(8,128)S(1)}, u32[]{:S(2)}, u32[]{:S(2)}) collective-permute-start(f32[1,64,2048]{2,1,0:T(8,128)S(1)} %get-tuple-element.26), channel_id=1, source_target_pairs={{0,16},{4,20},{8,24},{12,28},{16,0},{20,4},{24,8},{28,12},{1,17},{... | collective-permute-start | bytes 1572872 | tf_op jit(solution)/shard_map/ppermute | solution.py:361
  31.1 2.5 %sums.3 = (f32[1,64,2176]{2,1,0:T(8,128)S(1)}, f32[1,64,2048]{2,1,0:T(8,128)S(1)}) custom-call(s32[1]{0:T(128)} %bitcast.me_ref, f32[64,64]{1,0:T(8,128)S(1)} %weigh.1.own_w_ref, f32[64,64]{1,0:T(8,128)S(1)} %collective-permute-done.2.sib_w_ref, f32[64,64]{1,0:T(8,128)S(1)} %copy-done.2, f32[64,64]{1,0:T(8,128)S(1)} %collective-permute-done.3.sib_ctf_ref, ...), custom_call_target="tpu_custom_call" | custom-call | flops 67108864 | bytes 2621440 | tf_op jit(solution)/shard_map/sums/pallas_call | solution.py:288
  33.6 0.6 collective-permute-start.5
  34.5 2.7 %sums.4 = (f32[2,64,2176]{2,1,0:T(8,128)S(1)}, f32[2,64,2048]{2,1,0:T(8,128)S(1)}) custom-call(s32[1]{0:T(128)} %bitcast.me_ref, f32[64,64]{1,0:T(8,128)S(1)} %weigh.1.own_w_ref, f32[64,64]{1,0:T(8,128)S(1)} %collective-permute-done.2.sib_w_ref, f32[64,64]{1,0:T(8,128)S(1)} %copy-done.2, f32[64,64]{1,0:T(8,128)S(1)} %collective-permute-done.3.sib_ctf_ref, ...), custom_call_target="tpu_custom_call" | custom-call | flops 134217728 | bytes 5242880 | tf_op jit(solution)/shard_map/sums/pallas_call | solution.py:288
  37.2 6.1 %collective-permute-done.6 = f32[1,64,2176]{2,1,0:T(8,128)S(1)} collective-permute-done((f32[1,64,2176]{2,1,0:T(8,128)S(1)}, f32[1,64,2176]{2,1,0:T(8,128)S(1)}, u32[]{:S(2)}, u32[]{:S(2)}) %collective-permute-start.6) | collective-permute-done | bytes 557088 | tf_op jit(solution)/shard_map/ppermute | solution.py:361
  43.4 1.8 %collective-permute-start.7 = (f32[1,64,2176]{2,1,0:T(8,128)S(1)}, f32[1,64,2176]{2,1,0:T(8,128)S(1)}, u32[]{:S(2)}, u32[]{:S(2)}) collective-permute-start(f32[1,64,2176]{2,1,0:T(8,128)S(1)} %slice_add_fusion), channel_id=1, source_target_pairs={{0,16},{4,20},{8,24},{12,28},{16,0},{20,4},{24,8},{28,12},{1,17},{... | collective-permute-start | bytes 1671176 | tf_op jit(solution)/shard_map/ppermute | solution.py:361
  45.3 1.5 %collective-permute-start.10 = (f32[1,64,2048]{2,1,0:T(8,128)S(1)}, f32[1,64,2048]{2,1,0:T(8,128)S(1)}, u32[]{:S(2)}, u32[]{:S(2)}) collective-permute-start(f32[1,64,2048]{2,1,0:T(8,128)S(1)} %slice_add_fusion.1), channel_id=1, source_target_pairs={{0,8},{4,12},{8,0},{12,4},{16,24},{20,28},{24,16},{28,20},{1,9},{5... | collective-permute-start | bytes 1572872 | tf_op jit(solution)/shard_map/ppermute | solution.py:361
  46.8 8.8 %collective-permute-done.8.refs_3_ = f32[1,64,2048]{2,1,0:T(8,128)S(1)} collective-permute-done((f32[1,64,2048]{2,1,0:T(8,128)S(1)}, f32[1,64,2048]{2,1,0:T(8,128)S(1)}, u32[]{:S(2)}, u32[]{:S(2)}) %collective-permute-start.8) | collective-permute-done | bytes 524320 | tf_op jit(solution)/shard_map/ppermute | solution.py:361
  55.6 10.1 %collective-permute-done.10.refs_5_ = f32[1,64,2048]{2,1,0:T(8,128)S(1)} collective-permute-done((f32[1,64,2048]{2,1,0:T(8,128)S(1)}, f32[1,64,2048]{2,1,0:T(8,128)S(1)}, u32[]{:S(2)}, u32[]{:S(2)}) %collective-permute-start.10) | collective-permute-done | bytes 524320 | tf_op jit(solution)/shard_map/ppermute | solution.py:361
  65.7 0.8 %collective-permute-done.7.refs_2_ = f32[1,64,2176]{2,1,0:T(8,128)S(1)} collective-permute-done((f32[1,64,2176]{2,1,0:T(8,128)S(1)}, f32[1,64,2176]{2,1,0:T(8,128)S(1)}, u32[]{:S(2)}, u32[]{:S(2)}) %collective-permute-start.7) | collective-permute-done | bytes 557088 | tf_op jit(solution)/shard_map/ppermute | solution.py:361
  66.5 1.3 %finish.1 = f32[64,4096]{1,0:T(8,128)} custom-call(s32[1]{0:T(128)} %bitcast.me_ref, s32[1,32768]{1,0:T(1,128)S(1)} %copy-done.3, f32[1,64,2176]{2,1,0:T(8,128)S(1)} %collective-permute-done.5.refs_0_, f32[2,64,2176]{2,1,0:T(8,128)S(1)} %get-tuple-element.22.refs_1_, f32[1,64,2176]{2,1,0:T(8,128)S(1)} %collective-permute-done.7.refs_2_, ...), custom_call_target="tpu_custom_call" | custom-call | tf_op jit(solution)/shard_map/finish/pallas_call | solution.py:342
  (23 shorter events, 0.7 us)
Async XLA Ops:
  0.0 19.5 %copy-start.2 = (f32[64,64]{1,0:T(8,128)S(1)}, f32[64,64]{1,0:T(8,128)}, u32[]{:S(2)}) copy-start(f32[64,64]{1,0:T(8,128)} %own_ctf_ref.5) | copy-start | bytes 49156
  0.0 19.5 %copy-start.6 = (s32[64,2,64]{2,1,0:T(2,128)S(1)}, s32[64,2,64]{2,1,0:T(2,128)}, u32[]{:S(2)}) copy-start(s32[64,2,64]{2,1,0:T(2,128)} %param.10) | copy-start | bytes 98308
  0.0 19.6 %copy-start.4 = (f32[2]{0:T(128)S(1)}, f32[2]{0:T(128)}, u32[]{:S(2)}) copy-start(f32[2]{0:T(128)} %param.13) | copy-start | bytes 28
  0.0 19.6 %copy-start.5 = (f32[64]{0:T(128)S(1)}, f32[64]{0:T(128)}, u32[]{:S(2)}) copy-start(f32[64]{0:T(128)} %param.12) | copy-start | bytes 772
  9.4 2.0 %copy-start = (bf16[64,32768]{1,0:T(8,128)(2,1)}, bf16[64,32768]{1,0:T(8,128)(2,1)S(1)}, u32[]{:S(2)}) copy-start(bf16[64,32768]{1,0:T(8,128)(2,1)S(1)} %get-tuple-element.19.weighted_ref) | copy-start | bytes 12582916
  11.4 11.7 %collective-permute-start.4 = (f32[4,64,4096]{2,1,0:T(8,128)}, f32[4,64,4096]{2,1,0:T(8,128)}, u32[]{:S(2)}, u32[]{:S(2)}) collective-permute-start(f32[4,64,4096]{2,1,0:T(8,128)} %get-tuple-element.20), channel_id=1, source_target_pairs={{0,4},{4,0},{8,12},{12,8},{16,20},{20,16},{24,28},{28,24},{1,5},{5... | collective-permute-start | bytes 12582920 | tf_op jit(solution)/shard_map/ppermute | solution.py:361
  11.8 4.7 %collective-permute-start = (f32[64,64]{1,0:T(8,128)S(1)}, f32[64,64]{1,0:T(8,128)S(1)}, u32[]{:S(2)}, u32[]{:S(2)}) collective-permute-start(f32[64,64]{1,0:T(8,128)S(1)} %get-tuple-element.18), channel_id=1, source_target_pairs={{0,1},{1,0},{2,3},{3,2},{4,5},{5,4},{6,7},{7,6},{8,9},{9,8},{10,11... | collective-permute-start | bytes 49160 | tf_op jit(solution)/shard_map/ppermute | solution.py:384
  16.6 4.8 %collective-permute-start.1 = (f32[64,128]{1,0:T(8,128)S(1)}, f32[64,128]{1,0:T(8,128)S(1)}, u32[]{:S(2)}, u32[]{:S(2)}) collective-permute-start(f32[64,128]{1,0:T(8,128)S(1)} %pad_maximum_fusion.refs_0_), channel_id=1, source_target_pairs={{0,2},{1,3},{2,0},{3,1},{4,6},{5,7},{6,4},{7,5},{8,10},{9,11},{10,... | collective-permute-start | bytes 98312 | tf_op jit(solution)/shard_map/ppermute | solution.py:384
  19.5 2.4 %collective-permute-start.3 = (f32[64,64]{1,0:T(8,128)S(1)}, f32[64,64]{1,0:T(8,128)S(1)}, u32[]{:S(2)}, u32[]{:S(2)}) collective-permute-start(f32[64,64]{1,0:T(8,128)S(1)} %copy-done.2), channel_id=1, source_target_pairs={{0,4},{4,0},{8,12},{12,8},{16,20},{20,16},{24,28},{28,24},{1,5},{5... | collective-permute-start | bytes 49160 | tf_op jit(solution)/shard_map/ppermute | solution.py:361
  21.8 1.2 %collective-permute-start.2 = (f32[64,64]{1,0:T(8,128)S(1)}, f32[64,64]{1,0:T(8,128)S(1)}, u32[]{:S(2)}, u32[]{:S(2)}) collective-permute-start(f32[64,64]{1,0:T(8,128)S(1)} %weigh.1.own_w_ref), channel_id=1, source_target_pairs={{0,4},{4,0},{8,12},{12,8},{16,20},{20,16},{24,28},{28,24},{1,5},{5... | collective-permute-start | bytes 49160 | tf_op jit(solution)/shard_map/ppermute | solution.py:361
  23.0 2.2 %copy-start.1 = (bf16[64,32768]{1,0:T(8,128)(2,1)S(1)}, bf16[64,32768]{1,0:T(8,128)(2,1)}, u32[]{:S(2)}) copy-start(bf16[64,32768]{1,0:T(8,128)(2,1)} %copy-done) | copy-start | bytes 12582916
  27.8 15.5 %collective-permute-start.6 = (f32[1,64,2176]{2,1,0:T(8,128)S(1)}, f32[1,64,2176]{2,1,0:T(8,128)S(1)}, u32[]{:S(2)}, u32[]{:S(2)}) collective-permute-start(f32[1,64,2176]{2,1,0:T(8,128)S(1)} %get-tuple-element.23), channel_id=1, source_target_pairs={{0,8},{4,12},{8,0},{12,4},{16,24},{20,28},{24,16},{28,20},{1,9},{5... | collective-permute-start | bytes 1671176 | tf_op jit(solution)/shard_map/ppermute | solution.py:361
  29.6 15.6 %collective-permute-start.9 = (f32[1,64,2048]{2,1,0:T(8,128)S(1)}, f32[1,64,2048]{2,1,0:T(8,128)S(1)}, u32[]{:S(2)}, u32[]{:S(2)}) collective-permute-start(f32[1,64,2048]{2,1,0:T(8,128)S(1)} %get-tuple-element.26), channel_id=1, source_target_pairs={{0,16},{4,20},{8,24},{12,28},{16,0},{20,4},{24,8},{28,12},{1,17},{... | collective-permute-start | bytes 1572872 | tf_op jit(solution)/shard_map/ppermute | solution.py:361
  33.6 22.0 %collective-permute-start.5 = (f32[1,64,2176]{2,1,0:T(8,128)S(1)}, f32[1,64,2176]{2,1,0:T(8,128)S(1)}, u32[]{:S(2)}, u32[]{:S(2)}) collective-permute-start(f32[1,64,2176]{2,1,0:T(8,128)S(1)} %get-tuple-element.21), channel_id=1, source_target_pairs={{0,8},{4,12},{8,0},{12,4},{16,24},{20,28},{24,16},{28,20},{1,9},{5... | collective-permute-start | bytes 1671176 | tf_op jit(solution)/shard_map/ppermute | solution.py:361
  34.2 32.2 %copy-start.3 = (s32[1,32768]{1,0:T(1,128)S(1)}, s32[1,32768]{1,0:T(1,128)}, u32[]{:S(2)}) copy-start(s32[1,32768]{1,0:T(1,128)} %constant.14.clone.index_hbm) | copy-start | bytes 393220
  34.2 21.4 %collective-permute-start.8 = (f32[1,64,2048]{2,1,0:T(8,128)S(1)}, f32[1,64,2048]{2,1,0:T(8,128)S(1)}, u32[]{:S(2)}, u32[]{:S(2)}) collective-permute-start(f32[1,64,2048]{2,1,0:T(8,128)S(1)} %get-tuple-element.24), channel_id=1, source_target_pairs={{0,16},{4,20},{8,24},{12,28},{16,0},{20,4},{24,8},{28,12},{1,17},{... | collective-permute-start | bytes 1572872 | tf_op jit(solution)/shard_map/ppermute | solution.py:361
  43.4 23.1 %collective-permute-start.7 = (f32[1,64,2176]{2,1,0:T(8,128)S(1)}, f32[1,64,2176]{2,1,0:T(8,128)S(1)}, u32[]{:S(2)}, u32[]{:S(2)}) collective-permute-start(f32[1,64,2176]{2,1,0:T(8,128)S(1)} %slice_add_fusion), channel_id=1, source_target_pairs={{0,16},{4,20},{8,24},{12,28},{16,0},{20,4},{24,8},{28,12},{1,17},{... | collective-permute-start | bytes 1671176 | tf_op jit(solution)/shard_map/ppermute | solution.py:361
  45.3 20.5 %collective-permute-start.10 = (f32[1,64,2048]{2,1,0:T(8,128)S(1)}, f32[1,64,2048]{2,1,0:T(8,128)S(1)}, u32[]{:S(2)}, u32[]{:S(2)}) collective-permute-start(f32[1,64,2048]{2,1,0:T(8,128)S(1)} %slice_add_fusion.1), channel_id=1, source_target_pairs={{0,8},{4,12},{8,0},{12,4},{16,24},{20,28},{24,16},{28,20},{1,9},{5... | collective-permute-start | bytes 1572872 | tf_op jit(solution)/shard_map/ppermute | solution.py:361

commit v5 on v3

--- a/solution.py
+++ b/solution.py
@@ -198,7 +198,7 @@
     each = listed // classes
     local = width // slabs
     lane = lax.broadcasted_iota(jnp.int32, (rows, width), 1)
-    home = lax.rem(slab_ref[0] - lane // local + slabs, slabs)
+    home = slab_ref[0] ^ (lane // local)
     plane = home * local + lax.rem(lane, local)
     for one in range(classes):
         sums = jnp.zeros((rows, width), F32)
@@ -336,46 +336,58 @@
     )(own_w, sib_w, own_ctf, sib_ctf, keep, got)
 
 
-def finish_kernel(numbers, me_ref, index_ref, *refs):
-    out_ref = refs[-1]
-    left = functools.reduce(jnp.add, [ref[0] for ref in refs[: numbers[0]]])
-    shells = functools.reduce(jnp.add, [ref[0] for ref in refs[numbers[0] : 2 * numbers[0]]])
-    right = functools.reduce(jnp.add, [ref[0] for ref in refs[2 * numbers[0] : -1]])
-    tile = left.shape[1]
-    for side, block in ((0, left), (1, right)):
-        for start in range(0, tile, LANES):
-            cut = slice(side * tile + start, side * tile + start + LANES)
-            weight = spread(shells, index_ref[:, cut])
-            out_ref[:, cut] = block[:, start : start + LANES] / (weight + 1.0)
+def finish_kernel(numbers, me_ref, index_hbm, *refs):
+    total = sum(numbers)
+    parts, (out_hbm, index, out, in_sem, out_sem) = refs[:total], refs[total:]
+    planes, share = out.shape
+    tile = share // 4
+    wide = share // 2
+    mine = pl.ds(pl.multiple_of(me_ref[0] * share, share), share)
+    fetch = pltpu.make_async_copy(index_hbm.at[:, mine], index, in_sem)
+    fetch.start()
+    left, right = parts[: numbers[0]], parts[numbers[0] :]
+    shells = functools.reduce(jnp.add, [ref[0, :, wide:] for ref in left])
+    fetch.wait()
+    stores = []
+    for cell in range(2):
+        for side, refs in ((0, left), (1, right)):
+            for start in range(0, tile, LANES):
+                place = (2 * cell + side) * tile + start
+                cut = slice(cell * tile + start, cell * tile + start + LANES)
+                block = functools.reduce(jnp.add, [ref[0, :, cut] for ref in refs])
+                weight = spread(shells, index[:, place : place + LANES])
+                out[:, place : place + LANES] = block / (weight + 1.0)
+        cut = slice(cell * wide, (cell + 1) * wide)
+        stores.append(pltpu.make_async_copy(out.at[:, cut], out_hbm.at[:, cut], out_sem.at[cell]))
+        stores[-1].start()
+    for store in stores:
+        store.wait()
 
 
 def finish(me, index, left, right, share):
     planes = left[0][0].shape[1]
-    tile = share // 4
-    cells = share // (2 * tile)
-
-    def side(place):
-        return pl.BlockSpec((1, planes, tile), lambda cell, m: (place, 0, cell))
-
-    def tail(place):
-        return pl.BlockSpec((1, planes, LANES), lambda cell, m: (place, 0, share // 2 // LANES))
-
-    grid_spec = pltpu.PrefetchScalarGridSpec(
-        num_scalar_prefetch=1,
-        grid=(cells,),
-        in_specs=[pl.BlockSpec((1, 2 * tile), lambda cell, m: (0, m[0] * cells + cell))]
-        + [side(place) for _, place in left]
-        + [tail(place) for _, place in left]
-        + [side(place) for _, place in right],
-        out_specs=pl.BlockSpec((planes, 2 * tile), lambda cell, m: (0, cell)),
-    )
+    numbers = len(left), len(right)
+    held = pl.BlockSpec(memory_space=pl.ANY)
+
+    def first(part, place):
+        return pl.BlockSpec((1,) + part.shape[1:], lambda step: (place, 0, 0))
+
     return pl.pallas_call(
-        functools.partial(finish_kernel, (len(left), len(right))),
-        grid_spec=grid_spec,
+        functools.partial(finish_kernel, numbers),
+        grid=(1,),
+        in_specs=[pl.BlockSpec(memory_space=pltpu.SMEM), held]
+        + [first(part, place) if part.shape[0] > 1 else pl.BlockSpec(memory_space=pltpu.VMEM) for part, place in left + right],
+        out_specs=held,
         out_shape=jax.ShapeDtypeStruct((planes, share), F32),
+        scratch_shapes=[
+            pltpu.VMEM((1, share), jnp.int32),
+            pltpu.VMEM((planes, share), F32),
+            pltpu.SemaphoreType.DMA(()),
+            pltpu.SemaphoreType.DMA((2,)),
+        ],
         compiler_params=params(12),
         name="finish",
-    )(me, index, *[part for part, _ in left + left + right])
+    )(me, index, *[part for part, _ in left + right])
 
 
 def swap(array, bit, size):
@@ -399,8 +411,8 @@
     give, keep, table = estep(me, top_index, images, planes, ctf_table, share)
     sib_ctf = swap(ctf_table, 1, size)
     tables = [table] + [
-        lax.ppermute(table, "slab", [(one, (one + hop) % slabs) for one in range(slabs)])
-        for hop in range(1, slabs)
+        lax.ppermute(table, "slab", [(one, one ^ other) for one in range(slabs)])
+        for other in range(1, slabs)
     ]
     got = swap(give, 1, size)
     base, scale = count_planes(

time: 62 us -> 63.3 us (1.021)
  waiting for transfers between devices: 29.1 us -> 32.2 us
  starting transfers between devices: 14.5 us -> 13.2 us
    ppermute x3, waiting for transfers between devices: 1.05 us -> 4.19 us  [shards(): lax.ppermute(table, 'slab', [(one, one ^ other) for one in range(slabs)])]
    ppermute x3, starting transfers between devices: 6.61 us -> 5.28 us  [shards(): lax.ppermute(table, 'slab', [(one, one ^ other) for one in range(slabs)])]
  transfers between devices with their start and end apart: 12 -> 12, of which waited for: 6 -> 7; matrix products, arithmetic and copies ran while one was open for 0% -> 0% of each run, Pallas kernels for 9% -> 9%
where the time goes in v5:
time: 63.3 us; the launch traced here: 63.1 us
  waiting for transfers between devices  32.2 us (51%)
  Pallas kernels  17.4 us (27%)
  starting transfers between devices  13.2 us (21%)
    ppermute x9, waiting for transfers between devices, swap(): return lax.ppermute(array, 'img', [(one, one ^ bit) for one in range(size)])  28 us
    pallas_call x1, Pallas kernels, estep(): pl.pallas_call(functools.partial(estep_kernel, blocks), in_specs=[pl.Bloc...  8.56 us
    ppermute x9, starting transfers between devices, swap(): return lax.ppermute(array, 'img', [(one, one ^ bit) for one in range(size)])  7.9 us
    pallas_call x3, Pallas kernels, partial_sums(): pl.pallas_call(functools.partial(sums_kernel, items), in_specs=[vmem] * 4...  5.79 us
    ppermute x3, starting transfers between devices, shards(): lax.ppermute(table, 'slab', [(one, one ^ other) for one in range(slabs)])  5.28 us
    ppermute x3, waiting for transfers between devices, shards(): lax.ppermute(table, 'slab', [(one, one ^ other) for one in range(slabs)])  4.19 us
    pallas_call x1, Pallas kernels, count_planes(): pl.pallas_call(functools.partial(count_kernel, slabs), in_specs=[pl.Block...  1.38 us
    pallas_call x1, Pallas kernels, finish(): pl.pallas_call(functools.partial(finish_kernel, numbers), grid=(1,), in_s...  1.3 us
  transfers between devices with their start and end apart: 12, of which 7 were waited for; matrix products, arithmetic and copies ran while one was open for 0% of the time, Pallas kernels for 9%

profile of v5, /device:TPU:0, one launch (start us, length us, event | category | flops | bytes accessed | tf_op | source)
XLA Modules:
  0.0 63.1 jit_solution(17643340485416288998)
XLA Ops:
  0.0 8.6 %estep.1 = (f32[4,64,4096]{2,1,0:T(8,128)}, bf16[4,64,4096]{2,1,0:T(8,128)(2,1)S(1)}, f32[64,64]{1,0:T(8,128)S(1)}) custom-call(s32[1]{0:T(128)} %bitcast.me_ref, s32[1,16640]{1,0:T(1,128)} %constant.13.clone.index_hbm, bf16[64,32768]{1,0:T(8,128)(2,1)} %image_hbm.1, bf16[64,32768]{1,0:T(8,128)(2,1)} %bitcast.8, f32[64,64]{1,0:T(8,128)} %own_ctf_ref.5), custom_call_target="tpu_custom_call" | custom-call | tf_op jit(solution)/shard_map/estep/pallas_call | solution.py:168
  8.6 0.5 collective-permute-start.5
  9.1 2.7 %collective-permute-start = (f32[64,64]{1,0:T(8,128)S(1)}, f32[64,64]{1,0:T(8,128)S(1)}, u32[]{:S(2)}, u32[]{:S(2)}) collective-permute-start(f32[64,64]{1,0:T(8,128)S(1)} %get-tuple-element.18.refs_0_), channel_id=1, source_target_pairs={{0,1},{1,0},{2,3},{3,2},{4,5},{5,4},{6,7},{7,6},{8,9},{9,8},{10,11... | collective-permute-start | bytes 49160 | tf_op jit(solution)/shard_map/ppermute | solution.py:414
  11.8 2.6 %collective-permute-start.1 = (f32[64,64]{1,0:T(8,128)S(1)}, f32[64,64]{1,0:T(8,128)S(1)}, u32[]{:S(2)}, u32[]{:S(2)}) collective-permute-start(f32[64,64]{1,0:T(8,128)S(1)} %get-tuple-element.18.refs_0_), channel_id=1, source_target_pairs={{0,2},{1,3},{2,0},{3,1},{4,6},{5,7},{6,4},{7,5},{8,10},{9,11},{10,... | collective-permute-start | bytes 49160 | tf_op jit(solution)/shard_map/ppermute | solution.py:414
  14.4 0.1 reshape.25.list_ref
  14.5 1.4 %count.1 = (f32[2,64,128]{2,1,0:T(8,128)S(1)}, f32[64,128]{1,0:T(8,128)S(1)}) custom-call(s32[1]{0:T(128)} %bitcast.1.slab_ref, f32[1,2]{1,0:T(1,128)S(1)} %bitcast.6, f32[1,64]{1,0:T(1,128)S(1)} %bitcast.7, s32[64,128]{1,0:T(8,128)S(1)} %reshape.25.list_ref), custom_call_target="tpu_custom_call" | custom-call | flops 10000000 | bytes 1000000 | tf_op jit(solution)/shard_map/count/pallas_call | solution.py:220
  15.9 1.3 %collective-permute-done.1.refs_2_ = f32[64,64]{1,0:T(8,128)S(1)} collective-permute-done((f32[64,64]{1,0:T(8,128)S(1)}, f32[64,64]{1,0:T(8,128)S(1)}, u32[]{:S(2)}, u32[]{:S(2)}) %collective-permute-start.1) | collective-permute-done | bytes 16416 | tf_op jit(solution)/shard_map/ppermute | solution.py:414
  17.1 2.9 %collective-permute-done.2.refs_3_ = f32[64,64]{1,0:T(8,128)S(1)} collective-permute-done((f32[64,64]{1,0:T(8,128)S(1)}, f32[64,64]{1,0:T(8,128)S(1)}, u32[]{:S(2)}, u32[]{:S(2)}) %collective-permute-start.2) | collective-permute-done | bytes 16416 | tf_op jit(solution)/shard_map/ppermute | solution.py:414
  20.1 0.4 weigh.1.own_w_ref
  20.5 1.2 %collective-permute-done.3.sib_w_ref = f32[64,64]{1,0:T(8,128)S(1)} collective-permute-done((f32[64,64]{1,0:T(8,128)S(1)}, f32[64,64]{1,0:T(8,128)S(1)}, u32[]{:S(2)}, u32[]{:S(2)}) %collective-permute-start.3) | collective-permute-done | bytes 16416 | tf_op jit(solution)/shard_map/ppermute | solution.py:394
  21.7 1.7 %sums.5 = (f32[1,64,2176]{2,1,0:T(8,128)S(1)}, f32[1,64,2048]{2,1,0:T(8,128)S(1)}) custom-call(f32[64,64]{1,0:T(8,128)S(1)} %weigh.1.own_w_ref, f32[64,64]{1,0:T(8,128)S(1)} %collective-permute-done.3.sib_w_ref, f32[64,64]{1,0:T(8,128)S(1)} %copy-done, f32[64,64]{1,0:T(8,128)S(1)} %collective-permute-done.4.sib_ctf_ref, ...), custom_call_target="tpu_custom_call" | custom-call | flops 67108864 | bytes 2621440 | tf_op jit(solution)/shard_map/sums/pallas_call | solution.py:314
  23.4 1.5 %collective-permute-start.7 = (f32[1,64,2176]{2,1,0:T(8,128)S(1)}, f32[1,64,2176]{2,1,0:T(8,128)S(1)}, u32[]{:S(2)}, u32[]{:S(2)}) collective-permute-start(f32[1,64,2176]{2,1,0:T(8,128)S(1)} %get-tuple-element.23), channel_id=1, source_target_pairs={{0,8},{4,12},{8,0},{12,4},{16,24},{20,28},{24,16},{28,20},{1,9},{5... | collective-permute-start | bytes 1671176 | tf_op jit(solution)/shard_map/ppermute | solution.py:394
  24.9 1.6 %collective-permute-start.10 = (f32[1,64,2048]{2,1,0:T(8,128)S(1)}, f32[1,64,2048]{2,1,0:T(8,128)S(1)}, u32[]{:S(2)}, u32[]{:S(2)}) collective-permute-start(f32[1,64,2048]{2,1,0:T(8,128)S(1)} %get-tuple-element.26), channel_id=1, source_target_pairs={{0,16},{4,20},{8,24},{12,28},{16,0},{20,4},{24,8},{28,12},{1,17},{... | collective-permute-start | bytes 1572872 | tf_op jit(solution)/shard_map/ppermute | solution.py:394
  26.5 1.7 %sums.3 = (f32[1,64,2176]{2,1,0:T(8,128)S(1)}, f32[1,64,2048]{2,1,0:T(8,128)S(1)}) custom-call(f32[64,64]{1,0:T(8,128)S(1)} %weigh.1.own_w_ref, f32[64,64]{1,0:T(8,128)S(1)} %collective-permute-done.3.sib_w_ref, f32[64,64]{1,0:T(8,128)S(1)} %copy-done, f32[64,64]{1,0:T(8,128)S(1)} %collective-permute-done.4.sib_ctf_ref, ...), custom_call_target="tpu_custom_call" | custom-call | flops 67108864 | bytes 2621440 | tf_op jit(solution)/shard_map/sums/pallas_call | solution.py:314
  28.2 0.6 collective-permute-start.6
  28.8 0.5 collective-permute-start.9
  29.3 2.4 %sums.4 = (f32[2,64,2176]{2,1,0:T(8,128)S(1)}, f32[2,64,2048]{2,1,0:T(8,128)S(1)}) custom-call(f32[64,64]{1,0:T(8,128)S(1)} %weigh.1.own_w_ref, f32[64,64]{1,0:T(8,128)S(1)} %collective-permute-done.3.sib_w_ref, f32[64,64]{1,0:T(8,128)S(1)} %copy-done, f32[64,64]{1,0:T(8,128)S(1)} %collective-permute-done.4.sib_ctf_ref, ...), custom_call_target="tpu_custom_call" | custom-call | flops 134217728 | bytes 5242880 | tf_op jit(solution)/shard_map/sums/pallas_call | solution.py:314
  31.7 7.3 %collective-permute-done.7 = f32[1,64,2176]{2,1,0:T(8,128)S(1)} collective-permute-done((f32[1,64,2176]{2,1,0:T(8,128)S(1)}, f32[1,64,2176]{2,1,0:T(8,128)S(1)}, u32[]{:S(2)}, u32[]{:S(2)}) %collective-permute-start.7) | collective-permute-done | bytes 557088 | tf_op jit(solution)/shard_map/ppermute | solution.py:394
  39.0 1.6 %collective-permute-start.8 = (f32[1,64,2176]{2,1,0:T(8,128)S(1)}, f32[1,64,2176]{2,1,0:T(8,128)S(1)}, u32[]{:S(2)}, u32[]{:S(2)}) collective-permute-start(f32[1,64,2176]{2,1,0:T(8,128)S(1)} %slice_add_fusion), channel_id=1, source_target_pairs={{0,16},{4,20},{8,24},{12,28},{16,0},{20,4},{24,8},{28,12},{1,17},{... | collective-permute-start | bytes 1671176 | tf_op jit(solution)/shard_map/ppermute | solution.py:394
  40.6 1.6 %collective-permute-start.11 = (f32[1,64,2048]{2,1,0:T(8,128)S(1)}, f32[1,64,2048]{2,1,0:T(8,128)S(1)}, u32[]{:S(2)}, u32[]{:S(2)}) collective-permute-start(f32[1,64,2048]{2,1,0:T(8,128)S(1)} %slice_add_fusion.1), channel_id=1, source_target_pairs={{0,8},{4,12},{8,0},{12,4},{16,24},{20,28},{24,16},{28,20},{1,9},{5... | collective-permute-start | bytes 1572872 | tf_op jit(solution)/shard_map/ppermute | solution.py:394
  42.2 8.8 %collective-permute-done.9.refs_3_ = f32[1,64,2048]{2,1,0:T(8,128)S(1)} collective-permute-done((f32[1,64,2048]{2,1,0:T(8,128)S(1)}, f32[1,64,2048]{2,1,0:T(8,128)S(1)}, u32[]{:S(2)}, u32[]{:S(2)}) %collective-permute-start.9) | collective-permute-done | bytes 524320 | tf_op jit(solution)/shard_map/ppermute | solution.py:394
  51.0 10.3 %collective-permute-done.11.refs_5_ = f32[1,64,2048]{2,1,0:T(8,128)S(1)} collective-permute-done((f32[1,64,2048]{2,1,0:T(8,128)S(1)}, f32[1,64,2048]{2,1,0:T(8,128)S(1)}, u32[]{:S(2)}, u32[]{:S(2)}) %collective-permute-start.11) | collective-permute-done | bytes 524320 | tf_op jit(solution)/shard_map/ppermute | solution.py:394
  61.3 0.5 collective-permute-done.8.refs_2_
  61.8 1.3 %finish.1 = f32[64,4096]{1,0:T(8,128)} custom-call(s32[1]{0:T(128)} %bitcast.me_ref, s32[1,32768]{1,0:T(1,128)S(1)} %copy-done.1, f32[1,64,2176]{2,1,0:T(8,128)S(1)} %collective-permute-done.6.refs_0_, f32[2,64,2176]{2,1,0:T(8,128)S(1)} %get-tuple-element.22.refs_1_, f32[1,64,2176]{2,1,0:T(8,128)S(1)} %collective-permute-done.8.refs_2_, ...), custom_call_target="tpu_custom_call" | custom-call | tf_op jit(solution)/shard_map/finish/pallas_call | solution.py:375
  (20 shorter events, 0.2 us)
Async XLA Ops:
  0.0 14.4 %copy-start = (f32[64,64]{1,0:T(8,128)S(1)}, f32[64,64]{1,0:T(8,128)}, u32[]{:S(2)}) copy-start(f32[64,64]{1,0:T(8,128)} %own_ctf_ref.5) | copy-start | bytes 49156
  0.0 14.4 %copy-start.4 = (s32[64,2,64]{2,1,0:T(2,128)S(1)}, s32[64,2,64]{2,1,0:T(2,128)}, u32[]{:S(2)}) copy-start(s32[64,2,64]{2,1,0:T(2,128)} %param.10) | copy-start | bytes 98308
  0.0 14.5 %copy-start.2 = (f32[2]{0:T(128)S(1)}, f32[2]{0:T(128)}, u32[]{:S(2)}) copy-start(f32[2]{0:T(128)} %param.13) | copy-start | bytes 28
  0.0 14.5 %copy-start.3 = (f32[64]{0:T(128)S(1)}, f32[64]{0:T(128)}, u32[]{:S(2)}) copy-start(f32[64]{0:T(128)} %param.12) | copy-start | bytes 772
  8.6 13.1 %collective-permute-start.5 = (f32[4,64,4096]{2,1,0:T(8,128)}, f32[4,64,4096]{2,1,0:T(8,128)}, u32[]{:S(2)}, u32[]{:S(2)}) collective-permute-start(f32[4,64,4096]{2,1,0:T(8,128)} %get-tuple-element.20), channel_id=1, source_target_pairs={{0,4},{4,0},{8,12},{12,8},{16,20},{20,16},{24,28},{28,24},{1,5},{5... | collective-permute-start | bytes 12582920 | tf_op jit(solution)/shard_map/ppermute | solution.py:394
  9.1 6.8 %collective-permute-start = (f32[64,64]{1,0:T(8,128)S(1)}, f32[64,64]{1,0:T(8,128)S(1)}, u32[]{:S(2)}, u32[]{:S(2)}) collective-permute-start(f32[64,64]{1,0:T(8,128)S(1)} %get-tuple-element.18.refs_0_), channel_id=1, source_target_pairs={{0,1},{1,0},{2,3},{3,2},{4,5},{5,4},{6,7},{7,6},{8,9},{9,8},{10,11... | collective-permute-start | bytes 49160 | tf_op jit(solution)/shard_map/ppermute | solution.py:414
  11.8 5.4 %collective-permute-start.1 = (f32[64,64]{1,0:T(8,128)S(1)}, f32[64,64]{1,0:T(8,128)S(1)}, u32[]{:S(2)}, u32[]{:S(2)}) collective-permute-start(f32[64,64]{1,0:T(8,128)S(1)} %get-tuple-element.18.refs_0_), channel_id=1, source_target_pairs={{0,2},{1,3},{2,0},{3,1},{4,6},{5,7},{6,4},{7,5},{8,10},{9,11},{10,... | collective-permute-start | bytes 49160 | tf_op jit(solution)/shard_map/ppermute | solution.py:414
  14.4 5.7 %collective-permute-start.2 = (f32[64,64]{1,0:T(8,128)S(1)}, f32[64,64]{1,0:T(8,128)S(1)}, u32[]{:S(2)}, u32[]{:S(2)}) collective-permute-start(f32[64,64]{1,0:T(8,128)S(1)} %get-tuple-element.18.refs_0_), channel_id=1, source_target_pairs={{0,3},{1,2},{2,1},{3,0},{4,7},{5,6},{6,5},{7,4},{8,11},{9,10},{10,... | collective-permute-start | bytes 49160 | tf_op jit(solution)/shard_map/ppermute | solution.py:414
  14.4 6.1 %collective-permute-start.4 = (f32[64,64]{1,0:T(8,128)S(1)}, f32[64,64]{1,0:T(8,128)S(1)}, u32[]{:S(2)}, u32[]{:S(2)}) collective-permute-start(f32[64,64]{1,0:T(8,128)S(1)} %copy-done), channel_id=1, source_target_pairs={{0,4},{4,0},{8,12},{12,8},{16,20},{20,16},{24,28},{28,24},{1,5},{5... | collective-permute-start | bytes 49160 | tf_op jit(solution)/shard_map/ppermute | solution.py:394
  20.4 1.2 %collective-permute-start.3 = (f32[64,64]{1,0:T(8,128)S(1)}, f32[64,64]{1,0:T(8,128)S(1)}, u32[]{:S(2)}, u32[]{:S(2)}) collective-permute-start(f32[64,64]{1,0:T(8,128)S(1)} %weigh.1.own_w_ref), channel_id=1, source_target_pairs={{0,4},{4,0},{8,12},{12,8},{16,20},{20,16},{24,28},{28,24},{1,5},{5... | collective-permute-start | bytes 49160 | tf_op jit(solution)/shard_map/ppermute | solution.py:394
  23.4 15.5 %collective-permute-start.7 = (f32[1,64,2176]{2,1,0:T(8,128)S(1)}, f32[1,64,2176]{2,1,0:T(8,128)S(1)}, u32[]{:S(2)}, u32[]{:S(2)}) collective-permute-start(f32[1,64,2176]{2,1,0:T(8,128)S(1)} %get-tuple-element.23), channel_id=1, source_target_pairs={{0,8},{4,12},{8,0},{12,4},{16,24},{20,28},{24,16},{28,20},{1,9},{5... | collective-permute-start | bytes 1671176 | tf_op jit(solution)/shard_map/ppermute | solution.py:394
  24.9 15.6 %collective-permute-start.10 = (f32[1,64,2048]{2,1,0:T(8,128)S(1)}, f32[1,64,2048]{2,1,0:T(8,128)S(1)}, u32[]{:S(2)}, u32[]{:S(2)}) collective-permute-start(f32[1,64,2048]{2,1,0:T(8,128)S(1)} %get-tuple-element.26), channel_id=1, source_target_pairs={{0,16},{4,20},{8,24},{12,28},{16,0},{20,4},{24,8},{28,12},{1,17},{... | collective-permute-start | bytes 1572872 | tf_op jit(solution)/shard_map/ppermute | solution.py:394
  28.2 22.8 %collective-permute-start.6 = (f32[1,64,2176]{2,1,0:T(8,128)S(1)}, f32[1,64,2176]{2,1,0:T(8,128)S(1)}, u32[]{:S(2)}, u32[]{:S(2)}) collective-permute-start(f32[1,64,2176]{2,1,0:T(8,128)S(1)} %get-tuple-element.21), channel_id=1, source_target_pairs={{0,8},{4,12},{8,0},{12,4},{16,24},{20,28},{24,16},{28,20},{1,9},{5... | collective-permute-start | bytes 1671176 | tf_op jit(solution)/shard_map/ppermute | solution.py:394
  28.8 33.0 %copy-start.1 = (s32[1,32768]{1,0:T(1,128)S(1)}, s32[1,32768]{1,0:T(1,128)}, u32[]{:S(2)}) copy-start(s32[1,32768]{1,0:T(1,128)} %constant.14.clone.index_hbm) | copy-start | bytes 393220
  28.8 22.2 %collective-permute-start.9 = (f32[1,64,2048]{2,1,0:T(8,128)S(1)}, f32[1,64,2048]{2,1,0:T(8,128)S(1)}, u32[]{:S(2)}, u32[]{:S(2)}) collective-permute-start(f32[1,64,2048]{2,1,0:T(8,128)S(1)} %get-tuple-element.24), channel_id=1, source_target_pairs={{0,16},{4,20},{8,24},{12,28},{16,0},{20,4},{24,8},{28,12},{1,17},{... | collective-permute-start | bytes 1572872 | tf_op jit(solution)/shard_map/ppermute | solution.py:394
  39.0 22.8 %collective-permute-start.8 = (f32[1,64,2176]{2,1,0:T(8,128)S(1)}, f32[1,64,2176]{2,1,0:T(8,128)S(1)}, u32[]{:S(2)}, u32[]{:S(2)}) collective-permute-start(f32[1,64,2176]{2,1,0:T(8,128)S(1)} %slice_add_fusion), channel_id=1, source_target_pairs={{0,16},{4,20},{8,24},{12,28},{16,0},{20,4},{24,8},{28,12},{1,17},{... | collective-permute-start | bytes 1671176 | tf_op jit(solution)/shard_map/ppermute | solution.py:394
  40.6 20.7 %collective-permute-start.11 = (f32[1,64,2048]{2,1,0:T(8,128)S(1)}, f32[1,64,2048]{2,1,0:T(8,128)S(1)}, u32[]{:S(2)}, u32[]{:S(2)}) collective-permute-start(f32[1,64,2048]{2,1,0:T(8,128)S(1)} %slice_add_fusion.1), channel_id=1, source_target_pairs={{0,8},{4,12},{8,0},{12,4},{16,24},{20,28},{24,16},{28,20},{1,9},{5... | collective-permute-start | bytes 1572872 | tf_op jit(solution)/shard_map/ppermute | solution.py:394

commit v6 on v4

--- a/solution.py
+++ b/solution.py
@@ -27,6 +27,16 @@
     return np.repeat(shell, 2).astype(np.int32)[None, :]
 
 
+def split_share(share):
+    met = max(LANES, 3 * share // 16 // LANES * LANES)
+    return share // 2 - met, met
+
+
+def met_column(share, owner, slab):
+    wide, met = split_share(share)
+    return pl.multiple_of(owner * share + 2 * wide + lax.rem(slab, 2) * met, LANES)
+
+
 def params(mib):
     return pltpu.CompilerParams(vmem_limit_bytes=mib * MIB)
 
@@ -47,11 +57,14 @@
 
 
 def estep_kernel(
-    blocks, me_ref, index_hbm, image_hbm, plane_hbm, ctf_hbm, give, weighted, score_ref,
-    index, image, plane, ctf_held, squared, energy_of, small_sem, in_sem,
+    blocks, share, near, me_ref, slab_ref, index_hbm, image_hbm, plane_hbm, ctf_hbm, *refs,
 ):
+    give_hbm, keep_hbm, score_ref = refs[:3]
+    near_refs = refs[3 : 3 + len(near)]
+    index, image, plane, ctf_held, weighted, give, squared, energy_of = refs[-11:-3]
+    small_sem, in_sem, out_sem = refs[-3:]
     rows, width = image.shape
-    chips, _, share = give.shape
+    chips, summed = width // share // 2, 2 * split_share(share)[0]
     box = math.isqrt(width // 2)
     line = 2 * box
     deep = box // (2 * blocks)
@@ -116,6 +129,7 @@
         return 2.0 * low - energy(block % 2, span)
 
     chip, core = me_ref[0] // 2, lax.rem(me_ref[0], 2)
+    outgoing = []
 
     def hand_over(done):
         for pair in range(chips):
@@ -123,9 +137,22 @@
             if pair in handed or not all(row in done for row in range(first, last)):
                 continue
             handed.add(pair)
-            given = pl.ds(pl.multiple_of((2 * pair + 1 - core) * share, share), share)
-            give[pair ^ chip] = weighted[:, given].astype(F32)
-
+            place = pair ^ chip
+            given = pl.ds(pl.multiple_of((2 * pair + 1 - core) * share, share), summed)
+            kept = pl.ds(pl.multiple_of((2 * pair + core) * share, share), summed)
+            at = pl.ds(pl.multiple_of(place * summed, LANES), summed)
+            give[:, at] = weighted[:, given].astype(F32)
+            outgoing.extend([
+                pltpu.make_async_copy(give.at[:, at], give_hbm.at[:, at], out_sem.at[pair, 0]),
+                pltpu.make_async_copy(weighted.at[:, kept], keep_hbm.at[:, at], out_sem.at[pair, 1]),
+            ])
+            outgoing[-2].start()
+            outgoing[-1].start()
+
+    tail = slice(chips * summed, chips * summed + LANES)
+    give[:, tail] = table
+    outgoing.append(pltpu.make_async_copy(give.at[:, tail], give_hbm.at[:, tail], out_sem.at[chips, 0]))
+    outgoing[-1].start()
     handed, done = set(), set()
     total = jnp.zeros(score_ref.shape, F32)
     for block in range(blocks):
@@ -144,39 +171,119 @@
     middle = width // 2
     total += 2.0 * fit(middle, middle + line) - energy(2, line)
     score_ref[...] = total
-
-
-def estep(me, index, images, planes, ctf_table, share):
+    for k, near_ref in zip(near, near_refs):
+        for other in range(2):
+            owner = (k ^ chip) * 2 + lax.rem(core + other, 2)
+            part = weighted[:, pl.ds(met_column(share, owner, slab_ref[0]), near_ref.shape[2])]
+            near_ref[other] = part.astype(near_ref.dtype)
+    for copy in outgoing:
+        copy.wait()
+
+
+def far(*operands):
+    return [pltpu.with_memory_space_constraint(operand, pltpu.HBM) for operand in operands]
+
+
+def estep(me, slab, index, images, planes, ctf_table, share, near):
     rows, width = images.shape
     chips = width // share // 2
+    wide, met = split_share(share)
+    summed = 2 * wide
     count = planes.shape[0]
     blocks = 4
     span = width // (2 * blocks)
+    held = pl.BlockSpec(memory_space=pl.ANY)
     vmem = pl.BlockSpec(memory_space=pltpu.VMEM)
-    far = pl.BlockSpec(memory_space=pltpu.HBM)
-    operands = (index, images, planes, ctf_table)
+    hbm = pl.BlockSpec(memory_space=pltpu.HBM)
     return pl.pallas_call(
-        functools.partial(estep_kernel, blocks),
-        in_specs=[pl.BlockSpec(memory_space=pltpu.SMEM)] + [far] * 4,
-        out_specs=[vmem] * 3,
+        functools.partial(estep_kernel, blocks, share, near),
+        in_specs=[pl.BlockSpec(memory_space=pltpu.SMEM)] * 2 + [hbm] * 4,
+        out_specs=[held, held] + [vmem] * (1 + len(near)),
         out_shape=[
-            jax.ShapeDtypeStruct((chips, rows, share), F32),
-            jax.ShapeDtypeStruct((rows, width), BF16),
+            jax.ShapeDtypeStruct((rows, chips * summed + LANES), F32),
+            pltpu.HBM((rows, chips * summed), BF16),
             jax.ShapeDtypeStruct((rows, count), F32),
+        ]
+        + [
+            jax.ShapeDtypeStruct((2, rows, met), F32) if k else pltpu.HBM((2, rows, met), BF16)
+            for k in near
         ],
         scratch_shapes=[
             pltpu.VMEM(index.shape, jnp.int32),
             pltpu.VMEM((rows, width), BF16),
             pltpu.VMEM((count, width), BF16),
             pltpu.VMEM(ctf_table.shape, F32),
+            pltpu.VMEM((rows, width), BF16),
+            pltpu.VMEM((rows, chips * summed + LANES), F32),
             pltpu.VMEM((3, rows, span), BF16),
             pltpu.VMEM((3, count, span), BF16),
             pltpu.SemaphoreType.DMA((2,)),
             pltpu.SemaphoreType.DMA((blocks, 2, 2)),
+            pltpu.SemaphoreType.DMA((chips + 1, 2)),
         ],
         compiler_params=params(28),
         name="estep",
-    )(me, *[pltpu.with_memory_space_constraint(operand, pltpu.HBM) for operand in operands])
+    )(me, slab, *far(index, images, planes, ctf_table))
+
+
+def early_kernel(share, beyond, me_ref, slab_ref, index_hbm, image_hbm, ctf_hbm, *refs):
+    outs = refs[: len(beyond)]
+    index, image, ctf_held, index_sem, image_sem, ctf_sem = refs[len(beyond) :]
+    _, rows, met = outs[0].shape
+    chip, core = me_ref[0] // 2, lax.rem(me_ref[0], 2)
+    fetch = pltpu.make_async_copy(ctf_hbm, ctf_held, ctf_sem)
+    fetch.start()
+    copies = []
+    for place, k in enumerate(beyond):
+        for other in range(2):
+            owner = (k ^ chip) * 2 + lax.rem(core + other, 2)
+            cut = pl.ds(met_column(share, owner, slab_ref[0]), met)
+            copies.append([
+                pltpu.make_async_copy(
+                    index_hbm.at[:, cut], index.at[place, other], index_sem.at[place, other]
+                ),
+                pltpu.make_async_copy(
+                    image_hbm.at[:, cut], image.at[place, other], image_sem.at[place, other]
+                ),
+            ])
+            for copy in copies[-1]:
+                copy.start()
+    fetch.wait()
+    table = lanes_wide(ctf_held[...])
+    for place, out_ref in enumerate(outs):
+        for other in range(2):
+            for copy in copies[2 * place + other]:
+                copy.wait()
+            for start in range(0, met, LANES):
+                cut = slice(start, start + LANES)
+                ctf = spread(table, index[place, other, :, cut])
+                part = (image[place, other, :, cut].astype(F32) * ctf).astype(BF16)
+                out_ref[other, :, cut] = part.astype(F32)
+
+
+def early_images(me, slab, index, images, ctf_table, share, beyond):
+    rows = images.shape[0]
+    met = split_share(share)[1]
+    number = len(beyond)
+    vmem = pl.BlockSpec(memory_space=pltpu.VMEM)
+    smem = pl.BlockSpec(memory_space=pltpu.SMEM)
+    hbm = pl.BlockSpec(memory_space=pltpu.HBM)
+    return pl.pallas_call(
+        functools.partial(early_kernel, share, beyond),
+        in_specs=[smem, smem, hbm, hbm, hbm],
+        out_specs=[vmem] * number,
+        out_shape=[jax.ShapeDtypeStruct((2, rows, met), F32)] * number,
+        scratch_shapes=[
+            pltpu.VMEM((number, 2, 1, met), jnp.int32),
+            pltpu.VMEM((number, 2, rows, met), BF16),
+            pltpu.VMEM(ctf_table.shape, F32),
+            pltpu.SemaphoreType.DMA((number, 2)),
+            pltpu.SemaphoreType.DMA((number, 2)),
+            pltpu.SemaphoreType.DMA(()),
+        ],
+        compiler_params=params(12),
+        name="early",
+    )(me, slab, *far(index, images, ctf_table))
 
 
 def count_kernel(slabs, slab_ref, prior_ref, noise_ref, list_ref, base_ref, scale_ref):
@@ -213,7 +320,6 @@
             jax.ShapeDtypeStruct((rows, width), F32),
         ],
         compiler_params=params(4),
-        cost_estimate=pl.CostEstimate(flops=10**7, bytes_accessed=10**6, transcendentals=0),
         name="count",
     )(
         slab,
@@ -224,137 +330,194 @@
 
 
 def weigh_kernel(base_ref, scale_ref, *refs):
-    out_ref = refs[-1]
+    table_refs, (own_ref, both_ref) = refs[:-2], refs[-2:]
     classes = base_ref.shape[0]
-    planes = out_ref.shape[0]
+    planes = own_ref.shape[0]
     local = planes // classes
     scores = []
     for one in range(classes):
         parts = [
             ref[:, start + one * local : start + (one + 1) * local]
-            for ref in refs[:-1]
+            for ref in table_refs
             for start in range(0, ref.shape[1], planes)
         ]
         scores.append(base_ref[one] + scale_ref[...] * jnp.concatenate(parts, axis=1))
     peak = functools.reduce(jnp.maximum, [jnp.max(score, axis=1, keepdims=True) for score in scores])
     raw = [jnp.exp(score - peak) for score in scores]
     total = functools.reduce(jnp.add, [jnp.sum(part, axis=1, keepdims=True) for part in raw])
-    own = jnp.concatenate([part[:, :local] for part in raw], axis=1) / total
-    out_ref[...] = own.T
+    slabs = [
+        jnp.concatenate([part[:, place * local : (place + 1) * local] for part in raw], axis=1) / total
+        for place in range(2)
+    ]
+    own_ref[...] = slabs[0].T
+    both_ref[...] = jnp.concatenate(slabs, axis=1)
 
 
 def weigh(base, scale, tables, planes):
+    rows = base.shape[1]
     return pl.pallas_call(
         weigh_kernel,
-        out_shape=jax.ShapeDtypeStruct((planes, base.shape[1]), F32),
+        out_shape=[
+            jax.ShapeDtypeStruct((planes, rows), F32),
+            jax.ShapeDtypeStruct((rows, 2 * planes), F32),
+        ],
         compiler_params=params(4),
         name="weigh",
     )(base, scale, *tables)
 
 
-def sums_kernel(items, me_ref, own_w_ref, sib_w_ref, own_ctf_ref, sib_ctf_ref, weighted_ref, got_ref, *outs):
-    share = got_ref.shape[2]
-    tile = share // 4
-    wide = share // 2
-    chip, core = me_ref[0] // 2, lax.rem(me_ref[0], 2)
+def sums_kernel(items, own_w_ref, sib_w_ref, both_w_ref, own_ctf_ref, keep_hbm, got_hbm, *refs):
+    outs = refs[: len(items)]
+    keep, got, sib_ctf, in_sem, ctf_sem = refs[len(items) :]
+    number, _, wide = keep.shape
+    tail = slice(keep_hbm.shape[1], keep_hbm.shape[1] + LANES)
+    fetch = pltpu.make_async_copy(got_hbm.at[:, tail], sib_ctf, ctf_sem)
+    fetch.start()
+    places = [(slot, k, side) for side, ks in enumerate(items) for slot, k in enumerate(ks)]
+    incoming = []
+    for place, (slot, k, side) in enumerate(places):
+        source = slice((2 * k + side) * wide, (2 * k + side + 1) * wide)
+        incoming.append([
+            pltpu.make_async_copy(keep_hbm.at[:, source], keep.at[place], in_sem.at[place, 0]),
+            pltpu.make_async_copy(got_hbm.at[:, source], got.at[place], in_sem.at[place, 1]),
+        ])
+        for copy in incoming[-1]:
+            copy.start()
     weights = jnp.concatenate([own_w_ref[...], sib_w_ref[...]], axis=1).astype(BF16)
-    ctf = jnp.concatenate([own_ctf_ref[...], sib_ctf_ref[...]], axis=0)
-    shells = jnp.dot(weights, lanes_wide((ctf * ctf).astype(BF16)), preferred_element_type=F32)
-    for side, ks in enumerate(items):
-        for slot, k in enumerate(ks):
-            start = pl.multiple_of(((k ^ chip) * 2 + core) * share, share)
-            for cell in range(wide // tile):
-                place = (2 * cell + side) * tile
-                images = jnp.concatenate(
-                    [
-                        weighted_ref[:, pl.ds(pl.multiple_of(start + place, tile), tile)],
-                        got_ref[k, :, place : place + tile].astype(BF16),
-                    ],
-                    axis=0,
-                )
-                outs[side][slot, :, cell * tile : (cell + 1) * tile] = jnp.dot(
-                    weights, images, preferred_element_type=F32
-                )
-            if side == 0:
-                outs[side][slot, :, wide:] = shells
-
-
-def partial_sums(items, me, own_w, sib_w, own_ctf, sib_ctf, weighted, got):
-    chips, rows, share = got.shape
+    fetch.wait()
+    ctf = jnp.concatenate([lanes_wide(own_ctf_ref[...]), sib_ctf[...]], axis=0)
+    shell_sums = jnp.dot(weights, (ctf * ctf).astype(BF16), preferred_element_type=F32)
+    for place, (slot, k, side) in enumerate(places):
+        for copy in incoming[place]:
+            copy.wait()
+        images = jnp.concatenate([keep[place], got[place].astype(BF16)], axis=0)
+        outs[side][slot, :, :wide] = jnp.dot(weights, images, preferred_element_type=F32)
+        if side == 0:
+            outs[side][slot, :, wide : wide + LANES] = shell_sums
+        behind = wide + (LANES if side == 0 else 0)
+        if outs[side].shape[2] > behind:
+            outs[side][slot, :, behind:] = both_w_ref[...]
+
+
+def partial_sums(items, with_weights, own_w, sib_w, both_w, own_ctf, keep, got, wide):
+    rows = keep.shape[0]
     planes = own_w.shape[0]
-    wide = share // 2
     number = sum(len(ks) for ks in items)
+    held = pl.BlockSpec(memory_space=pl.ANY)
     vmem = pl.BlockSpec(memory_space=pltpu.VMEM)
+    rider = both_w.shape[1] if with_weights else 0
     return pl.pallas_call(
         functools.partial(sums_kernel, items),
-        in_specs=[pl.BlockSpec(memory_space=pltpu.SMEM)] + [vmem] * 6,
+        in_specs=[vmem] * 4 + [held] * 2,
         out_specs=[vmem] * 2,
         out_shape=[
-            jax.ShapeDtypeStruct((len(ks), planes, wide + extra), F32)
+            jax.ShapeDtypeStruct((len(ks), planes, wide + extra + rider), F32)
             for ks, extra in zip(items, (LANES, 0))
         ],
+        scratch_shapes=[
+            pltpu.VMEM((number, rows, wide), BF16),
+            pltpu.VMEM((number, rows, wide), F32),
+            pltpu.VMEM((rows, LANES), F32),
+            pltpu.SemaphoreType.DMA((number, 2)),
+            pltpu.SemaphoreType.DMA(()),
+        ],
+        compiler_params=params(12),
+        name="sums",
+    )(own_w, sib_w, both_w, own_ctf, keep, got)
+
+
+def meet_kernel(chips, *refs):
+    weight_refs, image_refs, outs = refs[:chips], refs[chips : 2 * chips], refs[2 * chips :]
+    planes = outs[0].shape[0]
+    weights = []
+    for ref in weight_refs:
+        wide = ref.shape[-1]
+        part = ref[:, wide - planes :] if len(ref.shape) == 2 else ref[0, :, wide - planes :]
+        weights.append(part.astype(BF16))
+    weights = jnp.concatenate(weights, axis=0)
+    for other, out_ref in enumerate(outs):
+        images = jnp.concatenate([ref[other].astype(BF16) for ref in image_refs], axis=0)
+        out_ref[...] = lax.dot_general(
+            weights, images, (((0,), (0,)), ((), ())), preferred_element_type=F32
+        )
+
+
+def meet(weights, images):
+    _, rows, met = images[0].shape
+    planes = weights[0].shape[1]
+    return pl.pallas_call(
+        functools.partial(meet_kernel, len(weights)),
+        out_shape=[jax.ShapeDtypeStruct((planes, met), F32)] * 2,
         compiler_params=params(16),
-        cost_estimate=pl.CostEstimate(
-            flops=4 * planes * rows * wide * number,
-            bytes_accessed=10 * planes * wide * number,
-            transcendentals=0,
-        ),
-        name="sums",
-    )(me, own_w, sib_w, own_ctf, sib_ctf, weighted, got)
-
-
-def finish_kernel(numbers, me_ref, index_hbm, *refs):
+        name="meet",
+    )(*weights, *images)
+
+
+def finish_kernel(numbers, me_ref, slab_ref, index_hbm, met_ref, sib_met_ref, partner_ref, *refs):
     total = sum(numbers)
     parts, (out_hbm, index, out, in_sem, out_sem) = refs[:total], refs[total:]
     planes, share = out.shape
-    tile = share // 4
-    wide = share // 2
+    wide, met = split_share(share)
     mine = pl.ds(pl.multiple_of(me_ref[0] * share, share), share)
     fetch = pltpu.make_async_copy(index_hbm.at[:, mine], index, in_sem)
     fetch.start()
     left, right = parts[: numbers[0]], parts[numbers[0] :]
-    shells = functools.reduce(jnp.add, [ref[0, :, wide:] for ref in left])
+    shells = functools.reduce(jnp.add, [ref[0, :, wide : wide + LANES] for ref in left])
+    half = lax.rem(slab_ref[0], 2)
     fetch.wait()
+
+    def divide(block_of, place, size):
+        for start in range(0, size, LANES):
+            at = pl.ds(pl.multiple_of(place + start, LANES), LANES)
+            weight = spread(shells, index[:, at])
+            out[:, at] = block_of(slice(start, start + LANES)) / (weight + 1.0)
+
+    def summed(sides):
+        return lambda cut: functools.reduce(jnp.add, [ref[0, :, cut] for ref in sides])
+
+    divide(lambda cut: met_ref[:planes, cut] + sib_met_ref[:planes, cut], 2 * wide + half * met, met)
+    divide(lambda cut: partner_ref[:, cut], 2 * wide + (1 - half) * met, met)
     stores = []
-    for cell in range(2):
-        for side, refs in ((0, left), (1, right)):
-            for start in range(0, tile, LANES):
-                place = (2 * cell + side) * tile + start
-                cut = slice(cell * tile + start, cell * tile + start + LANES)
-                block = functools.reduce(jnp.add, [ref[0, :, cut] for ref in refs])
-                weight = spread(shells, index[:, place : place + LANES])
-                out[:, place : place + LANES] = block / (weight + 1.0)
-        cut = slice(cell * wide, (cell + 1) * wide)
-        stores.append(pltpu.make_async_copy(out.at[:, cut], out_hbm.at[:, cut], out_sem.at[cell]))
+    for step, work in enumerate((None, (left, 0), (right, 1))):
+        cut = slice(2 * wide, share)
+        if work is not None:
+            sides, place = work
+            divide(summed(sides), place * wide, wide)
+            cut = slice(place * wide, (place + 1) * wide)
+        stores.append(pltpu.make_async_copy(out.at[:, cut], out_hbm.at[:, cut], out_sem.at[step]))
         stores[-1].start()
     for store in stores:
         store.wait()
 
 
-def finish(me, index, left, right, share):
-    planes = left[0][0].shape[1]
+def finish(me, slab, index, met, sib_met, partner, left, right, share):
+    planes = partner.shape[0]
     numbers = len(left), len(right)
     held = pl.BlockSpec(memory_space=pl.ANY)
+    vmem = pl.BlockSpec(memory_space=pltpu.VMEM)
 
     def first(part, place):
+        if part.shape[0] == 1:
+            return vmem
         return pl.BlockSpec((1,) + part.shape[1:], lambda step: (place, 0, 0))
 
     return pl.pallas_call(
         functools.partial(finish_kernel, numbers),
         grid=(1,),
-        in_specs=[pl.BlockSpec(memory_space=pltpu.SMEM), held]
-        + [first(part, place) if part.shape[0] > 1 else pl.BlockSpec(memory_space=pltpu.VMEM) for part, place in left + right],
+        in_specs=[pl.BlockSpec(memory_space=pltpu.SMEM)] * 2
+        + [held, vmem, vmem, vmem]
+        + [first(part, place) for part, place in left + right],
         out_specs=held,
         out_shape=jax.ShapeDtypeStruct((planes, share), F32),
         scratch_shapes=[
             pltpu.VMEM((1, share), jnp.int32),
             pltpu.VMEM((planes, share), F32),
             pltpu.SemaphoreType.DMA(()),
-            pltpu.SemaphoreType.DMA((2,)),
+            pltpu.SemaphoreType.DMA((3,)),
         ],
         compiler_params=params(12),
         name="finish",
-    )(me, index, *[part for part, _ in left + right])
+    )(me, slab, index, met, sib_met, partner, *[part for part, _ in left + right])
 
 
 def swap(array, bit, size):
@@ -375,25 +538,45 @@
     index = jnp.asarray(index)
     planes = references.reshape(classes * local_planes, width)
 
-    give, weighted, table = estep(me, top_index, images, planes, ctf_table, share)
-    sib_ctf = swap(ctf_table, 1, size)
+    beyond = tuple(k for k in range(chips) if k & (k - 1))
+    near = tuple(k for k in range(chips) if k not in beyond)
+    met_images = {}
+    if beyond:
+        early = early_images(me, slab, index, images, ctf_table, share, beyond)
+        images, *early = lax.optimization_barrier((images, *early))
+        met_images = {k: swap(part, 2 * k, size) for k, part in zip(beyond, early)}
+    give, keep, table, *parts_near = estep(
+        me, slab, top_index, images, planes, ctf_table, share, near
+    )
+    if beyond:
+        give, keep, met_images[beyond[-1]], *parts_near = lax.optimization_barrier(
+            (give, keep, met_images[beyond[-1]], *parts_near)
+        )
+    for k, part in zip(near, parts_near):
+        met_images[k] = swap(part, 2 * k, size) if k else part
+    keep, *met_images = lax.optimization_barrier(
+        (keep, *[met_images[k] for k in range(chips)])
+    )
+    keep, *met_images = far(keep, *met_images)
+    base, scale = count_planes(
+        slab, class_weight, inv_noise, orientations, slabs * local_planes, slabs
+    )
     tables, bit = [table], 1
     while bit < slabs:
-        held = tables[0] if len(tables) == 1 else jnp.concatenate(tables, axis=1)
-        tables = [
-            held, lax.ppermute(held, "slab", [(one, one ^ bit) for one in range(slabs)])
-        ]
+        held = tables[0]
+        if len(tables) > 1:
+            held = jnp.concatenate(tables, axis=1)
+        pairs = [(one, one ^ bit) for one in range(slabs)]
+        tables = [held, lax.ppermute(held, "slab", pairs)]
         bit *= 2
     got = swap(give, 1, size)
-    base, scale = count_planes(
-        slab, class_weight, inv_noise, orientations, slabs * local_planes, slabs
-    )
-    own_w = weigh(base, scale, tables, classes * local_planes)
+    own_w, both_w = weigh(base, scale, tables, classes * local_planes)
     sib_w = swap(own_w, 1, size)
 
     sums = functools.partial(
         partial_sums,
-        me=me, own_w=own_w, sib_w=sib_w, own_ctf=ctf_table, sib_ctf=sib_ctf, weighted=weighted, got=got,
+        own_w=own_w, sib_w=sib_w, both_w=both_w, own_ctf=ctf_table, keep=keep, got=got,
+        wide=split_share(share)[0],
     )
     low = [1 << place for place in range(chips.bit_length() - 1)]
     orders = (low, low[::-1])
@@ -407,13 +590,20 @@
         arrived = swap(array, 2 * bit, size)
         for place, k in enumerate(ks):
             parts[side][k ^ bit].append((arrived, place))
-
-    def compute(groups):
-        return sums(tuple(tuple(ks) for ks in groups))
-
-    sent = compute(onward)
+        return arrived
+
+    def compute(groups, with_weights=False):
+        return sums(tuple(tuple(ks) for ks in groups), with_weights)
+
+    sent = compute(onward, True)
+    far_w = {0: both_w}
     for side in (0, 1):
-        deliver(side, onward[side], sent[side], orders[side][0])
+        bit = orders[side][0]
+        far_w[bit] = deliver(side, onward[side], sent[side], bit)
+    both_w, _ = lax.optimization_barrier((both_w, sent[1]))
+    for k in range(1, chips):
+        if k not in far_w:
+            far_w[k] = swap(both_w, 2 * k, size)
     sent = compute(direct)
     for side in (0, 1):
         deliver(side, direct[side], sent[side], orders[side][0])
@@ -421,13 +611,24 @@
     for side in (0, 1):
         for place, k in enumerate(stay[side]):
             parts[side][k].append((kept[side], place))
+
+    met, for_sib = meet([far_w[k] for k in range(chips)], met_images)
+    sib_met = swap(for_sib, 1, size)
+    own_planes = classes * local_planes
+    partner = lax.ppermute(
+        met[own_planes:] + sib_met[own_planes:], "slab", [(one, one ^ 1) for one in range(slabs)]
+    )
+
     for turn in range(1, len(low)):
         for side in (0, 1):
             bit = orders[side][turn]
             ks = [k for k in parts[side] if k & bit]
-            sent = jnp.stack([sum(part[place] for part, place in parts[side].pop(k)) for k in ks])
+            size_out = kept[side].shape[2]
+            sent = jnp.stack(
+                [sum(part[place, :, :size_out] for part, place in parts[side].pop(k)) for k in ks]
+            )
             deliver(side, ks, sent, bit)
-    out = finish(me, index, parts[0][0], parts[1][0], share)
+    out = finish(me, slab, index, met, sib_met, partner, parts[0][0], parts[1][0], share)
     return out.reshape(classes, local_planes, share)
 
 

time: 68 us -> 57.8 us (0.85)
  waiting for transfers between devices: 29.4 us -> 18 us
  starting transfers between devices: 13.6 us -> 19.7 us
  local copies, waits for them, and re-layouts: 4.31 us -> 0.13 us
    ppermute x9 -> x13, waiting for transfers between devices: 26.9 us -> 14.9 us  [swap(): return lax.ppermute(array, 'img', [(one, one ^ bit) for one in range(size)])]
    ppermute x9 -> x13, starting transfers between devices: 8.11 us -> 13.8 us  [swap(): return lax.ppermute(array, 'img', [(one, one ^ bit) for one in range(size)])]
    unnamed x14 -> x12, local copies, waits for them, and re-layouts: 4.2 us -> 0.03 us
    pallas_call x5 -> x7, Pallas kernels: 17.5 us -> 16.8 us  [the longest x1 9.12 us: estep(): pl.pallas_call(functools.partial(estep_kernel, blocks, share, near), in_s...]
    ppermute x2 -> x3, waiting for transfers between devices: 2.53 us -> 3.07 us  [the longest x2 3.07 us: shards(): tables = [held, lax.ppermute(held, 'slab', pairs)]]
    ppermute x2 -> x3, starting transfers between devices: 5.49 us -> 5.85 us  [the longest x2 4.21 us: shards(): tables = [held, lax.ppermute(held, 'slab', pairs)]]
  transfers between devices with their start and end apart: 11 -> 16, of which waited for: 7 -> 9; matrix products, arithmetic and copies ran while one was open for 0% -> 1% of each run, Pallas kernels for 10% -> 27%
where the time goes in v6:
time: 57.8 us; the launch traced here: 57.6 us
  starting transfers between devices  19.7 us (34%)
  Pallas kernels  19.5 us (34%)
  waiting for transfers between devices  18 us (31%)
    ppermute x13, waiting for transfers between devices, swap(): return lax.ppermute(array, 'img', [(one, one ^ bit) for one in range(size)])  14.9 us
    ppermute x13, starting transfers between devices, swap(): return lax.ppermute(array, 'img', [(one, one ^ bit) for one in range(size)])  13.8 us
    pallas_call x1, Pallas kernels, estep(): pl.pallas_call(functools.partial(estep_kernel, blocks, share, near), in_s...  9.12 us
    pallas_call x3, Pallas kernels, partial_sums(): pl.pallas_call(functools.partial(sums_kernel, items), in_specs=[vmem] * 4...  4.49 us
    ppermute x2, starting transfers between devices, shards(): tables = [held, lax.ppermute(held, 'slab', pairs)]  4.21 us
    ppermute x2, waiting for transfers between devices, shards(): tables = [held, lax.ppermute(held, 'slab', pairs)]  3.07 us
    ppermute x1, starting transfers between devices, shards(): lax.ppermute(met[own_planes:] + sib_met[own_planes:], 'slab', [(one, one...  1.64 us
    pallas_call x1, Pallas kernels, meet(): pl.pallas_call(functools.partial(meet_kernel, len(weights)), out_shape=[j...  1.61 us
  transfers between devices with their start and end apart: 16, of which 9 were waited for; matrix products, arithmetic and copies ran while one was open for 1% of the time, Pallas kernels for 27%

profile of v6, /device:TPU:0, one launch (start us, length us, event | category | flops | bytes accessed | tf_op | source)
XLA Modules:
  0.0 57.6 jit_solution(11896909288650509821)
XLA Ops:
  0.0 1.2 %early.1 = f32[2,64,768]{2,1,0:T(8,128)S(1)} custom-call(s32[1]{0:T(128)} %bitcast.me_ref, s32[1]{0:T(128)} %bitcast.1.slab_ref, s32[1,32768]{1,0:T(1,128)} %constant.14.clone.index_hbm, bf16[64,32768]{1,0:T(8,128)(2,1)} %image_hbm.2, f32[64,64]{1,0:T(8,128)} %own_ctf_ref.5), custom_call_target="tpu_custom_call" | custom-call | tf_op jit(solution)/shard_map/early/pallas_call | solution.py:271
  1.2 4.0 %collective-permute-start.3 = (f32[2,64,768]{2,1,0:T(8,128)S(1)}, f32[2,64,768]{2,1,0:T(8,128)S(1)}, u32[]{:S(2)}, u32[]{:S(2)}) collective-permute-start(f32[2,64,768]{2,1,0:T(8,128)S(1)} %early.1), channel_id=1, source_target_pairs={{0,24},{4,28},{8,16},{12,20},{16,8},{20,12},{24,0},{28,4},{1,25},{... | collective-permute-start | bytes 1179656 | tf_op jit(solution)/shard_map/ppermute | solution.py:524
  5.2 9.1 %estep.1 = (f32[64,10368]{1,0:T(8,128)}, bf16[64,10240]{1,0:T(8,128)(2,1)}, f32[64,64]{1,0:T(8,128)S(1)}, bf16[2,64,768]{2,1,0:T(8,128)(2,1)}, f32[2,64,768]{2,1,0:T(8,128)}, /*index=5*/f32[2,64,768]{2,1,0:T(8,128)S(1)}) custom-call(s32[1]{0:T(128)} %bitcast.me_ref, s32[1]{0:T(128)} %bitcast.1.slab_ref, s32[1,16640]{1,0:T(1,128)} %constant.13.clone.index_hbm, ...), custom_call_target="tpu_custom_call" | custom-call | tf_op jit(solution)/shard_map/estep/pallas_call | solution.py:198
  14.4 1.6 %collective-permute-start.4 = (f32[2,64,768]{2,1,0:T(8,128)}, f32[2,64,768]{2,1,0:T(8,128)}, u32[]{:S(2)}, u32[]{:S(2)}) collective-permute-start(f32[2,64,768]{2,1,0:T(8,128)} %get-tuple-element.51), channel_id=1, source_target_pairs={{0,8},{4,12},{8,0},{12,4},{16,24},{20,28},{24,16},{28,20},{1,9},{5... | collective-permute-start | bytes 1179656 | tf_op jit(solution)/shard_map/ppermute | solution.py:524
  16.0 1.5 %collective-permute-start.5 = (f32[2,64,768]{2,1,0:T(8,128)S(1)}, f32[2,64,768]{2,1,0:T(8,128)}, u32[]{:S(2)}, u32[]{:S(2)}) collective-permute-start(f32[2,64,768]{2,1,0:T(8,128)S(1)} %get-tuple-element.52), channel_id=1, source_target_pairs={{0,16},{4,20},{8,24},{12,28},{16,0},{20,4},{24,8},{28,12},{1,17},{... | collective-permute-start | bytes 1179656 | tf_op jit(solution)/shard_map/ppermute | solution.py:524
  17.5 1.6 %collective-permute-start = (f32[64,64]{1,0:T(8,128)S(1)}, f32[64,64]{1,0:T(8,128)S(1)}, u32[]{:S(2)}, u32[]{:S(2)}) collective-permute-start(f32[64,64]{1,0:T(8,128)S(1)} %get-tuple-element.40), channel_id=1, source_target_pairs={{0,1},{1,0},{2,3},{3,2},{4,5},{5,4},{6,7},{7,6},{8,9},{9,8},{10,11... | collective-permute-start | bytes 49160 | tf_op jit(solution)/shard_map/ppermute | solution.py:570
  19.1 2.3 %collective-permute-done = f32[64,64]{1,0:T(8,128)S(1)} collective-permute-done((f32[64,64]{1,0:T(8,128)S(1)}, f32[64,64]{1,0:T(8,128)S(1)}, u32[]{:S(2)}, u32[]{:S(2)}) %collective-permute-start) | collective-permute-done | bytes 16416 | tf_op jit(solution)/shard_map/ppermute | solution.py:570
  21.5 2.6 %collective-permute-start.1 = (f32[64,128]{1,0:T(8,128)S(1)}, f32[64,128]{1,0:T(8,128)S(1)}, u32[]{:S(2)}, u32[]{:S(2)}) collective-permute-start(f32[64,128]{1,0:T(8,128)S(1)} %pad_maximum_fusion.refs_0_), channel_id=1, source_target_pairs={{0,2},{1,3},{2,0},{3,1},{4,6},{5,7},{6,4},{7,5},{8,10},{9,11},{10,... | collective-permute-start | bytes 98312 | tf_op jit(solution)/shard_map/ppermute | solution.py:570
  24.3 1.4 %count.1 = (f32[2,64,128]{2,1,0:T(8,128)S(1)}, f32[64,128]{1,0:T(8,128)S(1)}) custom-call(s32[1]{0:T(128)} %bitcast.1.slab_ref, f32[1,2]{1,0:T(1,128)S(1)} %bitcast.6, f32[1,64]{1,0:T(1,128)S(1)} %bitcast.7, s32[64,128]{1,0:T(8,128)S(1)} %reshape.25.list_ref), custom_call_target="tpu_custom_call" | custom-call | tf_op jit(solution)/shard_map/count/pallas_call | solution.py:314
  25.6 0.7 %collective-permute-done.1.refs_1_ = f32[64,128]{1,0:T(8,128)S(1)} collective-permute-done((f32[64,128]{1,0:T(8,128)S(1)}, f32[64,128]{1,0:T(8,128)S(1)}, u32[]{:S(2)}, u32[]{:S(2)}) %collective-permute-start.1) | collective-permute-done | bytes 32800 | tf_op jit(solution)/shard_map/ppermute | solution.py:570
  28.0 1.4 %sums.3 = (f32[1,64,1536]{2,1,0:T(8,128)S(1)}, f32[1,64,1408]{2,1,0:T(8,128)S(1)}) custom-call(f32[64,64]{1,0:T(8,128)S(1)} %get-tuple-element.42.own_w_ref, f32[64,64]{1,0:T(8,128)S(1)} %collective-permute-done.2.sib_w_ref, f32[64,128]{1,0:T(8,128)S(1)} %get-tuple-element.58.both_w_ref.refs_0_, f32[64,64]{1,0:T(8,128)S(1)} %copy-done, ...), custom_call_target="tpu_custom_call" | custom-call | tf_op jit(solution)/shard_map/sums/pallas_call | solution.py:409
  29.4 0.9 %collective-permute-start.8 = (f32[1,64,1408]{2,1,0:T(8,128)S(1)}, f32[1,64,1408]{2,1,0:T(8,128)S(1)}, u32[]{:S(2)}, u32[]{:S(2)}) collective-permute-start(f32[1,64,1408]{2,1,0:T(8,128)S(1)} %get-tuple-element.57), channel_id=1, source_target_pairs={{0,16},{4,20},{8,24},{12,28},{16,0},{20,4},{24,8},{28,12},{1,17},{... | collective-permute-start | bytes 1081352 | tf_op jit(solution)/shard_map/ppermute | solution.py:524
  30.9 2.1 %collective-permute-start.9 = (f32[64,128]{1,0:T(8,128)S(1)}, f32[64,128]{1,0:T(8,128)S(1)}, u32[]{:S(2)}, u32[]{:S(2)}) collective-permute-start(f32[64,128]{1,0:T(8,128)S(1)} %get-tuple-element.58.both_w_ref.refs_0_), channel_id=1, source_target_pairs={{0,24},{4,28},{8,16},{12,20},{16,8},{20,12},{24,0},{28,4},{1,25},{... | collective-permute-start | bytes 98312 | tf_op jit(solution)/shard_map/ppermute | solution.py:524
  33.0 1.4 %sums.4 = (f32[1,64,1408]{2,1,0:T(8,128)S(1)}, f32[1,64,1280]{2,1,0:T(8,128)S(1)}) custom-call(f32[64,64]{1,0:T(8,128)S(1)} %get-tuple-element.42.own_w_ref, f32[64,64]{1,0:T(8,128)S(1)} %collective-permute-done.2.sib_w_ref, f32[64,128]{1,0:T(8,128)S(1)} %get-tuple-element.58.both_w_ref.refs_0_, f32[64,64]{1,0:T(8,128)S(1)} %copy-done, ...), custom_call_target="tpu_custom_call" | custom-call | tf_op jit(solution)/shard_map/sums/pallas_call | solution.py:409
  34.9 0.9 %collective-permute-start.14 = (f32[1,64,1280]{2,1,0:T(8,128)S(1)}, f32[1,64,1280]{2,1,0:T(8,128)S(1)}, u32[]{:S(2)}, u32[]{:S(2)}) collective-permute-start(f32[1,64,1280]{2,1,0:T(8,128)S(1)} %get-tuple-element.67), channel_id=1, source_target_pairs={{0,16},{4,20},{8,24},{12,28},{16,0},{20,4},{24,8},{28,12},{1,17},{... | collective-permute-start | bytes 983048 | tf_op jit(solution)/shard_map/ppermute | solution.py:524
  35.8 1.8 %sums.5 = (f32[2,64,1408]{2,1,0:T(8,128)S(1)}, f32[2,64,1280]{2,1,0:T(8,128)S(1)}) custom-call(f32[64,64]{1,0:T(8,128)S(1)} %get-tuple-element.42.own_w_ref, f32[64,64]{1,0:T(8,128)S(1)} %collective-permute-done.2.sib_w_ref, f32[64,128]{1,0:T(8,128)S(1)} %get-tuple-element.58.both_w_ref.refs_0_, f32[64,64]{1,0:T(8,128)S(1)} %copy-done, ...), custom_call_target="tpu_custom_call" | custom-call | tf_op jit(solution)/shard_map/sums/pallas_call | solution.py:409
  37.6 3.1 %collective-permute-done.8.refs_2_ = f32[1,64,1408]{2,1,0:T(8,128)S(1)} collective-permute-done((f32[1,64,1408]{2,1,0:T(8,128)S(1)}, f32[1,64,1408]{2,1,0:T(8,128)S(1)}, u32[]{:S(2)}, u32[]{:S(2)}) %collective-permute-start.8) | collective-permute-done | bytes 360480 | tf_op jit(solution)/shard_map/ppermute | solution.py:524
  41.4 2.3 %collective-permute-done.9.refs_3_ = f32[64,128]{1,0:T(8,128)S(1)} collective-permute-done((f32[64,128]{1,0:T(8,128)S(1)}, f32[64,128]{1,0:T(8,128)S(1)}, u32[]{:S(2)}, u32[]{:S(2)}) %collective-permute-start.9) | collective-permute-done | bytes 32800 | tf_op jit(solution)/shard_map/ppermute | solution.py:524
  43.6 1.6 %meet.1 = (f32[128,768]{1,0:T(8,128)S(1)}, f32[128,768]{1,0:T(8,128)S(1)}) custom-call(f32[64,128]{1,0:T(8,128)S(1)} %get-tuple-element.58.both_w_ref.refs_0_, f32[1,64,1536]{2,1,0:T(8,128)S(1)} %collective-permute-done.7.refs_1_, f32[1,64,1408]{2,1,0:T(8,128)S(1)} %collective-permute-done.8.refs_2_, f32[64,128]{1,0:T(8,128)S(1)} %collective-permute-done.9.refs_3_, ...), custom_call_target="tpu_custom_call" | custom-call | tf_op jit(solution)/shard_map/meet/pallas_call | solution.py:448
  45.4 1.0 %collective-permute-start.13 = (f32[1,64,1408]{2,1,0:T(8,128)S(1)}, f32[1,64,1408]{2,1,0:T(8,128)S(1)}, u32[]{:S(2)}, u32[]{:S(2)}) collective-permute-start(f32[1,64,1408]{2,1,0:T(8,128)S(1)} %slice_add_fusion), channel_id=1, source_target_pairs={{0,16},{4,20},{8,24},{12,28},{16,0},{20,4},{24,8},{28,12},{1,17},{... | collective-permute-start | bytes 1081352 | tf_op jit(solution)/shard_map/ppermute | solution.py:524
  47.1 1.6 %collective-permute-start.11 = (f32[64,768]{1,0:T(8,128)S(1)}, f32[64,768]{1,0:T(8,128)S(1)}, u32[]{:S(2)}, u32[]{:S(2)}) collective-permute-start(f32[64,768]{1,0:T(8,128)S(1)} %slice_add_fusion.2), channel_id=1, source_target_pairs={{0,1},{1,0},{2,3},{3,2},{4,5},{5,4},{6,7},{7,6},{8,9},{9,8},{10,11... | collective-permute-start | bytes 589832 | tf_op jit(solution)/shard_map/ppermute | solution.py:618
  48.7 2.1 %collective-permute-done.12.refs_0_ = f32[1,64,1408]{2,1,0:T(8,128)S(1)} collective-permute-done((f32[1,64,1408]{2,1,0:T(8,128)S(1)}, f32[1,64,1408]{2,1,0:T(8,128)S(1)}, u32[]{:S(2)}, u32[]{:S(2)}) %collective-permute-start.12) | collective-permute-done | bytes 360480 | tf_op jit(solution)/shard_map/ppermute | solution.py:524
  50.8 5.5 %collective-permute-done.15.refs_5_ = f32[1,64,1280]{2,1,0:T(8,128)S(1)} collective-permute-done((f32[1,64,1280]{2,1,0:T(8,128)S(1)}, f32[1,64,1280]{2,1,0:T(8,128)S(1)}, u32[]{:S(2)}, u32[]{:S(2)}) %collective-permute-start.15) | collective-permute-done | bytes 327712 | tf_op jit(solution)/shard_map/ppermute | solution.py:524
  56.3 1.2 %finish.1 = f32[64,4096]{1,0:T(8,128)} custom-call(s32[1]{0:T(128)} %bitcast.me_ref, s32[1]{0:T(128)} %bitcast.1.slab_ref, s32[1,32768]{1,0:T(1,128)S(1)} %copy-done.1, f32[128,768]{1,0:T(8,128)S(1)} %get-tuple-element.63.met_ref, f32[128,768]{1,0:T(8,128)S(1)} %collective-permute-done.10.sib_met_ref, f32[64,768]{1,0:T(8,128)S(1)} %collective-permute-done.11.partner_ref, ...), custom_call_target="tpu_custom_call" | custom-call | tf_op jit(solution)/shard_map/finish/pallas_call | solution.py:504
  (34 shorter events, 4.5 us)
Async XLA Ops:
  1.2 13.1 %collective-permute-start.3 = (f32[2,64,768]{2,1,0:T(8,128)S(1)}, f32[2,64,768]{2,1,0:T(8,128)S(1)}, u32[]{:S(2)}, u32[]{:S(2)}) collective-permute-start(f32[2,64,768]{2,1,0:T(8,128)S(1)} %early.1), channel_id=1, source_target_pairs={{0,24},{4,28},{8,16},{12,20},{16,8},{20,12},{24,0},{28,4},{1,25},{... | collective-permute-start | bytes 1179656 | tf_op jit(solution)/shard_map/ppermute | solution.py:524
  5.2 19.0 %copy-start.5 = (s32[64,2,64]{2,1,0:T(2,128)S(1)}, s32[64,2,64]{2,1,0:T(2,128)}, u32[]{:S(2)}) copy-start(s32[64,2,64]{2,1,0:T(2,128)} %param.10) | copy-start | bytes 98308
  5.2 19.1 %copy-start.2 = (f32[2]{0:T(128)S(1)}, f32[2]{0:T(128)}, u32[]{:S(2)}) copy-start(f32[2]{0:T(128)} %param.13) | copy-start | bytes 28
  5.2 19.1 %copy-start.3 = (f32[64]{0:T(128)S(1)}, f32[64]{0:T(128)}, u32[]{:S(2)}) copy-start(f32[64]{0:T(128)} %param.12) | copy-start | bytes 772
  5.2 22.8 %copy-start = (f32[64,64]{1,0:T(8,128)S(1)}, f32[64,64]{1,0:T(8,128)}, u32[]{:S(2)}) copy-start(f32[64,64]{1,0:T(8,128)} %own_ctf_ref.5) | copy-start | bytes 49156
  14.4 7.2 %copy-start.4 = (f32[2,64,768]{2,1,0:T(8,128)}, f32[2,64,768]{2,1,0:T(8,128)S(1)}, u32[]{:S(2)}) copy-start(f32[2,64,768]{2,1,0:T(8,128)S(1)} %collective-permute-done.3.refs_7_) | copy-start | bytes 1179652
  14.4 13.7 %collective-permute-start.6 = (f32[64,10368]{1,0:T(8,128)}, f32[64,10368]{1,0:T(8,128)S(1)}, u32[]{:S(2)}, u32[]{:S(2)}) collective-permute-start(f32[64,10368]{1,0:T(8,128)} %get-tuple-element.55), channel_id=1, source_target_pairs={{0,4},{4,0},{8,12},{12,8},{16,20},{20,16},{24,28},{28,24},{1,5},{5... | collective-permute-start | bytes 7962632 | tf_op jit(solution)/shard_map/ppermute | solution.py:524
  14.4 12.4 %collective-permute-start.4 = (f32[2,64,768]{2,1,0:T(8,128)}, f32[2,64,768]{2,1,0:T(8,128)}, u32[]{:S(2)}, u32[]{:S(2)}) collective-permute-start(f32[2,64,768]{2,1,0:T(8,128)} %get-tuple-element.51), channel_id=1, source_target_pairs={{0,8},{4,12},{8,0},{12,4},{16,24},{20,28},{24,16},{28,20},{1,9},{5... | collective-permute-start | bytes 1179656 | tf_op jit(solution)/shard_map/ppermute | solution.py:524
  16.0 11.4 %collective-permute-start.5 = (f32[2,64,768]{2,1,0:T(8,128)S(1)}, f32[2,64,768]{2,1,0:T(8,128)}, u32[]{:S(2)}, u32[]{:S(2)}) collective-permute-start(f32[2,64,768]{2,1,0:T(8,128)S(1)} %get-tuple-element.52), channel_id=1, source_target_pairs={{0,16},{4,20},{8,24},{12,28},{16,0},{20,4},{24,8},{28,12},{1,17},{... | collective-permute-start | bytes 1179656 | tf_op jit(solution)/shard_map/ppermute | solution.py:524
  17.5 3.9 %collective-permute-start = (f32[64,64]{1,0:T(8,128)S(1)}, f32[64,64]{1,0:T(8,128)S(1)}, u32[]{:S(2)}, u32[]{:S(2)}) collective-permute-start(f32[64,64]{1,0:T(8,128)S(1)} %get-tuple-element.40), channel_id=1, source_target_pairs={{0,1},{1,0},{2,3},{3,2},{4,5},{5,4},{6,7},{7,6},{8,9},{9,8},{10,11... | collective-permute-start | bytes 49160 | tf_op jit(solution)/shard_map/ppermute | solution.py:570
  21.5 4.9 %collective-permute-start.1 = (f32[64,128]{1,0:T(8,128)S(1)}, f32[64,128]{1,0:T(8,128)S(1)}, u32[]{:S(2)}, u32[]{:S(2)}) collective-permute-start(f32[64,128]{1,0:T(8,128)S(1)} %pad_maximum_fusion.refs_0_), channel_id=1, source_target_pairs={{0,2},{1,3},{2,0},{3,1},{4,6},{5,7},{6,4},{7,5},{8,10},{9,11},{10,... | collective-permute-start | bytes 98312 | tf_op jit(solution)/shard_map/ppermute | solution.py:570
  26.8 1.3 %collective-permute-start.2 = (f32[64,64]{1,0:T(8,128)S(1)}, f32[64,64]{1,0:T(8,128)S(1)}, u32[]{:S(2)}, u32[]{:S(2)}) collective-permute-start(f32[64,64]{1,0:T(8,128)S(1)} %get-tuple-element.42.own_w_ref), channel_id=1, source_target_pairs={{0,4},{4,0},{8,12},{12,8},{16,20},{20,16},{24,28},{28,24},{1,5},{5... | collective-permute-start | bytes 49160 | tf_op jit(solution)/shard_map/ppermute | solution.py:524
  29.4 11.3 %collective-permute-start.8 = (f32[1,64,1408]{2,1,0:T(8,128)S(1)}, f32[1,64,1408]{2,1,0:T(8,128)S(1)}, u32[]{:S(2)}, u32[]{:S(2)}) collective-permute-start(f32[1,64,1408]{2,1,0:T(8,128)S(1)} %get-tuple-element.57), channel_id=1, source_target_pairs={{0,16},{4,20},{8,24},{12,28},{16,0},{20,4},{24,8},{28,12},{1,17},{... | collective-permute-start | bytes 1081352 | tf_op jit(solution)/shard_map/ppermute | solution.py:524
  30.3 13.3 %collective-permute-start.7 = (f32[1,64,1536]{2,1,0:T(8,128)S(1)}, f32[1,64,1536]{2,1,0:T(8,128)S(1)}, u32[]{:S(2)}, u32[]{:S(2)}) collective-permute-start(f32[1,64,1536]{2,1,0:T(8,128)S(1)} %get-tuple-element.56), channel_id=1, source_target_pairs={{0,8},{4,12},{8,0},{12,4},{16,24},{20,28},{24,16},{28,20},{1,9},{5... | collective-permute-start | bytes 1179656 | tf_op jit(solution)/shard_map/ppermute | solution.py:524
  30.9 12.8 %collective-permute-start.9 = (f32[64,128]{1,0:T(8,128)S(1)}, f32[64,128]{1,0:T(8,128)S(1)}, u32[]{:S(2)}, u32[]{:S(2)}) collective-permute-start(f32[64,128]{1,0:T(8,128)S(1)} %get-tuple-element.58.both_w_ref.refs_0_), channel_id=1, source_target_pairs={{0,24},{4,28},{8,16},{12,20},{16,8},{20,12},{24,0},{28,4},{1,25},{... | collective-permute-start | bytes 98312 | tf_op jit(solution)/shard_map/ppermute | solution.py:524
  34.3 16.5 %collective-permute-start.12 = (f32[1,64,1408]{2,1,0:T(8,128)S(1)}, f32[1,64,1408]{2,1,0:T(8,128)S(1)}, u32[]{:S(2)}, u32[]{:S(2)}) collective-permute-start(f32[1,64,1408]{2,1,0:T(8,128)S(1)} %get-tuple-element.65), channel_id=1, source_target_pairs={{0,8},{4,12},{8,0},{12,4},{16,24},{20,28},{24,16},{28,20},{1,9},{5... | collective-permute-start | bytes 1081352 | tf_op jit(solution)/shard_map/ppermute | solution.py:524
  34.9 13.8 %collective-permute-start.14 = (f32[1,64,1280]{2,1,0:T(8,128)S(1)}, f32[1,64,1280]{2,1,0:T(8,128)S(1)}, u32[]{:S(2)}, u32[]{:S(2)}) collective-permute-start(f32[1,64,1280]{2,1,0:T(8,128)S(1)} %get-tuple-element.67), channel_id=1, source_target_pairs={{0,16},{4,20},{8,24},{12,28},{16,0},{20,4},{24,8},{28,12},{1,17},{... | collective-permute-start | bytes 983048 | tf_op jit(solution)/shard_map/ppermute | solution.py:524
  37.6 18.8 %copy-start.1 = (s32[1,32768]{1,0:T(1,128)S(1)}, s32[1,32768]{1,0:T(1,128)}, u32[]{:S(2)}) copy-start(s32[1,32768]{1,0:T(1,128)} %constant.14.clone.index_hbm) | copy-start | bytes 393220
  40.8 15.6 %collective-permute-start.15 = (f32[1,64,1280]{2,1,0:T(8,128)S(1)}, f32[1,64,1280]{2,1,0:T(8,128)S(1)}, u32[]{:S(2)}, u32[]{:S(2)}) collective-permute-start(f32[1,64,1280]{2,1,0:T(8,128)S(1)} %slice_add_fusion.1), channel_id=1, source_target_pairs={{0,8},{4,12},{8,0},{12,4},{16,24},{20,28},{24,16},{28,20},{1,9},{5... | collective-permute-start | bytes 983048 | tf_op jit(solution)/shard_map/ppermute | solution.py:524
  45.3 1.8 %collective-permute-start.10 = (f32[128,768]{1,0:T(8,128)S(1)}, f32[128,768]{1,0:T(8,128)S(1)}, u32[]{:S(2)}, u32[]{:S(2)}) collective-permute-start(f32[128,768]{1,0:T(8,128)S(1)} %get-tuple-element.64), channel_id=1, source_target_pairs={{0,4},{4,0},{8,12},{12,8},{16,20},{20,16},{24,28},{28,24},{1,5},{5... | collective-permute-start | bytes 1179656 | tf_op jit(solution)/shard_map/ppermute | solution.py:524
  45.4 10.9 %collective-permute-start.13 = (f32[1,64,1408]{2,1,0:T(8,128)S(1)}, f32[1,64,1408]{2,1,0:T(8,128)S(1)}, u32[]{:S(2)}, u32[]{:S(2)}) collective-permute-start(f32[1,64,1408]{2,1,0:T(8,128)S(1)} %slice_add_fusion), channel_id=1, source_target_pairs={{0,16},{4,20},{8,24},{12,28},{16,0},{20,4},{24,8},{28,12},{1,17},{... | collective-permute-start | bytes 1081352 | tf_op jit(solution)/shard_map/ppermute | solution.py:524
  47.1 9.3 %collective-permute-start.11 = (f32[64,768]{1,0:T(8,128)S(1)}, f32[64,768]{1,0:T(8,128)S(1)}, u32[]{:S(2)}, u32[]{:S(2)}) collective-permute-start(f32[64,768]{1,0:T(8,128)S(1)} %slice_add_fusion.2), channel_id=1, source_target_pairs={{0,1},{1,0},{2,3},{3,2},{4,5},{5,4},{6,7},{7,6},{8,9},{9,8},{10,11... | collective-permute-start | bytes 589832 | tf_op jit(solution)/shard_map/ppermute | solution.py:618

commit v7 on v6

--- a/solution.py
+++ b/solution.py
@@ -28,7 +28,7 @@
 
 
 def split_share(share):
-    met = max(LANES, 3 * share // 16 // LANES * LANES)
+    met = max(LANES, 6 * share // 32 // LANES * LANES)
     return share // 2 - met, met
 
 
@@ -64,7 +64,8 @@
     index, image, plane, ctf_held, weighted, give, squared, energy_of = refs[-11:-3]
     small_sem, in_sem, out_sem = refs[-3:]
     rows, width = image.shape
-    chips, summed = width // share // 2, 2 * split_share(share)[0]
+    wide, met = split_share(share)
+    chips, summed = width // share // 2, 2 * wide
     box = math.isqrt(width // 2)
     line = 2 * box
     deep = box // (2 * blocks)
@@ -149,10 +150,6 @@
             outgoing[-2].start()
             outgoing[-1].start()
 
-    tail = slice(chips * summed, chips * summed + LANES)
-    give[:, tail] = table
-    outgoing.append(pltpu.make_async_copy(give.at[:, tail], give_hbm.at[:, tail], out_sem.at[chips, 0]))
-    outgoing[-1].start()
     handed, done = set(), set()
     total = jnp.zeros(score_ref.shape, F32)
     for block in range(blocks):
@@ -174,8 +171,10 @@
     for k, near_ref in zip(near, near_refs):
         for other in range(2):
             owner = (k ^ chip) * 2 + lax.rem(core + other, 2)
-            part = weighted[:, pl.ds(met_column(share, owner, slab_ref[0]), near_ref.shape[2])]
-            near_ref[other] = part.astype(near_ref.dtype)
+            part = weighted[:, pl.ds(met_column(share, owner, slab_ref[0]), met)]
+            near_ref[:, other * met : (other + 1) * met] = part.astype(near_ref.dtype)
+        if k:
+            near_ref[:, 2 * met :] = table
     for copy in outgoing:
         copy.wait()
 
@@ -200,12 +199,14 @@
         in_specs=[pl.BlockSpec(memory_space=pltpu.SMEM)] * 2 + [hbm] * 4,
         out_specs=[held, held] + [vmem] * (1 + len(near)),
         out_shape=[
-            jax.ShapeDtypeStruct((rows, chips * summed + LANES), F32),
+            jax.ShapeDtypeStruct((rows, chips * summed), F32),
             pltpu.HBM((rows, chips * summed), BF16),
             jax.ShapeDtypeStruct((rows, count), F32),
         ]
         + [
-            jax.ShapeDtypeStruct((2, rows, met), F32) if k else pltpu.HBM((2, rows, met), BF16)
+            jax.ShapeDtypeStruct((rows, 2 * met + LANES), F32)
+            if k
+            else pltpu.HBM((rows, 2 * met), BF16)
             for k in near
         ],
         scratch_shapes=[
@@ -214,12 +215,12 @@
             pltpu.VMEM((count, width), BF16),
             pltpu.VMEM(ctf_table.shape, F32),
             pltpu.VMEM((rows, width), BF16),
-            pltpu.VMEM((rows, chips * summed + LANES), F32),
+            pltpu.VMEM((rows, chips * summed), F32),
             pltpu.VMEM((3, rows, span), BF16),
             pltpu.VMEM((3, count, span), BF16),
             pltpu.SemaphoreType.DMA((2,)),
             pltpu.SemaphoreType.DMA((blocks, 2, 2)),
-            pltpu.SemaphoreType.DMA((chips + 1, 2)),
+            pltpu.SemaphoreType.DMA((chips, 2)),
         ],
         compiler_params=params(28),
         name="estep",
@@ -229,7 +230,7 @@
 def early_kernel(share, beyond, me_ref, slab_ref, index_hbm, image_hbm, ctf_hbm, *refs):
     outs = refs[: len(beyond)]
     index, image, ctf_held, index_sem, image_sem, ctf_sem = refs[len(beyond) :]
-    _, rows, met = outs[0].shape
+    met = split_share(share)[1]
     chip, core = me_ref[0] // 2, lax.rem(me_ref[0], 2)
     fetch = pltpu.make_async_copy(ctf_hbm, ctf_held, ctf_sem)
     fetch.start()
@@ -258,7 +259,8 @@
                 cut = slice(start, start + LANES)
                 ctf = spread(table, index[place, other, :, cut])
                 part = (image[place, other, :, cut].astype(F32) * ctf).astype(BF16)
-                out_ref[other, :, cut] = part.astype(F32)
+                out_ref[:, other * met + start : other * met + start + LANES] = part.astype(F32)
+        out_ref[:, 2 * met :] = table
 
 
 def early_images(me, slab, index, images, ctf_table, share, beyond):
@@ -272,7 +274,7 @@
         functools.partial(early_kernel, share, beyond),
         in_specs=[smem, smem, hbm, hbm, hbm],
         out_specs=[vmem] * number,
-        out_shape=[jax.ShapeDtypeStruct((2, rows, met), F32)] * number,
+        out_shape=[jax.ShapeDtypeStruct((rows, 2 * met + LANES), F32)] * number,
         scratch_shapes=[
             pltpu.VMEM((number, 2, 1, met), jnp.int32),
             pltpu.VMEM((number, 2, rows, met), BF16),
@@ -366,13 +368,76 @@
     )(base, scale, *tables)
 
 
-def sums_kernel(items, own_w_ref, sib_w_ref, both_w_ref, own_ctf_ref, keep_hbm, got_hbm, *refs):
+def gather_kernel(items, keep_hbm, got_hbm, out_ref, got, in_sem):
+    number, rows2, wide = out_ref.shape
+    rows = rows2 // 2
+    incoming = []
+    for place, (side, k) in enumerate(items):
+        cut = slice((2 * k + side) * wide, (2 * k + side + 1) * wide)
+        incoming.append([
+            pltpu.make_async_copy(keep_hbm.at[:, cut], out_ref.at[place, :rows], in_sem.at[place, 0]),
+            pltpu.make_async_copy(got_hbm.at[:, cut], got.at[place], in_sem.at[place, 1]),
+        ])
+        for copy in incoming[-1]:
+            copy.start()
+    for place in range(number):
+        for copy in incoming[place]:
+            copy.wait()
+        out_ref[place, rows:] = got[place].astype(BF16)
+
+
+def gather_images(items, keep, got, wide):
+    rows = keep.shape[0]
+    number = len(items)
+    held = pl.BlockSpec(memory_space=pl.ANY)
+    return pl.pallas_call(
+        functools.partial(gather_kernel, items),
+        in_specs=[held] * 2,
+        out_specs=pl.BlockSpec(memory_space=pltpu.VMEM),
+        out_shape=jax.ShapeDtypeStruct((number, 2 * rows, wide), BF16),
+        scratch_shapes=[
+            pltpu.VMEM((number, rows, wide), F32),
+            pltpu.SemaphoreType.DMA((number, 2)),
+        ],
+        compiler_params=params(8),
+        name="gather",
+    )(keep, got)
+
+
+def first_sums_kernel(items, own_w_ref, sib_w_ref, both_w_ref, image_ref, *outs):
+    wide = image_ref.shape[2]
+    weights = jnp.concatenate([own_w_ref[...], sib_w_ref[...]], axis=1).astype(BF16)
+    slots = [0] * len(outs)
+    for place, (side, _) in enumerate(items):
+        out_ref, slot = outs[side], slots[side]
+        slots[side] += 1
+        out_ref[slot, :, :wide] = jnp.dot(weights, image_ref[place], preferred_element_type=F32)
+        out_ref[slot, :, wide:] = both_w_ref[...]
+
+
+def first_sums(items, own_w, sib_w, both_w, images):
+    planes = own_w.shape[0]
+    wide = images.shape[2]
+    vmem = pl.BlockSpec(memory_space=pltpu.VMEM)
+    return pl.pallas_call(
+        functools.partial(first_sums_kernel, items),
+        in_specs=[vmem] * 4,
+        out_specs=[vmem] * 2,
+        out_shape=[
+            jax.ShapeDtypeStruct(
+                (sum(side == one for side, _ in items), planes, wide + both_w.shape[1]), F32
+            )
+            for one in (0, 1)
+        ],
+        compiler_params=params(8),
+        name="first_sums",
+    )(own_w, sib_w, both_w, images)
+
+
+def sums_kernel(items, own_w_ref, sib_w_ref, keep_hbm, got_hbm, *refs):
     outs = refs[: len(items)]
-    keep, got, sib_ctf, in_sem, ctf_sem = refs[len(items) :]
+    keep, got, in_sem = refs[len(items) :]
     number, _, wide = keep.shape
-    tail = slice(keep_hbm.shape[1], keep_hbm.shape[1] + LANES)
-    fetch = pltpu.make_async_copy(got_hbm.at[:, tail], sib_ctf, ctf_sem)
-    fetch.start()
     places = [(slot, k, side) for side, ks in enumerate(items) for slot, k in enumerate(ks)]
     incoming = []
     for place, (slot, k, side) in enumerate(places):
@@ -384,73 +449,70 @@
         for copy in incoming[-1]:
             copy.start()
     weights = jnp.concatenate([own_w_ref[...], sib_w_ref[...]], axis=1).astype(BF16)
-    fetch.wait()
-    ctf = jnp.concatenate([lanes_wide(own_ctf_ref[...]), sib_ctf[...]], axis=0)
-    shell_sums = jnp.dot(weights, (ctf * ctf).astype(BF16), preferred_element_type=F32)
     for place, (slot, k, side) in enumerate(places):
         for copy in incoming[place]:
             copy.wait()
         images = jnp.concatenate([keep[place], got[place].astype(BF16)], axis=0)
-        outs[side][slot, :, :wide] = jnp.dot(weights, images, preferred_element_type=F32)
-        if side == 0:
-            outs[side][slot, :, wide : wide + LANES] = shell_sums
-        behind = wide + (LANES if side == 0 else 0)
-        if outs[side].shape[2] > behind:
-            outs[side][slot, :, behind:] = both_w_ref[...]
-
-
-def partial_sums(items, with_weights, own_w, sib_w, both_w, own_ctf, keep, got, wide):
+        outs[side][slot] = jnp.dot(weights, images, preferred_element_type=F32)
+
+
+def partial_sums(items, own_w, sib_w, keep, got, wide):
     rows = keep.shape[0]
     planes = own_w.shape[0]
     number = sum(len(ks) for ks in items)
     held = pl.BlockSpec(memory_space=pl.ANY)
     vmem = pl.BlockSpec(memory_space=pltpu.VMEM)
-    rider = both_w.shape[1] if with_weights else 0
     return pl.pallas_call(
         functools.partial(sums_kernel, items),
-        in_specs=[vmem] * 4 + [held] * 2,
+        in_specs=[vmem] * 2 + [held] * 2,
         out_specs=[vmem] * 2,
-        out_shape=[
-            jax.ShapeDtypeStruct((len(ks), planes, wide + extra + rider), F32)
-            for ks, extra in zip(items, (LANES, 0))
-        ],
+        out_shape=[jax.ShapeDtypeStruct((len(ks), planes, wide), F32) for ks in items],
         scratch_shapes=[
             pltpu.VMEM((number, rows, wide), BF16),
             pltpu.VMEM((number, rows, wide), F32),
-            pltpu.VMEM((rows, LANES), F32),
             pltpu.SemaphoreType.DMA((number, 2)),
-            pltpu.SemaphoreType.DMA(()),
         ],
         compiler_params=params(12),
         name="sums",
-    )(own_w, sib_w, both_w, own_ctf, keep, got)
-
-
-def meet_kernel(chips, *refs):
+    )(own_w, sib_w, keep, got)
+
+
+def meet_kernel(chips, ctf_ref, *refs):
     weight_refs, image_refs, outs = refs[:chips], refs[chips : 2 * chips], refs[2 * chips :]
-    planes = outs[0].shape[0]
-    weights = []
+    planes, width = outs[0].shape
+    met = width - LANES
+    weights, ctf = [], []
     for ref in weight_refs:
         wide = ref.shape[-1]
         part = ref[:, wide - planes :] if len(ref.shape) == 2 else ref[0, :, wide - planes :]
         weights.append(part.astype(BF16))
     weights = jnp.concatenate(weights, axis=0)
+
+    def sums(parts):
+        return lax.dot_general(
+            weights,
+            jnp.concatenate(parts, axis=0),
+            (((0,), (0,)), ((), ())),
+            preferred_element_type=F32,
+        )
+
+    ctf = [lanes_wide(ctf_ref[...])] + [ref[:, 2 * met :] for ref in image_refs[1:]]
+    shells = sums([(part * part).astype(BF16) for part in ctf])
     for other, out_ref in enumerate(outs):
-        images = jnp.concatenate([ref[other].astype(BF16) for ref in image_refs], axis=0)
-        out_ref[...] = lax.dot_general(
-            weights, images, (((0,), (0,)), ((), ())), preferred_element_type=F32
-        )
-
-
-def meet(weights, images):
-    _, rows, met = images[0].shape
+        cut = slice(other * met, (other + 1) * met)
+        out_ref[:, :met] = sums([ref[:, cut].astype(BF16) for ref in image_refs])
+        out_ref[:, met:] = shells
+
+
+def meet(ctf_table, weights, images):
+    met = images[0].shape[1] // 2
     planes = weights[0].shape[1]
     return pl.pallas_call(
         functools.partial(meet_kernel, len(weights)),
-        out_shape=[jax.ShapeDtypeStruct((planes, met), F32)] * 2,
+        out_shape=[jax.ShapeDtypeStruct((planes, met + LANES), F32)] * 2,
         compiler_params=params(16),
         name="meet",
-    )(*weights, *images)
+    )(ctf_table, *weights, *images)
 
 
 def finish_kernel(numbers, me_ref, slab_ref, index_hbm, met_ref, sib_met_ref, partner_ref, *refs):
@@ -462,7 +524,7 @@
     fetch = pltpu.make_async_copy(index_hbm.at[:, mine], index, in_sem)
     fetch.start()
     left, right = parts[: numbers[0]], parts[numbers[0] :]
-    shells = functools.reduce(jnp.add, [ref[0, :, wide : wide + LANES] for ref in left])
+    shells = met_ref[:planes, met:] + sib_met_ref[:planes, met:]
     half = lax.rem(slab_ref[0], 2)
     fetch.wait()
 
@@ -531,6 +593,7 @@
     slabs = lax.axis_size("slab")
     chips = size // 2
     share = width // size
+    wide, met_wide = split_share(share)
     me = lax.axis_index("img").astype(jnp.int32).reshape(1)
     slab = lax.axis_index("slab").astype(jnp.int32).reshape(1)
     index = entry_shells(width, ctf_table.shape[1])
@@ -554,10 +617,7 @@
         )
     for k, part in zip(near, parts_near):
         met_images[k] = swap(part, 2 * k, size) if k else part
-    keep, *met_images = lax.optimization_barrier(
-        (keep, *[met_images[k] for k in range(chips)])
-    )
-    keep, *met_images = far(keep, *met_images)
+    keep, *met_images = far(keep, *[met_images[k] for k in range(chips)])
     base, scale = count_planes(
         slab, class_weight, inv_noise, orientations, slabs * local_planes, slabs
     )
@@ -574,9 +634,7 @@
     sib_w = swap(own_w, 1, size)
 
     sums = functools.partial(
-        partial_sums,
-        own_w=own_w, sib_w=sib_w, both_w=both_w, own_ctf=ctf_table, keep=keep, got=got,
-        wide=split_share(share)[0],
+        partial_sums, own_w=own_w, sib_w=sib_w, keep=keep, got=got, wide=wide,
     )
     low = [1 << place for place in range(chips.bit_length() - 1)]
     orders = (low, low[::-1])
@@ -592,10 +650,11 @@
             parts[side][k ^ bit].append((arrived, place))
         return arrived
 
-    def compute(groups, with_weights=False):
-        return sums(tuple(tuple(ks) for ks in groups), with_weights)
-
-    sent = compute(onward, True)
+    def compute(groups):
+        return sums(tuple(tuple(ks) for ks in groups))
+
+    items = tuple((side, k) for side, ks in enumerate(onward) for k in ks)
+    sent = first_sums(items, own_w, sib_w, both_w, gather_images(items, keep, got, wide))
     far_w = {0: both_w}
     for side in (0, 1):
         bit = orders[side][0]
@@ -604,6 +663,7 @@
     for k in range(1, chips):
         if k not in far_w:
             far_w[k] = swap(both_w, 2 * k, size)
+    sums.keywords["keep"], *met_images = lax.optimization_barrier((keep, *met_images))
     sent = compute(direct)
     for side in (0, 1):
         deliver(side, direct[side], sent[side], orders[side][0])
@@ -612,20 +672,20 @@
         for place, k in enumerate(stay[side]):
             parts[side][k].append((kept[side], place))
 
-    met, for_sib = meet([far_w[k] for k in range(chips)], met_images)
+    met_images[0], _ = lax.optimization_barrier((met_images[0], sent[0]))
+    met, for_sib = meet(ctf_table, [far_w[k] for k in range(chips)], met_images)
     sib_met = swap(for_sib, 1, size)
     own_planes = classes * local_planes
     partner = lax.ppermute(
-        met[own_planes:] + sib_met[own_planes:], "slab", [(one, one ^ 1) for one in range(slabs)]
+        met[own_planes:, :met_wide] + sib_met[own_planes:, :met_wide], "slab", [(one, one ^ 1) for one in range(slabs)]
     )
 
     for turn in range(1, len(low)):
         for side in (0, 1):
             bit = orders[side][turn]
             ks = [k for k in parts[side] if k & bit]
-            size_out = kept[side].shape[2]
             sent = jnp.stack(
-                [sum(part[place, :, :size_out] for part, place in parts[side].pop(k)) for k in ks]
+                [sum(part[place, :, :wide] for part, place in parts[side].pop(k)) for k in ks]
             )
             deliver(side, ks, sent, bit)
     out = finish(me, slab, index, met, sib_met, partner, parts[0][0], parts[1][0], share)

time: 57.8 us -> 54.3 us (0.939)
  waiting for transfers between devices: 18 us -> 12.9 us
  starting transfers between devices: 19.7 us -> 21.3 us
    ppermute x13, waiting for transfers between devices: 14.9 us -> 12.2 us  [swap(): return lax.ppermute(array, 'img', [(one, one ^ bit) for one in range(size)])]
    ppermute x2, waiting for transfers between devices: 3.07 us -> 0.75 us  [shards(): tables = [held, lax.ppermute(held, 'slab', pairs)]]
    ppermute x13, starting transfers between devices: 13.8 us -> 15.3 us  [swap(): return lax.ppermute(array, 'img', [(one, one ^ bit) for one in range(size)])]
    pallas_call x3 -> x4, Pallas kernels: 4.49 us -> 4.46 us  [the longest x2 3.12 us: partial_sums(): pl.pallas_call(functools.partial(sums_kernel, items), in_specs=[vmem] * 2...]
  transfers between devices with their start and end apart: 16 -> 16, of which waited for: 9 -> 8; matrix products, arithmetic and copies ran while one was open for 1% -> 1% of each run, Pallas kernels for 27% -> 31%
where the time goes in v7:
time: 54.3 us; the launch traced here: 54.1 us
  starting transfers between devices  21.3 us (39%)
  Pallas kernels  19.4 us (36%)
  waiting for transfers between devices  12.9 us (24%)
    ppermute x13, starting transfers between devices, swap(): return lax.ppermute(array, 'img', [(one, one ^ bit) for one in range(size)])  15.3 us
    ppermute x13, waiting for transfers between devices, swap(): return lax.ppermute(array, 'img', [(one, one ^ bit) for one in range(size)])  12.2 us
    pallas_call x1, Pallas kernels, estep(): pl.pallas_call(functools.partial(estep_kernel, blocks, share, near), in_s...  9.09 us
    ppermute x2, starting transfers between devices, shards(): tables = [held, lax.ppermute(held, 'slab', pairs)]  4.41 us
    pallas_call x2, Pallas kernels, partial_sums(): pl.pallas_call(functools.partial(sums_kernel, items), in_specs=[vmem] * 2...  3.12 us
    pallas_call x1, Pallas kernels, meet(): pl.pallas_call(functools.partial(meet_kernel, len(weights)), out_shape=[j...  1.68 us
    ppermute x1, starting transfers between devices, shards(): lax.ppermute(met[own_planes:, :met_wide] + sib_met[own_planes:, :met_wide...  1.64 us
    pallas_call x1, Pallas kernels, count_planes(): pl.pallas_call(functools.partial(count_kernel, slabs), in_specs=[pl.Block...  1.38 us
  transfers between devices with their start and end apart: 16, of which 8 were waited for; matrix products, arithmetic and copies ran while one was open for 1% of the time, Pallas kernels for 31%

profile of v7, /device:TPU:0, one launch (start us, length us, event | category | flops | bytes accessed | tf_op | source)
XLA Modules:
  0.0 54.1 jit_solution(15164709163669431764)
XLA Ops:
  0.0 1.2 %early.1 = f32[64,1664]{1,0:T(8,128)S(1)} custom-call(s32[1]{0:T(128)} %bitcast.me_ref, s32[1]{0:T(128)} %bitcast.1.slab_ref, s32[1,32768]{1,0:T(1,128)} %constant.14.clone.index_hbm, bf16[64,32768]{1,0:T(8,128)(2,1)} %image_hbm.2, f32[64,64]{1,0:T(8,128)} %ctf_ref.1), custom_call_target="tpu_custom_call" | custom-call | tf_op jit(solution)/shard_map/early/pallas_call | solution.py:273
  1.2 4.0 %collective-permute-start.3 = (f32[64,1664]{1,0:T(8,128)S(1)}, f32[64,1664]{1,0:T(8,128)S(1)}, u32[]{:S(2)}, u32[]{:S(2)}) collective-permute-start(f32[64,1664]{1,0:T(8,128)S(1)} %early.1), channel_id=1, source_target_pairs={{0,24},{4,28},{8,16},{12,20},{16,8},{20,12},{24,0},{28,4},{1,25},{... | collective-permute-start | bytes 1277960 | tf_op jit(solution)/shard_map/ppermute | solution.py:586
  5.2 9.1 %estep.1 = (f32[64,10240]{1,0:T(8,128)}, bf16[64,10240]{1,0:T(8,128)(2,1)}, f32[64,64]{1,0:T(8,128)S(1)}, bf16[64,1536]{1,0:T(8,128)(2,1)}, f32[64,1664]{1,0:T(8,128)}, /*index=5*/f32[64,1664]{1,0:T(8,128)S(1)}) custom-call(s32[1]{0:T(128)} %bitcast.me_ref, s32[1]{0:T(128)} %bitcast.1.slab_ref, s32[1,16640]{1,0:T(1,128)} %constant.13.clone.index_hbm, ...), custom_call_target="tpu_custom_call" | custom-call | tf_op jit(solution)/shard_map/estep/pallas_call | solution.py:197
  15.0 1.8 %collective-permute-start = (f32[64,64]{1,0:T(8,128)S(1)}, f32[64,64]{1,0:T(8,128)S(1)}, u32[]{:S(2)}, u32[]{:S(2)}) collective-permute-start(f32[64,64]{1,0:T(8,128)S(1)} %get-tuple-element.41), channel_id=1, source_target_pairs={{0,1},{1,0},{2,3},{3,2},{4,5},{5,4},{6,7},{7,6},{8,9},{9,8},{10,11... | collective-permute-start | bytes 49160 | tf_op jit(solution)/shard_map/ppermute | solution.py:630
  16.8 1.5 %collective-permute-start.8 = (f32[64,1664]{1,0:T(8,128)}, f32[64,1664]{1,0:T(8,128)}, u32[]{:S(2)}, u32[]{:S(2)}) collective-permute-start(f32[64,1664]{1,0:T(8,128)} %get-tuple-element.56), channel_id=1, source_target_pairs={{0,8},{4,12},{8,0},{12,4},{16,24},{20,28},{24,16},{28,20},{1,9},{5... | collective-permute-start | bytes 1277960 | tf_op jit(solution)/shard_map/ppermute | solution.py:586
  18.3 1.5 %collective-permute-start.9 = (f32[64,1664]{1,0:T(8,128)S(1)}, f32[64,1664]{1,0:T(8,128)}, u32[]{:S(2)}, u32[]{:S(2)}) collective-permute-start(f32[64,1664]{1,0:T(8,128)S(1)} %get-tuple-element.57), channel_id=1, source_target_pairs={{0,16},{4,20},{8,24},{12,28},{16,0},{20,4},{24,8},{28,12},{1,17},{... | collective-permute-start | bytes 1277960 | tf_op jit(solution)/shard_map/ppermute | solution.py:586
  19.9 2.6 %collective-permute-start.1 = (f32[64,128]{1,0:T(8,128)S(1)}, f32[64,128]{1,0:T(8,128)S(1)}, u32[]{:S(2)}, u32[]{:S(2)}) collective-permute-start(f32[64,128]{1,0:T(8,128)S(1)} %pad_maximum_fusion.refs_0_), channel_id=1, source_target_pairs={{0,2},{1,3},{2,0},{3,1},{4,6},{5,7},{6,4},{7,5},{8,10},{9,11},{10,... | collective-permute-start | bytes 98312 | tf_op jit(solution)/shard_map/ppermute | solution.py:630
  22.6 1.4 %count.1 = (f32[2,64,128]{2,1,0:T(8,128)S(1)}, f32[64,128]{1,0:T(8,128)S(1)}) custom-call(s32[1]{0:T(128)} %bitcast.1.slab_ref, f32[1,2]{1,0:T(1,128)S(1)} %bitcast.6, f32[1,64]{1,0:T(1,128)S(1)} %bitcast.7, s32[64,128]{1,0:T(8,128)S(1)} %reshape.25.list_ref), custom_call_target="tpu_custom_call" | custom-call | tf_op jit(solution)/shard_map/count/pallas_call | solution.py:316
  24.0 0.7 %collective-permute-done.1.refs_1_ = f32[64,128]{1,0:T(8,128)S(1)} collective-permute-done((f32[64,128]{1,0:T(8,128)S(1)}, f32[64,128]{1,0:T(8,128)S(1)}, u32[]{:S(2)}, u32[]{:S(2)}) %collective-permute-start.1) | collective-permute-done | bytes 32800 | tf_op jit(solution)/shard_map/ppermute | solution.py:630
  25.2 1.1 %gather.1.image_ref = bf16[2,128,1280]{2,1,0:T(8,128)(2,1)S(1)} custom-call(bf16[64,10240]{1,0:T(8,128)(2,1)} %get-tuple-element.60.keep_hbm, f32[64,10240]{1,0:T(8,128)S(1)} %collective-permute-done.4.got_hbm), custom_call_target="tpu_custom_call" | custom-call | tf_op jit(solution)/shard_map/gather/pallas_call | solution.py:393
  26.7 0.9 %collective-permute-start.5 = (f32[1,64,1408]{2,1,0:T(8,128)S(1)}, f32[1,64,1408]{2,1,0:T(8,128)S(1)}, u32[]{:S(2)}, u32[]{:S(2)}) collective-permute-start(f32[1,64,1408]{2,1,0:T(8,128)S(1)} %get-tuple-element.52), channel_id=1, source_target_pairs={{0,8},{4,12},{8,0},{12,4},{16,24},{20,28},{24,16},{28,20},{1,9},{5... | collective-permute-start | bytes 1081352 | tf_op jit(solution)/shard_map/ppermute | solution.py:586
  27.6 1.5 %collective-permute-start.6 = (f32[1,64,1408]{2,1,0:T(8,128)S(1)}, f32[1,64,1408]{2,1,0:T(8,128)S(1)}, u32[]{:S(2)}, u32[]{:S(2)}) collective-permute-start(f32[1,64,1408]{2,1,0:T(8,128)S(1)} %get-tuple-element.53), channel_id=1, source_target_pairs={{0,16},{4,20},{8,24},{12,28},{16,0},{20,4},{24,8},{28,12},{1,17},{... | collective-permute-start | bytes 1081352 | tf_op jit(solution)/shard_map/ppermute | solution.py:586
  29.1 1.2 %collective-permute-start.7 = (f32[64,128]{1,0:T(8,128)S(1)}, f32[64,128]{1,0:T(8,128)S(1)}, u32[]{:S(2)}, u32[]{:S(2)}) collective-permute-start(f32[64,128]{1,0:T(8,128)S(1)} %get-tuple-element.54.both_w_ref.refs_0_), channel_id=1, source_target_pairs={{0,24},{4,28},{8,16},{12,20},{16,8},{20,12},{24,0},{28,4},{1,25},{... | collective-permute-start | bytes 98312 | tf_op jit(solution)/shard_map/ppermute | solution.py:586
  30.3 1.3 %sums.2 = (f32[1,64,1280]{2,1,0:T(8,128)S(1)}, f32[1,64,1280]{2,1,0:T(8,128)S(1)}) custom-call(f32[64,64]{1,0:T(8,128)S(1)} %get-tuple-element.43.own_w_ref, f32[64,64]{1,0:T(8,128)S(1)} %collective-permute-done.2.sib_w_ref, bf16[64,10240]{1,0:T(8,128)(2,1)} %get-tuple-element.60.keep_hbm, f32[64,10240]{1,0:T(8,128)S(1)} %collective-permute-done.4.got_hbm), custom_call_target="tpu_custom_call" | custom-call | tf_op jit(solution)/shard_map/sums/pallas_call | solution.py:465
  31.6 0.9 %collective-permute-start.12 = (f32[1,64,1280]{2,1,0:T(8,128)S(1)}, f32[1,64,1280]{2,1,0:T(8,128)S(1)}, u32[]{:S(2)}, u32[]{:S(2)}) collective-permute-start(f32[1,64,1280]{2,1,0:T(8,128)S(1)} %get-tuple-element.61), channel_id=1, source_target_pairs={{0,8},{4,12},{8,0},{12,4},{16,24},{20,28},{24,16},{28,20},{1,9},{5... | collective-permute-start | bytes 983048 | tf_op jit(solution)/shard_map/ppermute | solution.py:586
  32.5 1.5 %collective-permute-start.14 = (f32[1,64,1280]{2,1,0:T(8,128)S(1)}, f32[1,64,1280]{2,1,0:T(8,128)S(1)}, u32[]{:S(2)}, u32[]{:S(2)}) collective-permute-start(f32[1,64,1280]{2,1,0:T(8,128)S(1)} %get-tuple-element.69), channel_id=1, source_target_pairs={{0,16},{4,20},{8,24},{12,28},{16,0},{20,4},{24,8},{28,12},{1,17},{... | collective-permute-start | bytes 983048 | tf_op jit(solution)/shard_map/ppermute | solution.py:586
  34.0 1.8 %sums.3 = (f32[2,64,1280]{2,1,0:T(8,128)S(1)}, f32[2,64,1280]{2,1,0:T(8,128)S(1)}) custom-call(f32[64,64]{1,0:T(8,128)S(1)} %get-tuple-element.43.own_w_ref, f32[64,64]{1,0:T(8,128)S(1)} %collective-permute-done.2.sib_w_ref, bf16[64,10240]{1,0:T(8,128)(2,1)} %get-tuple-element.60.keep_hbm, f32[64,10240]{1,0:T(8,128)S(1)} %collective-permute-done.4.got_hbm), custom_call_target="tpu_custom_call" | custom-call | tf_op jit(solution)/shard_map/sums/pallas_call | solution.py:465
  35.8 3.2 %collective-permute-done.7.refs_3_ = f32[64,128]{1,0:T(8,128)S(1)} collective-permute-done((f32[64,128]{1,0:T(8,128)S(1)}, f32[64,128]{1,0:T(8,128)S(1)}, u32[]{:S(2)}, u32[]{:S(2)}) %collective-permute-start.7) | collective-permute-done | bytes 32800 | tf_op jit(solution)/shard_map/ppermute | solution.py:586
  39.6 1.7 %meet.1 = (f32[128,896]{1,0:T(8,128)S(1)}, f32[128,896]{1,0:T(8,128)S(1)}) custom-call(f32[64,64]{1,0:T(8,128)S(1)} %copy-done.1, f32[64,128]{1,0:T(8,128)S(1)} %get-tuple-element.54.both_w_ref.refs_0_, f32[1,64,1408]{2,1,0:T(8,128)S(1)} %collective-permute-done.5.refs_1_, f32[1,64,1408]{2,1,0:T(8,128)S(1)} %collective-permute-done.6.refs_2_, ...), custom_call_target="tpu_custom_call" | custom-call | tf_op jit(solution)/shard_map/meet/pallas_call | solution.py:510
  41.4 1.6 %collective-permute-start.13 = (f32[1,64,1280]{2,1,0:T(8,128)S(1)}, f32[1,64,1280]{2,1,0:T(8,128)S(1)}, u32[]{:S(2)}, u32[]{:S(2)}) collective-permute-start(f32[1,64,1280]{2,1,0:T(8,128)S(1)} %slice_add_fusion.1), channel_id=1, source_target_pairs={{0,16},{4,20},{8,24},{12,28},{16,0},{20,4},{24,8},{28,12},{1,17},{... | collective-permute-start | bytes 983048 | tf_op jit(solution)/shard_map/ppermute | solution.py:586
  43.6 1.6 %collective-permute-start.11 = (f32[64,768]{1,0:T(8,128)S(1)}, f32[64,768]{1,0:T(8,128)S(1)}, u32[]{:S(2)}, u32[]{:S(2)}) collective-permute-start(f32[64,768]{1,0:T(8,128)S(1)} %slice_add_fusion.2), channel_id=1, source_target_pairs={{0,1},{1,0},{2,3},{3,2},{4,5},{5,4},{6,7},{7,6},{8,9},{9,8},{10,11... | collective-permute-start | bytes 589832 | tf_op jit(solution)/shard_map/ppermute | solution.py:679
  45.3 1.3 %collective-permute-done.14.refs_3_ = f32[1,64,1280]{2,1,0:T(8,128)S(1)} collective-permute-done((f32[1,64,1280]{2,1,0:T(8,128)S(1)}, f32[1,64,1280]{2,1,0:T(8,128)S(1)}, u32[]{:S(2)}, u32[]{:S(2)}) %collective-permute-start.14) | collective-permute-done | bytes 327712 | tf_op jit(solution)/shard_map/ppermute | solution.py:586
  46.6 6.2 %collective-permute-done.13.refs_2_ = f32[1,64,1280]{2,1,0:T(8,128)S(1)} collective-permute-done((f32[1,64,1280]{2,1,0:T(8,128)S(1)}, f32[1,64,1280]{2,1,0:T(8,128)S(1)}, u32[]{:S(2)}, u32[]{:S(2)}) %collective-permute-start.13) | collective-permute-done | bytes 327712 | tf_op jit(solution)/shard_map/ppermute | solution.py:586
  52.9 1.2 %finish.1 = f32[64,4096]{1,0:T(8,128)} custom-call(s32[1]{0:T(128)} %bitcast.me_ref, s32[1]{0:T(128)} %bitcast.1.slab_ref, s32[1,32768]{1,0:T(1,128)S(1)} %copy-done, f32[128,896]{1,0:T(8,128)S(1)} %get-tuple-element.66.met_ref, f32[128,896]{1,0:T(8,128)S(1)} %collective-permute-done.10.sib_met_ref, f32[64,768]{1,0:T(8,128)S(1)} %collective-permute-done.11.partner_ref, ...), custom_call_target="tpu_custom_call" | custom-call | tf_op jit(solution)/shard_map/finish/pallas_call | solution.py:566
  (35 shorter events, 3.3 us)
Async XLA Ops:
  1.2 13.8 %collective-permute-start.3 = (f32[64,1664]{1,0:T(8,128)S(1)}, f32[64,1664]{1,0:T(8,128)S(1)}, u32[]{:S(2)}, u32[]{:S(2)}) collective-permute-start(f32[64,1664]{1,0:T(8,128)S(1)} %early.1), channel_id=1, source_target_pairs={{0,24},{4,28},{8,16},{12,20},{16,8},{20,12},{24,0},{28,4},{1,25},{... | collective-permute-start | bytes 1277960 | tf_op jit(solution)/shard_map/ppermute | solution.py:586
  5.2 17.3 %copy-start.5 = (s32[64,2,64]{2,1,0:T(2,128)S(1)}, s32[64,2,64]{2,1,0:T(2,128)}, u32[]{:S(2)}) copy-start(s32[64,2,64]{2,1,0:T(2,128)} %param.10) | copy-start | bytes 98308
  5.2 17.4 %copy-start.2 = (f32[2]{0:T(128)S(1)}, f32[2]{0:T(128)}, u32[]{:S(2)}) copy-start(f32[2]{0:T(128)} %param.13) | copy-start | bytes 28
  5.2 17.4 %copy-start.3 = (f32[64]{0:T(128)S(1)}, f32[64]{0:T(128)}, u32[]{:S(2)}) copy-start(f32[64]{0:T(128)} %param.12) | copy-start | bytes 772
  15.0 4.9 %copy-start.4 = (f32[64,1664]{1,0:T(8,128)}, f32[64,1664]{1,0:T(8,128)S(1)}, u32[]{:S(2)}) copy-start(f32[64,1664]{1,0:T(8,128)S(1)} %collective-permute-done.3.refs_7_) | copy-start | bytes 1277956
  15.0 10.2 %collective-permute-start.4 = (f32[64,10240]{1,0:T(8,128)}, f32[64,10240]{1,0:T(8,128)S(1)}, u32[]{:S(2)}, u32[]{:S(2)}) collective-permute-start(f32[64,10240]{1,0:T(8,128)} %get-tuple-element.51), channel_id=1, source_target_pairs={{0,4},{4,0},{8,12},{12,8},{16,20},{20,16},{24,28},{28,24},{1,5},{5... | collective-permute-start | bytes 7864328 | tf_op jit(solution)/shard_map/ppermute | solution.py:586
  15.0 4.8 %collective-permute-start = (f32[64,64]{1,0:T(8,128)S(1)}, f32[64,64]{1,0:T(8,128)S(1)}, u32[]{:S(2)}, u32[]{:S(2)}) collective-permute-start(f32[64,64]{1,0:T(8,128)S(1)} %get-tuple-element.41), channel_id=1, source_target_pairs={{0,1},{1,0},{2,3},{3,2},{4,5},{5,4},{6,7},{7,6},{8,9},{9,8},{10,11... | collective-permute-start | bytes 49160 | tf_op jit(solution)/shard_map/ppermute | solution.py:630
  16.8 13.5 %collective-permute-start.8 = (f32[64,1664]{1,0:T(8,128)}, f32[64,1664]{1,0:T(8,128)}, u32[]{:S(2)}, u32[]{:S(2)}) collective-permute-start(f32[64,1664]{1,0:T(8,128)} %get-tuple-element.56), channel_id=1, source_target_pairs={{0,8},{4,12},{8,0},{12,4},{16,24},{20,28},{24,16},{28,20},{1,9},{5... | collective-permute-start | bytes 1277960 | tf_op jit(solution)/shard_map/ppermute | solution.py:586
  18.3 12.0 %collective-permute-start.9 = (f32[64,1664]{1,0:T(8,128)S(1)}, f32[64,1664]{1,0:T(8,128)}, u32[]{:S(2)}, u32[]{:S(2)}) collective-permute-start(f32[64,1664]{1,0:T(8,128)S(1)} %get-tuple-element.57), channel_id=1, source_target_pairs={{0,16},{4,20},{8,24},{12,28},{16,0},{20,4},{24,8},{28,12},{1,17},{... | collective-permute-start | bytes 1277960 | tf_op jit(solution)/shard_map/ppermute | solution.py:586
  19.9 4.9 %collective-permute-start.1 = (f32[64,128]{1,0:T(8,128)S(1)}, f32[64,128]{1,0:T(8,128)S(1)}, u32[]{:S(2)}, u32[]{:S(2)}) collective-permute-start(f32[64,128]{1,0:T(8,128)S(1)} %pad_maximum_fusion.refs_0_), channel_id=1, source_target_pairs={{0,2},{1,3},{2,0},{3,1},{4,6},{5,7},{6,4},{7,5},{8,10},{9,11},{10,... | collective-permute-start | bytes 98312 | tf_op jit(solution)/shard_map/ppermute | solution.py:630
  25.1 1.3 %collective-permute-start.2 = (f32[64,64]{1,0:T(8,128)S(1)}, f32[64,64]{1,0:T(8,128)S(1)}, u32[]{:S(2)}, u32[]{:S(2)}) collective-permute-start(f32[64,64]{1,0:T(8,128)S(1)} %get-tuple-element.43.own_w_ref), channel_id=1, source_target_pairs={{0,4},{4,0},{8,12},{12,8},{16,20},{20,16},{24,28},{28,24},{1,5},{5... | collective-permute-start | bytes 49160 | tf_op jit(solution)/shard_map/ppermute | solution.py:586
  26.7 12.3 %collective-permute-start.5 = (f32[1,64,1408]{2,1,0:T(8,128)S(1)}, f32[1,64,1408]{2,1,0:T(8,128)S(1)}, u32[]{:S(2)}, u32[]{:S(2)}) collective-permute-start(f32[1,64,1408]{2,1,0:T(8,128)S(1)} %get-tuple-element.52), channel_id=1, source_target_pairs={{0,8},{4,12},{8,0},{12,4},{16,24},{20,28},{24,16},{28,20},{1,9},{5... | collective-permute-start | bytes 1081352 | tf_op jit(solution)/shard_map/ppermute | solution.py:586
  27.6 12.0 %collective-permute-start.6 = (f32[1,64,1408]{2,1,0:T(8,128)S(1)}, f32[1,64,1408]{2,1,0:T(8,128)S(1)}, u32[]{:S(2)}, u32[]{:S(2)}) collective-permute-start(f32[1,64,1408]{2,1,0:T(8,128)S(1)} %get-tuple-element.53), channel_id=1, source_target_pairs={{0,16},{4,20},{8,24},{12,28},{16,0},{20,4},{24,8},{28,12},{1,17},{... | collective-permute-start | bytes 1081352 | tf_op jit(solution)/shard_map/ppermute | solution.py:586
  29.1 9.9 %collective-permute-start.7 = (f32[64,128]{1,0:T(8,128)S(1)}, f32[64,128]{1,0:T(8,128)S(1)}, u32[]{:S(2)}, u32[]{:S(2)}) collective-permute-start(f32[64,128]{1,0:T(8,128)S(1)} %get-tuple-element.54.both_w_ref.refs_0_), channel_id=1, source_target_pairs={{0,24},{4,28},{8,16},{12,20},{16,8},{20,12},{24,0},{28,4},{1,25},{... | collective-permute-start | bytes 98312 | tf_op jit(solution)/shard_map/ppermute | solution.py:586
  31.6 7.9 %copy-start.1 = (f32[64,64]{1,0:T(8,128)S(1)}, f32[64,64]{1,0:T(8,128)}, u32[]{:S(2)}) copy-start(f32[64,64]{1,0:T(8,128)} %ctf_ref.1) | copy-start | bytes 49156
  31.6 13.6 %collective-permute-start.12 = (f32[1,64,1280]{2,1,0:T(8,128)S(1)}, f32[1,64,1280]{2,1,0:T(8,128)S(1)}, u32[]{:S(2)}, u32[]{:S(2)}) collective-permute-start(f32[1,64,1280]{2,1,0:T(8,128)S(1)} %get-tuple-element.61), channel_id=1, source_target_pairs={{0,8},{4,12},{8,0},{12,4},{16,24},{20,28},{24,16},{28,20},{1,9},{5... | collective-permute-start | bytes 983048 | tf_op jit(solution)/shard_map/ppermute | solution.py:586
  32.5 14.1 %collective-permute-start.14 = (f32[1,64,1280]{2,1,0:T(8,128)S(1)}, f32[1,64,1280]{2,1,0:T(8,128)S(1)}, u32[]{:S(2)}, u32[]{:S(2)}) collective-permute-start(f32[1,64,1280]{2,1,0:T(8,128)S(1)} %get-tuple-element.69), channel_id=1, source_target_pairs={{0,16},{4,20},{8,24},{12,28},{16,0},{20,4},{24,8},{28,12},{1,17},{... | collective-permute-start | bytes 983048 | tf_op jit(solution)/shard_map/ppermute | solution.py:586
  35.8 17.1 %copy-start = (s32[1,32768]{1,0:T(1,128)S(1)}, s32[1,32768]{1,0:T(1,128)}, u32[]{:S(2)}) copy-start(s32[1,32768]{1,0:T(1,128)} %constant.14.clone.index_hbm) | copy-start | bytes 393220
  41.2 2.3 %collective-permute-start.10 = (f32[128,896]{1,0:T(8,128)S(1)}, f32[128,896]{1,0:T(8,128)S(1)}, u32[]{:S(2)}, u32[]{:S(2)}) collective-permute-start(f32[128,896]{1,0:T(8,128)S(1)} %get-tuple-element.67), channel_id=1, source_target_pairs={{0,4},{4,0},{8,12},{12,8},{16,20},{20,16},{24,28},{28,24},{1,5},{5... | collective-permute-start | bytes 1376264 | tf_op jit(solution)/shard_map/ppermute | solution.py:586
  41.4 11.4 %collective-permute-start.13 = (f32[1,64,1280]{2,1,0:T(8,128)S(1)}, f32[1,64,1280]{2,1,0:T(8,128)S(1)}, u32[]{:S(2)}, u32[]{:S(2)}) collective-permute-start(f32[1,64,1280]{2,1,0:T(8,128)S(1)} %slice_add_fusion.1), channel_id=1, source_target_pairs={{0,16},{4,20},{8,24},{12,28},{16,0},{20,4},{24,8},{28,12},{1,17},{... | collective-permute-start | bytes 983048 | tf_op jit(solution)/shard_map/ppermute | solution.py:586
  43.0 9.9 %collective-permute-start.15 = (f32[1,64,1280]{2,1,0:T(8,128)S(1)}, f32[1,64,1280]{2,1,0:T(8,128)S(1)}, u32[]{:S(2)}, u32[]{:S(2)}) collective-permute-start(f32[1,64,1280]{2,1,0:T(8,128)S(1)} %slice_add_fusion), channel_id=1, source_target_pairs={{0,8},{4,12},{8,0},{12,4},{16,24},{20,28},{24,16},{28,20},{1,9},{5... | collective-permute-start | bytes 983048 | tf_op jit(solution)/shard_map/ppermute | solution.py:586
  43.6 9.3 %collective-permute-start.11 = (f32[64,768]{1,0:T(8,128)S(1)}, f32[64,768]{1,0:T(8,128)S(1)}, u32[]{:S(2)}, u32[]{:S(2)}) collective-permute-start(f32[64,768]{1,0:T(8,128)S(1)} %slice_add_fusion.2), channel_id=1, source_target_pairs={{0,1},{1,0},{2,3},{3,2},{4,5},{5,4},{6,7},{7,6},{8,9},{9,8},{10,11... | collective-permute-start | bytes 589832 | tf_op jit(solution)/shard_map/ppermute | solution.py:679

commit v8 on v7

--- a/solution.py
+++ b/solution.py
@@ -57,7 +57,7 @@
 
 
 def estep_kernel(
-    blocks, share, near, me_ref, slab_ref, index_hbm, image_hbm, plane_hbm, ctf_hbm, *refs,
+    blocks, share, near, index_hbm, image_hbm, plane_hbm, ctf_hbm, *refs,
 ):
     give_hbm, keep_hbm, score_ref = refs[:3]
     near_refs = refs[3 : 3 + len(near)]
@@ -129,7 +129,7 @@
         low += fit(high - span + line, stop)
         return 2.0 * low - energy(block % 2, span)
 
-    chip, core = me_ref[0] // 2, lax.rem(me_ref[0], 2)
+    chip, core = lax.axis_index("img") // 2, lax.rem(lax.axis_index("img"), 2)
     outgoing = []
 
     def hand_over(done):
@@ -171,7 +171,7 @@
     for k, near_ref in zip(near, near_refs):
         for other in range(2):
             owner = (k ^ chip) * 2 + lax.rem(core + other, 2)
-            part = weighted[:, pl.ds(met_column(share, owner, slab_ref[0]), met)]
+            part = weighted[:, pl.ds(met_column(share, owner, lax.axis_index("slab")), met)]
             near_ref[:, other * met : (other + 1) * met] = part.astype(near_ref.dtype)
         if k:
             near_ref[:, 2 * met :] = table
@@ -183,7 +183,7 @@
     return [pltpu.with_memory_space_constraint(operand, pltpu.HBM) for operand in operands]
 
 
-def estep(me, slab, index, images, planes, ctf_table, share, near):
+def estep(index, images, planes, ctf_table, share, near):
     rows, width = images.shape
     chips = width // share // 2
     wide, met = split_share(share)
@@ -196,7 +196,7 @@
     hbm = pl.BlockSpec(memory_space=pltpu.HBM)
     return pl.pallas_call(
         functools.partial(estep_kernel, blocks, share, near),
-        in_specs=[pl.BlockSpec(memory_space=pltpu.SMEM)] * 2 + [hbm] * 4,
+        in_specs=[hbm] * 4,
         out_specs=[held, held] + [vmem] * (1 + len(near)),
         out_shape=[
             jax.ShapeDtypeStruct((rows, chips * summed), F32),
@@ -224,21 +224,21 @@
         ],
         compiler_params=params(28),
         name="estep",
-    )(me, slab, *far(index, images, planes, ctf_table))
-
-
-def early_kernel(share, beyond, me_ref, slab_ref, index_hbm, image_hbm, ctf_hbm, *refs):
+    )(*far(index, images, planes, ctf_table))
+
+
+def early_kernel(share, beyond, index_hbm, image_hbm, ctf_hbm, *refs):
     outs = refs[: len(beyond)]
     index, image, ctf_held, index_sem, image_sem, ctf_sem = refs[len(beyond) :]
     met = split_share(share)[1]
-    chip, core = me_ref[0] // 2, lax.rem(me_ref[0], 2)
+    chip, core = lax.axis_index("img") // 2, lax.rem(lax.axis_index("img"), 2)
     fetch = pltpu.make_async_copy(ctf_hbm, ctf_held, ctf_sem)
     fetch.start()
     copies = []
     for place, k in enumerate(beyond):
         for other in range(2):
             owner = (k ^ chip) * 2 + lax.rem(core + other, 2)
-            cut = pl.ds(met_column(share, owner, slab_ref[0]), met)
+            cut = pl.ds(met_column(share, owner, lax.axis_index("slab")), met)
             copies.append([
                 pltpu.make_async_copy(
                     index_hbm.at[:, cut], index.at[place, other], index_sem.at[place, other]
@@ -263,16 +263,15 @@
         out_ref[:, 2 * met :] = table
 
 
-def early_images(me, slab, index, images, ctf_table, share, beyond):
+def early_images(index, images, ctf_table, share, beyond):
     rows = images.shape[0]
     met = split_share(share)[1]
     number = len(beyond)
     vmem = pl.BlockSpec(memory_space=pltpu.VMEM)
-    smem = pl.BlockSpec(memory_space=pltpu.SMEM)
     hbm = pl.BlockSpec(memory_space=pltpu.HBM)
     return pl.pallas_call(
         functools.partial(early_kernel, share, beyond),
-        in_specs=[smem, smem, hbm, hbm, hbm],
+        in_specs=[hbm, hbm, hbm],
         out_specs=[vmem] * number,
         out_shape=[jax.ShapeDtypeStruct((rows, 2 * met + LANES), F32)] * number,
         scratch_shapes=[
@@ -285,16 +284,16 @@
         ],
         compiler_params=params(12),
         name="early",
-    )(me, slab, *far(index, images, ctf_table))
-
-
-def count_kernel(slabs, slab_ref, prior_ref, noise_ref, list_ref, base_ref, scale_ref):
+    )(*far(index, images, ctf_table))
+
+
+def count_kernel(slabs, prior_ref, noise_ref, list_ref, base_ref, scale_ref):
     rows, listed = list_ref.shape
     classes, _, width = base_ref.shape
     each = listed // classes
     local = width // slabs
     lane = lax.broadcasted_iota(jnp.int32, (rows, width), 1)
-    home = slab_ref[0] ^ (lane // local)
+    home = lax.axis_index("slab") ^ (lane // local)
     plane = home * local + lax.rem(lane, local)
     for one in range(classes):
         sums = jnp.zeros((rows, width), F32)
@@ -310,12 +309,12 @@
     scale_ref[...] = jnp.broadcast_to(column, (rows, width))
 
 
-def count_planes(slab, class_weight, inv_noise, orientations, width, slabs):
+def count_planes(class_weight, inv_noise, orientations, width, slabs):
     rows, classes, each = orientations.shape
     vmem = pl.BlockSpec(memory_space=pltpu.VMEM)
     return pl.pallas_call(
         functools.partial(count_kernel, slabs),
-        in_specs=[pl.BlockSpec(memory_space=pltpu.SMEM), vmem, vmem, vmem],
+        in_specs=[vmem] * 3,
         out_specs=[vmem, vmem],
         out_shape=[
             jax.ShapeDtypeStruct((classes, rows, width), F32),
@@ -324,7 +323,6 @@
         compiler_params=params(4),
         name="count",
     )(
-        slab,
         class_weight.reshape(1, classes),
         inv_noise.reshape(1, rows),
         orientations.reshape(rows, classes * each),
@@ -515,71 +513,96 @@
     )(ctf_table, *weights, *images)
 
 
-def finish_kernel(numbers, me_ref, slab_ref, index_hbm, met_ref, sib_met_ref, partner_ref, *refs):
-    total = sum(numbers)
-    parts, (out_hbm, index, out, in_sem, out_sem) = refs[:total], refs[total:]
+def prepare_kernel(places, index_hbm, met_ref, sib_met_ref, *refs):
+    total = sum(map(len, places))
+    parts, (base_ref, scale_ref, index, in_sem) = refs[:total], refs[total:]
+    planes, share = base_ref.shape
+    wide, met = split_share(share)
+    mine = pl.ds(pl.multiple_of(lax.axis_index("img") * share, share), share)
+    fetch = pltpu.make_async_copy(index_hbm.at[:, mine], index, in_sem)
+    fetch.start()
+    start = 0
+    for side, numbers in enumerate(places):
+        refs = list(zip(parts[start : start + len(numbers)], numbers))
+        start += len(numbers)
+        base_ref[:, side * wide : (side + 1) * wide] = functools.reduce(
+            jnp.add, [ref[place] for ref, place in refs]
+        )
+    half = lax.rem(lax.axis_index("slab"), 2)
+    own = pl.ds(pl.multiple_of(2 * wide + half * met, LANES), met)
+    other = pl.ds(pl.multiple_of(2 * wide + (1 - half) * met, LANES), met)
+    base_ref[:, own] = met_ref[:planes, :met] + sib_met_ref[:planes, :met]
+    base_ref[:, other] = jnp.zeros((planes, met), F32)
+    shells = met_ref[:planes, met:] + sib_met_ref[:planes, met:]
+    fetch.wait()
+    for start in range(0, share, LANES):
+        cut = slice(start, start + LANES)
+        scale_ref[:, cut] = 1.0 / (spread(shells, index[:, cut]) + 1.0)
+
+
+def prepare(index, met, sib_met, sides, share):
+    planes = met.shape[0] // 2
+    held = pl.BlockSpec(memory_space=pl.ANY)
+    vmem = pl.BlockSpec(memory_space=pltpu.VMEM)
+    places = [[place for _, place in side] for side in sides]
+    parts = [part for side in sides for part, _ in side]
+    return pl.pallas_call(
+        functools.partial(prepare_kernel, places),
+        in_specs=[held] + [vmem] * (2 + len(parts)),
+        out_specs=[vmem, vmem],
+        out_shape=[jax.ShapeDtypeStruct((planes, share), F32)] * 2,
+        scratch_shapes=[pltpu.VMEM((1, share), jnp.int32), pltpu.SemaphoreType.DMA(())],
+        compiler_params=params(8),
+        name="prepare",
+    )(index, met, sib_met, *parts)
+
+
+def finish_kernel(base_ref, scale_ref, left_ref, right_ref, partner_ref, out_hbm, out, out_sem):
     planes, share = out.shape
     wide, met = split_share(share)
-    mine = pl.ds(pl.multiple_of(me_ref[0] * share, share), share)
-    fetch = pltpu.make_async_copy(index_hbm.at[:, mine], index, in_sem)
-    fetch.start()
-    left, right = parts[: numbers[0]], parts[numbers[0] :]
-    shells = met_ref[:planes, met:] + sib_met_ref[:planes, met:]
-    half = lax.rem(slab_ref[0], 2)
-    fetch.wait()
-
-    def divide(block_of, place, size):
+    half = lax.rem(lax.axis_index("slab"), 2)
+    own = pl.multiple_of(2 * wide + half * met, LANES)
+    other = pl.multiple_of(2 * wide + (1 - half) * met, LANES)
+
+    def scaled(place, size, last=None):
         for start in range(0, size, LANES):
             at = pl.ds(pl.multiple_of(place + start, LANES), LANES)
-            weight = spread(shells, index[:, at])
-            out[:, at] = block_of(slice(start, start + LANES)) / (weight + 1.0)
-
-    def summed(sides):
-        return lambda cut: functools.reduce(jnp.add, [ref[0, :, cut] for ref in sides])
-
-    divide(lambda cut: met_ref[:planes, cut] + sib_met_ref[:planes, cut], 2 * wide + half * met, met)
-    divide(lambda cut: partner_ref[:, cut], 2 * wide + (1 - half) * met, met)
+            value = base_ref[:, at]
+            if last is not None:
+                value += last(slice(start, start + LANES))
+            out[:, at] = value * scale_ref[:, at]
+
     stores = []
-    for step, work in enumerate((None, (left, 0), (right, 1))):
-        cut = slice(2 * wide, share)
-        if work is not None:
-            sides, place = work
-            divide(summed(sides), place * wide, wide)
-            cut = slice(place * wide, (place + 1) * wide)
-        stores.append(pltpu.make_async_copy(out.at[:, cut], out_hbm.at[:, cut], out_sem.at[step]))
+
+    def store(start, stop):
+        cut = slice(start, stop)
+        stores.append(
+            pltpu.make_async_copy(out.at[:, cut], out_hbm.at[:, cut], out_sem.at[len(stores)])
+        )
         stores[-1].start()
-    for store in stores:
-        store.wait()
-
-
-def finish(me, slab, index, met, sib_met, partner, left, right, share):
-    planes = partner.shape[0]
-    numbers = len(left), len(right)
-    held = pl.BlockSpec(memory_space=pl.ANY)
+
+    scaled(own, met)
+    scaled(other, met, lambda cut: partner_ref[:, cut])
+    store(2 * wide, share)
+    scaled(0, wide, lambda cut: left_ref[0, :, cut])
+    store(0, wide)
+    scaled(wide, wide, lambda cut: right_ref[0, :, cut])
+    store(wide, 2 * wide)
+    for copy in stores:
+        copy.wait()
+
+
+def finish(base, scale, left, right, partner):
     vmem = pl.BlockSpec(memory_space=pltpu.VMEM)
-
-    def first(part, place):
-        if part.shape[0] == 1:
-            return vmem
-        return pl.BlockSpec((1,) + part.shape[1:], lambda step: (place, 0, 0))
-
-    return pl.pallas_call(
-        functools.partial(finish_kernel, numbers),
-        grid=(1,),
-        in_specs=[pl.BlockSpec(memory_space=pltpu.SMEM)] * 2
-        + [held, vmem, vmem, vmem]
-        + [first(part, place) for part, place in left + right],
-        out_specs=held,
-        out_shape=jax.ShapeDtypeStruct((planes, share), F32),
-        scratch_shapes=[
-            pltpu.VMEM((1, share), jnp.int32),
-            pltpu.VMEM((planes, share), F32),
-            pltpu.SemaphoreType.DMA(()),
-            pltpu.SemaphoreType.DMA((3,)),
-        ],
-        compiler_params=params(12),
+    return pl.pallas_call(
+        finish_kernel,
+        in_specs=[vmem] * 5,
+        out_specs=pl.BlockSpec(memory_space=pl.ANY),
+        out_shape=jax.ShapeDtypeStruct(base.shape, F32),
+        scratch_shapes=[pltpu.VMEM(base.shape, F32), pltpu.SemaphoreType.DMA((3,))],
+        compiler_params=params(8),
         name="finish",
-    )(me, slab, index, met, sib_met, partner, *[part for part, _ in left + right])
+    )(base, scale, left, right, partner)
 
 
 def swap(array, bit, size):
@@ -594,8 +617,6 @@
     chips = size // 2
     share = width // size
     wide, met_wide = split_share(share)
-    me = lax.axis_index("img").astype(jnp.int32).reshape(1)
-    slab = lax.axis_index("slab").astype(jnp.int32).reshape(1)
     index = entry_shells(width, ctf_table.shape[1])
     top_index = jnp.asarray(index[:, : width // 2 + 2 * math.isqrt(width // 2)])
     index = jnp.asarray(index)
@@ -605,11 +626,11 @@
     near = tuple(k for k in range(chips) if k not in beyond)
     met_images = {}
     if beyond:
-        early = early_images(me, slab, index, images, ctf_table, share, beyond)
+        early = early_images(index, images, ctf_table, share, beyond)
         images, *early = lax.optimization_barrier((images, *early))
         met_images = {k: swap(part, 2 * k, size) for k, part in zip(beyond, early)}
     give, keep, table, *parts_near = estep(
-        me, slab, top_index, images, planes, ctf_table, share, near
+        top_index, images, planes, ctf_table, share, near
     )
     if beyond:
         give, keep, met_images[beyond[-1]], *parts_near = lax.optimization_barrier(
@@ -619,7 +640,7 @@
         met_images[k] = swap(part, 2 * k, size) if k else part
     keep, *met_images = far(keep, *[met_images[k] for k in range(chips)])
     base, scale = count_planes(
-        slab, class_weight, inv_noise, orientations, slabs * local_planes, slabs
+        class_weight, inv_noise, orientations, slabs * local_planes, slabs
     )
     tables, bit = [table], 1
     while bit < slabs:
@@ -655,14 +676,10 @@
 
     items = tuple((side, k) for side, ks in enumerate(onward) for k in ks)
     sent = first_sums(items, own_w, sib_w, both_w, gather_images(items, keep, got, wide))
-    far_w = {0: both_w}
-    for side in (0, 1):
-        bit = orders[side][0]
-        far_w[bit] = deliver(side, onward[side], sent[side], bit)
+    arrived = [swap(sent[side], 2 * orders[side][0], size) for side in (0, 1)]
     both_w, _ = lax.optimization_barrier((both_w, sent[1]))
-    for k in range(1, chips):
-        if k not in far_w:
-            far_w[k] = swap(both_w, 2 * k, size)
+    others = [k for k in range(1, chips) if k not in (orders[0][0], orders[1][0])]
+    far_w = [swap(both_w, 2 * k, size) for k in others]
     sums.keywords["keep"], *met_images = lax.optimization_barrier((keep, *met_images))
     sent = compute(direct)
     for side in (0, 1):
@@ -672,7 +689,16 @@
         for place, k in enumerate(stay[side]):
             parts[side][k].append((kept[side], place))
 
-    met_images[0], _ = lax.optimization_barrier((met_images[0], sent[0]))
+    met_images[0], _, *arrived = lax.optimization_barrier(
+        (met_images[0], sent[0], *arrived, *far_w)
+    )
+    far_w = dict(zip(others, arrived[2:]))
+    far_w[0] = both_w
+    for side in (0, 1):
+        bit = orders[side][0]
+        far_w[bit] = arrived[side]
+        for place, k in enumerate(onward[side]):
+            parts[side][k ^ bit].append((arrived[side], place))
     met, for_sib = meet(ctf_table, [far_w[k] for k in range(chips)], met_images)
     sib_met = swap(for_sib, 1, size)
     own_planes = classes * local_planes
@@ -688,7 +714,10 @@
                 [sum(part[place, :, :wide] for part, place in parts[side].pop(k)) for k in ks]
             )
             deliver(side, ks, sent, bit)
-    out = finish(me, slab, index, met, sib_met, partner, parts[0][0], parts[1][0], share)
+    base, scale = prepare(
+        index, met, sib_met, [parts[side][0][:-1] for side in (0, 1)], share
+    )
+    out = finish(base, scale, parts[0][0][-1][0], parts[1][0][-1][0], partner)
     return out.reshape(classes, local_planes, share)
 
 

time: 54.3 us -> 54.1 us (level)
  waiting for transfers between devices: 12.9 us -> 12.2 us
    ppermute x13, waiting for transfers between devices: 12.2 us -> 11.5 us  [swap(): return lax.ppermute(array, 'img', [(one, one ^ bit) for one in range(size)])]
    pallas_call x2 -> x3, Pallas kernels: 2.61 us -> 3.06 us  [the longest x1 1.38 us: count_planes(): pl.pallas_call(functools.partial(count_kernel, slabs), in_specs=[vmem] *...]
  transfers between devices with their start and end apart: 16 -> 16, of which waited for: 8 -> 9; matrix products, arithmetic and copies ran while one was open for 1% -> 0% of each run, Pallas kernels for 31% -> 33%
where the time goes in v8:
time: 54.1 us; the launch traced here: 53.9 us
  starting transfers between devices  21.3 us (39%)
  Pallas kernels  19.9 us (37%)
  waiting for transfers between devices  12.2 us (23%)
    ppermute x13, starting transfers between devices, swap(): return lax.ppermute(array, 'img', [(one, one ^ bit) for one in range(size)])  15.3 us
    ppermute x13, waiting for transfers between devices, swap(): return lax.ppermute(array, 'img', [(one, one ^ bit) for one in range(size)])  11.5 us
    pallas_call x1, Pallas kernels, estep(): pl.pallas_call(functools.partial(estep_kernel, blocks, share, near), in_s...  9.08 us
    ppermute x2, starting transfers between devices, shards(): tables = [held, lax.ppermute(held, 'slab', pairs)]  4.41 us
    pallas_call x2, Pallas kernels, partial_sums(): pl.pallas_call(functools.partial(sums_kernel, items), in_specs=[vmem] * 2...  3.12 us
    pallas_call x1, Pallas kernels, meet(): pl.pallas_call(functools.partial(meet_kernel, len(weights)), out_shape=[j...  1.68 us
    ppermute x1, starting transfers between devices, shards(): lax.ppermute(met[own_planes:, :met_wide] + sib_met[own_planes:, :met_wide...  1.64 us
    pallas_call x1, Pallas kernels, count_planes(): pl.pallas_call(functools.partial(count_kernel, slabs), in_specs=[vmem] *...  1.38 us
  transfers between devices with their start and end apart: 16, of which 9 were waited for; matrix products, arithmetic and copies ran while one was open for 0% of the time, Pallas kernels for 33%

profile of v8, /device:TPU:0, one launch (start us, length us, event | category | flops | bytes accessed | tf_op | source)
XLA Modules:
  0.0 53.9 jit_solution(5675417978776204001)
XLA Ops:
  0.0 1.2 %early.1 = f32[64,1664]{1,0:T(8,128)S(1)} custom-call(s32[1,32768]{1,0:T(1,128)} %constant.5.clone.index_hbm, bf16[64,32768]{1,0:T(8,128)(2,1)} %image_hbm.2, f32[64,64]{1,0:T(8,128)} %ctf_ref.1), custom_call_target="tpu_custom_call" | custom-call | tf_op jit(solution)/shard_map/early/pallas_call | solution.py:272
  1.3 4.0 %collective-permute-start.3 = (f32[64,1664]{1,0:T(8,128)S(1)}, f32[64,1664]{1,0:T(8,128)S(1)}, u32[]{:S(2)}, u32[]{:S(2)}) collective-permute-start(f32[64,1664]{1,0:T(8,128)S(1)} %early.1), channel_id=1, source_target_pairs={{0,24},{4,28},{8,16},{12,20},{16,8},{20,12},{24,0},{28,4},{1,25},{... | collective-permute-start | bytes 1277960 | tf_op jit(solution)/shard_map/ppermute | solution.py:609
  5.2 9.1 %estep.1 = (f32[64,10240]{1,0:T(8,128)}, bf16[64,10240]{1,0:T(8,128)(2,1)}, f32[64,64]{1,0:T(8,128)S(1)}, bf16[64,1536]{1,0:T(8,128)(2,1)}, f32[64,1664]{1,0:T(8,128)}, /*index=5*/f32[64,1664]{1,0:T(8,128)S(1)}) custom-call(s32[1,16640]{1,0:T(1,128)} %constant.4.clone.index_hbm, bf16[64,32768]{1,0:T(8,128)(2,1)} %image_hbm.2, bf16[64,32768]{1,0:T(8,128)(2,1)} %bitcast.6, ...), custom_call_target="tpu_custom_call" | custom-call | tf_op jit(solution)/shard_map/estep/pallas_call | solution.py:197
  15.0 1.8 %collective-permute-start = (f32[64,64]{1,0:T(8,128)S(1)}, f32[64,64]{1,0:T(8,128)S(1)}, u32[]{:S(2)}, u32[]{:S(2)}) collective-permute-start(f32[64,64]{1,0:T(8,128)S(1)} %get-tuple-element.46), channel_id=1, source_target_pairs={{0,1},{1,0},{2,3},{3,2},{4,5},{5,4},{6,7},{7,6},{8,9},{9,8},{10,11... | collective-permute-start | bytes 49160 | tf_op jit(solution)/shard_map/ppermute | solution.py:651
  16.8 1.5 %collective-permute-start.5 = (f32[64,1664]{1,0:T(8,128)}, f32[64,1664]{1,0:T(8,128)}, u32[]{:S(2)}, u32[]{:S(2)}) collective-permute-start(f32[64,1664]{1,0:T(8,128)} %get-tuple-element.60), channel_id=1, source_target_pairs={{0,8},{4,12},{8,0},{12,4},{16,24},{20,28},{24,16},{28,20},{1,9},{5... | collective-permute-start | bytes 1277960 | tf_op jit(solution)/shard_map/ppermute | solution.py:609
  18.3 1.5 %collective-permute-start.6 = (f32[64,1664]{1,0:T(8,128)S(1)}, f32[64,1664]{1,0:T(8,128)}, u32[]{:S(2)}, u32[]{:S(2)}) collective-permute-start(f32[64,1664]{1,0:T(8,128)S(1)} %get-tuple-element.61), channel_id=1, source_target_pairs={{0,16},{4,20},{8,24},{12,28},{16,0},{20,4},{24,8},{28,12},{1,17},{... | collective-permute-start | bytes 1277960 | tf_op jit(solution)/shard_map/ppermute | solution.py:609
  19.9 2.6 %collective-permute-start.1 = (f32[64,128]{1,0:T(8,128)S(1)}, f32[64,128]{1,0:T(8,128)S(1)}, u32[]{:S(2)}, u32[]{:S(2)}) collective-permute-start(f32[64,128]{1,0:T(8,128)S(1)} %pad_maximum_fusion.refs_0_), channel_id=1, source_target_pairs={{0,2},{1,3},{2,0},{3,1},{4,6},{5,7},{6,4},{7,5},{8,10},{9,11},{10,... | collective-permute-start | bytes 98312 | tf_op jit(solution)/shard_map/ppermute | solution.py:651
  22.7 1.4 %count.1 = (f32[2,64,128]{2,1,0:T(8,128)S(1)}, f32[64,128]{1,0:T(8,128)S(1)}) custom-call(f32[1,2]{1,0:T(1,128)S(1)} %bitcast.4, f32[1,64]{1,0:T(1,128)S(1)} %bitcast.5, s32[64,128]{1,0:T(8,128)S(1)} %reshape.17.list_ref), custom_call_target="tpu_custom_call" | custom-call | tf_op jit(solution)/shard_map/count/pallas_call | solution.py:315
  24.0 0.7 %collective-permute-done.1.refs_1_ = f32[64,128]{1,0:T(8,128)S(1)} collective-permute-done((f32[64,128]{1,0:T(8,128)S(1)}, f32[64,128]{1,0:T(8,128)S(1)}, u32[]{:S(2)}, u32[]{:S(2)}) %collective-permute-start.1) | collective-permute-done | bytes 32800 | tf_op jit(solution)/shard_map/ppermute | solution.py:651
  25.2 1.1 %gather.1.image_ref = bf16[2,128,1280]{2,1,0:T(8,128)(2,1)S(1)} custom-call(bf16[64,10240]{1,0:T(8,128)(2,1)} %get-tuple-element.64.keep_hbm, f32[64,10240]{1,0:T(8,128)S(1)} %collective-permute-done.4.got_hbm), custom_call_target="tpu_custom_call" | custom-call | tf_op jit(solution)/shard_map/gather/pallas_call | solution.py:391
  26.7 0.9 %collective-permute-start.7 = (f32[1,64,1408]{2,1,0:T(8,128)S(1)}, f32[1,64,1408]{2,1,0:T(8,128)S(1)}, u32[]{:S(2)}, u32[]{:S(2)}) collective-permute-start(f32[1,64,1408]{2,1,0:T(8,128)S(1)} %get-tuple-element.66), channel_id=1, source_target_pairs={{0,8},{4,12},{8,0},{12,4},{16,24},{20,28},{24,16},{28,20},{1,9},{5... | collective-permute-start | bytes 1081352 | tf_op jit(solution)/shard_map/ppermute | solution.py:609
  27.6 1.5 %collective-permute-start.8 = (f32[1,64,1408]{2,1,0:T(8,128)S(1)}, f32[1,64,1408]{2,1,0:T(8,128)S(1)}, u32[]{:S(2)}, u32[]{:S(2)}) collective-permute-start(f32[1,64,1408]{2,1,0:T(8,128)S(1)} %get-tuple-element.57), channel_id=1, source_target_pairs={{0,16},{4,20},{8,24},{12,28},{16,0},{20,4},{24,8},{28,12},{1,17},{... | collective-permute-start | bytes 1081352 | tf_op jit(solution)/shard_map/ppermute | solution.py:609
  29.1 1.2 %collective-permute-start.9 = (f32[64,128]{1,0:T(8,128)S(1)}, f32[64,128]{1,0:T(8,128)S(1)}, u32[]{:S(2)}, u32[]{:S(2)}) collective-permute-start(f32[64,128]{1,0:T(8,128)S(1)} %get-tuple-element.58.both_w_ref.refs_0_), channel_id=1, source_target_pairs={{0,24},{4,28},{8,16},{12,20},{16,8},{20,12},{24,0},{28,4},{1,25},{... | collective-permute-start | bytes 98312 | tf_op jit(solution)/shard_map/ppermute | solution.py:609
  30.3 1.3 %sums.2 = (f32[1,64,1280]{2,1,0:T(8,128)S(1)}, f32[1,64,1280]{2,1,0:T(8,128)S(1)}) custom-call(f32[64,64]{1,0:T(8,128)S(1)} %get-tuple-element.48.own_w_ref, f32[64,64]{1,0:T(8,128)S(1)} %collective-permute-done.2.sib_w_ref, bf16[64,10240]{1,0:T(8,128)(2,1)} %get-tuple-element.64.keep_hbm, f32[64,10240]{1,0:T(8,128)S(1)} %collective-permute-done.4.got_hbm), custom_call_target="tpu_custom_call" | custom-call | tf_op jit(solution)/shard_map/sums/pallas_call | solution.py:463
  31.7 0.9 %collective-permute-start.11 = (f32[1,64,1280]{2,1,0:T(8,128)S(1)}, f32[1,64,1280]{2,1,0:T(8,128)S(1)}, u32[]{:S(2)}, u32[]{:S(2)}) collective-permute-start(f32[1,64,1280]{2,1,0:T(8,128)S(1)} %get-tuple-element.65), channel_id=1, source_target_pairs={{0,8},{4,12},{8,0},{12,4},{16,24},{20,28},{24,16},{28,20},{1,9},{5... | collective-permute-start | bytes 983048 | tf_op jit(solution)/shard_map/ppermute | solution.py:609
  32.5 1.5 %collective-permute-start.12 = (f32[1,64,1280]{2,1,0:T(8,128)S(1)}, f32[1,64,1280]{2,1,0:T(8,128)S(1)}, u32[]{:S(2)}, u32[]{:S(2)}) collective-permute-start(f32[1,64,1280]{2,1,0:T(8,128)S(1)} %get-tuple-element.77), channel_id=1, source_target_pairs={{0,16},{4,20},{8,24},{12,28},{16,0},{20,4},{24,8},{28,12},{1,17},{... | collective-permute-start | bytes 983048 | tf_op jit(solution)/shard_map/ppermute | solution.py:609
  34.1 1.8 %sums.3 = (f32[2,64,1280]{2,1,0:T(8,128)S(1)}, f32[2,64,1280]{2,1,0:T(8,128)S(1)}) custom-call(f32[64,64]{1,0:T(8,128)S(1)} %get-tuple-element.48.own_w_ref, f32[64,64]{1,0:T(8,128)S(1)} %collective-permute-done.2.sib_w_ref, bf16[64,10240]{1,0:T(8,128)(2,1)} %get-tuple-element.64.keep_hbm, f32[64,10240]{1,0:T(8,128)S(1)} %collective-permute-done.4.got_hbm), custom_call_target="tpu_custom_call" | custom-call | tf_op jit(solution)/shard_map/sums/pallas_call | solution.py:463
  35.8 3.2 %collective-permute-done.9.refs_3_ = f32[64,128]{1,0:T(8,128)S(1)} collective-permute-done((f32[64,128]{1,0:T(8,128)S(1)}, f32[64,128]{1,0:T(8,128)S(1)}, u32[]{:S(2)}, u32[]{:S(2)}) %collective-permute-start.9) | collective-permute-done | bytes 32800 | tf_op jit(solution)/shard_map/ppermute | solution.py:609
  39.6 1.7 %meet.1 = (f32[128,896]{1,0:T(8,128)S(1)}, f32[128,896]{1,0:T(8,128)S(1)}) custom-call(f32[64,64]{1,0:T(8,128)S(1)} %copy-done.1, f32[64,128]{1,0:T(8,128)S(1)} %get-tuple-element.58.both_w_ref.refs_0_, f32[1,64,1408]{2,1,0:T(8,128)S(1)} %collective-permute-done.7.refs_1_, f32[1,64,1408]{2,1,0:T(8,128)S(1)} %collective-permute-done.8.refs_2_, ...), custom_call_target="tpu_custom_call" | custom-call | tf_op jit(solution)/shard_map/meet/pallas_call | solution.py:508
  41.4 1.3 %collective-permute-start.14 = (f32[1,64,1280]{2,1,0:T(8,128)S(1)}, f32[1,64,1280]{2,1,0:T(8,128)S(1)}, u32[]{:S(2)}, u32[]{:S(2)}) collective-permute-start(f32[1,64,1280]{2,1,0:T(8,128)S(1)} %slice_add_fusion), channel_id=1, source_target_pairs={{0,8},{4,12},{8,0},{12,4},{16,24},{20,28},{24,16},{28,20},{1,9},{5... | collective-permute-start | bytes 983048 | tf_op jit(solution)/shard_map/ppermute | solution.py:609
  42.7 0.9 %collective-permute-start.13 = (f32[1,64,1280]{2,1,0:T(8,128)S(1)}, f32[1,64,1280]{2,1,0:T(8,128)S(1)}, u32[]{:S(2)}, u32[]{:S(2)}) collective-permute-start(f32[1,64,1280]{2,1,0:T(8,128)S(1)} %slice_add_fusion.1), channel_id=1, source_target_pairs={{0,16},{4,20},{8,24},{12,28},{16,0},{20,4},{24,8},{28,12},{1,17},{... | collective-permute-start | bytes 983048 | tf_op jit(solution)/shard_map/ppermute | solution.py:609
  43.6 1.6 %collective-permute-start.15 = (f32[64,768]{1,0:T(8,128)S(1)}, f32[64,768]{1,0:T(8,128)S(1)}, u32[]{:S(2)}, u32[]{:S(2)}) collective-permute-start(f32[64,768]{1,0:T(8,128)S(1)} %slice_add_fusion.2), channel_id=1, source_target_pairs={{0,1},{1,0},{2,3},{3,2},{4,5},{5,4},{6,7},{7,6},{8,9},{9,8},{10,11... | collective-permute-start | bytes 589832 | tf_op jit(solution)/shard_map/ppermute | solution.py:705
  46.4 5.8 %collective-permute-done.14.right_ref = f32[1,64,1280]{2,1,0:T(8,128)S(1)} collective-permute-done((f32[1,64,1280]{2,1,0:T(8,128)S(1)}, f32[1,64,1280]{2,1,0:T(8,128)S(1)}, u32[]{:S(2)}, u32[]{:S(2)}) %collective-permute-start.14) | collective-permute-done | bytes 327712 | tf_op jit(solution)/shard_map/ppermute | solution.py:609
  52.8 1.1 %finish.1 = f32[64,4096]{1,0:T(8,128)} custom-call(f32[64,4096]{1,0:T(8,128)S(1)} %get-tuple-element.79.base_ref, f32[64,4096]{1,0:T(8,128)S(1)} %get-tuple-element.80.scale_ref, f32[1,64,1280]{2,1,0:T(8,128)S(1)} %collective-permute-done.13.left_ref, f32[1,64,1280]{2,1,0:T(8,128)S(1)} %collective-permute-done.14.right_ref, ...), custom_call_target="tpu_custom_call" | custom-call | tf_op jit(solution)/shard_map/finish/pallas_call | solution.py:597
  (36 shorter events, 4.1 us)
Async XLA Ops:
  1.3 13.8 %collective-permute-start.3 = (f32[64,1664]{1,0:T(8,128)S(1)}, f32[64,1664]{1,0:T(8,128)S(1)}, u32[]{:S(2)}, u32[]{:S(2)}) collective-permute-start(f32[64,1664]{1,0:T(8,128)S(1)} %early.1), channel_id=1, source_target_pairs={{0,24},{4,28},{8,16},{12,20},{16,8},{20,12},{24,0},{28,4},{1,25},{... | collective-permute-start | bytes 1277960 | tf_op jit(solution)/shard_map/ppermute | solution.py:609
  5.2 17.3 %copy-start.5 = (s32[64,2,64]{2,1,0:T(2,128)S(1)}, s32[64,2,64]{2,1,0:T(2,128)}, u32[]{:S(2)}) copy-start(s32[64,2,64]{2,1,0:T(2,128)} %param.10) | copy-start | bytes 98308
  5.2 17.4 %copy-start.2 = (f32[2]{0:T(128)S(1)}, f32[2]{0:T(128)}, u32[]{:S(2)}) copy-start(f32[2]{0:T(128)} %param.13) | copy-start | bytes 28
  5.2 17.4 %copy-start.3 = (f32[64]{0:T(128)S(1)}, f32[64]{0:T(128)}, u32[]{:S(2)}) copy-start(f32[64]{0:T(128)} %param.12) | copy-start | bytes 772
  15.0 4.9 %copy-start.4 = (f32[64,1664]{1,0:T(8,128)}, f32[64,1664]{1,0:T(8,128)S(1)}, u32[]{:S(2)}) copy-start(f32[64,1664]{1,0:T(8,128)S(1)} %collective-permute-done.3.refs_7_) | copy-start | bytes 1277956
  15.0 10.2 %collective-permute-start.4 = (f32[64,10240]{1,0:T(8,128)}, f32[64,10240]{1,0:T(8,128)S(1)}, u32[]{:S(2)}, u32[]{:S(2)}) collective-permute-start(f32[64,10240]{1,0:T(8,128)} %get-tuple-element.56), channel_id=1, source_target_pairs={{0,4},{4,0},{8,12},{12,8},{16,20},{20,16},{24,28},{28,24},{1,5},{5... | collective-permute-start | bytes 7864328 | tf_op jit(solution)/shard_map/ppermute | solution.py:609
  15.0 4.8 %collective-permute-start = (f32[64,64]{1,0:T(8,128)S(1)}, f32[64,64]{1,0:T(8,128)S(1)}, u32[]{:S(2)}, u32[]{:S(2)}) collective-permute-start(f32[64,64]{1,0:T(8,128)S(1)} %get-tuple-element.46), channel_id=1, source_target_pairs={{0,1},{1,0},{2,3},{3,2},{4,5},{5,4},{6,7},{7,6},{8,9},{9,8},{10,11... | collective-permute-start | bytes 49160 | tf_op jit(solution)/shard_map/ppermute | solution.py:651
  16.8 13.5 %collective-permute-start.5 = (f32[64,1664]{1,0:T(8,128)}, f32[64,1664]{1,0:T(8,128)}, u32[]{:S(2)}, u32[]{:S(2)}) collective-permute-start(f32[64,1664]{1,0:T(8,128)} %get-tuple-element.60), channel_id=1, source_target_pairs={{0,8},{4,12},{8,0},{12,4},{16,24},{20,28},{24,16},{28,20},{1,9},{5... | collective-permute-start | bytes 1277960 | tf_op jit(solution)/shard_map/ppermute | solution.py:609
  18.3 12.0 %collective-permute-start.6 = (f32[64,1664]{1,0:T(8,128)S(1)}, f32[64,1664]{1,0:T(8,128)}, u32[]{:S(2)}, u32[]{:S(2)}) collective-permute-start(f32[64,1664]{1,0:T(8,128)S(1)} %get-tuple-element.61), channel_id=1, source_target_pairs={{0,16},{4,20},{8,24},{12,28},{16,0},{20,4},{24,8},{28,12},{1,17},{... | collective-permute-start | bytes 1277960 | tf_op jit(solution)/shard_map/ppermute | solution.py:609
  19.9 4.9 %collective-permute-start.1 = (f32[64,128]{1,0:T(8,128)S(1)}, f32[64,128]{1,0:T(8,128)S(1)}, u32[]{:S(2)}, u32[]{:S(2)}) collective-permute-start(f32[64,128]{1,0:T(8,128)S(1)} %pad_maximum_fusion.refs_0_), channel_id=1, source_target_pairs={{0,2},{1,3},{2,0},{3,1},{4,6},{5,7},{6,4},{7,5},{8,10},{9,11},{10,... | collective-permute-start | bytes 98312 | tf_op jit(solution)/shard_map/ppermute | solution.py:651
  25.2 1.3 %collective-permute-start.2 = (f32[64,64]{1,0:T(8,128)S(1)}, f32[64,64]{1,0:T(8,128)S(1)}, u32[]{:S(2)}, u32[]{:S(2)}) collective-permute-start(f32[64,64]{1,0:T(8,128)S(1)} %get-tuple-element.48.own_w_ref), channel_id=1, source_target_pairs={{0,4},{4,0},{8,12},{12,8},{16,20},{20,16},{24,28},{28,24},{1,5},{5... | collective-permute-start | bytes 49160 | tf_op jit(solution)/shard_map/ppermute | solution.py:609
  26.7 12.3 %collective-permute-start.7 = (f32[1,64,1408]{2,1,0:T(8,128)S(1)}, f32[1,64,1408]{2,1,0:T(8,128)S(1)}, u32[]{:S(2)}, u32[]{:S(2)}) collective-permute-start(f32[1,64,1408]{2,1,0:T(8,128)S(1)} %get-tuple-element.66), channel_id=1, source_target_pairs={{0,8},{4,12},{8,0},{12,4},{16,24},{20,28},{24,16},{28,20},{1,9},{5... | collective-permute-start | bytes 1081352 | tf_op jit(solution)/shard_map/ppermute | solution.py:609
  27.6 12.0 %collective-permute-start.8 = (f32[1,64,1408]{2,1,0:T(8,128)S(1)}, f32[1,64,1408]{2,1,0:T(8,128)S(1)}, u32[]{:S(2)}, u32[]{:S(2)}) collective-permute-start(f32[1,64,1408]{2,1,0:T(8,128)S(1)} %get-tuple-element.57), channel_id=1, source_target_pairs={{0,16},{4,20},{8,24},{12,28},{16,0},{20,4},{24,8},{28,12},{1,17},{... | collective-permute-start | bytes 1081352 | tf_op jit(solution)/shard_map/ppermute | solution.py:609
  29.1 9.9 %collective-permute-start.9 = (f32[64,128]{1,0:T(8,128)S(1)}, f32[64,128]{1,0:T(8,128)S(1)}, u32[]{:S(2)}, u32[]{:S(2)}) collective-permute-start(f32[64,128]{1,0:T(8,128)S(1)} %get-tuple-element.58.both_w_ref.refs_0_), channel_id=1, source_target_pairs={{0,24},{4,28},{8,16},{12,20},{16,8},{20,12},{24,0},{28,4},{1,25},{... | collective-permute-start | bytes 98312 | tf_op jit(solution)/shard_map/ppermute | solution.py:609
  31.6 7.9 %copy-start.1 = (f32[64,64]{1,0:T(8,128)S(1)}, f32[64,64]{1,0:T(8,128)}, u32[]{:S(2)}) copy-start(f32[64,64]{1,0:T(8,128)} %ctf_ref.1) | copy-start | bytes 49156
  31.7 14.1 %collective-permute-start.11 = (f32[1,64,1280]{2,1,0:T(8,128)S(1)}, f32[1,64,1280]{2,1,0:T(8,128)S(1)}, u32[]{:S(2)}, u32[]{:S(2)}) collective-permute-start(f32[1,64,1280]{2,1,0:T(8,128)S(1)} %get-tuple-element.65), channel_id=1, source_target_pairs={{0,8},{4,12},{8,0},{12,4},{16,24},{20,28},{24,16},{28,20},{1,9},{5... | collective-permute-start | bytes 983048 | tf_op jit(solution)/shard_map/ppermute | solution.py:609
  32.5 13.3 %collective-permute-start.12 = (f32[1,64,1280]{2,1,0:T(8,128)S(1)}, f32[1,64,1280]{2,1,0:T(8,128)S(1)}, u32[]{:S(2)}, u32[]{:S(2)}) collective-permute-start(f32[1,64,1280]{2,1,0:T(8,128)S(1)} %get-tuple-element.77), channel_id=1, source_target_pairs={{0,16},{4,20},{8,24},{12,28},{16,0},{20,4},{24,8},{28,12},{1,17},{... | collective-permute-start | bytes 983048 | tf_op jit(solution)/shard_map/ppermute | solution.py:609
  35.8 10.0 %copy-start = (s32[1,32768]{1,0:T(1,128)S(1)}, s32[1,32768]{1,0:T(1,128)}, u32[]{:S(2)}) copy-start(s32[1,32768]{1,0:T(1,128)} %constant.5.clone.index_hbm) | copy-start | bytes 393220
  41.3 2.3 %collective-permute-start.10 = (f32[128,896]{1,0:T(8,128)S(1)}, f32[128,896]{1,0:T(8,128)S(1)}, u32[]{:S(2)}, u32[]{:S(2)}) collective-permute-start(f32[128,896]{1,0:T(8,128)S(1)} %get-tuple-element.75), channel_id=1, source_target_pairs={{0,4},{4,0},{8,12},{12,8},{16,20},{20,16},{24,28},{28,24},{1,5},{5... | collective-permute-start | bytes 1376264 | tf_op jit(solution)/shard_map/ppermute | solution.py:609
  41.4 10.8 %collective-permute-start.14 = (f32[1,64,1280]{2,1,0:T(8,128)S(1)}, f32[1,64,1280]{2,1,0:T(8,128)S(1)}, u32[]{:S(2)}, u32[]{:S(2)}) collective-permute-start(f32[1,64,1280]{2,1,0:T(8,128)S(1)} %slice_add_fusion), channel_id=1, source_target_pairs={{0,8},{4,12},{8,0},{12,4},{16,24},{20,28},{24,16},{28,20},{1,9},{5... | collective-permute-start | bytes 983048 | tf_op jit(solution)/shard_map/ppermute | solution.py:609
  42.7 10.0 %collective-permute-start.13 = (f32[1,64,1280]{2,1,0:T(8,128)S(1)}, f32[1,64,1280]{2,1,0:T(8,128)S(1)}, u32[]{:S(2)}, u32[]{:S(2)}) collective-permute-start(f32[1,64,1280]{2,1,0:T(8,128)S(1)} %slice_add_fusion.1), channel_id=1, source_target_pairs={{0,16},{4,20},{8,24},{12,28},{16,0},{20,4},{24,8},{28,12},{1,17},{... | collective-permute-start | bytes 983048 | tf_op jit(solution)/shard_map/ppermute | solution.py:609
  43.6 9.1 %collective-permute-start.15 = (f32[64,768]{1,0:T(8,128)S(1)}, f32[64,768]{1,0:T(8,128)S(1)}, u32[]{:S(2)}, u32[]{:S(2)}) collective-permute-start(f32[64,768]{1,0:T(8,128)S(1)} %slice_add_fusion.2), channel_id=1, source_target_pairs={{0,1},{1,0},{2,3},{3,2},{4,5},{5,4},{6,7},{7,6},{8,9},{9,8},{10,11... | collective-permute-start | bytes 589832 | tf_op jit(solution)/shard_map/ppermute | solution.py:705

commit v9 on v8

--- a/solution.py
+++ b/solution.py
@@ -260,10 +260,11 @@
                 ctf = spread(table, index[place, other, :, cut])
                 part = (image[place, other, :, cut].astype(F32) * ctf).astype(BF16)
                 out_ref[:, other * met + start : other * met + start + LANES] = part.astype(F32)
-        out_ref[:, 2 * met :] = table
-
-
-def early_images(index, images, ctf_table, share, beyond):
+        if out_ref.shape[1] > 2 * met:
+            out_ref[:, 2 * met :] = table
+
+
+def early_images(index, images, ctf_table, share, beyond, relayed):
     rows = images.shape[0]
     met = split_share(share)[1]
     number = len(beyond)
@@ -273,7 +274,9 @@
         functools.partial(early_kernel, share, beyond),
         in_specs=[hbm, hbm, hbm],
         out_specs=[vmem] * number,
-        out_shape=[jax.ShapeDtypeStruct((rows, 2 * met + LANES), F32)] * number,
+        out_shape=[
+            jax.ShapeDtypeStruct((rows, 2 * met + LANES * (k != relayed)), F32) for k in beyond
+        ],
         scratch_shapes=[
             pltpu.VMEM((number, 2, 1, met), jnp.int32),
             pltpu.VMEM((number, 2, rows, met), BF16),
@@ -432,9 +435,11 @@
     )(own_w, sib_w, both_w, images)
 
 
-def sums_kernel(items, own_w_ref, sib_w_ref, keep_hbm, got_hbm, *refs):
+def sums_kernel(items, relay, own_w_ref, sib_w_ref, keep_hbm, got_hbm, *refs):
+    if relay:
+        ctf_hbm, refs = refs[0], refs[1:]
     outs = refs[: len(items)]
-    keep, got, in_sem = refs[len(items) :]
+    keep, got, in_sem = refs[len(items) : len(items) + 3]
     number, _, wide = keep.shape
     places = [(slot, k, side) for side, ks in enumerate(items) for slot, k in enumerate(ks)]
     incoming = []
@@ -446,74 +451,115 @@
         ])
         for copy in incoming[-1]:
             copy.start()
+    if relay:
+        ctf, ctf_sem = refs[-2:]
+        fetch = pltpu.make_async_copy(ctf_hbm.at[:, ctf_hbm.shape[1] - LANES :], ctf, ctf_sem)
+        fetch.start()
     weights = jnp.concatenate([own_w_ref[...], sib_w_ref[...]], axis=1).astype(BF16)
     for place, (slot, k, side) in enumerate(places):
         for copy in incoming[place]:
             copy.wait()
         images = jnp.concatenate([keep[place], got[place].astype(BF16)], axis=0)
-        outs[side][slot] = jnp.dot(weights, images, preferred_element_type=F32)
-
-
-def partial_sums(items, own_w, sib_w, keep, got, wide):
+        outs[side][slot, :, :wide] = jnp.dot(weights, images, preferred_element_type=F32)
+    if relay:
+        fetch.wait()
+        for slot in range(outs[0].shape[0]):
+            outs[0][slot, :, wide:] = ctf[...]
+
+
+def partial_sums(items, own_w, sib_w, keep, got, wide, relay=()):
     rows = keep.shape[0]
     planes = own_w.shape[0]
     number = sum(len(ks) for ks in items)
     held = pl.BlockSpec(memory_space=pl.ANY)
     vmem = pl.BlockSpec(memory_space=pltpu.VMEM)
     return pl.pallas_call(
-        functools.partial(sums_kernel, items),
-        in_specs=[vmem] * 2 + [held] * 2,
+        functools.partial(sums_kernel, items, bool(relay)),
+        in_specs=[vmem] * 2 + [held] * (2 + len(relay)),
         out_specs=[vmem] * 2,
-        out_shape=[jax.ShapeDtypeStruct((len(ks), planes, wide), F32) for ks in items],
+        out_shape=[
+            jax.ShapeDtypeStruct((len(ks), planes, wide + extra), F32)
+            for ks, extra in zip(items, (LANES * len(relay), 0))
+        ],
         scratch_shapes=[
             pltpu.VMEM((number, rows, wide), BF16),
             pltpu.VMEM((number, rows, wide), F32),
             pltpu.SemaphoreType.DMA((number, 2)),
-        ],
+        ]
+        + [pltpu.VMEM((rows, LANES), F32), pltpu.SemaphoreType.DMA(())] * len(relay),
         compiler_params=params(12),
         name="sums",
-    )(own_w, sib_w, keep, got)
-
-
-def meet_kernel(chips, ctf_ref, *refs):
+    )(own_w, sib_w, keep, got, *relay)
+
+
+def meet_kernel(chips, *refs):
     weight_refs, image_refs, outs = refs[:chips], refs[chips : 2 * chips], refs[2 * chips :]
-    planes, width = outs[0].shape
-    met = width - LANES
-    weights, ctf = [], []
+    planes, met = outs[0].shape
+    weights = []
     for ref in weight_refs:
         wide = ref.shape[-1]
         part = ref[:, wide - planes :] if len(ref.shape) == 2 else ref[0, :, wide - planes :]
         weights.append(part.astype(BF16))
     weights = jnp.concatenate(weights, axis=0)
-
-    def sums(parts):
-        return lax.dot_general(
-            weights,
-            jnp.concatenate(parts, axis=0),
-            (((0,), (0,)), ((), ())),
-            preferred_element_type=F32,
-        )
-
-    ctf = [lanes_wide(ctf_ref[...])] + [ref[:, 2 * met :] for ref in image_refs[1:]]
-    shells = sums([(part * part).astype(BF16) for part in ctf])
     for other, out_ref in enumerate(outs):
         cut = slice(other * met, (other + 1) * met)
-        out_ref[:, :met] = sums([ref[:, cut].astype(BF16) for ref in image_refs])
-        out_ref[:, met:] = shells
-
-
-def meet(ctf_table, weights, images):
+        images = jnp.concatenate([ref[:, cut].astype(BF16) for ref in image_refs], axis=0)
+        out_ref[...] = lax.dot_general(
+            weights, images, (((0,), (0,)), ((), ())), preferred_element_type=F32
+        )
+
+
+def meet(weights, images):
     met = images[0].shape[1] // 2
     planes = weights[0].shape[1]
     return pl.pallas_call(
         functools.partial(meet_kernel, len(weights)),
-        out_shape=[jax.ShapeDtypeStruct((planes, met + LANES), F32)] * 2,
+        out_shape=[jax.ShapeDtypeStruct((planes, met), F32)] * 2,
         compiler_params=params(16),
         name="meet",
-    )(ctf_table, *weights, *images)
-
-
-def prepare_kernel(places, index_hbm, met_ref, sib_met_ref, *refs):
+    )(*weights, *images)
+
+
+def shells_kernel(chips, ctf_ref, *refs):
+    weight_refs, tail_refs, out_ref = refs[:chips], refs[chips:-1], refs[-1]
+    planes = out_ref.shape[0]
+    weights = []
+    for ref in weight_refs:
+        cut = slice(ref.shape[-1] - 2 * planes, ref.shape[-1] - planes)
+        weights.append((ref[:, cut] if len(ref.shape) == 2 else ref[0, :, cut]).astype(BF16))
+    ctf = [lanes_wide(ctf_ref[...])]
+    ctf += [ref[...] if len(ref.shape) == 2 else ref[0] for ref in tail_refs]
+    squares = jnp.concatenate([(part * part).astype(BF16) for part in ctf], axis=0)
+    out_ref[...] = lax.dot_general(
+        jnp.concatenate(weights, axis=0), squares, (((0,), (0,)), ((), ())), preferred_element_type=F32
+    )
+
+
+def shell_sums(ctf_table, weights, tails):
+    rows = ctf_table.shape[0]
+    planes = weights[0].shape[1] // 2
+
+    def whole(array):
+        return pl.BlockSpec(array.shape, lambda step: (0,) * len(array.shape))
+
+    def last(array):
+        place = array.shape[-1] // LANES - 1
+        if len(array.shape) == 2:
+            return pl.BlockSpec((rows, LANES), lambda step: (0, place))
+        return pl.BlockSpec((1, rows, LANES), lambda step: (0, 0, place))
+
+    return pl.pallas_call(
+        functools.partial(shells_kernel, len(weights)),
+        grid=(1,),
+        in_specs=[whole(ctf_table)] + [whole(part) for part in weights] + [last(part) for part in tails],
+        out_specs=pl.BlockSpec((planes, LANES), lambda step: (0, 0)),
+        out_shape=jax.ShapeDtypeStruct((planes, LANES), F32),
+        compiler_params=params(8),
+        name="shells",
+    )(ctf_table, *weights, *tails)
+
+
+def prepare_kernel(places, index_hbm, met_ref, sib_met_ref, shell_ref, sib_shell_ref, *refs):
     total = sum(map(len, places))
     parts, (base_ref, scale_ref, index, in_sem) = refs[:total], refs[total:]
     planes, share = base_ref.shape
@@ -526,21 +572,21 @@
         refs = list(zip(parts[start : start + len(numbers)], numbers))
         start += len(numbers)
         base_ref[:, side * wide : (side + 1) * wide] = functools.reduce(
-            jnp.add, [ref[place] for ref, place in refs]
+            jnp.add, [ref[place, :, :wide] for ref, place in refs]
         )
     half = lax.rem(lax.axis_index("slab"), 2)
     own = pl.ds(pl.multiple_of(2 * wide + half * met, LANES), met)
     other = pl.ds(pl.multiple_of(2 * wide + (1 - half) * met, LANES), met)
     base_ref[:, own] = met_ref[:planes, :met] + sib_met_ref[:planes, :met]
     base_ref[:, other] = jnp.zeros((planes, met), F32)
-    shells = met_ref[:planes, met:] + sib_met_ref[:planes, met:]
+    shells = shell_ref[...] + sib_shell_ref[...]
     fetch.wait()
     for start in range(0, share, LANES):
         cut = slice(start, start + LANES)
         scale_ref[:, cut] = 1.0 / (spread(shells, index[:, cut]) + 1.0)
 
 
-def prepare(index, met, sib_met, sides, share):
+def prepare(index, met, sib_met, shells, sib_shells, sides, share):
     planes = met.shape[0] // 2
     held = pl.BlockSpec(memory_space=pl.ANY)
     vmem = pl.BlockSpec(memory_space=pltpu.VMEM)
@@ -548,13 +594,13 @@
     parts = [part for side in sides for part, _ in side]
     return pl.pallas_call(
         functools.partial(prepare_kernel, places),
-        in_specs=[held] + [vmem] * (2 + len(parts)),
+        in_specs=[held] + [vmem] * (4 + len(parts)),
         out_specs=[vmem, vmem],
         out_shape=[jax.ShapeDtypeStruct((planes, share), F32)] * 2,
         scratch_shapes=[pltpu.VMEM((1, share), jnp.int32), pltpu.SemaphoreType.DMA(())],
         compiler_params=params(8),
         name="prepare",
-    )(index, met, sib_met, *parts)
+    )(index, met, sib_met, shells, sib_shells, *parts)
 
 
 def finish_kernel(base_ref, scale_ref, left_ref, right_ref, partner_ref, out_hbm, out, out_sem):
@@ -624,9 +670,10 @@
 
     beyond = tuple(k for k in range(chips) if k & (k - 1))
     near = tuple(k for k in range(chips) if k not in beyond)
+    relayed = 1 | chips // 2
     met_images = {}
     if beyond:
-        early = early_images(index, images, ctf_table, share, beyond)
+        early = early_images(index, images, ctf_table, share, beyond, relayed)
         images, *early = lax.optimization_barrier((images, *early))
         met_images = {k: swap(part, 2 * k, size) for k, part in zip(beyond, early)}
     give, keep, table, *parts_near = estep(
@@ -671,8 +718,8 @@
             parts[side][k ^ bit].append((arrived, place))
         return arrived
 
-    def compute(groups):
-        return sums(tuple(tuple(ks) for ks in groups))
+    def compute(groups, relay=()):
+        return sums(tuple(tuple(ks) for ks in groups), relay=relay)
 
     items = tuple((side, k) for side, ks in enumerate(onward) for k in ks)
     sent = first_sums(items, own_w, sib_w, both_w, gather_images(items, keep, got, wide))
@@ -681,9 +728,8 @@
     others = [k for k in range(1, chips) if k not in (orders[0][0], orders[1][0])]
     far_w = [swap(both_w, 2 * k, size) for k in others]
     sums.keywords["keep"], *met_images = lax.optimization_barrier((keep, *met_images))
-    sent = compute(direct)
-    for side in (0, 1):
-        deliver(side, direct[side], sent[side], orders[side][0])
+    sent = compute(direct, (met_images[chips // 2],))
+    relays = [deliver(side, direct[side], sent[side], orders[side][0]) for side in (0, 1)]
     kept = compute(stay)
     for side in (0, 1):
         for place, k in enumerate(stay[side]):
@@ -699,7 +745,11 @@
         far_w[bit] = arrived[side]
         for place, k in enumerate(onward[side]):
             parts[side][k ^ bit].append((arrived[side], place))
-    met, for_sib = meet(ctf_table, [far_w[k] for k in range(chips)], met_images)
+    weights = [far_w[k] for k in range(chips)]
+    met, for_sib = meet(weights, met_images)
+    tails = [relays[0] if k == relayed else met_images[k] for k in range(1, chips)]
+    shells = shell_sums(ctf_table, weights, tails)
+    sib_shells = swap(shells, 1, size)
     sib_met = swap(for_sib, 1, size)
     own_planes = classes * local_planes
     partner = lax.ppermute(
@@ -715,7 +765,7 @@
             )
             deliver(side, ks, sent, bit)
     base, scale = prepare(
-        index, met, sib_met, [parts[side][0][:-1] for side in (0, 1)], share
+        index, met, sib_met, shells, sib_shells, [parts[side][0][:-1] for side in (0, 1)], share
     )
     out = finish(base, scale, parts[0][0][-1][0], parts[1][0][-1][0], partner)
     return out.reshape(classes, local_planes, share)

time: 54.1 us -> 53.8 us (level)
  waiting for transfers between devices: 12.2 us -> 9.92 us
  Pallas kernels: 19.9 us -> 20.9 us
  local copies, waits for them, and re-layouts: 0.13 us -> 0.96 us
    ppermute x13 -> x14, waiting for transfers between devices: 11.5 us -> 9.91 us  [swap(): return lax.ppermute(array, 'img', [(one, one ^ bit) for one in range(size)])]
    pallas_call x2 -> x3, Pallas kernels: 3.12 us -> 4.09 us  [the longest x2 3.13 us: partial_sums(): pl.pallas_call(functools.partial(sums_kernel, items, bool(relay)), in_spe...]
    reshape x1, local copies, waits for them, and re-layouts: 0.1 us -> 0.94 us  [count_planes(): orientations.reshape(rows, classes * each)]
    ppermute x2, waiting for transfers between devices: 0.75 us -> 0.01 us  [shards(): tables = [held, lax.ppermute(held, 'slab', pairs)]]
    ppermute x13 -> x14, starting transfers between devices: 15.3 us -> 15.4 us  [swap(): return lax.ppermute(array, 'img', [(one, one ^ bit) for one in range(size)])]
  transfers between devices with their start and end apart: 16 -> 17, of which waited for: 9 -> 7; matrix products, arithmetic and copies ran while one was open for 0% -> 2% of each run, Pallas kernels for 33% -> 35%
where the time goes in v9:
time: 53.8 us; the launch traced here: 53.4 us
  starting transfers between devices  21.3 us (40%)
  Pallas kernels  20.9 us (39%)
  waiting for transfers between devices  9.92 us (18%)
  local copies, waits for them, and re-layouts  0.96 us (2%)
    ppermute x14, starting transfers between devices, swap(): return lax.ppermute(array, 'img', [(one, one ^ bit) for one in range(size)])  15.4 us
    ppermute x14, waiting for transfers between devices, swap(): return lax.ppermute(array, 'img', [(one, one ^ bit) for one in range(size)])  9.91 us
    pallas_call x1, Pallas kernels, estep(): pl.pallas_call(functools.partial(estep_kernel, blocks, share, near), in_s...  9.08 us
    ppermute x2, starting transfers between devices, shards(): tables = [held, lax.ppermute(held, 'slab', pairs)]  4.29 us
    pallas_call x2, Pallas kernels, partial_sums(): pl.pallas_call(functools.partial(sums_kernel, items, bool(relay)), in_spe...  3.13 us
    ppermute x1, starting transfers between devices, shards(): lax.ppermute(met[own_planes:, :met_wide] + sib_met[own_planes:, :met_wide...  1.64 us
    pallas_call x1, Pallas kernels, meet(): pl.pallas_call(functools.partial(meet_kernel, len(weights)), out_shape=[j...  1.63 us
    pallas_call x1, Pallas kernels, count_planes(): pl.pallas_call(functools.partial(count_kernel, slabs), in_specs=[vmem] *...  1.39 us
  transfers between devices with their start and end apart: 17, of which 7 were waited for; matrix products, arithmetic and copies ran while one was open for 2% of the time, Pallas kernels for 35%

profile of v9, /device:TPU:0, one launch (start us, length us, event | category | flops | bytes accessed | tf_op | source)
XLA Modules:
  0.0 53.4 jit_solution(13682367609348189048)
XLA Ops:
  0.0 1.2 %early.1 = f32[64,1536]{1,0:T(8,128)S(1)} custom-call(s32[1,32768]{1,0:T(1,128)} %constant.5.clone.index_hbm, bf16[64,32768]{1,0:T(8,128)(2,1)} %image_hbm.2, f32[64,64]{1,0:T(8,128)} %ctf_ref.1), custom_call_target="tpu_custom_call" | custom-call | tf_op jit(solution)/shard_map/early/pallas_call | solution.py:273
  1.3 4.0 %collective-permute-start.3 = (f32[64,1536]{1,0:T(8,128)S(1)}, f32[64,1536]{1,0:T(8,128)S(1)}, u32[]{:S(2)}, u32[]{:S(2)}) collective-permute-start(f32[64,1536]{1,0:T(8,128)S(1)} %early.1), channel_id=1, source_target_pairs={{0,24},{4,28},{8,16},{12,20},{16,8},{20,12},{24,0},{28,4},{1,25},{... | collective-permute-start | bytes 1179656 | tf_op jit(solution)/shard_map/ppermute | solution.py:655
  5.2 9.1 %estep.1 = (f32[64,10240]{1,0:T(8,128)}, bf16[64,10240]{1,0:T(8,128)(2,1)}, f32[64,64]{1,0:T(8,128)S(1)}, bf16[64,1536]{1,0:T(8,128)(2,1)}, f32[64,1664]{1,0:T(8,128)}, /*index=5*/f32[64,1664]{1,0:T(8,128)S(1)}) custom-call(s32[1,16640]{1,0:T(1,128)} %constant.4.clone.index_hbm, bf16[64,32768]{1,0:T(8,128)(2,1)} %image_hbm.2, bf16[64,32768]{1,0:T(8,128)(2,1)} %bitcast.6, ...), custom_call_target="tpu_custom_call" | custom-call | tf_op jit(solution)/shard_map/estep/pallas_call | solution.py:197
  14.4 1.7 %collective-permute-start = (f32[64,64]{1,0:T(8,128)S(1)}, f32[64,64]{1,0:T(8,128)S(1)}, u32[]{:S(2)}, u32[]{:S(2)}) collective-permute-start(f32[64,64]{1,0:T(8,128)S(1)} %get-tuple-element.46), channel_id=1, source_target_pairs={{0,1},{1,0},{2,3},{3,2},{4,5},{5,4},{6,7},{7,6},{8,9},{9,8},{10,11... | collective-permute-start | bytes 49160 | tf_op jit(solution)/shard_map/ppermute | solution.py:698
  16.1 1.5 %collective-permute-start.5 = (f32[64,1664]{1,0:T(8,128)}, f32[64,1664]{1,0:T(8,128)}, u32[]{:S(2)}, u32[]{:S(2)}) collective-permute-start(f32[64,1664]{1,0:T(8,128)} %get-tuple-element.60), channel_id=1, source_target_pairs={{0,8},{4,12},{8,0},{12,4},{16,24},{20,28},{24,16},{28,20},{1,9},{5... | collective-permute-start | bytes 1277960 | tf_op jit(solution)/shard_map/ppermute | solution.py:655
  17.6 1.5 %collective-permute-start.6 = (f32[64,1664]{1,0:T(8,128)S(1)}, f32[64,1664]{1,0:T(8,128)}, u32[]{:S(2)}, u32[]{:S(2)}) collective-permute-start(f32[64,1664]{1,0:T(8,128)S(1)} %get-tuple-element.61), channel_id=1, source_target_pairs={{0,16},{4,20},{8,24},{12,28},{16,0},{20,4},{24,8},{28,12},{1,17},{... | collective-permute-start | bytes 1277960 | tf_op jit(solution)/shard_map/ppermute | solution.py:655
  19.2 2.6 %collective-permute-start.1 = (f32[64,128]{1,0:T(8,128)S(1)}, f32[64,128]{1,0:T(8,128)S(1)}, u32[]{:S(2)}, u32[]{:S(2)}) collective-permute-start(f32[64,128]{1,0:T(8,128)S(1)} %pad_maximum_fusion.refs_0_), channel_id=1, source_target_pairs={{0,2},{1,3},{2,0},{3,1},{4,6},{5,7},{6,4},{7,5},{8,10},{9,11},{10,... | collective-permute-start | bytes 98312 | tf_op jit(solution)/shard_map/ppermute | solution.py:698
  21.8 0.9 %reshape.17.list_ref = s32[64,128]{1,0:T(8,128)S(1)} reshape(s32[64,2,64]{2,1,0:T(2,128)} %param.10) | data formatting | bytes 65536 | tf_op jit(solution)/shard_map/reshape | solution.py:331
  22.7 1.4 %count.1 = (f32[2,64,128]{2,1,0:T(8,128)S(1)}, f32[64,128]{1,0:T(8,128)S(1)}) custom-call(f32[1,2]{1,0:T(1,128)S(1)} %bitcast.4, f32[1,64]{1,0:T(1,128)S(1)} %bitcast.5, s32[64,128]{1,0:T(8,128)S(1)} %reshape.17.list_ref), custom_call_target="tpu_custom_call" | custom-call | tf_op jit(solution)/shard_map/count/pallas_call | solution.py:318
  24.6 1.1 %gather.1.image_ref = bf16[2,128,1280]{2,1,0:T(8,128)(2,1)S(1)} custom-call(bf16[64,10240]{1,0:T(8,128)(2,1)} %get-tuple-element.64.keep_hbm, f32[64,10240]{1,0:T(8,128)S(1)} %collective-permute-done.4.got_hbm), custom_call_target="tpu_custom_call" | custom-call | tf_op jit(solution)/shard_map/gather/pallas_call | solution.py:394
  26.1 0.9 %collective-permute-start.7 = (f32[1,64,1408]{2,1,0:T(8,128)S(1)}, f32[1,64,1408]{2,1,0:T(8,128)S(1)}, u32[]{:S(2)}, u32[]{:S(2)}) collective-permute-start(f32[1,64,1408]{2,1,0:T(8,128)S(1)} %get-tuple-element.67), channel_id=1, source_target_pairs={{0,8},{4,12},{8,0},{12,4},{16,24},{20,28},{24,16},{28,20},{1,9},{5... | collective-permute-start | bytes 1081352 | tf_op jit(solution)/shard_map/ppermute | solution.py:655
  27.0 1.5 %collective-permute-start.8 = (f32[1,64,1408]{2,1,0:T(8,128)S(1)}, f32[1,64,1408]{2,1,0:T(8,128)S(1)}, u32[]{:S(2)}, u32[]{:S(2)}) collective-permute-start(f32[1,64,1408]{2,1,0:T(8,128)S(1)} %get-tuple-element.57), channel_id=1, source_target_pairs={{0,16},{4,20},{8,24},{12,28},{16,0},{20,4},{24,8},{28,12},{1,17},{... | collective-permute-start | bytes 1081352 | tf_op jit(solution)/shard_map/ppermute | solution.py:655
  28.5 1.2 %collective-permute-start.9 = (f32[64,128]{1,0:T(8,128)S(1)}, f32[64,128]{1,0:T(8,128)S(1)}, u32[]{:S(2)}, u32[]{:S(2)}) collective-permute-start(f32[64,128]{1,0:T(8,128)S(1)} %get-tuple-element.58.both_w_ref.refs_0_), channel_id=1, source_target_pairs={{0,24},{4,28},{8,16},{12,20},{16,8},{20,12},{24,0},{28,4},{1,25},{... | collective-permute-start | bytes 98312 | tf_op jit(solution)/shard_map/ppermute | solution.py:655
  29.7 1.4 %sums.2 = (f32[1,64,1408]{2,1,0:T(8,128)S(1)}, f32[1,64,1280]{2,1,0:T(8,128)S(1)}) custom-call(f32[64,64]{1,0:T(8,128)S(1)} %get-tuple-element.48.own_w_ref, f32[64,64]{1,0:T(8,128)S(1)} %collective-permute-done.2.sib_w_ref, bf16[64,10240]{1,0:T(8,128)(2,1)} %get-tuple-element.64.keep_hbm, f32[64,10240]{1,0:T(8,128)S(1)} %collective-permute-done.4.got_hbm, ...), custom_call_target="tpu_custom_call" | custom-call | tf_op jit(solution)/shard_map/sums/pallas_call | solution.py:476
  31.9 1.5 %collective-permute-start.13 = (f32[1,64,1280]{2,1,0:T(8,128)S(1)}, f32[1,64,1280]{2,1,0:T(8,128)S(1)}, u32[]{:S(2)}, u32[]{:S(2)}) collective-permute-start(f32[1,64,1280]{2,1,0:T(8,128)S(1)} %get-tuple-element.77), channel_id=1, source_target_pairs={{0,16},{4,20},{8,24},{12,28},{16,0},{20,4},{24,8},{28,12},{1,17},{... | collective-permute-start | bytes 983048 | tf_op jit(solution)/shard_map/ppermute | solution.py:655
  33.4 1.8 %sums.3 = (f32[2,64,1280]{2,1,0:T(8,128)S(1)}, f32[2,64,1280]{2,1,0:T(8,128)S(1)}) custom-call(f32[64,64]{1,0:T(8,128)S(1)} %get-tuple-element.48.own_w_ref, f32[64,64]{1,0:T(8,128)S(1)} %collective-permute-done.2.sib_w_ref, bf16[64,10240]{1,0:T(8,128)(2,1)} %get-tuple-element.64.keep_hbm, f32[64,10240]{1,0:T(8,128)S(1)} %collective-permute-done.4.got_hbm), custom_call_target="tpu_custom_call" | custom-call | tf_op jit(solution)/shard_map/sums/pallas_call | solution.py:476
  35.2 3.2 %collective-permute-done.9.refs_3_ = f32[64,128]{1,0:T(8,128)S(1)} collective-permute-done((f32[64,128]{1,0:T(8,128)S(1)}, f32[64,128]{1,0:T(8,128)S(1)}, u32[]{:S(2)}, u32[]{:S(2)}) %collective-permute-start.9) | collective-permute-done | bytes 32800 | tf_op jit(solution)/shard_map/ppermute | solution.py:655
  39.0 1.6 %meet.1 = (f32[128,768]{1,0:T(8,128)S(1)}, f32[128,768]{1,0:T(8,128)S(1)}) custom-call(f32[64,128]{1,0:T(8,128)S(1)} %get-tuple-element.58.both_w_ref.refs_0_, f32[1,64,1408]{2,1,0:T(8,128)S(1)} %collective-permute-done.7.refs_1_, f32[1,64,1408]{2,1,0:T(8,128)S(1)} %collective-permute-done.8.refs_2_, f32[64,128]{1,0:T(8,128)S(1)} %collective-permute-done.9.refs_3_, ...), custom_call_target="tpu_custom_call" | custom-call | tf_op jit(solution)/shard_map/meet/pallas_call | solution.py:515
  40.7 1.6 %collective-permute-start.14 = (f32[1,64,1280]{2,1,0:T(8,128)S(1)}, f32[1,64,1280]{2,1,0:T(8,128)S(1)}, u32[]{:S(2)}, u32[]{:S(2)}) collective-permute-start(f32[1,64,1280]{2,1,0:T(8,128)S(1)} %slice_add_fusion.1), channel_id=1, source_target_pairs={{0,16},{4,20},{8,24},{12,28},{16,0},{20,4},{24,8},{28,12},{1,17},{... | collective-permute-start | bytes 983048 | tf_op jit(solution)/shard_map/ppermute | solution.py:655
  43.0 1.6 %collective-permute-start.16 = (f32[64,768]{1,0:T(8,128)S(1)}, f32[64,768]{1,0:T(8,128)S(1)}, u32[]{:S(2)}, u32[]{:S(2)}) collective-permute-start(f32[64,768]{1,0:T(8,128)S(1)} %slice_add_fusion.2), channel_id=1, source_target_pairs={{0,1},{1,0},{2,3},{3,2},{4,5},{5,4},{6,7},{7,6},{8,9},{9,8},{10,11... | collective-permute-start | bytes 589832 | tf_op jit(solution)/shard_map/ppermute | solution.py:755
  45.3 1.0 %shells.1.shell_ref = f32[64,128]{1,0:T(8,128)S(1)} custom-call(f32[64,64]{1,0:T(8,128)S(1)} %copy-done.1, f32[64,128]{1,0:T(8,128)S(1)} %get-tuple-element.58.both_w_ref.refs_0_, f32[1,64,1408]{2,1,0:T(8,128)S(1)} %collective-permute-done.7.refs_1_, f32[1,64,1408]{2,1,0:T(8,128)S(1)} %collective-permute-done.8.refs_2_, ...), custom_call_target="tpu_custom_call" | custom-call | tf_op jit(solution)/shard_map/shells/pallas_call | solution.py:551
  46.3 1.2 %collective-permute-done.12.sib_shell_ref = f32[64,128]{1,0:T(8,128)S(1)} collective-permute-done((f32[64,128]{1,0:T(8,128)S(1)}, f32[64,128]{1,0:T(8,128)S(1)}, u32[]{:S(2)}, u32[]{:S(2)}) %collective-permute-start.12) | collective-permute-done | bytes 32800 | tf_op jit(solution)/shard_map/ppermute | solution.py:655
  48.1 4.0 %collective-permute-done.14.left_ref = f32[1,64,1280]{2,1,0:T(8,128)S(1)} collective-permute-done((f32[1,64,1280]{2,1,0:T(8,128)S(1)}, f32[1,64,1280]{2,1,0:T(8,128)S(1)}, u32[]{:S(2)}, u32[]{:S(2)}) %collective-permute-start.14) | collective-permute-done | bytes 327712 | tf_op jit(solution)/shard_map/ppermute | solution.py:655
  52.3 1.1 %finish.1 = f32[64,4096]{1,0:T(8,128)} custom-call(f32[64,4096]{1,0:T(8,128)S(1)} %get-tuple-element.79.base_ref, f32[64,4096]{1,0:T(8,128)S(1)} %get-tuple-element.80.scale_ref, f32[1,64,1280]{2,1,0:T(8,128)S(1)} %collective-permute-done.14.left_ref, f32[1,64,1280]{2,1,0:T(8,128)S(1)} %collective-permute-done.15.right_ref, ...), custom_call_target="tpu_custom_call" | custom-call | tf_op jit(solution)/shard_map/finish/pallas_call | solution.py:643
  (37 shorter events, 4.7 us)
Async XLA Ops:
  1.3 13.1 %collective-permute-start.3 = (f32[64,1536]{1,0:T(8,128)S(1)}, f32[64,1536]{1,0:T(8,128)S(1)}, u32[]{:S(2)}, u32[]{:S(2)}) collective-permute-start(f32[64,1536]{1,0:T(8,128)S(1)} %early.1), channel_id=1, source_target_pairs={{0,24},{4,28},{8,16},{12,20},{16,8},{20,12},{24,0},{28,4},{1,25},{... | collective-permute-start | bytes 1179656 | tf_op jit(solution)/shard_map/ppermute | solution.py:655
  5.2 17.5 %copy-start.2 = (f32[2]{0:T(128)S(1)}, f32[2]{0:T(128)}, u32[]{:S(2)}) copy-start(f32[2]{0:T(128)} %param.13) | copy-start | bytes 28
  5.2 17.5 %copy-start.3 = (f32[64]{0:T(128)S(1)}, f32[64]{0:T(128)}, u32[]{:S(2)}) copy-start(f32[64]{0:T(128)} %param.12) | copy-start | bytes 772
  14.3 11.8 %copy-start.4 = (f32[64,1536]{1,0:T(8,128)}, f32[64,1536]{1,0:T(8,128)S(1)}, u32[]{:S(2)}) copy-start(f32[64,1536]{1,0:T(8,128)S(1)} %collective-permute-done.3.refs_7_) | copy-start | bytes 1179652
  14.3 10.3 %collective-permute-start.4 = (f32[64,10240]{1,0:T(8,128)}, f32[64,10240]{1,0:T(8,128)S(1)}, u32[]{:S(2)}, u32[]{:S(2)}) collective-permute-start(f32[64,10240]{1,0:T(8,128)} %get-tuple-element.56), channel_id=1, source_target_pairs={{0,4},{4,0},{8,12},{12,8},{16,20},{20,16},{24,28},{28,24},{1,5},{5... | collective-permute-start | bytes 7864328 | tf_op jit(solution)/shard_map/ppermute | solution.py:655
  14.4 4.7 %collective-permute-start = (f32[64,64]{1,0:T(8,128)S(1)}, f32[64,64]{1,0:T(8,128)S(1)}, u32[]{:S(2)}, u32[]{:S(2)}) collective-permute-start(f32[64,64]{1,0:T(8,128)S(1)} %get-tuple-element.46), channel_id=1, source_target_pairs={{0,1},{1,0},{2,3},{3,2},{4,5},{5,4},{6,7},{7,6},{8,9},{9,8},{10,11... | collective-permute-start | bytes 49160 | tf_op jit(solution)/shard_map/ppermute | solution.py:698
  16.1 13.6 %collective-permute-start.5 = (f32[64,1664]{1,0:T(8,128)}, f32[64,1664]{1,0:T(8,128)}, u32[]{:S(2)}, u32[]{:S(2)}) collective-permute-start(f32[64,1664]{1,0:T(8,128)} %get-tuple-element.60), channel_id=1, source_target_pairs={{0,8},{4,12},{8,0},{12,4},{16,24},{20,28},{24,16},{28,20},{1,9},{5... | collective-permute-start | bytes 1277960 | tf_op jit(solution)/shard_map/ppermute | solution.py:655
  17.6 12.1 %collective-permute-start.6 = (f32[64,1664]{1,0:T(8,128)S(1)}, f32[64,1664]{1,0:T(8,128)}, u32[]{:S(2)}, u32[]{:S(2)}) collective-permute-start(f32[64,1664]{1,0:T(8,128)S(1)} %get-tuple-element.61), channel_id=1, source_target_pairs={{0,16},{4,20},{8,24},{12,28},{16,0},{20,4},{24,8},{28,12},{1,17},{... | collective-permute-start | bytes 1277960 | tf_op jit(solution)/shard_map/ppermute | solution.py:655
  19.2 4.9 %collective-permute-start.1 = (f32[64,128]{1,0:T(8,128)S(1)}, f32[64,128]{1,0:T(8,128)S(1)}, u32[]{:S(2)}, u32[]{:S(2)}) collective-permute-start(f32[64,128]{1,0:T(8,128)S(1)} %pad_maximum_fusion.refs_0_), channel_id=1, source_target_pairs={{0,2},{1,3},{2,0},{3,1},{4,6},{5,7},{6,4},{7,5},{8,10},{9,11},{10,... | collective-permute-start | bytes 98312 | tf_op jit(solution)/shard_map/ppermute | solution.py:698
  24.5 1.3 %collective-permute-start.2 = (f32[64,64]{1,0:T(8,128)S(1)}, f32[64,64]{1,0:T(8,128)S(1)}, u32[]{:S(2)}, u32[]{:S(2)}) collective-permute-start(f32[64,64]{1,0:T(8,128)S(1)} %get-tuple-element.48.own_w_ref), channel_id=1, source_target_pairs={{0,4},{4,0},{8,12},{12,8},{16,20},{20,16},{24,28},{28,24},{1,5},{5... | collective-permute-start | bytes 49160 | tf_op jit(solution)/shard_map/ppermute | solution.py:655
  26.1 12.3 %collective-permute-start.7 = (f32[1,64,1408]{2,1,0:T(8,128)S(1)}, f32[1,64,1408]{2,1,0:T(8,128)S(1)}, u32[]{:S(2)}, u32[]{:S(2)}) collective-permute-start(f32[1,64,1408]{2,1,0:T(8,128)S(1)} %get-tuple-element.67), channel_id=1, source_target_pairs={{0,8},{4,12},{8,0},{12,4},{16,24},{20,28},{24,16},{28,20},{1,9},{5... | collective-permute-start | bytes 1081352 | tf_op jit(solution)/shard_map/ppermute | solution.py:655
  27.0 12.0 %collective-permute-start.8 = (f32[1,64,1408]{2,1,0:T(8,128)S(1)}, f32[1,64,1408]{2,1,0:T(8,128)S(1)}, u32[]{:S(2)}, u32[]{:S(2)}) collective-permute-start(f32[1,64,1408]{2,1,0:T(8,128)S(1)} %get-tuple-element.57), channel_id=1, source_target_pairs={{0,16},{4,20},{8,24},{12,28},{16,0},{20,4},{24,8},{28,12},{1,17},{... | collective-permute-start | bytes 1081352 | tf_op jit(solution)/shard_map/ppermute | solution.py:655
  28.5 9.9 %collective-permute-start.9 = (f32[64,128]{1,0:T(8,128)S(1)}, f32[64,128]{1,0:T(8,128)S(1)}, u32[]{:S(2)}, u32[]{:S(2)}) collective-permute-start(f32[64,128]{1,0:T(8,128)S(1)} %get-tuple-element.58.both_w_ref.refs_0_), channel_id=1, source_target_pairs={{0,24},{4,28},{8,16},{12,20},{16,8},{20,12},{24,0},{28,4},{1,25},{... | collective-permute-start | bytes 98312 | tf_op jit(solution)/shard_map/ppermute | solution.py:655
  31.0 14.2 %collective-permute-start.11 = (f32[1,64,1408]{2,1,0:T(8,128)S(1)}, f32[1,64,1408]{2,1,0:T(8,128)S(1)}, u32[]{:S(2)}, u32[]{:S(2)}) collective-permute-start(f32[1,64,1408]{2,1,0:T(8,128)S(1)} %get-tuple-element.66), channel_id=1, source_target_pairs={{0,8},{4,12},{8,0},{12,4},{16,24},{20,28},{24,16},{28,20},{1,9},{5... | collective-permute-start | bytes 1081352 | tf_op jit(solution)/shard_map/ppermute | solution.py:655
  31.9 14.4 %collective-permute-start.13 = (f32[1,64,1280]{2,1,0:T(8,128)S(1)}, f32[1,64,1280]{2,1,0:T(8,128)S(1)}, u32[]{:S(2)}, u32[]{:S(2)}) collective-permute-start(f32[1,64,1280]{2,1,0:T(8,128)S(1)} %get-tuple-element.77), channel_id=1, source_target_pairs={{0,16},{4,20},{8,24},{12,28},{16,0},{20,4},{24,8},{28,12},{1,17},{... | collective-permute-start | bytes 983048 | tf_op jit(solution)/shard_map/ppermute | solution.py:655
  35.2 10.1 %copy-start.1 = (f32[64,64]{1,0:T(8,128)S(1)}, f32[64,64]{1,0:T(8,128)}, u32[]{:S(2)}) copy-start(f32[64,64]{1,0:T(8,128)} %ctf_ref.1) | copy-start | bytes 49156
  40.6 6.9 %copy-start = (s32[1,32768]{1,0:T(1,128)S(1)}, s32[1,32768]{1,0:T(1,128)}, u32[]{:S(2)}) copy-start(s32[1,32768]{1,0:T(1,128)} %constant.5.clone.index_hbm) | copy-start | bytes 393220
  40.6 2.3 %collective-permute-start.10 = (f32[128,768]{1,0:T(8,128)S(1)}, f32[128,768]{1,0:T(8,128)S(1)}, u32[]{:S(2)}, u32[]{:S(2)}) collective-permute-start(f32[128,768]{1,0:T(8,128)S(1)} %get-tuple-element.75), channel_id=1, source_target_pairs={{0,4},{4,0},{8,12},{12,8},{16,20},{20,16},{24,28},{28,24},{1,5},{5... | collective-permute-start | bytes 1179656 | tf_op jit(solution)/shard_map/ppermute | solution.py:655
  40.7 11.4 %collective-permute-start.14 = (f32[1,64,1280]{2,1,0:T(8,128)S(1)}, f32[1,64,1280]{2,1,0:T(8,128)S(1)}, u32[]{:S(2)}, u32[]{:S(2)}) collective-permute-start(f32[1,64,1280]{2,1,0:T(8,128)S(1)} %slice_add_fusion.1), channel_id=1, source_target_pairs={{0,16},{4,20},{8,24},{12,28},{16,0},{20,4},{24,8},{28,12},{1,17},{... | collective-permute-start | bytes 983048 | tf_op jit(solution)/shard_map/ppermute | solution.py:655
  42.4 9.9 %collective-permute-start.15 = (f32[1,64,1280]{2,1,0:T(8,128)S(1)}, f32[1,64,1280]{2,1,0:T(8,128)S(1)}, u32[]{:S(2)}, u32[]{:S(2)}) collective-permute-start(f32[1,64,1280]{2,1,0:T(8,128)S(1)} %slice_add_fusion), channel_id=1, source_target_pairs={{0,8},{4,12},{8,0},{12,4},{16,24},{20,28},{24,16},{28,20},{1,9},{5... | collective-permute-start | bytes 983048 | tf_op jit(solution)/shard_map/ppermute | solution.py:655
  43.0 9.3 %collective-permute-start.16 = (f32[64,768]{1,0:T(8,128)S(1)}, f32[64,768]{1,0:T(8,128)S(1)}, u32[]{:S(2)}, u32[]{:S(2)}) collective-permute-start(f32[64,768]{1,0:T(8,128)S(1)} %slice_add_fusion.2), channel_id=1, source_target_pairs={{0,1},{1,0},{2,3},{3,2},{4,5},{5,4},{6,7},{7,6},{8,9},{9,8},{10,11... | collective-permute-start | bytes 589832 | tf_op jit(solution)/shard_map/ppermute | solution.py:755
  46.2 1.3 %collective-permute-start.12 = (f32[64,128]{1,0:T(8,128)S(1)}, f32[64,128]{1,0:T(8,128)S(1)}, u32[]{:S(2)}, u32[]{:S(2)}) collective-permute-start(f32[64,128]{1,0:T(8,128)S(1)} %shells.1.shell_ref), channel_id=1, source_target_pairs={{0,4},{4,0},{8,12},{12,8},{16,20},{20,16},{24,28},{28,24},{1,5},{5... | collective-permute-start | bytes 98312 | tf_op jit(solution)/shard_map/ppermute | solution.py:655

commit v10 on v9

--- a/solution.py
+++ b/solution.py
@@ -12,6 +12,7 @@
 F32 = jnp.float32
 BF16 = jnp.bfloat16
 LANES = 128
+PIECE = 5 * LANES
 MIB = 1024 * 1024
 
 
@@ -620,32 +621,35 @@
 
     stores = []
 
-    def store(start, stop):
-        cut = slice(start, stop)
-        stores.append(
-            pltpu.make_async_copy(out.at[:, cut], out_hbm.at[:, cut], out_sem.at[len(stores)])
-        )
-        stores[-1].start()
-
-    scaled(own, met)
-    scaled(other, met, lambda cut: partner_ref[:, cut])
-    store(2 * wide, share)
-    scaled(0, wide, lambda cut: left_ref[0, :, cut])
-    store(0, wide)
-    scaled(wide, wide, lambda cut: right_ref[0, :, cut])
-    store(wide, 2 * wide)
+    def scale_and_store(place, size, last=None):
+        for first in range(0, size, PIECE):
+            piece = min(PIECE, size - first)
+            from_here = None if last is None else lambda cut: last(slice(cut.start + first, cut.stop + first))
+            scaled(place + first, piece, from_here)
+            cut = pl.ds(pl.multiple_of(place + first, LANES), piece)
+            stores.append(
+                pltpu.make_async_copy(out.at[:, cut], out_hbm.at[:, cut], out_sem.at[len(stores)])
+            )
+            stores[-1].start()
+
+    scale_and_store(own, met)
+    scale_and_store(other, met, lambda cut: partner_ref[:, cut])
+    scale_and_store(0, wide, lambda cut: left_ref[0, :, cut])
+    scale_and_store(wide, wide, lambda cut: right_ref[0, :, cut])
     for copy in stores:
         copy.wait()
 
 
 def finish(base, scale, left, right, partner):
+    wide, met = split_share(base.shape[1])
+    pieces = 2 * (pl.cdiv(wide, PIECE) + pl.cdiv(met, PIECE))
     vmem = pl.BlockSpec(memory_space=pltpu.VMEM)
     return pl.pallas_call(
         finish_kernel,
         in_specs=[vmem] * 5,
         out_specs=pl.BlockSpec(memory_space=pl.ANY),
         out_shape=jax.ShapeDtypeStruct(base.shape, F32),
-        scratch_shapes=[pltpu.VMEM(base.shape, F32), pltpu.SemaphoreType.DMA((3,))],
+        scratch_shapes=[pltpu.VMEM(base.shape, F32), pltpu.SemaphoreType.DMA((pieces,))],
         compiler_params=params(8),
         name="finish",
     )(base, scale, left, right, partner)

time: 53.8 us -> 53.7 us (level)
  no operation moved by 1% of the time
where the time goes in v10:
time: 53.7 us; the launch traced here: 53.4 us
  starting transfers between devices  21.3 us (40%)
  Pallas kernels  20.8 us (39%)
  waiting for transfers between devices  9.92 us (18%)
  local copies, waits for them, and re-layouts  0.96 us (2%)
    ppermute x14, starting transfers between devices, swap(): return lax.ppermute(array, 'img', [(one, one ^ bit) for one in range(size)])  15.4 us
    ppermute x14, waiting for transfers between devices, swap(): return lax.ppermute(array, 'img', [(one, one ^ bit) for one in range(size)])  9.91 us
    pallas_call x1, Pallas kernels, estep(): pl.pallas_call(functools.partial(estep_kernel, blocks, share, near), in_s...  9.08 us
    ppermute x2, starting transfers between devices, shards(): tables = [held, lax.ppermute(held, 'slab', pairs)]  4.29 us
    pallas_call x2, Pallas kernels, partial_sums(): pl.pallas_call(functools.partial(sums_kernel, items, bool(relay)), in_spe...  3.13 us
    ppermute x1, starting transfers between devices, shards(): lax.ppermute(met[own_planes:, :met_wide] + sib_met[own_planes:, :met_wide...  1.64 us
    pallas_call x1, Pallas kernels, meet(): pl.pallas_call(functools.partial(meet_kernel, len(weights)), out_shape=[j...  1.63 us
    pallas_call x1, Pallas kernels, count_planes(): pl.pallas_call(functools.partial(count_kernel, slabs), in_specs=[vmem] *...  1.39 us
  transfers between devices with their start and end apart: 17, of which 7 were waited for; matrix products, arithmetic and copies ran while one was open for 2% of the time, Pallas kernels for 35%

profile of v10, /device:TPU:0, one launch (start us, length us, event | category | flops | bytes accessed | tf_op | source)
XLA Modules:
  0.0 53.4 jit_solution(17721755444129553529)
XLA Ops:
  0.0 1.2 %early.1 = f32[64,1536]{1,0:T(8,128)S(1)} custom-call(s32[1,32768]{1,0:T(1,128)} %constant.5.clone.index_hbm, bf16[64,32768]{1,0:T(8,128)(2,1)} %image_hbm.2, f32[64,64]{1,0:T(8,128)} %ctf_ref.1), custom_call_target="tpu_custom_call" | custom-call | tf_op jit(solution)/shard_map/early/pallas_call | solution.py:274
  1.3 4.0 %collective-permute-start.3 = (f32[64,1536]{1,0:T(8,128)S(1)}, f32[64,1536]{1,0:T(8,128)S(1)}, u32[]{:S(2)}, u32[]{:S(2)}) collective-permute-start(f32[64,1536]{1,0:T(8,128)S(1)} %early.1), channel_id=1, source_target_pairs={{0,24},{4,28},{8,16},{12,20},{16,8},{20,12},{24,0},{28,4},{1,25},{... | collective-permute-start | bytes 1179656 | tf_op jit(solution)/shard_map/ppermute | solution.py:659
  5.2 9.1 %estep.1 = (f32[64,10240]{1,0:T(8,128)}, bf16[64,10240]{1,0:T(8,128)(2,1)}, f32[64,64]{1,0:T(8,128)S(1)}, bf16[64,1536]{1,0:T(8,128)(2,1)}, f32[64,1664]{1,0:T(8,128)}, /*index=5*/f32[64,1664]{1,0:T(8,128)S(1)}) custom-call(s32[1,16640]{1,0:T(1,128)} %constant.4.clone.index_hbm, bf16[64,32768]{1,0:T(8,128)(2,1)} %image_hbm.2, bf16[64,32768]{1,0:T(8,128)(2,1)} %bitcast.6, ...), custom_call_target="tpu_custom_call" | custom-call | tf_op jit(solution)/shard_map/estep/pallas_call | solution.py:198
  14.4 1.7 %collective-permute-start = (f32[64,64]{1,0:T(8,128)S(1)}, f32[64,64]{1,0:T(8,128)S(1)}, u32[]{:S(2)}, u32[]{:S(2)}) collective-permute-start(f32[64,64]{1,0:T(8,128)S(1)} %get-tuple-element.46), channel_id=1, source_target_pairs={{0,1},{1,0},{2,3},{3,2},{4,5},{5,4},{6,7},{7,6},{8,9},{9,8},{10,11... | collective-permute-start | bytes 49160 | tf_op jit(solution)/shard_map/ppermute | solution.py:702
  16.1 1.5 %collective-permute-start.5 = (f32[64,1664]{1,0:T(8,128)}, f32[64,1664]{1,0:T(8,128)}, u32[]{:S(2)}, u32[]{:S(2)}) collective-permute-start(f32[64,1664]{1,0:T(8,128)} %get-tuple-element.60), channel_id=1, source_target_pairs={{0,8},{4,12},{8,0},{12,4},{16,24},{20,28},{24,16},{28,20},{1,9},{5... | collective-permute-start | bytes 1277960 | tf_op jit(solution)/shard_map/ppermute | solution.py:659
  17.6 1.5 %collective-permute-start.6 = (f32[64,1664]{1,0:T(8,128)S(1)}, f32[64,1664]{1,0:T(8,128)}, u32[]{:S(2)}, u32[]{:S(2)}) collective-permute-start(f32[64,1664]{1,0:T(8,128)S(1)} %get-tuple-element.61), channel_id=1, source_target_pairs={{0,16},{4,20},{8,24},{12,28},{16,0},{20,4},{24,8},{28,12},{1,17},{... | collective-permute-start | bytes 1277960 | tf_op jit(solution)/shard_map/ppermute | solution.py:659
  19.2 2.6 %collective-permute-start.1 = (f32[64,128]{1,0:T(8,128)S(1)}, f32[64,128]{1,0:T(8,128)S(1)}, u32[]{:S(2)}, u32[]{:S(2)}) collective-permute-start(f32[64,128]{1,0:T(8,128)S(1)} %pad_maximum_fusion.refs_0_), channel_id=1, source_target_pairs={{0,2},{1,3},{2,0},{3,1},{4,6},{5,7},{6,4},{7,5},{8,10},{9,11},{10,... | collective-permute-start | bytes 98312 | tf_op jit(solution)/shard_map/ppermute | solution.py:702
  21.8 0.9 %reshape.17.list_ref = s32[64,128]{1,0:T(8,128)S(1)} reshape(s32[64,2,64]{2,1,0:T(2,128)} %param.10) | data formatting | bytes 65536 | tf_op jit(solution)/shard_map/reshape | solution.py:332
  22.7 1.4 %count.1 = (f32[2,64,128]{2,1,0:T(8,128)S(1)}, f32[64,128]{1,0:T(8,128)S(1)}) custom-call(f32[1,2]{1,0:T(1,128)S(1)} %bitcast.4, f32[1,64]{1,0:T(1,128)S(1)} %bitcast.5, s32[64,128]{1,0:T(8,128)S(1)} %reshape.17.list_ref), custom_call_target="tpu_custom_call" | custom-call | tf_op jit(solution)/shard_map/count/pallas_call | solution.py:319
  24.6 1.1 %gather.1.image_ref = bf16[2,128,1280]{2,1,0:T(8,128)(2,1)S(1)} custom-call(bf16[64,10240]{1,0:T(8,128)(2,1)} %get-tuple-element.64.keep_hbm, f32[64,10240]{1,0:T(8,128)S(1)} %collective-permute-done.4.got_hbm), custom_call_target="tpu_custom_call" | custom-call | tf_op jit(solution)/shard_map/gather/pallas_call | solution.py:395
  26.1 0.9 %collective-permute-start.7 = (f32[1,64,1408]{2,1,0:T(8,128)S(1)}, f32[1,64,1408]{2,1,0:T(8,128)S(1)}, u32[]{:S(2)}, u32[]{:S(2)}) collective-permute-start(f32[1,64,1408]{2,1,0:T(8,128)S(1)} %get-tuple-element.67), channel_id=1, source_target_pairs={{0,8},{4,12},{8,0},{12,4},{16,24},{20,28},{24,16},{28,20},{1,9},{5... | collective-permute-start | bytes 1081352 | tf_op jit(solution)/shard_map/ppermute | solution.py:659
  27.0 1.5 %collective-permute-start.8 = (f32[1,64,1408]{2,1,0:T(8,128)S(1)}, f32[1,64,1408]{2,1,0:T(8,128)S(1)}, u32[]{:S(2)}, u32[]{:S(2)}) collective-permute-start(f32[1,64,1408]{2,1,0:T(8,128)S(1)} %get-tuple-element.57), channel_id=1, source_target_pairs={{0,16},{4,20},{8,24},{12,28},{16,0},{20,4},{24,8},{28,12},{1,17},{... | collective-permute-start | bytes 1081352 | tf_op jit(solution)/shard_map/ppermute | solution.py:659
  28.5 1.2 %collective-permute-start.9 = (f32[64,128]{1,0:T(8,128)S(1)}, f32[64,128]{1,0:T(8,128)S(1)}, u32[]{:S(2)}, u32[]{:S(2)}) collective-permute-start(f32[64,128]{1,0:T(8,128)S(1)} %get-tuple-element.58.both_w_ref.refs_0_), channel_id=1, source_target_pairs={{0,24},{4,28},{8,16},{12,20},{16,8},{20,12},{24,0},{28,4},{1,25},{... | collective-permute-start | bytes 98312 | tf_op jit(solution)/shard_map/ppermute | solution.py:659
  29.7 1.4 %sums.2 = (f32[1,64,1408]{2,1,0:T(8,128)S(1)}, f32[1,64,1280]{2,1,0:T(8,128)S(1)}) custom-call(f32[64,64]{1,0:T(8,128)S(1)} %get-tuple-element.48.own_w_ref, f32[64,64]{1,0:T(8,128)S(1)} %collective-permute-done.2.sib_w_ref, bf16[64,10240]{1,0:T(8,128)(2,1)} %get-tuple-element.64.keep_hbm, f32[64,10240]{1,0:T(8,128)S(1)} %collective-permute-done.4.got_hbm, ...), custom_call_target="tpu_custom_call" | custom-call | tf_op jit(solution)/shard_map/sums/pallas_call | solution.py:477
  31.9 1.5 %collective-permute-start.13 = (f32[1,64,1280]{2,1,0:T(8,128)S(1)}, f32[1,64,1280]{2,1,0:T(8,128)S(1)}, u32[]{:S(2)}, u32[]{:S(2)}) collective-permute-start(f32[1,64,1280]{2,1,0:T(8,128)S(1)} %get-tuple-element.77), channel_id=1, source_target_pairs={{0,16},{4,20},{8,24},{12,28},{16,0},{20,4},{24,8},{28,12},{1,17},{... | collective-permute-start | bytes 983048 | tf_op jit(solution)/shard_map/ppermute | solution.py:659
  33.4 1.8 %sums.3 = (f32[2,64,1280]{2,1,0:T(8,128)S(1)}, f32[2,64,1280]{2,1,0:T(8,128)S(1)}) custom-call(f32[64,64]{1,0:T(8,128)S(1)} %get-tuple-element.48.own_w_ref, f32[64,64]{1,0:T(8,128)S(1)} %collective-permute-done.2.sib_w_ref, bf16[64,10240]{1,0:T(8,128)(2,1)} %get-tuple-element.64.keep_hbm, f32[64,10240]{1,0:T(8,128)S(1)} %collective-permute-done.4.got_hbm), custom_call_target="tpu_custom_call" | custom-call | tf_op jit(solution)/shard_map/sums/pallas_call | solution.py:477
  35.2 3.2 %collective-permute-done.9.refs_3_ = f32[64,128]{1,0:T(8,128)S(1)} collective-permute-done((f32[64,128]{1,0:T(8,128)S(1)}, f32[64,128]{1,0:T(8,128)S(1)}, u32[]{:S(2)}, u32[]{:S(2)}) %collective-permute-start.9) | collective-permute-done | bytes 32800 | tf_op jit(solution)/shard_map/ppermute | solution.py:659
  39.0 1.6 %meet.1 = (f32[128,768]{1,0:T(8,128)S(1)}, f32[128,768]{1,0:T(8,128)S(1)}) custom-call(f32[64,128]{1,0:T(8,128)S(1)} %get-tuple-element.58.both_w_ref.refs_0_, f32[1,64,1408]{2,1,0:T(8,128)S(1)} %collective-permute-done.7.refs_1_, f32[1,64,1408]{2,1,0:T(8,128)S(1)} %collective-permute-done.8.refs_2_, f32[64,128]{1,0:T(8,128)S(1)} %collective-permute-done.9.refs_3_, ...), custom_call_target="tpu_custom_call" | custom-call | tf_op jit(solution)/shard_map/meet/pallas_call | solution.py:516
  40.7 1.6 %collective-permute-start.14 = (f32[1,64,1280]{2,1,0:T(8,128)S(1)}, f32[1,64,1280]{2,1,0:T(8,128)S(1)}, u32[]{:S(2)}, u32[]{:S(2)}) collective-permute-start(f32[1,64,1280]{2,1,0:T(8,128)S(1)} %slice_add_fusion.1), channel_id=1, source_target_pairs={{0,16},{4,20},{8,24},{12,28},{16,0},{20,4},{24,8},{28,12},{1,17},{... | collective-permute-start | bytes 983048 | tf_op jit(solution)/shard_map/ppermute | solution.py:659
  43.0 1.6 %collective-permute-start.16 = (f32[64,768]{1,0:T(8,128)S(1)}, f32[64,768]{1,0:T(8,128)S(1)}, u32[]{:S(2)}, u32[]{:S(2)}) collective-permute-start(f32[64,768]{1,0:T(8,128)S(1)} %slice_add_fusion.2), channel_id=1, source_target_pairs={{0,1},{1,0},{2,3},{3,2},{4,5},{5,4},{6,7},{7,6},{8,9},{9,8},{10,11... | collective-permute-start | bytes 589832 | tf_op jit(solution)/shard_map/ppermute | solution.py:759
  45.3 1.0 %shells.1.shell_ref = f32[64,128]{1,0:T(8,128)S(1)} custom-call(f32[64,64]{1,0:T(8,128)S(1)} %copy-done.1, f32[64,128]{1,0:T(8,128)S(1)} %get-tuple-element.58.both_w_ref.refs_0_, f32[1,64,1408]{2,1,0:T(8,128)S(1)} %collective-permute-done.7.refs_1_, f32[1,64,1408]{2,1,0:T(8,128)S(1)} %collective-permute-done.8.refs_2_, ...), custom_call_target="tpu_custom_call" | custom-call | tf_op jit(solution)/shard_map/shells/pallas_call | solution.py:552
  46.3 1.2 %collective-permute-done.12.sib_shell_ref = f32[64,128]{1,0:T(8,128)S(1)} collective-permute-done((f32[64,128]{1,0:T(8,128)S(1)}, f32[64,128]{1,0:T(8,128)S(1)}, u32[]{:S(2)}, u32[]{:S(2)}) %collective-permute-start.12) | collective-permute-done | bytes 32800 | tf_op jit(solution)/shard_map/ppermute | solution.py:659
  48.1 4.0 %collective-permute-done.14.left_ref = f32[1,64,1280]{2,1,0:T(8,128)S(1)} collective-permute-done((f32[1,64,1280]{2,1,0:T(8,128)S(1)}, f32[1,64,1280]{2,1,0:T(8,128)S(1)}, u32[]{:S(2)}, u32[]{:S(2)}) %collective-permute-start.14) | collective-permute-done | bytes 327712 | tf_op jit(solution)/shard_map/ppermute | solution.py:659
  52.3 1.1 %finish.1 = f32[64,4096]{1,0:T(8,128)} custom-call(f32[64,4096]{1,0:T(8,128)S(1)} %get-tuple-element.79.base_ref, f32[64,4096]{1,0:T(8,128)S(1)} %get-tuple-element.80.scale_ref, f32[1,64,1280]{2,1,0:T(8,128)S(1)} %collective-permute-done.14.left_ref, f32[1,64,1280]{2,1,0:T(8,128)S(1)} %collective-permute-done.15.right_ref, ...), custom_call_target="tpu_custom_call" | custom-call | tf_op jit(solution)/shard_map/finish/pallas_call | solution.py:647
  (37 shorter events, 4.7 us)
Async XLA Ops:
  1.3 13.1 %collective-permute-start.3 = (f32[64,1536]{1,0:T(8,128)S(1)}, f32[64,1536]{1,0:T(8,128)S(1)}, u32[]{:S(2)}, u32[]{:S(2)}) collective-permute-start(f32[64,1536]{1,0:T(8,128)S(1)} %early.1), channel_id=1, source_target_pairs={{0,24},{4,28},{8,16},{12,20},{16,8},{20,12},{24,0},{28,4},{1,25},{... | collective-permute-start | bytes 1179656 | tf_op jit(solution)/shard_map/ppermute | solution.py:659
  5.2 17.5 %copy-start.2 = (f32[2]{0:T(128)S(1)}, f32[2]{0:T(128)}, u32[]{:S(2)}) copy-start(f32[2]{0:T(128)} %param.13) | copy-start | bytes 28
  5.2 17.5 %copy-start.3 = (f32[64]{0:T(128)S(1)}, f32[64]{0:T(128)}, u32[]{:S(2)}) copy-start(f32[64]{0:T(128)} %param.12) | copy-start | bytes 772
  14.3 11.8 %copy-start.4 = (f32[64,1536]{1,0:T(8,128)}, f32[64,1536]{1,0:T(8,128)S(1)}, u32[]{:S(2)}) copy-start(f32[64,1536]{1,0:T(8,128)S(1)} %collective-permute-done.3.refs_7_) | copy-start | bytes 1179652
  14.3 10.3 %collective-permute-start.4 = (f32[64,10240]{1,0:T(8,128)}, f32[64,10240]{1,0:T(8,128)S(1)}, u32[]{:S(2)}, u32[]{:S(2)}) collective-permute-start(f32[64,10240]{1,0:T(8,128)} %get-tuple-element.56), channel_id=1, source_target_pairs={{0,4},{4,0},{8,12},{12,8},{16,20},{20,16},{24,28},{28,24},{1,5},{5... | collective-permute-start | bytes 7864328 | tf_op jit(solution)/shard_map/ppermute | solution.py:659
  14.4 4.7 %collective-permute-start = (f32[64,64]{1,0:T(8,128)S(1)}, f32[64,64]{1,0:T(8,128)S(1)}, u32[]{:S(2)}, u32[]{:S(2)}) collective-permute-start(f32[64,64]{1,0:T(8,128)S(1)} %get-tuple-element.46), channel_id=1, source_target_pairs={{0,1},{1,0},{2,3},{3,2},{4,5},{5,4},{6,7},{7,6},{8,9},{9,8},{10,11... | collective-permute-start | bytes 49160 | tf_op jit(solution)/shard_map/ppermute | solution.py:702
  16.1 13.6 %collective-permute-start.5 = (f32[64,1664]{1,0:T(8,128)}, f32[64,1664]{1,0:T(8,128)}, u32[]{:S(2)}, u32[]{:S(2)}) collective-permute-start(f32[64,1664]{1,0:T(8,128)} %get-tuple-element.60), channel_id=1, source_target_pairs={{0,8},{4,12},{8,0},{12,4},{16,24},{20,28},{24,16},{28,20},{1,9},{5... | collective-permute-start | bytes 1277960 | tf_op jit(solution)/shard_map/ppermute | solution.py:659
  17.6 12.1 %collective-permute-start.6 = (f32[64,1664]{1,0:T(8,128)S(1)}, f32[64,1664]{1,0:T(8,128)}, u32[]{:S(2)}, u32[]{:S(2)}) collective-permute-start(f32[64,1664]{1,0:T(8,128)S(1)} %get-tuple-element.61), channel_id=1, source_target_pairs={{0,16},{4,20},{8,24},{12,28},{16,0},{20,4},{24,8},{28,12},{1,17},{... | collective-permute-start | bytes 1277960 | tf_op jit(solution)/shard_map/ppermute | solution.py:659
  19.2 4.9 %collective-permute-start.1 = (f32[64,128]{1,0:T(8,128)S(1)}, f32[64,128]{1,0:T(8,128)S(1)}, u32[]{:S(2)}, u32[]{:S(2)}) collective-permute-start(f32[64,128]{1,0:T(8,128)S(1)} %pad_maximum_fusion.refs_0_), channel_id=1, source_target_pairs={{0,2},{1,3},{2,0},{3,1},{4,6},{5,7},{6,4},{7,5},{8,10},{9,11},{10,... | collective-permute-start | bytes 98312 | tf_op jit(solution)/shard_map/ppermute | solution.py:702
  24.5 1.3 %collective-permute-start.2 = (f32[64,64]{1,0:T(8,128)S(1)}, f32[64,64]{1,0:T(8,128)S(1)}, u32[]{:S(2)}, u32[]{:S(2)}) collective-permute-start(f32[64,64]{1,0:T(8,128)S(1)} %get-tuple-element.48.own_w_ref), channel_id=1, source_target_pairs={{0,4},{4,0},{8,12},{12,8},{16,20},{20,16},{24,28},{28,24},{1,5},{5... | collective-permute-start | bytes 49160 | tf_op jit(solution)/shard_map/ppermute | solution.py:659
  26.1 12.3 %collective-permute-start.7 = (f32[1,64,1408]{2,1,0:T(8,128)S(1)}, f32[1,64,1408]{2,1,0:T(8,128)S(1)}, u32[]{:S(2)}, u32[]{:S(2)}) collective-permute-start(f32[1,64,1408]{2,1,0:T(8,128)S(1)} %get-tuple-element.67), channel_id=1, source_target_pairs={{0,8},{4,12},{8,0},{12,4},{16,24},{20,28},{24,16},{28,20},{1,9},{5... | collective-permute-start | bytes 1081352 | tf_op jit(solution)/shard_map/ppermute | solution.py:659
  27.0 12.0 %collective-permute-start.8 = (f32[1,64,1408]{2,1,0:T(8,128)S(1)}, f32[1,64,1408]{2,1,0:T(8,128)S(1)}, u32[]{:S(2)}, u32[]{:S(2)}) collective-permute-start(f32[1,64,1408]{2,1,0:T(8,128)S(1)} %get-tuple-element.57), channel_id=1, source_target_pairs={{0,16},{4,20},{8,24},{12,28},{16,0},{20,4},{24,8},{28,12},{1,17},{... | collective-permute-start | bytes 1081352 | tf_op jit(solution)/shard_map/ppermute | solution.py:659
  28.5 9.9 %collective-permute-start.9 = (f32[64,128]{1,0:T(8,128)S(1)}, f32[64,128]{1,0:T(8,128)S(1)}, u32[]{:S(2)}, u32[]{:S(2)}) collective-permute-start(f32[64,128]{1,0:T(8,128)S(1)} %get-tuple-element.58.both_w_ref.refs_0_), channel_id=1, source_target_pairs={{0,24},{4,28},{8,16},{12,20},{16,8},{20,12},{24,0},{28,4},{1,25},{... | collective-permute-start | bytes 98312 | tf_op jit(solution)/shard_map/ppermute | solution.py:659
  31.0 14.2 %collective-permute-start.11 = (f32[1,64,1408]{2,1,0:T(8,128)S(1)}, f32[1,64,1408]{2,1,0:T(8,128)S(1)}, u32[]{:S(2)}, u32[]{:S(2)}) collective-permute-start(f32[1,64,1408]{2,1,0:T(8,128)S(1)} %get-tuple-element.66), channel_id=1, source_target_pairs={{0,8},{4,12},{8,0},{12,4},{16,24},{20,28},{24,16},{28,20},{1,9},{5... | collective-permute-start | bytes 1081352 | tf_op jit(solution)/shard_map/ppermute | solution.py:659
  31.9 14.4 %collective-permute-start.13 = (f32[1,64,1280]{2,1,0:T(8,128)S(1)}, f32[1,64,1280]{2,1,0:T(8,128)S(1)}, u32[]{:S(2)}, u32[]{:S(2)}) collective-permute-start(f32[1,64,1280]{2,1,0:T(8,128)S(1)} %get-tuple-element.77), channel_id=1, source_target_pairs={{0,16},{4,20},{8,24},{12,28},{16,0},{20,4},{24,8},{28,12},{1,17},{... | collective-permute-start | bytes 983048 | tf_op jit(solution)/shard_map/ppermute | solution.py:659
  35.2 10.1 %copy-start.1 = (f32[64,64]{1,0:T(8,128)S(1)}, f32[64,64]{1,0:T(8,128)}, u32[]{:S(2)}) copy-start(f32[64,64]{1,0:T(8,128)} %ctf_ref.1) | copy-start | bytes 49156
  40.6 6.9 %copy-start = (s32[1,32768]{1,0:T(1,128)S(1)}, s32[1,32768]{1,0:T(1,128)}, u32[]{:S(2)}) copy-start(s32[1,32768]{1,0:T(1,128)} %constant.5.clone.index_hbm) | copy-start | bytes 393220
  40.6 2.3 %collective-permute-start.10 = (f32[128,768]{1,0:T(8,128)S(1)}, f32[128,768]{1,0:T(8,128)S(1)}, u32[]{:S(2)}, u32[]{:S(2)}) collective-permute-start(f32[128,768]{1,0:T(8,128)S(1)} %get-tuple-element.75), channel_id=1, source_target_pairs={{0,4},{4,0},{8,12},{12,8},{16,20},{20,16},{24,28},{28,24},{1,5},{5... | collective-permute-start | bytes 1179656 | tf_op jit(solution)/shard_map/ppermute | solution.py:659
  40.7 11.4 %collective-permute-start.14 = (f32[1,64,1280]{2,1,0:T(8,128)S(1)}, f32[1,64,1280]{2,1,0:T(8,128)S(1)}, u32[]{:S(2)}, u32[]{:S(2)}) collective-permute-start(f32[1,64,1280]{2,1,0:T(8,128)S(1)} %slice_add_fusion.1), channel_id=1, source_target_pairs={{0,16},{4,20},{8,24},{12,28},{16,0},{20,4},{24,8},{28,12},{1,17},{... | collective-permute-start | bytes 983048 | tf_op jit(solution)/shard_map/ppermute | solution.py:659
  42.4 9.9 %collective-permute-start.15 = (f32[1,64,1280]{2,1,0:T(8,128)S(1)}, f32[1,64,1280]{2,1,0:T(8,128)S(1)}, u32[]{:S(2)}, u32[]{:S(2)}) collective-permute-start(f32[1,64,1280]{2,1,0:T(8,128)S(1)} %slice_add_fusion), channel_id=1, source_target_pairs={{0,8},{4,12},{8,0},{12,4},{16,24},{20,28},{24,16},{28,20},{1,9},{5... | collective-permute-start | bytes 983048 | tf_op jit(solution)/shard_map/ppermute | solution.py:659
  43.0 9.3 %collective-permute-start.16 = (f32[64,768]{1,0:T(8,128)S(1)}, f32[64,768]{1,0:T(8,128)S(1)}, u32[]{:S(2)}, u32[]{:S(2)}) collective-permute-start(f32[64,768]{1,0:T(8,128)S(1)} %slice_add_fusion.2), channel_id=1, source_target_pairs={{0,1},{1,0},{2,3},{3,2},{4,5},{5,4},{6,7},{7,6},{8,9},{9,8},{10,11... | collective-permute-start | bytes 589832 | tf_op jit(solution)/shard_map/ppermute | solution.py:759
  46.2 1.3 %collective-permute-start.12 = (f32[64,128]{1,0:T(8,128)S(1)}, f32[64,128]{1,0:T(8,128)S(1)}, u32[]{:S(2)}, u32[]{:S(2)}) collective-permute-start(f32[64,128]{1,0:T(8,128)S(1)} %shells.1.shell_ref), channel_id=1, source_target_pairs={{0,4},{4,0},{8,12},{12,8},{16,20},{20,16},{24,28},{28,24},{1,5},{5... | collective-permute-start | bytes 98312 | tf_op jit(solution)/shard_map/ppermute | solution.py:659

commit v11 on v10

--- a/solution.py
+++ b/solution.py
@@ -584,7 +584,9 @@
     fetch.wait()
     for start in range(0, share, LANES):
         cut = slice(start, start + LANES)
-        scale_ref[:, cut] = 1.0 / (spread(shells, index[:, cut]) + 1.0)
+        scale = 1.0 / (spread(shells, index[:, cut]) + 1.0)
+        scale_ref[:, cut] = scale
+        base_ref[:, cut] = base_ref[:, cut] * scale
 
 
 def prepare(index, met, sib_met, shells, sib_shells, sides, share):
@@ -611,28 +613,28 @@
     own = pl.multiple_of(2 * wide + half * met, LANES)
     other = pl.multiple_of(2 * wide + (1 - half) * met, LANES)
 
-    def scaled(place, size, last=None):
+    def scaled(place, size, last):
         for start in range(0, size, LANES):
             at = pl.ds(pl.multiple_of(place + start, LANES), LANES)
-            value = base_ref[:, at]
-            if last is not None:
-                value += last(slice(start, start + LANES))
-            out[:, at] = value * scale_ref[:, at]
+            out[:, at] = base_ref[:, at] + last(slice(start, start + LANES)) * scale_ref[:, at]
 
     stores = []
 
-    def scale_and_store(place, size, last=None):
+    def scale_and_store(place, size, last):
         for first in range(0, size, PIECE):
             piece = min(PIECE, size - first)
-            from_here = None if last is None else lambda cut: last(slice(cut.start + first, cut.stop + first))
-            scaled(place + first, piece, from_here)
+            scaled(place + first, piece, lambda cut: last(slice(cut.start + first, cut.stop + first)))
             cut = pl.ds(pl.multiple_of(place + first, LANES), piece)
             stores.append(
                 pltpu.make_async_copy(out.at[:, cut], out_hbm.at[:, cut], out_sem.at[len(stores)])
             )
             stores[-1].start()
 
-    scale_and_store(own, met)
+    cut = pl.ds(own, met)
+    stores.append(
+        pltpu.make_async_copy(base_ref.at[:, cut], out_hbm.at[:, cut], out_sem.at[len(stores)])
+    )
+    stores[-1].start()
     scale_and_store(other, met, lambda cut: partner_ref[:, cut])
     scale_and_store(0, wide, lambda cut: left_ref[0, :, cut])
     scale_and_store(wide, wide, lambda cut: right_ref[0, :, cut])

time: 53.7 us -> 53.7 us (level)
  no operation moved by 1% of the time
where the time goes in v11:
time: 53.7 us; the launch traced here: 53.4 us
  starting transfers between devices  21.3 us (40%)
  Pallas kernels  20.8 us (39%)
  waiting for transfers between devices  9.92 us (18%)
  local copies, waits for them, and re-layouts  0.96 us (2%)
    ppermute x14, starting transfers between devices, swap(): return lax.ppermute(array, 'img', [(one, one ^ bit) for one in range(size)])  15.4 us
    ppermute x14, waiting for transfers between devices, swap(): return lax.ppermute(array, 'img', [(one, one ^ bit) for one in range(size)])  9.91 us
    pallas_call x1, Pallas kernels, estep(): pl.pallas_call(functools.partial(estep_kernel, blocks, share, near), in_s...  9.08 us
    ppermute x2, starting transfers between devices, shards(): tables = [held, lax.ppermute(held, 'slab', pairs)]  4.29 us
    pallas_call x2, Pallas kernels, partial_sums(): pl.pallas_call(functools.partial(sums_kernel, items, bool(relay)), in_spe...  3.13 us
    ppermute x1, starting transfers between devices, shards(): lax.ppermute(met[own_planes:, :met_wide] + sib_met[own_planes:, :met_wide...  1.64 us
    pallas_call x1, Pallas kernels, meet(): pl.pallas_call(functools.partial(meet_kernel, len(weights)), out_shape=[j...  1.63 us
    pallas_call x1, Pallas kernels, count_planes(): pl.pallas_call(functools.partial(count_kernel, slabs), in_specs=[vmem] *...  1.39 us
  transfers between devices with their start and end apart: 17, of which 7 were waited for; matrix products, arithmetic and copies ran while one was open for 2% of the time, Pallas kernels for 35%

profile of v11, /device:TPU:0, one launch (start us, length us, event | category | flops | bytes accessed | tf_op | source)
XLA Modules:
  0.0 53.4 jit_solution(536254558698098332)
XLA Ops:
  0.0 1.2 %early.1 = f32[64,1536]{1,0:T(8,128)S(1)} custom-call(s32[1,32768]{1,0:T(1,128)} %constant.5.clone.index_hbm, bf16[64,32768]{1,0:T(8,128)(2,1)} %image_hbm.2, f32[64,64]{1,0:T(8,128)} %ctf_ref.1), custom_call_target="tpu_custom_call" | custom-call | tf_op jit(solution)/shard_map/early/pallas_call | solution.py:274
  1.3 4.0 %collective-permute-start.3 = (f32[64,1536]{1,0:T(8,128)S(1)}, f32[64,1536]{1,0:T(8,128)S(1)}, u32[]{:S(2)}, u32[]{:S(2)}) collective-permute-start(f32[64,1536]{1,0:T(8,128)S(1)} %early.1), channel_id=1, source_target_pairs={{0,24},{4,28},{8,16},{12,20},{16,8},{20,12},{24,0},{28,4},{1,25},{... | collective-permute-start | bytes 1179656 | tf_op jit(solution)/shard_map/ppermute | solution.py:661
  5.2 9.1 %estep.1 = (f32[64,10240]{1,0:T(8,128)}, bf16[64,10240]{1,0:T(8,128)(2,1)}, f32[64,64]{1,0:T(8,128)S(1)}, bf16[64,1536]{1,0:T(8,128)(2,1)}, f32[64,1664]{1,0:T(8,128)}, /*index=5*/f32[64,1664]{1,0:T(8,128)S(1)}) custom-call(s32[1,16640]{1,0:T(1,128)} %constant.4.clone.index_hbm, bf16[64,32768]{1,0:T(8,128)(2,1)} %image_hbm.2, bf16[64,32768]{1,0:T(8,128)(2,1)} %bitcast.6, ...), custom_call_target="tpu_custom_call" | custom-call | tf_op jit(solution)/shard_map/estep/pallas_call | solution.py:198
  14.4 1.7 %collective-permute-start = (f32[64,64]{1,0:T(8,128)S(1)}, f32[64,64]{1,0:T(8,128)S(1)}, u32[]{:S(2)}, u32[]{:S(2)}) collective-permute-start(f32[64,64]{1,0:T(8,128)S(1)} %get-tuple-element.46), channel_id=1, source_target_pairs={{0,1},{1,0},{2,3},{3,2},{4,5},{5,4},{6,7},{7,6},{8,9},{9,8},{10,11... | collective-permute-start | bytes 49160 | tf_op jit(solution)/shard_map/ppermute | solution.py:704
  16.1 1.5 %collective-permute-start.5 = (f32[64,1664]{1,0:T(8,128)}, f32[64,1664]{1,0:T(8,128)}, u32[]{:S(2)}, u32[]{:S(2)}) collective-permute-start(f32[64,1664]{1,0:T(8,128)} %get-tuple-element.60), channel_id=1, source_target_pairs={{0,8},{4,12},{8,0},{12,4},{16,24},{20,28},{24,16},{28,20},{1,9},{5... | collective-permute-start | bytes 1277960 | tf_op jit(solution)/shard_map/ppermute | solution.py:661
  17.6 1.5 %collective-permute-start.6 = (f32[64,1664]{1,0:T(8,128)S(1)}, f32[64,1664]{1,0:T(8,128)}, u32[]{:S(2)}, u32[]{:S(2)}) collective-permute-start(f32[64,1664]{1,0:T(8,128)S(1)} %get-tuple-element.61), channel_id=1, source_target_pairs={{0,16},{4,20},{8,24},{12,28},{16,0},{20,4},{24,8},{28,12},{1,17},{... | collective-permute-start | bytes 1277960 | tf_op jit(solution)/shard_map/ppermute | solution.py:661
  19.2 2.6 %collective-permute-start.1 = (f32[64,128]{1,0:T(8,128)S(1)}, f32[64,128]{1,0:T(8,128)S(1)}, u32[]{:S(2)}, u32[]{:S(2)}) collective-permute-start(f32[64,128]{1,0:T(8,128)S(1)} %pad_maximum_fusion.refs_0_), channel_id=1, source_target_pairs={{0,2},{1,3},{2,0},{3,1},{4,6},{5,7},{6,4},{7,5},{8,10},{9,11},{10,... | collective-permute-start | bytes 98312 | tf_op jit(solution)/shard_map/ppermute | solution.py:704
  21.8 0.9 %reshape.17.list_ref = s32[64,128]{1,0:T(8,128)S(1)} reshape(s32[64,2,64]{2,1,0:T(2,128)} %param.10) | data formatting | bytes 65536 | tf_op jit(solution)/shard_map/reshape | solution.py:332
  22.7 1.4 %count.1 = (f32[2,64,128]{2,1,0:T(8,128)S(1)}, f32[64,128]{1,0:T(8,128)S(1)}) custom-call(f32[1,2]{1,0:T(1,128)S(1)} %bitcast.4, f32[1,64]{1,0:T(1,128)S(1)} %bitcast.5, s32[64,128]{1,0:T(8,128)S(1)} %reshape.17.list_ref), custom_call_target="tpu_custom_call" | custom-call | tf_op jit(solution)/shard_map/count/pallas_call | solution.py:319
  24.6 1.1 %gather.1.image_ref = bf16[2,128,1280]{2,1,0:T(8,128)(2,1)S(1)} custom-call(bf16[64,10240]{1,0:T(8,128)(2,1)} %get-tuple-element.64.keep_hbm, f32[64,10240]{1,0:T(8,128)S(1)} %collective-permute-done.4.got_hbm), custom_call_target="tpu_custom_call" | custom-call | tf_op jit(solution)/shard_map/gather/pallas_call | solution.py:395
  26.1 0.9 %collective-permute-start.7 = (f32[1,64,1408]{2,1,0:T(8,128)S(1)}, f32[1,64,1408]{2,1,0:T(8,128)S(1)}, u32[]{:S(2)}, u32[]{:S(2)}) collective-permute-start(f32[1,64,1408]{2,1,0:T(8,128)S(1)} %get-tuple-element.67), channel_id=1, source_target_pairs={{0,8},{4,12},{8,0},{12,4},{16,24},{20,28},{24,16},{28,20},{1,9},{5... | collective-permute-start | bytes 1081352 | tf_op jit(solution)/shard_map/ppermute | solution.py:661
  27.0 1.5 %collective-permute-start.8 = (f32[1,64,1408]{2,1,0:T(8,128)S(1)}, f32[1,64,1408]{2,1,0:T(8,128)S(1)}, u32[]{:S(2)}, u32[]{:S(2)}) collective-permute-start(f32[1,64,1408]{2,1,0:T(8,128)S(1)} %get-tuple-element.57), channel_id=1, source_target_pairs={{0,16},{4,20},{8,24},{12,28},{16,0},{20,4},{24,8},{28,12},{1,17},{... | collective-permute-start | bytes 1081352 | tf_op jit(solution)/shard_map/ppermute | solution.py:661
  28.5 1.2 %collective-permute-start.9 = (f32[64,128]{1,0:T(8,128)S(1)}, f32[64,128]{1,0:T(8,128)S(1)}, u32[]{:S(2)}, u32[]{:S(2)}) collective-permute-start(f32[64,128]{1,0:T(8,128)S(1)} %get-tuple-element.58.both_w_ref.refs_0_), channel_id=1, source_target_pairs={{0,24},{4,28},{8,16},{12,20},{16,8},{20,12},{24,0},{28,4},{1,25},{... | collective-permute-start | bytes 98312 | tf_op jit(solution)/shard_map/ppermute | solution.py:661
  29.7 1.4 %sums.2 = (f32[1,64,1408]{2,1,0:T(8,128)S(1)}, f32[1,64,1280]{2,1,0:T(8,128)S(1)}) custom-call(f32[64,64]{1,0:T(8,128)S(1)} %get-tuple-element.48.own_w_ref, f32[64,64]{1,0:T(8,128)S(1)} %collective-permute-done.2.sib_w_ref, bf16[64,10240]{1,0:T(8,128)(2,1)} %get-tuple-element.64.keep_hbm, f32[64,10240]{1,0:T(8,128)S(1)} %collective-permute-done.4.got_hbm, ...), custom_call_target="tpu_custom_call" | custom-call | tf_op jit(solution)/shard_map/sums/pallas_call | solution.py:477
  31.9 1.5 %collective-permute-start.13 = (f32[1,64,1280]{2,1,0:T(8,128)S(1)}, f32[1,64,1280]{2,1,0:T(8,128)S(1)}, u32[]{:S(2)}, u32[]{:S(2)}) collective-permute-start(f32[1,64,1280]{2,1,0:T(8,128)S(1)} %get-tuple-element.77), channel_id=1, source_target_pairs={{0,16},{4,20},{8,24},{12,28},{16,0},{20,4},{24,8},{28,12},{1,17},{... | collective-permute-start | bytes 983048 | tf_op jit(solution)/shard_map/ppermute | solution.py:661
  33.4 1.8 %sums.3 = (f32[2,64,1280]{2,1,0:T(8,128)S(1)}, f32[2,64,1280]{2,1,0:T(8,128)S(1)}) custom-call(f32[64,64]{1,0:T(8,128)S(1)} %get-tuple-element.48.own_w_ref, f32[64,64]{1,0:T(8,128)S(1)} %collective-permute-done.2.sib_w_ref, bf16[64,10240]{1,0:T(8,128)(2,1)} %get-tuple-element.64.keep_hbm, f32[64,10240]{1,0:T(8,128)S(1)} %collective-permute-done.4.got_hbm), custom_call_target="tpu_custom_call" | custom-call | tf_op jit(solution)/shard_map/sums/pallas_call | solution.py:477
  35.2 3.2 %collective-permute-done.9.refs_3_ = f32[64,128]{1,0:T(8,128)S(1)} collective-permute-done((f32[64,128]{1,0:T(8,128)S(1)}, f32[64,128]{1,0:T(8,128)S(1)}, u32[]{:S(2)}, u32[]{:S(2)}) %collective-permute-start.9) | collective-permute-done | bytes 32800 | tf_op jit(solution)/shard_map/ppermute | solution.py:661
  39.0 1.6 %meet.1 = (f32[128,768]{1,0:T(8,128)S(1)}, f32[128,768]{1,0:T(8,128)S(1)}) custom-call(f32[64,128]{1,0:T(8,128)S(1)} %get-tuple-element.58.both_w_ref.refs_0_, f32[1,64,1408]{2,1,0:T(8,128)S(1)} %collective-permute-done.7.refs_1_, f32[1,64,1408]{2,1,0:T(8,128)S(1)} %collective-permute-done.8.refs_2_, f32[64,128]{1,0:T(8,128)S(1)} %collective-permute-done.9.refs_3_, ...), custom_call_target="tpu_custom_call" | custom-call | tf_op jit(solution)/shard_map/meet/pallas_call | solution.py:516
  40.7 1.6 %collective-permute-start.14 = (f32[1,64,1280]{2,1,0:T(8,128)S(1)}, f32[1,64,1280]{2,1,0:T(8,128)S(1)}, u32[]{:S(2)}, u32[]{:S(2)}) collective-permute-start(f32[1,64,1280]{2,1,0:T(8,128)S(1)} %slice_add_fusion.1), channel_id=1, source_target_pairs={{0,16},{4,20},{8,24},{12,28},{16,0},{20,4},{24,8},{28,12},{1,17},{... | collective-permute-start | bytes 983048 | tf_op jit(solution)/shard_map/ppermute | solution.py:661
  43.0 1.6 %collective-permute-start.16 = (f32[64,768]{1,0:T(8,128)S(1)}, f32[64,768]{1,0:T(8,128)S(1)}, u32[]{:S(2)}, u32[]{:S(2)}) collective-permute-start(f32[64,768]{1,0:T(8,128)S(1)} %slice_add_fusion.2), channel_id=1, source_target_pairs={{0,1},{1,0},{2,3},{3,2},{4,5},{5,4},{6,7},{7,6},{8,9},{9,8},{10,11... | collective-permute-start | bytes 589832 | tf_op jit(solution)/shard_map/ppermute | solution.py:761
  45.3 1.0 %shells.1.shell_ref = f32[64,128]{1,0:T(8,128)S(1)} custom-call(f32[64,64]{1,0:T(8,128)S(1)} %copy-done.1, f32[64,128]{1,0:T(8,128)S(1)} %get-tuple-element.58.both_w_ref.refs_0_, f32[1,64,1408]{2,1,0:T(8,128)S(1)} %collective-permute-done.7.refs_1_, f32[1,64,1408]{2,1,0:T(8,128)S(1)} %collective-permute-done.8.refs_2_, ...), custom_call_target="tpu_custom_call" | custom-call | tf_op jit(solution)/shard_map/shells/pallas_call | solution.py:552
  46.3 1.2 %collective-permute-done.12.sib_shell_ref = f32[64,128]{1,0:T(8,128)S(1)} collective-permute-done((f32[64,128]{1,0:T(8,128)S(1)}, f32[64,128]{1,0:T(8,128)S(1)}, u32[]{:S(2)}, u32[]{:S(2)}) %collective-permute-start.12) | collective-permute-done | bytes 32800 | tf_op jit(solution)/shard_map/ppermute | solution.py:661
  48.1 4.0 %collective-permute-done.14.left_ref = f32[1,64,1280]{2,1,0:T(8,128)S(1)} collective-permute-done((f32[1,64,1280]{2,1,0:T(8,128)S(1)}, f32[1,64,1280]{2,1,0:T(8,128)S(1)}, u32[]{:S(2)}, u32[]{:S(2)}) %collective-permute-start.14) | collective-permute-done | bytes 327712 | tf_op jit(solution)/shard_map/ppermute | solution.py:661
  52.3 1.0 %finish.1 = f32[64,4096]{1,0:T(8,128)} custom-call(f32[64,4096]{1,0:T(8,128)S(1)} %get-tuple-element.79.base_ref, f32[64,4096]{1,0:T(8,128)S(1)} %get-tuple-element.80.scale_ref, f32[1,64,1280]{2,1,0:T(8,128)S(1)} %collective-permute-done.14.left_ref, f32[1,64,1280]{2,1,0:T(8,128)S(1)} %collective-permute-done.15.right_ref, ...), custom_call_target="tpu_custom_call" | custom-call | tf_op jit(solution)/shard_map/finish/pallas_call | solution.py:649
  (37 shorter events, 4.7 us)
Async XLA Ops:
  1.3 13.1 %collective-permute-start.3 = (f32[64,1536]{1,0:T(8,128)S(1)}, f32[64,1536]{1,0:T(8,128)S(1)}, u32[]{:S(2)}, u32[]{:S(2)}) collective-permute-start(f32[64,1536]{1,0:T(8,128)S(1)} %early.1), channel_id=1, source_target_pairs={{0,24},{4,28},{8,16},{12,20},{16,8},{20,12},{24,0},{28,4},{1,25},{... | collective-permute-start | bytes 1179656 | tf_op jit(solution)/shard_map/ppermute | solution.py:661
  5.2 17.5 %copy-start.2 = (f32[2]{0:T(128)S(1)}, f32[2]{0:T(128)}, u32[]{:S(2)}) copy-start(f32[2]{0:T(128)} %param.13) | copy-start | bytes 28
  5.2 17.5 %copy-start.3 = (f32[64]{0:T(128)S(1)}, f32[64]{0:T(128)}, u32[]{:S(2)}) copy-start(f32[64]{0:T(128)} %param.12) | copy-start | bytes 772
  14.3 11.8 %copy-start.4 = (f32[64,1536]{1,0:T(8,128)}, f32[64,1536]{1,0:T(8,128)S(1)}, u32[]{:S(2)}) copy-start(f32[64,1536]{1,0:T(8,128)S(1)} %collective-permute-done.3.refs_7_) | copy-start | bytes 1179652
  14.3 10.3 %collective-permute-start.4 = (f32[64,10240]{1,0:T(8,128)}, f32[64,10240]{1,0:T(8,128)S(1)}, u32[]{:S(2)}, u32[]{:S(2)}) collective-permute-start(f32[64,10240]{1,0:T(8,128)} %get-tuple-element.56), channel_id=1, source_target_pairs={{0,4},{4,0},{8,12},{12,8},{16,20},{20,16},{24,28},{28,24},{1,5},{5... | collective-permute-start | bytes 7864328 | tf_op jit(solution)/shard_map/ppermute | solution.py:661
  14.4 4.7 %collective-permute-start = (f32[64,64]{1,0:T(8,128)S(1)}, f32[64,64]{1,0:T(8,128)S(1)}, u32[]{:S(2)}, u32[]{:S(2)}) collective-permute-start(f32[64,64]{1,0:T(8,128)S(1)} %get-tuple-element.46), channel_id=1, source_target_pairs={{0,1},{1,0},{2,3},{3,2},{4,5},{5,4},{6,7},{7,6},{8,9},{9,8},{10,11... | collective-permute-start | bytes 49160 | tf_op jit(solution)/shard_map/ppermute | solution.py:704
  16.1 13.6 %collective-permute-start.5 = (f32[64,1664]{1,0:T(8,128)}, f32[64,1664]{1,0:T(8,128)}, u32[]{:S(2)}, u32[]{:S(2)}) collective-permute-start(f32[64,1664]{1,0:T(8,128)} %get-tuple-element.60), channel_id=1, source_target_pairs={{0,8},{4,12},{8,0},{12,4},{16,24},{20,28},{24,16},{28,20},{1,9},{5... | collective-permute-start | bytes 1277960 | tf_op jit(solution)/shard_map/ppermute | solution.py:661
  17.6 12.1 %collective-permute-start.6 = (f32[64,1664]{1,0:T(8,128)S(1)}, f32[64,1664]{1,0:T(8,128)}, u32[]{:S(2)}, u32[]{:S(2)}) collective-permute-start(f32[64,1664]{1,0:T(8,128)S(1)} %get-tuple-element.61), channel_id=1, source_target_pairs={{0,16},{4,20},{8,24},{12,28},{16,0},{20,4},{24,8},{28,12},{1,17},{... | collective-permute-start | bytes 1277960 | tf_op jit(solution)/shard_map/ppermute | solution.py:661
  19.2 4.9 %collective-permute-start.1 = (f32[64,128]{1,0:T(8,128)S(1)}, f32[64,128]{1,0:T(8,128)S(1)}, u32[]{:S(2)}, u32[]{:S(2)}) collective-permute-start(f32[64,128]{1,0:T(8,128)S(1)} %pad_maximum_fusion.refs_0_), channel_id=1, source_target_pairs={{0,2},{1,3},{2,0},{3,1},{4,6},{5,7},{6,4},{7,5},{8,10},{9,11},{10,... | collective-permute-start | bytes 98312 | tf_op jit(solution)/shard_map/ppermute | solution.py:704
  24.5 1.3 %collective-permute-start.2 = (f32[64,64]{1,0:T(8,128)S(1)}, f32[64,64]{1,0:T(8,128)S(1)}, u32[]{:S(2)}, u32[]{:S(2)}) collective-permute-start(f32[64,64]{1,0:T(8,128)S(1)} %get-tuple-element.48.own_w_ref), channel_id=1, source_target_pairs={{0,4},{4,0},{8,12},{12,8},{16,20},{20,16},{24,28},{28,24},{1,5},{5... | collective-permute-start | bytes 49160 | tf_op jit(solution)/shard_map/ppermute | solution.py:661
  26.1 12.3 %collective-permute-start.7 = (f32[1,64,1408]{2,1,0:T(8,128)S(1)}, f32[1,64,1408]{2,1,0:T(8,128)S(1)}, u32[]{:S(2)}, u32[]{:S(2)}) collective-permute-start(f32[1,64,1408]{2,1,0:T(8,128)S(1)} %get-tuple-element.67), channel_id=1, source_target_pairs={{0,8},{4,12},{8,0},{12,4},{16,24},{20,28},{24,16},{28,20},{1,9},{5... | collective-permute-start | bytes 1081352 | tf_op jit(solution)/shard_map/ppermute | solution.py:661
  27.0 12.0 %collective-permute-start.8 = (f32[1,64,1408]{2,1,0:T(8,128)S(1)}, f32[1,64,1408]{2,1,0:T(8,128)S(1)}, u32[]{:S(2)}, u32[]{:S(2)}) collective-permute-start(f32[1,64,1408]{2,1,0:T(8,128)S(1)} %get-tuple-element.57), channel_id=1, source_target_pairs={{0,16},{4,20},{8,24},{12,28},{16,0},{20,4},{24,8},{28,12},{1,17},{... | collective-permute-start | bytes 1081352 | tf_op jit(solution)/shard_map/ppermute | solution.py:661
  28.5 9.9 %collective-permute-start.9 = (f32[64,128]{1,0:T(8,128)S(1)}, f32[64,128]{1,0:T(8,128)S(1)}, u32[]{:S(2)}, u32[]{:S(2)}) collective-permute-start(f32[64,128]{1,0:T(8,128)S(1)} %get-tuple-element.58.both_w_ref.refs_0_), channel_id=1, source_target_pairs={{0,24},{4,28},{8,16},{12,20},{16,8},{20,12},{24,0},{28,4},{1,25},{... | collective-permute-start | bytes 98312 | tf_op jit(solution)/shard_map/ppermute | solution.py:661
  31.0 14.2 %collective-permute-start.11 = (f32[1,64,1408]{2,1,0:T(8,128)S(1)}, f32[1,64,1408]{2,1,0:T(8,128)S(1)}, u32[]{:S(2)}, u32[]{:S(2)}) collective-permute-start(f32[1,64,1408]{2,1,0:T(8,128)S(1)} %get-tuple-element.66), channel_id=1, source_target_pairs={{0,8},{4,12},{8,0},{12,4},{16,24},{20,28},{24,16},{28,20},{1,9},{5... | collective-permute-start | bytes 1081352 | tf_op jit(solution)/shard_map/ppermute | solution.py:661
  31.9 14.4 %collective-permute-start.13 = (f32[1,64,1280]{2,1,0:T(8,128)S(1)}, f32[1,64,1280]{2,1,0:T(8,128)S(1)}, u32[]{:S(2)}, u32[]{:S(2)}) collective-permute-start(f32[1,64,1280]{2,1,0:T(8,128)S(1)} %get-tuple-element.77), channel_id=1, source_target_pairs={{0,16},{4,20},{8,24},{12,28},{16,0},{20,4},{24,8},{28,12},{1,17},{... | collective-permute-start | bytes 983048 | tf_op jit(solution)/shard_map/ppermute | solution.py:661
  35.2 10.1 %copy-start.1 = (f32[64,64]{1,0:T(8,128)S(1)}, f32[64,64]{1,0:T(8,128)}, u32[]{:S(2)}) copy-start(f32[64,64]{1,0:T(8,128)} %ctf_ref.1) | copy-start | bytes 49156
  40.6 6.9 %copy-start = (s32[1,32768]{1,0:T(1,128)S(1)}, s32[1,32768]{1,0:T(1,128)}, u32[]{:S(2)}) copy-start(s32[1,32768]{1,0:T(1,128)} %constant.5.clone.index_hbm) | copy-start | bytes 393220
  40.6 2.3 %collective-permute-start.10 = (f32[128,768]{1,0:T(8,128)S(1)}, f32[128,768]{1,0:T(8,128)S(1)}, u32[]{:S(2)}, u32[]{:S(2)}) collective-permute-start(f32[128,768]{1,0:T(8,128)S(1)} %get-tuple-element.75), channel_id=1, source_target_pairs={{0,4},{4,0},{8,12},{12,8},{16,20},{20,16},{24,28},{28,24},{1,5},{5... | collective-permute-start | bytes 1179656 | tf_op jit(solution)/shard_map/ppermute | solution.py:661
  40.7 11.4 %collective-permute-start.14 = (f32[1,64,1280]{2,1,0:T(8,128)S(1)}, f32[1,64,1280]{2,1,0:T(8,128)S(1)}, u32[]{:S(2)}, u32[]{:S(2)}) collective-permute-start(f32[1,64,1280]{2,1,0:T(8,128)S(1)} %slice_add_fusion.1), channel_id=1, source_target_pairs={{0,16},{4,20},{8,24},{12,28},{16,0},{20,4},{24,8},{28,12},{1,17},{... | collective-permute-start | bytes 983048 | tf_op jit(solution)/shard_map/ppermute | solution.py:661
  42.4 9.9 %collective-permute-start.15 = (f32[1,64,1280]{2,1,0:T(8,128)S(1)}, f32[1,64,1280]{2,1,0:T(8,128)S(1)}, u32[]{:S(2)}, u32[]{:S(2)}) collective-permute-start(f32[1,64,1280]{2,1,0:T(8,128)S(1)} %slice_add_fusion), channel_id=1, source_target_pairs={{0,8},{4,12},{8,0},{12,4},{16,24},{20,28},{24,16},{28,20},{1,9},{5... | collective-permute-start | bytes 983048 | tf_op jit(solution)/shard_map/ppermute | solution.py:661
  43.0 9.3 %collective-permute-start.16 = (f32[64,768]{1,0:T(8,128)S(1)}, f32[64,768]{1,0:T(8,128)S(1)}, u32[]{:S(2)}, u32[]{:S(2)}) collective-permute-start(f32[64,768]{1,0:T(8,128)S(1)} %slice_add_fusion.2), channel_id=1, source_target_pairs={{0,1},{1,0},{2,3},{3,2},{4,5},{5,4},{6,7},{7,6},{8,9},{9,8},{10,11... | collective-permute-start | bytes 589832 | tf_op jit(solution)/shard_map/ppermute | solution.py:761
  46.2 1.3 %collective-permute-start.12 = (f32[64,128]{1,0:T(8,128)S(1)}, f32[64,128]{1,0:T(8,128)S(1)}, u32[]{:S(2)}, u32[]{:S(2)}) collective-permute-start(f32[64,128]{1,0:T(8,128)S(1)} %shells.1.shell_ref), channel_id=1, source_target_pairs={{0,4},{4,0},{8,12},{12,8},{16,20},{20,16},{24,28},{28,24},{1,5},{5... | collective-permute-start | bytes 98312 | tf_op jit(solution)/shard_map/ppermute | solution.py:661

commit v12 on v10

--- a/solution.py
+++ b/solution.py
@@ -12,7 +12,7 @@
 F32 = jnp.float32
 BF16 = jnp.bfloat16
 LANES = 128
-PIECE = 5 * LANES
+PIECE = 3 * LANES
 MIB = 1024 * 1024
 
 

time: 53.7 us -> 53.7 us (level)
  no operation moved by 1% of the time
where the time goes in v12:
time: 53.7 us; the launch traced here: 53.4 us
  starting transfers between devices  21.3 us (40%)
  Pallas kernels  20.8 us (39%)
  waiting for transfers between devices  9.92 us (18%)
  local copies, waits for them, and re-layouts  0.96 us (2%)
    ppermute x14, starting transfers between devices, swap(): return lax.ppermute(array, 'img', [(one, one ^ bit) for one in range(size)])  15.4 us
    ppermute x14, waiting for transfers between devices, swap(): return lax.ppermute(array, 'img', [(one, one ^ bit) for one in range(size)])  9.91 us
    pallas_call x1, Pallas kernels, estep(): pl.pallas_call(functools.partial(estep_kernel, blocks, share, near), in_s...  9.08 us
    ppermute x2, starting transfers between devices, shards(): tables = [held, lax.ppermute(held, 'slab', pairs)]  4.29 us
    pallas_call x2, Pallas kernels, partial_sums(): pl.pallas_call(functools.partial(sums_kernel, items, bool(relay)), in_spe...  3.13 us
    ppermute x1, starting transfers between devices, shards(): lax.ppermute(met[own_planes:, :met_wide] + sib_met[own_planes:, :met_wide...  1.64 us
    pallas_call x1, Pallas kernels, meet(): pl.pallas_call(functools.partial(meet_kernel, len(weights)), out_shape=[j...  1.63 us
    pallas_call x1, Pallas kernels, count_planes(): pl.pallas_call(functools.partial(count_kernel, slabs), in_specs=[vmem] *...  1.39 us
  transfers between devices with their start and end apart: 17, of which 7 were waited for; matrix products, arithmetic and copies ran while one was open for 2% of the time, Pallas kernels for 35%

profile of v12, /device:TPU:0, one launch (start us, length us, event | category | flops | bytes accessed | tf_op | source)
XLA Modules:
  0.0 53.4 jit_solution(13817446442765920121)
XLA Ops:
  0.0 1.2 %early.1 = f32[64,1536]{1,0:T(8,128)S(1)} custom-call(s32[1,32768]{1,0:T(1,128)} %constant.5.clone.index_hbm, bf16[64,32768]{1,0:T(8,128)(2,1)} %image_hbm.2, f32[64,64]{1,0:T(8,128)} %ctf_ref.1), custom_call_target="tpu_custom_call" | custom-call | tf_op jit(solution)/shard_map/early/pallas_call | solution.py:274
  1.3 4.0 %collective-permute-start.3 = (f32[64,1536]{1,0:T(8,128)S(1)}, f32[64,1536]{1,0:T(8,128)S(1)}, u32[]{:S(2)}, u32[]{:S(2)}) collective-permute-start(f32[64,1536]{1,0:T(8,128)S(1)} %early.1), channel_id=1, source_target_pairs={{0,24},{4,28},{8,16},{12,20},{16,8},{20,12},{24,0},{28,4},{1,25},{... | collective-permute-start | bytes 1179656 | tf_op jit(solution)/shard_map/ppermute | solution.py:659
  5.2 9.1 %estep.1 = (f32[64,10240]{1,0:T(8,128)}, bf16[64,10240]{1,0:T(8,128)(2,1)}, f32[64,64]{1,0:T(8,128)S(1)}, bf16[64,1536]{1,0:T(8,128)(2,1)}, f32[64,1664]{1,0:T(8,128)}, /*index=5*/f32[64,1664]{1,0:T(8,128)S(1)}) custom-call(s32[1,16640]{1,0:T(1,128)} %constant.4.clone.index_hbm, bf16[64,32768]{1,0:T(8,128)(2,1)} %image_hbm.2, bf16[64,32768]{1,0:T(8,128)(2,1)} %bitcast.6, ...), custom_call_target="tpu_custom_call" | custom-call | tf_op jit(solution)/shard_map/estep/pallas_call | solution.py:198
  14.4 1.7 %collective-permute-start = (f32[64,64]{1,0:T(8,128)S(1)}, f32[64,64]{1,0:T(8,128)S(1)}, u32[]{:S(2)}, u32[]{:S(2)}) collective-permute-start(f32[64,64]{1,0:T(8,128)S(1)} %get-tuple-element.46), channel_id=1, source_target_pairs={{0,1},{1,0},{2,3},{3,2},{4,5},{5,4},{6,7},{7,6},{8,9},{9,8},{10,11... | collective-permute-start | bytes 49160 | tf_op jit(solution)/shard_map/ppermute | solution.py:702
  16.1 1.5 %collective-permute-start.5 = (f32[64,1664]{1,0:T(8,128)}, f32[64,1664]{1,0:T(8,128)}, u32[]{:S(2)}, u32[]{:S(2)}) collective-permute-start(f32[64,1664]{1,0:T(8,128)} %get-tuple-element.60), channel_id=1, source_target_pairs={{0,8},{4,12},{8,0},{12,4},{16,24},{20,28},{24,16},{28,20},{1,9},{5... | collective-permute-start | bytes 1277960 | tf_op jit(solution)/shard_map/ppermute | solution.py:659
  17.6 1.5 %collective-permute-start.6 = (f32[64,1664]{1,0:T(8,128)S(1)}, f32[64,1664]{1,0:T(8,128)}, u32[]{:S(2)}, u32[]{:S(2)}) collective-permute-start(f32[64,1664]{1,0:T(8,128)S(1)} %get-tuple-element.61), channel_id=1, source_target_pairs={{0,16},{4,20},{8,24},{12,28},{16,0},{20,4},{24,8},{28,12},{1,17},{... | collective-permute-start | bytes 1277960 | tf_op jit(solution)/shard_map/ppermute | solution.py:659
  19.2 2.6 %collective-permute-start.1 = (f32[64,128]{1,0:T(8,128)S(1)}, f32[64,128]{1,0:T(8,128)S(1)}, u32[]{:S(2)}, u32[]{:S(2)}) collective-permute-start(f32[64,128]{1,0:T(8,128)S(1)} %pad_maximum_fusion.refs_0_), channel_id=1, source_target_pairs={{0,2},{1,3},{2,0},{3,1},{4,6},{5,7},{6,4},{7,5},{8,10},{9,11},{10,... | collective-permute-start | bytes 98312 | tf_op jit(solution)/shard_map/ppermute | solution.py:702
  21.8 0.9 %reshape.17.list_ref = s32[64,128]{1,0:T(8,128)S(1)} reshape(s32[64,2,64]{2,1,0:T(2,128)} %param.10) | data formatting | bytes 65536 | tf_op jit(solution)/shard_map/reshape | solution.py:332
  22.7 1.4 %count.1 = (f32[2,64,128]{2,1,0:T(8,128)S(1)}, f32[64,128]{1,0:T(8,128)S(1)}) custom-call(f32[1,2]{1,0:T(1,128)S(1)} %bitcast.4, f32[1,64]{1,0:T(1,128)S(1)} %bitcast.5, s32[64,128]{1,0:T(8,128)S(1)} %reshape.17.list_ref), custom_call_target="tpu_custom_call" | custom-call | tf_op jit(solution)/shard_map/count/pallas_call | solution.py:319
  24.6 1.1 %gather.1.image_ref = bf16[2,128,1280]{2,1,0:T(8,128)(2,1)S(1)} custom-call(bf16[64,10240]{1,0:T(8,128)(2,1)} %get-tuple-element.64.keep_hbm, f32[64,10240]{1,0:T(8,128)S(1)} %collective-permute-done.4.got_hbm), custom_call_target="tpu_custom_call" | custom-call | tf_op jit(solution)/shard_map/gather/pallas_call | solution.py:395
  26.1 0.9 %collective-permute-start.7 = (f32[1,64,1408]{2,1,0:T(8,128)S(1)}, f32[1,64,1408]{2,1,0:T(8,128)S(1)}, u32[]{:S(2)}, u32[]{:S(2)}) collective-permute-start(f32[1,64,1408]{2,1,0:T(8,128)S(1)} %get-tuple-element.67), channel_id=1, source_target_pairs={{0,8},{4,12},{8,0},{12,4},{16,24},{20,28},{24,16},{28,20},{1,9},{5... | collective-permute-start | bytes 1081352 | tf_op jit(solution)/shard_map/ppermute | solution.py:659
  27.0 1.5 %collective-permute-start.8 = (f32[1,64,1408]{2,1,0:T(8,128)S(1)}, f32[1,64,1408]{2,1,0:T(8,128)S(1)}, u32[]{:S(2)}, u32[]{:S(2)}) collective-permute-start(f32[1,64,1408]{2,1,0:T(8,128)S(1)} %get-tuple-element.57), channel_id=1, source_target_pairs={{0,16},{4,20},{8,24},{12,28},{16,0},{20,4},{24,8},{28,12},{1,17},{... | collective-permute-start | bytes 1081352 | tf_op jit(solution)/shard_map/ppermute | solution.py:659
  28.5 1.2 %collective-permute-start.9 = (f32[64,128]{1,0:T(8,128)S(1)}, f32[64,128]{1,0:T(8,128)S(1)}, u32[]{:S(2)}, u32[]{:S(2)}) collective-permute-start(f32[64,128]{1,0:T(8,128)S(1)} %get-tuple-element.58.both_w_ref.refs_0_), channel_id=1, source_target_pairs={{0,24},{4,28},{8,16},{12,20},{16,8},{20,12},{24,0},{28,4},{1,25},{... | collective-permute-start | bytes 98312 | tf_op jit(solution)/shard_map/ppermute | solution.py:659
  29.7 1.4 %sums.2 = (f32[1,64,1408]{2,1,0:T(8,128)S(1)}, f32[1,64,1280]{2,1,0:T(8,128)S(1)}) custom-call(f32[64,64]{1,0:T(8,128)S(1)} %get-tuple-element.48.own_w_ref, f32[64,64]{1,0:T(8,128)S(1)} %collective-permute-done.2.sib_w_ref, bf16[64,10240]{1,0:T(8,128)(2,1)} %get-tuple-element.64.keep_hbm, f32[64,10240]{1,0:T(8,128)S(1)} %collective-permute-done.4.got_hbm, ...), custom_call_target="tpu_custom_call" | custom-call | tf_op jit(solution)/shard_map/sums/pallas_call | solution.py:477
  31.9 1.5 %collective-permute-start.13 = (f32[1,64,1280]{2,1,0:T(8,128)S(1)}, f32[1,64,1280]{2,1,0:T(8,128)S(1)}, u32[]{:S(2)}, u32[]{:S(2)}) collective-permute-start(f32[1,64,1280]{2,1,0:T(8,128)S(1)} %get-tuple-element.77), channel_id=1, source_target_pairs={{0,16},{4,20},{8,24},{12,28},{16,0},{20,4},{24,8},{28,12},{1,17},{... | collective-permute-start | bytes 983048 | tf_op jit(solution)/shard_map/ppermute | solution.py:659
  33.4 1.8 %sums.3 = (f32[2,64,1280]{2,1,0:T(8,128)S(1)}, f32[2,64,1280]{2,1,0:T(8,128)S(1)}) custom-call(f32[64,64]{1,0:T(8,128)S(1)} %get-tuple-element.48.own_w_ref, f32[64,64]{1,0:T(8,128)S(1)} %collective-permute-done.2.sib_w_ref, bf16[64,10240]{1,0:T(8,128)(2,1)} %get-tuple-element.64.keep_hbm, f32[64,10240]{1,0:T(8,128)S(1)} %collective-permute-done.4.got_hbm), custom_call_target="tpu_custom_call" | custom-call | tf_op jit(solution)/shard_map/sums/pallas_call | solution.py:477
  35.2 3.2 %collective-permute-done.9.refs_3_ = f32[64,128]{1,0:T(8,128)S(1)} collective-permute-done((f32[64,128]{1,0:T(8,128)S(1)}, f32[64,128]{1,0:T(8,128)S(1)}, u32[]{:S(2)}, u32[]{:S(2)}) %collective-permute-start.9) | collective-permute-done | bytes 32800 | tf_op jit(solution)/shard_map/ppermute | solution.py:659
  39.0 1.6 %meet.1 = (f32[128,768]{1,0:T(8,128)S(1)}, f32[128,768]{1,0:T(8,128)S(1)}) custom-call(f32[64,128]{1,0:T(8,128)S(1)} %get-tuple-element.58.both_w_ref.refs_0_, f32[1,64,1408]{2,1,0:T(8,128)S(1)} %collective-permute-done.7.refs_1_, f32[1,64,1408]{2,1,0:T(8,128)S(1)} %collective-permute-done.8.refs_2_, f32[64,128]{1,0:T(8,128)S(1)} %collective-permute-done.9.refs_3_, ...), custom_call_target="tpu_custom_call" | custom-call | tf_op jit(solution)/shard_map/meet/pallas_call | solution.py:516
  40.7 1.6 %collective-permute-start.14 = (f32[1,64,1280]{2,1,0:T(8,128)S(1)}, f32[1,64,1280]{2,1,0:T(8,128)S(1)}, u32[]{:S(2)}, u32[]{:S(2)}) collective-permute-start(f32[1,64,1280]{2,1,0:T(8,128)S(1)} %slice_add_fusion.1), channel_id=1, source_target_pairs={{0,16},{4,20},{8,24},{12,28},{16,0},{20,4},{24,8},{28,12},{1,17},{... | collective-permute-start | bytes 983048 | tf_op jit(solution)/shard_map/ppermute | solution.py:659
  43.0 1.6 %collective-permute-start.16 = (f32[64,768]{1,0:T(8,128)S(1)}, f32[64,768]{1,0:T(8,128)S(1)}, u32[]{:S(2)}, u32[]{:S(2)}) collective-permute-start(f32[64,768]{1,0:T(8,128)S(1)} %slice_add_fusion.2), channel_id=1, source_target_pairs={{0,1},{1,0},{2,3},{3,2},{4,5},{5,4},{6,7},{7,6},{8,9},{9,8},{10,11... | collective-permute-start | bytes 589832 | tf_op jit(solution)/shard_map/ppermute | solution.py:759
  45.3 1.0 %shells.1.shell_ref = f32[64,128]{1,0:T(8,128)S(1)} custom-call(f32[64,64]{1,0:T(8,128)S(1)} %copy-done.1, f32[64,128]{1,0:T(8,128)S(1)} %get-tuple-element.58.both_w_ref.refs_0_, f32[1,64,1408]{2,1,0:T(8,128)S(1)} %collective-permute-done.7.refs_1_, f32[1,64,1408]{2,1,0:T(8,128)S(1)} %collective-permute-done.8.refs_2_, ...), custom_call_target="tpu_custom_call" | custom-call | tf_op jit(solution)/shard_map/shells/pallas_call | solution.py:552
  46.3 1.2 %collective-permute-done.12.sib_shell_ref = f32[64,128]{1,0:T(8,128)S(1)} collective-permute-done((f32[64,128]{1,0:T(8,128)S(1)}, f32[64,128]{1,0:T(8,128)S(1)}, u32[]{:S(2)}, u32[]{:S(2)}) %collective-permute-start.12) | collective-permute-done | bytes 32800 | tf_op jit(solution)/shard_map/ppermute | solution.py:659
  48.1 4.0 %collective-permute-done.14.left_ref = f32[1,64,1280]{2,1,0:T(8,128)S(1)} collective-permute-done((f32[1,64,1280]{2,1,0:T(8,128)S(1)}, f32[1,64,1280]{2,1,0:T(8,128)S(1)}, u32[]{:S(2)}, u32[]{:S(2)}) %collective-permute-start.14) | collective-permute-done | bytes 327712 | tf_op jit(solution)/shard_map/ppermute | solution.py:659
  52.3 1.1 %finish.1 = f32[64,4096]{1,0:T(8,128)} custom-call(f32[64,4096]{1,0:T(8,128)S(1)} %get-tuple-element.79.base_ref, f32[64,4096]{1,0:T(8,128)S(1)} %get-tuple-element.80.scale_ref, f32[1,64,1280]{2,1,0:T(8,128)S(1)} %collective-permute-done.14.left_ref, f32[1,64,1280]{2,1,0:T(8,128)S(1)} %collective-permute-done.15.right_ref, ...), custom_call_target="tpu_custom_call" | custom-call | tf_op jit(solution)/shard_map/finish/pallas_call | solution.py:647
  (37 shorter events, 4.7 us)
Async XLA Ops:
  1.3 13.1 %collective-permute-start.3 = (f32[64,1536]{1,0:T(8,128)S(1)}, f32[64,1536]{1,0:T(8,128)S(1)}, u32[]{:S(2)}, u32[]{:S(2)}) collective-permute-start(f32[64,1536]{1,0:T(8,128)S(1)} %early.1), channel_id=1, source_target_pairs={{0,24},{4,28},{8,16},{12,20},{16,8},{20,12},{24,0},{28,4},{1,25},{... | collective-permute-start | bytes 1179656 | tf_op jit(solution)/shard_map/ppermute | solution.py:659
  5.2 17.5 %copy-start.2 = (f32[2]{0:T(128)S(1)}, f32[2]{0:T(128)}, u32[]{:S(2)}) copy-start(f32[2]{0:T(128)} %param.13) | copy-start | bytes 28
  5.2 17.5 %copy-start.3 = (f32[64]{0:T(128)S(1)}, f32[64]{0:T(128)}, u32[]{:S(2)}) copy-start(f32[64]{0:T(128)} %param.12) | copy-start | bytes 772
  14.3 11.8 %copy-start.4 = (f32[64,1536]{1,0:T(8,128)}, f32[64,1536]{1,0:T(8,128)S(1)}, u32[]{:S(2)}) copy-start(f32[64,1536]{1,0:T(8,128)S(1)} %collective-permute-done.3.refs_7_) | copy-start | bytes 1179652
  14.3 10.3 %collective-permute-start.4 = (f32[64,10240]{1,0:T(8,128)}, f32[64,10240]{1,0:T(8,128)S(1)}, u32[]{:S(2)}, u32[]{:S(2)}) collective-permute-start(f32[64,10240]{1,0:T(8,128)} %get-tuple-element.56), channel_id=1, source_target_pairs={{0,4},{4,0},{8,12},{12,8},{16,20},{20,16},{24,28},{28,24},{1,5},{5... | collective-permute-start | bytes 7864328 | tf_op jit(solution)/shard_map/ppermute | solution.py:659
  14.4 4.7 %collective-permute-start = (f32[64,64]{1,0:T(8,128)S(1)}, f32[64,64]{1,0:T(8,128)S(1)}, u32[]{:S(2)}, u32[]{:S(2)}) collective-permute-start(f32[64,64]{1,0:T(8,128)S(1)} %get-tuple-element.46), channel_id=1, source_target_pairs={{0,1},{1,0},{2,3},{3,2},{4,5},{5,4},{6,7},{7,6},{8,9},{9,8},{10,11... | collective-permute-start | bytes 49160 | tf_op jit(solution)/shard_map/ppermute | solution.py:702
  16.1 13.6 %collective-permute-start.5 = (f32[64,1664]{1,0:T(8,128)}, f32[64,1664]{1,0:T(8,128)}, u32[]{:S(2)}, u32[]{:S(2)}) collective-permute-start(f32[64,1664]{1,0:T(8,128)} %get-tuple-element.60), channel_id=1, source_target_pairs={{0,8},{4,12},{8,0},{12,4},{16,24},{20,28},{24,16},{28,20},{1,9},{5... | collective-permute-start | bytes 1277960 | tf_op jit(solution)/shard_map/ppermute | solution.py:659
  17.6 12.1 %collective-permute-start.6 = (f32[64,1664]{1,0:T(8,128)S(1)}, f32[64,1664]{1,0:T(8,128)}, u32[]{:S(2)}, u32[]{:S(2)}) collective-permute-start(f32[64,1664]{1,0:T(8,128)S(1)} %get-tuple-element.61), channel_id=1, source_target_pairs={{0,16},{4,20},{8,24},{12,28},{16,0},{20,4},{24,8},{28,12},{1,17},{... | collective-permute-start | bytes 1277960 | tf_op jit(solution)/shard_map/ppermute | solution.py:659
  19.2 4.9 %collective-permute-start.1 = (f32[64,128]{1,0:T(8,128)S(1)}, f32[64,128]{1,0:T(8,128)S(1)}, u32[]{:S(2)}, u32[]{:S(2)}) collective-permute-start(f32[64,128]{1,0:T(8,128)S(1)} %pad_maximum_fusion.refs_0_), channel_id=1, source_target_pairs={{0,2},{1,3},{2,0},{3,1},{4,6},{5,7},{6,4},{7,5},{8,10},{9,11},{10,... | collective-permute-start | bytes 98312 | tf_op jit(solution)/shard_map/ppermute | solution.py:702
  24.5 1.3 %collective-permute-start.2 = (f32[64,64]{1,0:T(8,128)S(1)}, f32[64,64]{1,0:T(8,128)S(1)}, u32[]{:S(2)}, u32[]{:S(2)}) collective-permute-start(f32[64,64]{1,0:T(8,128)S(1)} %get-tuple-element.48.own_w_ref), channel_id=1, source_target_pairs={{0,4},{4,0},{8,12},{12,8},{16,20},{20,16},{24,28},{28,24},{1,5},{5... | collective-permute-start | bytes 49160 | tf_op jit(solution)/shard_map/ppermute | solution.py:659
  26.1 12.3 %collective-permute-start.7 = (f32[1,64,1408]{2,1,0:T(8,128)S(1)}, f32[1,64,1408]{2,1,0:T(8,128)S(1)}, u32[]{:S(2)}, u32[]{:S(2)}) collective-permute-start(f32[1,64,1408]{2,1,0:T(8,128)S(1)} %get-tuple-element.67), channel_id=1, source_target_pairs={{0,8},{4,12},{8,0},{12,4},{16,24},{20,28},{24,16},{28,20},{1,9},{5... | collective-permute-start | bytes 1081352 | tf_op jit(solution)/shard_map/ppermute | solution.py:659
  27.0 12.0 %collective-permute-start.8 = (f32[1,64,1408]{2,1,0:T(8,128)S(1)}, f32[1,64,1408]{2,1,0:T(8,128)S(1)}, u32[]{:S(2)}, u32[]{:S(2)}) collective-permute-start(f32[1,64,1408]{2,1,0:T(8,128)S(1)} %get-tuple-element.57), channel_id=1, source_target_pairs={{0,16},{4,20},{8,24},{12,28},{16,0},{20,4},{24,8},{28,12},{1,17},{... | collective-permute-start | bytes 1081352 | tf_op jit(solution)/shard_map/ppermute | solution.py:659
  28.5 9.9 %collective-permute-start.9 = (f32[64,128]{1,0:T(8,128)S(1)}, f32[64,128]{1,0:T(8,128)S(1)}, u32[]{:S(2)}, u32[]{:S(2)}) collective-permute-start(f32[64,128]{1,0:T(8,128)S(1)} %get-tuple-element.58.both_w_ref.refs_0_), channel_id=1, source_target_pairs={{0,24},{4,28},{8,16},{12,20},{16,8},{20,12},{24,0},{28,4},{1,25},{... | collective-permute-start | bytes 98312 | tf_op jit(solution)/shard_map/ppermute | solution.py:659
  31.0 14.2 %collective-permute-start.11 = (f32[1,64,1408]{2,1,0:T(8,128)S(1)}, f32[1,64,1408]{2,1,0:T(8,128)S(1)}, u32[]{:S(2)}, u32[]{:S(2)}) collective-permute-start(f32[1,64,1408]{2,1,0:T(8,128)S(1)} %get-tuple-element.66), channel_id=1, source_target_pairs={{0,8},{4,12},{8,0},{12,4},{16,24},{20,28},{24,16},{28,20},{1,9},{5... | collective-permute-start | bytes 1081352 | tf_op jit(solution)/shard_map/ppermute | solution.py:659
  31.9 14.4 %collective-permute-start.13 = (f32[1,64,1280]{2,1,0:T(8,128)S(1)}, f32[1,64,1280]{2,1,0:T(8,128)S(1)}, u32[]{:S(2)}, u32[]{:S(2)}) collective-permute-start(f32[1,64,1280]{2,1,0:T(8,128)S(1)} %get-tuple-element.77), channel_id=1, source_target_pairs={{0,16},{4,20},{8,24},{12,28},{16,0},{20,4},{24,8},{28,12},{1,17},{... | collective-permute-start | bytes 983048 | tf_op jit(solution)/shard_map/ppermute | solution.py:659
  35.2 10.1 %copy-start.1 = (f32[64,64]{1,0:T(8,128)S(1)}, f32[64,64]{1,0:T(8,128)}, u32[]{:S(2)}) copy-start(f32[64,64]{1,0:T(8,128)} %ctf_ref.1) | copy-start | bytes 49156
  40.6 6.9 %copy-start = (s32[1,32768]{1,0:T(1,128)S(1)}, s32[1,32768]{1,0:T(1,128)}, u32[]{:S(2)}) copy-start(s32[1,32768]{1,0:T(1,128)} %constant.5.clone.index_hbm) | copy-start | bytes 393220
  40.6 2.3 %collective-permute-start.10 = (f32[128,768]{1,0:T(8,128)S(1)}, f32[128,768]{1,0:T(8,128)S(1)}, u32[]{:S(2)}, u32[]{:S(2)}) collective-permute-start(f32[128,768]{1,0:T(8,128)S(1)} %get-tuple-element.75), channel_id=1, source_target_pairs={{0,4},{4,0},{8,12},{12,8},{16,20},{20,16},{24,28},{28,24},{1,5},{5... | collective-permute-start | bytes 1179656 | tf_op jit(solution)/shard_map/ppermute | solution.py:659
  40.7 11.4 %collective-permute-start.14 = (f32[1,64,1280]{2,1,0:T(8,128)S(1)}, f32[1,64,1280]{2,1,0:T(8,128)S(1)}, u32[]{:S(2)}, u32[]{:S(2)}) collective-permute-start(f32[1,64,1280]{2,1,0:T(8,128)S(1)} %slice_add_fusion.1), channel_id=1, source_target_pairs={{0,16},{4,20},{8,24},{12,28},{16,0},{20,4},{24,8},{28,12},{1,17},{... | collective-permute-start | bytes 983048 | tf_op jit(solution)/shard_map/ppermute | solution.py:659
  42.4 9.9 %collective-permute-start.15 = (f32[1,64,1280]{2,1,0:T(8,128)S(1)}, f32[1,64,1280]{2,1,0:T(8,128)S(1)}, u32[]{:S(2)}, u32[]{:S(2)}) collective-permute-start(f32[1,64,1280]{2,1,0:T(8,128)S(1)} %slice_add_fusion), channel_id=1, source_target_pairs={{0,8},{4,12},{8,0},{12,4},{16,24},{20,28},{24,16},{28,20},{1,9},{5... | collective-permute-start | bytes 983048 | tf_op jit(solution)/shard_map/ppermute | solution.py:659
  43.0 9.3 %collective-permute-start.16 = (f32[64,768]{1,0:T(8,128)S(1)}, f32[64,768]{1,0:T(8,128)S(1)}, u32[]{:S(2)}, u32[]{:S(2)}) collective-permute-start(f32[64,768]{1,0:T(8,128)S(1)} %slice_add_fusion.2), channel_id=1, source_target_pairs={{0,1},{1,0},{2,3},{3,2},{4,5},{5,4},{6,7},{7,6},{8,9},{9,8},{10,11... | collective-permute-start | bytes 589832 | tf_op jit(solution)/shard_map/ppermute | solution.py:759
  46.2 1.3 %collective-permute-start.12 = (f32[64,128]{1,0:T(8,128)S(1)}, f32[64,128]{1,0:T(8,128)S(1)}, u32[]{:S(2)}, u32[]{:S(2)}) collective-permute-start(f32[64,128]{1,0:T(8,128)S(1)} %shells.1.shell_ref), channel_id=1, source_target_pairs={{0,4},{4,0},{8,12},{12,8},{16,20},{20,16},{24,28},{28,24},{1,5},{5... | collective-permute-start | bytes 98312 | tf_op jit(solution)/shard_map/ppermute | solution.py:659
